TPU v7x, 128 devices: a whole 4x4x4 slice. The times are simulated.
128 devices in a mesh: table: 32 (over z, y, core), rep: 4 (over x).
Axes of the slice: x: 4, y: 4, z: 4, core: 2. Of those that a mesh axis runs over, the one named last changes fastest.
Arguments:
- titles: bfloat16 [3072, 64, 768], P(('table', 'rep')), may hold values from -6 to 6
- ln_gain: float32 [768], replicated, may hold values from 0.25 to 1.75
- w_up: bfloat16 [768, 3072], replicated, may hold values from -0.21875 to 0.21875
- w_down: bfloat16 [3072, 768], replicated, may hold values from -0.109375 to 0.109375
- w_proj: bfloat16 [768, 256], replicated, may hold values from -0.21875 to 0.21875
- sample_grad: bfloat16 [131072, 256], P(('table', 'rep')), may hold values from -6 to 6
- sample_item: int32 [131072], P(('table', 'rep')), may hold values from 0 to 3071
- sample_row: int32 [131072], P(('table', 'rep')), may hold values from 0 to 511
- row_ids: int32 [128, 512], P(('table', 'rep')), may hold values from 0 to 262143, as said below
- table: float32 [262144, 256], P(('table', 'rep')), may hold values from -6 to 6
- accum: float32 [262144, 256], P(('table', 'rep')), may hold values from 0.05 to 1
Outputs:
- d_titles: bfloat16 [3072, 64, 768], P(('table', 'rep'))
- grad_up: float32 [768, 3072], P(None, 'table')
- grad_down: float32 [3072, 768], P('table')
- grad_proj: float32 [768, 256], P('table')
- grad_gain: float32 [768], P('table')
- new_table: float32 [262144, 256], P(('table', 'rep'))
- new_accum: float32 [262144, 256], P(('table', 'rep'))
Inputs may be any that keep to these rules, and one draw needn't show every extreme that they name: `row_ids`: in each device's row list, entries k * 4 to (k + 1) * 4 - 1 are distinct rows of the block of 2048 rows held by device k, for every k.
All inputs are finite; a program needn't handle non-finite values.
Results may differ from a plain program's by a relative error of at most 0.0067.
Values sent between devices are 32-bit elements; how exact they have to be, the bound alone decides.
No kernel may reach another device: no remote copies, remote signals or barrier semaphores. Data moves between devices by JAX's collectives and lax.ppermute only.
A program may use at most 192 MiB of HBM per device.

v0:
```python
import jax
import jax.numpy as jnp
from jax import lax
from jax.sharding import PartitionSpec as P

GELU_C = 0.7978845608028654
NORM_EPS = 1e-05
LEARN_RATE = 0.1


def contract_first(left, right):
    return lax.dot_general(
        left, right, (((0,), (0,)), ((), ())), preferred_element_type=jnp.float32
    )


def contract_last(left, right):
    return lax.dot_general(
        left, right, (((1,), (1,)), ((), ())), preferred_element_type=jnp.float32
    )


def gelu_parts(pre):
    inner = GELU_C * (pre + 0.044715 * pre * pre * pre)
    tangent = jnp.tanh(inner)
    value = 0.5 * pre * (1.0 + tangent)
    slope = 0.5 * (1.0 + tangent) + 0.5 * pre * (1.0 - tangent * tangent) * GELU_C * (
        1.0 + 3.0 * 0.044715 * pre * pre
    )
    return (value, slope)


def encode_block(block, item_grad, ln_gain, w_up, w_down, w_proj):
    units, length, width = block.shape
    flat = block.reshape(units * length, width).astype(jnp.float32)
    center = jnp.mean(flat, axis=1, keepdims=True)
    offset = flat - center
    inv_scale = lax.rsqrt(jnp.mean(offset * offset, axis=1, keepdims=True) + NORM_EPS)
    normed = offset * inv_scale
    normed_b = (normed * ln_gain).astype(jnp.bfloat16)
    pre = jnp.dot(normed_b, w_up, preferred_element_type=jnp.float32)
    value, slope = gelu_parts(pre)
    mean_act = jnp.mean(value.reshape(units, length, -1), axis=1).astype(jnp.bfloat16)
    pooled = jnp.mean(flat.reshape(units, length, width), axis=1) + jnp.dot(
        mean_act, w_down, preferred_element_type=jnp.float32
    )
    pooled_b = pooled.astype(jnp.bfloat16)
    grad_b = item_grad.astype(jnp.bfloat16)
    proj_term = contract_first(pooled_b, grad_b)
    d_pooled = contract_last(grad_b, w_proj)
    d_pooled_b = d_pooled.astype(jnp.bfloat16)
    down_term = contract_first(mean_act, d_pooled_b)
    d_act = contract_last(d_pooled_b, w_down) / length
    d_pre = (
        (d_act[:, None, :] * slope.reshape(units, length, -1))
        .reshape(units * length, -1)
        .astype(jnp.bfloat16)
    )
    up_term = contract_first(normed_b, d_pre)
    d_normed = contract_last(d_pre, w_up)
    gain_term = jnp.sum(d_normed * normed, axis=0)
    d_hat = d_normed * ln_gain
    d_flat = inv_scale * (
        d_hat
        - jnp.mean(d_hat, axis=1, keepdims=True)
        - normed * jnp.mean(d_hat * normed, axis=1, keepdims=True)
    )
    d_block = d_flat.reshape(units, length, width) + (d_pooled / length)[:, None, :]
    return (d_block.astype(jnp.bfloat16), up_term, down_term, proj_term, gain_term)


def per_device(
    titles,
    ln_gain,
    w_up,
    w_down,
    w_proj,
    sample_grad,
    sample_item,
    sample_row,
    row_ids,
    table,
    accum,
):
    n_table = lax.axis_size("table")
    n_rep = lax.axis_size("rep")
    devices = n_table * n_rep
    units = titles.shape[0]
    wanted = lax.iota(jnp.int32, units * lax.axis_size(("table", "rep")))
    onehot = (sample_item[:, None] == wanted[None, :]).astype(jnp.bfloat16)
    item_grad = lax.psum_scatter(
        contract_first(onehot, sample_grad), ("table", "rep"), scatter_dimension=0, tiled=True
    )
    d_titles, up_term, down_term, proj_term, gain_term = encode_block(
        titles, item_grad, ln_gain, w_up, w_down, w_proj
    )
    terms = (up_term, down_term, proj_term, gain_term)
    table_share = (
        lax.psum_scatter(terms[0], "table", scatter_dimension=1, tiled=True),
        lax.psum_scatter(terms[1], "table", scatter_dimension=0, tiled=True),
        lax.psum_scatter(terms[2], "table", scatter_dimension=0, tiled=True),
        lax.psum_scatter(terms[3], "table", scatter_dimension=0, tiled=True),
    )
    grad_up, grad_down, grad_proj, grad_gain = lax.psum(
        (table_share[0], table_share[1], table_share[2], table_share[3]), "rep"
    )
    slot_count = row_ids.shape[1]
    capacity = slot_count // devices
    rows_here = table.shape[0]
    slot_hot = (sample_row[:, None] == lax.iota(jnp.int32, slot_count)[None, :]).astype(
        jnp.bfloat16
    )
    row_part = contract_first(slot_hot, sample_grad)
    local_rows = row_ids[0] % rows_here
    got_grads, got_rows = (
        lax.all_to_all(
            row_part.reshape(devices, capacity, -1),
            ("table", "rep"),
            split_axis=0,
            concat_axis=0,
            tiled=True,
        ),
        lax.all_to_all(
            local_rows.reshape(devices, capacity),
            ("table", "rep"),
            split_axis=0,
            concat_axis=0,
            tiled=True,
        ),
    )
    width_e = row_part.shape[1]
    row_grad = jax.ops.segment_sum(
        got_grads.reshape(-1, width_e), got_rows.reshape(-1), num_segments=rows_here
    )
    new_accum = accum + row_grad * row_grad
    new_table = table - LEARN_RATE * row_grad * lax.rsqrt(new_accum)
    return (d_titles, grad_up, grad_down, grad_proj, grad_gain, new_table, new_accum)


def solution(mesh):
    return jax.shard_map(
        per_device,
        mesh=mesh,
        in_specs=(
            P(("table", "rep"), None, None),
            P(),
            P(),
            P(),
            P(),
            P(("table", "rep"), None),
            P(("table", "rep")),
            P(("table", "rep")),
            P(("table", "rep"), None),
            P(("table", "rep"), None),
            P(("table", "rep"), None),
        ),
        out_specs=(
            P(("table", "rep"), None, None),
            P(None, "table"),
            P("table", None),
            P("table", None),
            P("table"),
            P(("table", "rep"), None),
            P(("table", "rep"), None),
        ),
        check_vma=False,
    )
```

profile of v0, /device:TPU:0, one launch (start us, length us, event | category | flops | bytes accessed | tf_op | source)
XLA Modules:
  0.0 593.5 jit_solution(2667952077021083210)
XLA Ops:
  7.2 1.0 copy-done
  8.2 5.9 %fusion.7 = f32[3072,256]{1,0:T(8,128)} fusion(bf16[1024,256]{1,0:T(8,128)(2,1)S(1)} %copy-done, s32[1024]{0:T(1024)} %param.17), kind=kOutput, calls=%fused_computation.12 | convolution fusion | flops 1613758464 | bytes 3674112 | tf_op jit(solution)/shard_map/dot_general | solution.py:12
  14.2 0.2 reduce-scatter.7.cloned.1.call-start
  14.4 0.4 convert_reduce_fusion.1
  14.8 0.1 div.29
  14.9 1.2 convert_reduce_fusion
  16.1 0.1 rsqrt.15
  16.2 2.0 multiply_convert_fusion
  18.2 208.3 %reduce-scatter.5.cloned.1.call-done = f32[24,256]{1,0:T(8,128)} async-done(((f32[3072,256]{1,0:T(8,128)}), f32[24,256]{1,0:T(8,128)}) %reduce-scatter.5.cloned.1.call-update) | async-done | bytes 24592 | tf_op jit(solution)/shard_map/reduce_scatter | solution.py:91
  226.6 1.1 broadcast_multiply_fusion
  227.7 3.7 convolution_multiply_fusion
  231.4 21.1 %multiply_multiply_fusion.1 = (f32[1536,3072]{1,0:T(8,128)}, bf16[1536,3072]{1,0:T(8,128)(2,1)S(1)}) fusion(f32[24,3072]{1,0:T(8,128)S(1)} %convolution_multiply_fusion, bf16[1536,768]{1,0:T(8,128)(2,1)S(1)} %copy-done.2, bf16[768,3072]{1,0:T(8,128)(2,1)} %param.13), kind=kOutput, calls=%fused_computation.10 | convolution fusion | flops 7342129152 | bytes 35684352 | tf_op jit(solution)/shard_map/dot_general | solution.py:41
  252.5 3.7 copy-done.3
  256.2 10.1 %fusion.28 = f32[768,3072]{0,1:T(8,128)} fusion(bf16[1536,768]{1,0:T(8,128)(2,1)S(1)} %copy-done.2, bf16[1536,3072]{1,0:T(8,128)(2,1)S(1)} %get-tuple-element.19), kind=kOutput, calls=%fused_computation.56 | convolution fusion | flops 7247757312 | bytes 21233664 | tf_op jit(solution)/shard_map/dot_general | solution.py:12
  266.4 0.3 reduce-scatter.9.cloned.1.call-start
  266.6 9.3 %reduce_sum.67 = f32[24,3072]{1,0:T(8,128)S(1)} reduce(f32[24,64,3072]{2,1,0:T(8,128)} %bitcast.31, f32[]{:T(128)} %constant.32.clone.1), dimensions={1}, to_apply=%region_7.0 | reduce | flops 4644864 | bytes 19169284 | tf_op jit(solution)/shard_map/reduce_sum | solution.py:43
  275.9 5.2 fusion.18
  281.1 0.5 broadcast.146
  281.6 0.2 copy-done.7
  281.8 0.7 reduce.8
  282.4 0.1 squeeze.3
  282.5 0.7 add_select_fusion
  283.2 5.9 all-to-all-start
  289.1 1.7 fusion.10
  290.8 2.0 reshape.137
  292.8 5.5 all-to-all-done
  298.3 5.7 all-to-all-start.1
  304.1 0.6 dynamic-slice
  305.4 0.8 reduce.9
  306.2 0.1 reshape.142
  306.3 10.7 %all-to-all-done.1 = f32[128,4,256]{2,1,0:T(4,128)} async-done(((f32[128,4,256]{2,1,0:T(4,128)}), f32[128,4,256]{2,1,0:T(4,128)}, u32[]{:S(2)}, u32[]{:S(2)}) %all-to-all-start.1) | async-done | bytes 524320 | tf_op jit(solution)/shard_map/all_to_all | solution.py:116
  316.9 2.0 reshape.144
  319.0 5.2 scatter_custom_fusion
  324.1 5.4 multiply_subtract_fusion
  329.5 4.4 fusion.12
  333.9 0.3 all-reduce.5.cloned.1.call-start
  334.3 14.0 %multiply_reduce_fusion = (f32[768]{0:T(1024)S(1)}, f32[1536]{0:T(1024)S(1)}, f32[1536]{0:T(1024)S(1)}, f32[1536,768]{1,0:T(8,128)}) fusion(bf16[24,64,768]{2,1,0:T(8,128)(2,1)S(1)} %copy-done.1, f32[1536]{0:T(1024)S(1)} %div.29, f32[1536]{0:T(1024)S(1)} %rsqrt.15, f32[768]{0:T(1024)S(1)} %copy-done.6, bf16[1536,3072]{1,0:T(8,128)(2,1)} %copy-done.3, ...), kind=kOutput, calls=%fused_computation.16 | convolution fusion | flops 7258370048 | bytes 21264384 | tf_op jit(solution)/shard_map/dot_general | solution.py:18
  348.3 11.2 %reduce-scatter.7.cloned.1.call-done = f32[768,96]{0,1:T(8,128)} async-done(((f32[768,3072]{0,1:T(8,128)}), f32[768,96]{0,1:T(8,128)}) %reduce-scatter.7.cloned.1.call-update) | async-done | bytes 294928 | tf_op jit(solution)/shard_map/reduce_scatter | solution.py:99
  359.5 99.1 %reduce-scatter.9.cloned.1.call-done = f32[96,768]{1,0:T(8,128)} async-done(((f32[3072,768]{1,0:T(8,128)}), f32[96,768]{1,0:T(8,128)}) %reduce-scatter.9.cloned.1.call-update) | async-done | bytes 294928 | tf_op jit(solution)/shard_map/reduce_scatter | solution.py:100
  458.6 4.5 subtract_multiply_fusion
  463.1 63.3 %all-reduce = f32[768]{0:T(1024)S(1)} all-reduce(f32[768]{0:T(1024)S(1)} %get-tuple-element.7), channel_id=6, replica_groups=mesh['table'=32,'rep'=4] {'table'}, use_global_device_ids=true, to_apply=%region_14.0.clone | all-reduce | flops 768 | bytes 6144
  526.4 0.1 dynamic-slice.1
  526.5 4.3 add_convert_fusion
  530.8 8.0 %reduce-scatter.11.cloned.1.call-done = f32[24,256]{1,0:T(8,128)} async-done(((f32[768,256]{1,0:T(8,128)}), f32[24,256]{1,0:T(8,128)}) %reduce-scatter.11.cloned.1.call-update) | async-done | bytes 24592 | tf_op jit(solution)/shard_map/reduce_scatter | solution.py:101
  538.7 18.2 %all-reduce.1 = (f32[24,256]{1,0:T(8,128)}, f32[24]{0:T(128)}) all-reduce(f32[24,256]{1,0:T(8,128)} %reduce-scatter.11.cloned.1.call-done, f32[24]{0:T(128)S(1)} %dynamic-slice.1), channel_id=1, replica_groups=mesh['table'=32,'rep'=4] {'rep'}, use_global_device_ids=true, to_apply=%region_12.0 | all-reduce | flops 6168 | bytes 49344 | tf_op jit(solution)/shard_map/psum | solution.py:104
  557.0 26.6 %all-reduce.5.cloned.1.call-done = (f32[768,96]{0,1:T(8,128)}, f32[96,768]{1,0:T(8,128)}) async-done(((f32[768,96]{0,1:T(8,128)}, f32[96,768]{1,0:T(8,128)}), (f32[768,96]{0,1:T(8,128)}, f32[96,768]{1,0:T(8,128)})) %all-reduce.5.cloned.1.call-update) | async-done | bytes 589840 | tf_op jit(solution)/shard_map/psum | solution.py:104
  583.6 1.7 copy.21
  585.3 1.7 copy.22
  (27 shorter events, 0.2 us)
Async XLA Ops:
  7.2 1.0 copy-start
  7.2 7.3 %copy-start.1 = (bf16[24,64,768]{2,1,0:T(8,128)(2,1)S(1)}, bf16[24,64,768]{2,1,0:T(8,128)(2,1)}, u32[]{:S(2)}) copy-start(bf16[24,64,768]{2,1,0:T(8,128)(2,1)} %param.11) | copy-start | bytes 7077892
  7.2 219.4 %reduce-scatter.5.cloned.1.call-start = ((), (), s32[]{:S(2)}) async-start(), calls=%async_computation.6 | async-start | bytes 3170304 | tf_op jit(solution)/shard_map/reduce_scatter | solution.py:91
  14.2 2.1 copy-start.6
  14.2 212.4 %copy-start.4 = (bf16[768,256]{1,0:T(8,128)(2,1)S(1)}, bf16[768,256]{1,0:T(8,128)(2,1)}, u32[]{:S(2)}) copy-start(bf16[768,256]{1,0:T(8,128)(2,1)} %param.15) | copy-start | bytes 1179652
  14.2 345.2 %reduce-scatter.7.cloned.1.call-start = ((), (), s32[]{:S(2)}) async-start(), calls=%async_computation.7 | async-start | bytes 9732096 | tf_op jit(solution)/shard_map/reduce_scatter | solution.py:99
  226.6 4.8 copy-start.2
  252.5 3.7 copy-start.3
  266.4 192.2 %reduce-scatter.9.cloned.1.call-start = ((), (), s32[]{:S(2)}) async-start(), calls=%async_computation.8 | async-start | bytes 9732096 | tf_op jit(solution)/shard_map/reduce_scatter | solution.py:100
  281.1 0.7 copy-start.7
  281.1 8.0 %copy-start.8 = (s32[1024]{0:T(1024)S(1)}, s32[1024]{0:T(1024)}, u32[]{:S(2)}) copy-start(s32[1024]{0:T(1024)} %param.18) | copy-start | bytes 12292
  281.1 23.1 %copy-start.9 = (u32[128]{0:T(128)S(1)}, u32[128]{0:T(128)}, u32[]{:S(2)}) copy-start(u32[128]{0:T(128)} %constant.49) | copy-start | bytes 1540
  283.2 15.1 %all-to-all-start = ((s32[128,1,4]{2,1,0:T(1,128)}), s32[128,1,4]{2,1,0:T(1,128)S(1)}, u32[]{:S(2)}, u32[]{:S(2)}) async-start(s32[128,1,4]{2,1,0:T(1,128)} %bitcast.4), calls=%async_computation.4 | async-start | bytes 131072 | tf_op jit(solution)/shard_map/all_to_all | solution.py:123
  298.3 18.6 %all-to-all-start.1 = ((f32[128,4,256]{2,1,0:T(4,128)}), f32[128,4,256]{2,1,0:T(4,128)}, u32[]{:S(2)}, u32[]{:S(2)}) async-start(f32[128,4,256]{2,1,0:T(4,128)} %reshape.137), calls=%async_computation.5 | async-start | bytes 1048576 | tf_op jit(solution)/shard_map/all_to_all | solution.py:116
  304.1 234.7 %reduce-scatter.11.cloned.1.call-start = ((), (), s32[]{:S(2)}) async-start(), calls=%async_computation.9 | async-start | bytes 811008 | tf_op jit(solution)/shard_map/reduce_scatter | solution.py:101
  324.1 5.4 copy-start.5
  333.9 249.7 %all-reduce.5.cloned.1.call-start = ((), (), s32[]{:S(2)}) async-start(), calls=%async_computation.10 | async-start | bytes 1179648 | tf_op jit(solution)/shard_map/psum | solution.py:104
Sparse Core Ops, SparseCore 0:
  14.3 212.2 reduce-scatter.4
  266.5 92.9 reduce-scatter.6
  363.7 94.8 reduce-scatter.8
  461.9 76.7 reduce-scatter.10
  541.0 42.5 all-reduce.4
where the time goes:
time: 594 us
  waiting for transfers between devices  370 us (62%)
  blocking collectives  81.5 us (14%)
  matrix products  67.2 us (11%)
  other arithmetic  34.4 us (6%)
  between operations  14.6 us (2%)
  local copies, waits for them, and re-layouts  13.9 us (2%)
  starting transfers between devices  12.5 us (2%)
    reduce_scatter x1, waiting for transfers between devices, per_device(): lax.psum_scatter(contract_first(onehot, sample_grad), ('table', 'rep'), s...  208 us
    reduce_scatter x1, waiting for transfers between devices, per_device(): lax.psum_scatter(terms[1], 'table', scatter_dimension=0, tiled=True)  99.1 us
    unnamed x1, blocking collectives  63.3 us
    dot_general x5, matrix products, contract_first(): lax.dot_general(left, right, (((0,), (0,)), ((), ())), preferred_element_...  27.3 us
    psum x1, waiting for transfers between devices, per_device(): lax.psum((table_share[0], table_share[1], table_share[2], table_share[3])...  26.6 us
    dot_general x1, matrix products, encode_block(): pre = jnp.dot(normed_b, w_up, preferred_element_type=jnp.float32)  21.1 us
    dot_general x3, matrix products, contract_last(): lax.dot_general(left, right, (((1,), (1,)), ((), ())), preferred_element_...  18.8 us
    psum x1, blocking collectives, per_device(): lax.psum((table_share[0], table_share[1], table_share[2], table_share[3])...  18.2 us
  transfers between devices with their start and end apart: 7, of which 7 were waited for; matrix products, arithmetic and copies ran while one was open for 11% of the time, Pallas kernels for 0%

commit v1 on v0

v1 whole, which is shorter than its diff:
```python
import functools

import jax
import jax.numpy as jnp
from jax import lax
from jax.experimental import pallas as pl
from jax.experimental.pallas import tpu as pltpu
from jax.sharding import Mesh
from jax.sharding import PartitionSpec as P

GELU_C = 0.7978845608028654
NORM_EPS = 1e-05
LEARN_RATE = 0.1
CHIPS = ("z", "y", "x")
DEVICES = ("z", "y", "c", "x")


def contract_first(left, right):
    return lax.dot_general(
        left, right, (((0,), (0,)), ((), ())), preferred_element_type=jnp.float32
    )


def contract_last(left, right):
    return lax.dot_general(
        left, right, (((1,), (1,)), ((), ())), preferred_element_type=jnp.float32
    )


def gelu_parts(pre):
    inner = GELU_C * (pre + 0.044715 * pre * pre * pre)
    tangent = jnp.tanh(inner)
    value = 0.5 * pre * (1.0 + tangent)
    slope = 0.5 * (1.0 + tangent) + 0.5 * pre * (1.0 - tangent * tangent) * GELU_C * (
        1.0 + 3.0 * 0.044715 * pre * pre
    )
    return (value, slope)


def swap_cores(block):
    return lax.ppermute(block, "c", [(0, 1), (1, 0)])


def factor_kernel(part_f, part_d, items_ref, columns_ref, proj_ref, down_out, proj_out):
    @pl.when(pl.program_id(0) == 0)
    def _():
        down_out[...] = jnp.zeros_like(down_out)
        proj_out[...] = jnp.zeros_like(proj_out)

    grad_b = items_ref[...].astype(jnp.bfloat16)
    d_pooled_b = contract_last(grad_b, proj_ref[...]).astype(jnp.bfloat16)
    columns = columns_ref[...].astype(jnp.bfloat16)
    down_out[...] += contract_first(columns, d_pooled_b)[:part_f]
    proj_out[...] += contract_first(columns, grad_b)[part_f : part_f + part_d]


def factor_products(all_items, columns, w_proj, part_f, part_d):
    items, width_e = all_items.shape
    width = w_proj.shape[0]
    step = items // 4
    return pl.pallas_call(
        functools.partial(factor_kernel, part_f, part_d),
        grid=(items // step,),
        in_specs=[
            pl.BlockSpec((step, width_e), lambda i: (i, 0)),
            pl.BlockSpec((step, columns.shape[1]), lambda i: (i, 0)),
            pl.BlockSpec((width, width_e), lambda i: (0, 0)),
        ],
        out_specs=[
            pl.BlockSpec((part_f, width), lambda i: (0, 0)),
            pl.BlockSpec((part_d, width_e), lambda i: (0, 0)),
        ],
        out_shape=[
            jax.ShapeDtypeStruct((part_f, width), jnp.float32),
            jax.ShapeDtypeStruct((part_d, width_e), jnp.float32),
        ],
        compiler_params=pltpu.CompilerParams(vmem_limit_bytes=32 << 20),
        cost_estimate=pl.CostEstimate(
            flops=2 * items * width_e * width, bytes_accessed=items * 2048, transcendentals=0
        ),
    )(all_items, columns, w_proj)


def per_device(
    titles,
    ln_gain,
    w_up,
    w_down,
    w_proj,
    sample_grad,
    sample_item,
    sample_row,
    row_ids,
    table,
    accum,
):
    n_z, n_y, n_c, n_x = (lax.axis_size(name) for name in DEVICES)
    chips = n_z * n_y * n_x
    devices = chips * n_c
    core = lax.axis_index("c")
    units, length, width = titles.shape
    hidden = w_up.shape[1]
    width_e = sample_grad.shape[1]
    part_f = hidden // devices
    part_d = width // devices

    place = lax.iota(jnp.int32, chips * units)
    chip, unit = place // units, place % units

    def item_part(of_core):
        wanted = (((chip // n_x) * n_c + of_core) * n_x + chip % n_x) * units + unit
        onehot = (sample_item[:, None] == wanted[None, :]).astype(jnp.bfloat16)
        return contract_first(onehot, sample_grad)

    got = swap_cores(item_part(1 - core))
    mine = (item_part(core) + got).reshape(chips, units, width_e)
    item_grad = jnp.sum(lax.all_to_all(mine, CHIPS, 0, 0, tiled=True), axis=0)

    flat = titles.reshape(units * length, width).astype(jnp.float32)
    center = jnp.mean(flat, axis=1, keepdims=True)
    offset = flat - center
    inv_scale = lax.rsqrt(jnp.mean(offset * offset, axis=1, keepdims=True) + NORM_EPS)
    normed = offset * inv_scale
    normed_b = (normed * ln_gain).astype(jnp.bfloat16)
    pre = jnp.dot(normed_b, w_up, preferred_element_type=jnp.float32)
    value, slope = gelu_parts(pre)
    mean_act = jnp.mean(value.reshape(units, length, -1), axis=1).astype(jnp.bfloat16)
    pooled = jnp.mean(flat.reshape(units, length, width), axis=1) + jnp.dot(
        mean_act, w_down, preferred_element_type=jnp.float32
    )
    pooled_b = pooled.astype(jnp.bfloat16)

    slot_count = row_ids.shape[1]
    capacity = slot_count // devices
    rows_here = table.shape[0]
    slot_hot = (sample_row[:, None] == lax.iota(jnp.int32, slot_count)[None, :]).astype(
        jnp.bfloat16
    )
    row_part = contract_first(slot_hot, sample_grad).reshape(devices, capacity * width_e)
    local_rows = (row_ids[0] % rows_here).reshape(devices, capacity).astype(jnp.float32)
    spare = -(part_f + part_d) % 32
    columns = jnp.concatenate(
        [
            mean_act.astype(jnp.float32).reshape(units, devices, part_f),
            pooled_b.astype(jnp.float32).reshape(units, devices, part_d),
            jnp.pad(local_rows.T[:, :, None], ((0, units - capacity), (0, 0), (0, spare - 1))),
        ],
        axis=2,
    )
    n_col = columns.shape[2]
    packed = jnp.concatenate(
        [row_part, jnp.swapaxes(columns, 0, 1).reshape(devices, units * n_col)], axis=1
    )
    arrived = lax.all_to_all(packed, DEVICES, 0, 0, tiled=True)
    got_grads = arrived[:, : capacity * width_e].reshape(slot_count, width_e)
    got_columns = arrived[:, capacity * width_e :].reshape(devices, units, n_col)
    got_rows = got_columns[:, :capacity, part_f + part_d].reshape(slot_count).astype(jnp.int32)
    row_grad = jax.ops.segment_sum(got_grads, got_rows, num_segments=rows_here)
    new_accum = accum + row_grad * row_grad
    new_table = table - LEARN_RATE * row_grad * lax.rsqrt(new_accum)

    grad_b = item_grad.astype(jnp.bfloat16)
    d_pooled = contract_last(grad_b, w_proj)
    d_pooled_b = d_pooled.astype(jnp.bfloat16)
    d_act = contract_last(d_pooled_b, w_down) / length
    d_pre = (
        (d_act[:, None, :] * slope.reshape(units, length, -1))
        .reshape(units * length, -1)
        .astype(jnp.bfloat16)
    )
    up_term = contract_first(d_pre, normed_b).reshape(n_z * n_y, n_c, n_x * part_f, width)
    first = core == 0
    got = swap_cores(jnp.where(first, up_term[:, 1], up_term[:, 0]))
    up_mine = (jnp.where(first, up_term[:, 0], up_term[:, 1]) + got).reshape(chips, part_f, width)
    up_share = jnp.sum(lax.all_to_all(up_mine, CHIPS, 0, 0, tiled=True), axis=0)
    grad_up = lax.all_gather(up_share, "x", axis=0, tiled=True).T

    all_items = lax.all_gather(item_grad, DEVICES, axis=0, tiled=True)
    down_share, proj_share = factor_products(
        all_items, got_columns.reshape(devices * units, n_col), w_proj, part_f, part_d
    )
    grad_down = lax.all_gather(down_share, "x", axis=0, tiled=True)
    grad_proj = lax.all_gather(proj_share, "x", axis=0, tiled=True)

    d_normed = contract_last(d_pre, w_up)
    gain_term = jnp.sum(d_normed * normed, axis=0)
    gains = lax.all_gather(gain_term, DEVICES, axis=0)
    t_index = (lax.axis_index("z") * n_y + lax.axis_index("y")) * n_c + core
    cut = width // (n_z * n_y * n_c)
    grad_gain = lax.dynamic_slice_in_dim(jnp.sum(gains, axis=0), t_index * cut, cut, 0)
    d_hat = d_normed * ln_gain
    d_flat = inv_scale * (
        d_hat
        - jnp.mean(d_hat, axis=1, keepdims=True)
        - normed * jnp.mean(d_hat * normed, axis=1, keepdims=True)
    )
    d_block = d_flat.reshape(units, length, width) + (d_pooled / length)[:, None, :]
    return (
        d_block.astype(jnp.bfloat16),
        grad_up,
        grad_down,
        grad_proj,
        grad_gain,
        new_table,
        new_accum,
    )


def solution(mesh):
    n_table, n_rep = mesh.devices.shape
    side = n_rep
    fine = Mesh(mesh.devices.reshape(n_table // (2 * side), side, 2, n_rep), DEVICES)
    split, tab = P(DEVICES), ("z", "y", "c")
    return jax.shard_map(
        per_device,
        mesh=fine,
        in_specs=(split, P(), P(), P(), P(), split, split, split, split, split, split),
        out_specs=(split, P(None, tab), P(tab), P(tab), P(tab), split, split),
        check_vma=False,
    )
```

time: 594 us -> 376 us (0.63)
  waiting for transfers between devices: 370 us -> 31 us
  blocking collectives: 81.5 us -> 142 us
  local copies, waits for them, and re-layouts: 13.9 us -> 40.7 us
  other arithmetic: 34.4 us -> 51.4 us
  starting transfers between devices: 12.5 us -> 23.8 us
    reduce_scatter x4 -> x0, waiting for transfers between devices: 327 us -> none  [the longest x1 208 us: per_device(): lax.psum_scatter(contract_first(onehot, sample_grad), ('table', 'rep'), s...]
    all_gather x0 -> x4, blocking collectives: none -> 142 us  [the longest x1 105 us: per_device(): gains = lax.all_gather(gain_term, DEVICES, axis=0)]
    unnamed x1 -> x0, blocking collectives: 63.3 us -> none
    psum x1 -> x0, waiting for transfers between devices: 26.6 us -> none  [per_device(): lax.psum((table_share[0], table_share[1], table_share[2], table_share[3])...]
    psum x1 -> x0, blocking collectives: 18.2 us -> none  [per_device(): lax.psum((table_share[0], table_share[1], table_share[2], table_share[3])...]
    dot_general x0 -> x1, local copies, waits for them, and re-layouts: none -> 12.7 us  [contract_first(): lax.dot_general(left, right, (((0,), (0,)), ((), ())), preferred_element_...]
    all_to_all x2 -> x3, starting transfers between devices: 11.6 us -> 23.5 us  [the longest x1 11.9 us: per_device(): item_grad = jnp.sum(lax.all_to_all(mine, CHIPS, 0, 0, tiled=True), axis=0)]
    all_to_all x2 -> x3, waiting for transfers between devices: 16.2 us -> 28 us  [the longest x1 19.1 us: per_device(): item_grad = jnp.sum(lax.all_to_all(mine, CHIPS, 0, 0, tiled=True), axis=0)]
  transfers between devices with their start and end apart: 7 -> 6, of which waited for: 7 -> 3; matrix products, arithmetic and copies ran while one was open for 11% -> 22% of each run, Pallas kernels for 0% -> 1%
where the time goes in v1:
time: 376 us; the launch traced here: 370 us
  blocking collectives  142 us (38%)
  matrix products  63.1 us (17%)
  other arithmetic  51.4 us (14%)
  local copies, waits for them, and re-layouts  40.7 us (11%)
  waiting for transfers between devices  31 us (8%)
  starting transfers between devices  23.8 us (6%)
  between operations  14.8 us (4%)
    all_gather x1, blocking collectives, per_device(): gains = lax.all_gather(gain_term, DEVICES, axis=0)  105 us
    dot_general x1, matrix products, per_device(): pre = jnp.dot(normed_b, w_up, preferred_element_type=jnp.float32)  23.5 us
    all_to_all x1, waiting for transfers between devices, per_device(): item_grad = jnp.sum(lax.all_to_all(mine, CHIPS, 0, 0, tiled=True), axis=0)  19.1 us
    dot_general x4, matrix products, contract_first(): lax.dot_general(left, right, (((0,), (0,)), ((), ())), preferred_element_...  18.6 us
    dot_general x3, matrix products, contract_last(): lax.dot_general(left, right, (((1,), (1,)), ((), ())), preferred_element_...  17.9 us
    dot_general x1, local copies, waits for them, and re-layouts, contract_first(): lax.dot_general(left, right, (((0,), (0,)), ((), ())), preferred_element_...  12.7 us
    all_gather x1, blocking collectives, per_device(): grad_down = lax.all_gather(down_share, 'x', axis=0, tiled=True)  12.7 us
    all_gather x1, blocking collectives, per_device(): grad_up = lax.all_gather(up_share, 'x', axis=0, tiled=True).T  12.3 us
  transfers between devices with their start and end apart: 6, of which 3 were waited for; matrix products, arithmetic and copies ran while one was open for 22% of the time, Pallas kernels for 1%

profile of v1, /device:TPU:0, one launch (start us, length us, event | category | flops | bytes accessed | tf_op | source)
XLA Modules:
  0.0 369.8 jit_solution(16691861767145440548)
XLA Ops:
  7.2 1.0 copy-done
  8.2 2.7 fusion.7
  11.5 3.0 collective-permute-done
  14.4 3.1 fusion.18
  17.6 11.9 %all-to-all-start = ((f32[64,24,256]{2,1,0:T(8,128)}), f32[64,24,256]{2,1,0:T(8,128)}, u32[]{:S(2)}, u32[]{:S(2)}) async-start(f32[64,24,256]{2,1,0:T(8,128)} %bitcast.83), calls=%async_computation | async-start | bytes 3145728 | tf_op jit(solution)/shard_map/all_to_all | solution.py:117
  29.6 1.2 convert_reduce_fusion
  30.9 2.0 multiply_convert_fusion
  32.9 2.0 multiply_convert_fusion.1
  34.9 19.1 %all-to-all-done = f32[64,24,256]{2,1,0:T(8,128)} async-done(((f32[64,24,256]{2,1,0:T(8,128)}), f32[64,24,256]{2,1,0:T(8,128)}, u32[]{:S(2)}, u32[]{:S(2)}) %all-to-all-start) | async-done | bytes 1572896 | tf_op jit(solution)/shard_map/all_to_all | solution.py:117
  54.0 1.5 reduce_sum.92
  55.8 3.8 %convolution_multiply_fusion = f32[24,3072]{1,0:T(8,128)S(1)} fusion(bf16[3072,768]{1,0:T(8,128)(2,1)} %param.14, bf16[24,768]{1,0:T(8,128)(2,1)S(1)} %get-tuple-element.22), kind=kOutput, calls=%fused_computation.31 | convolution fusion | flops 113319936 | bytes 5050368 | tf_op jit(solution)/shard_map/dot_general | solution.py:25
  59.7 23.5 %multiply_multiply_fusion.1 = (f32[1536,3072]{1,0:T(8,128)}, bf16[1536,3072]{1,0:T(8,128)(2,1)}) fusion(f32[24,3072]{1,0:T(8,128)S(1)} %convolution_multiply_fusion, bf16[1536,768]{1,0:T(8,128)(2,1)S(1)} %copy-done.6, bf16[768,3072]{1,0:T(8,128)(2,1)} %param.13), kind=kOutput, calls=%fused_computation.10 | convolution fusion | flops 7342129152 | bytes 35684352 | tf_op jit(solution)/shard_map/dot_general | solution.py:125
  83.2 12.7 %copy.69 = bf16[3072,1536]{1,0:T(8,128)(2,1)} copy(bf16[3072,1536]{0,1:T(8,128)(2,1)} %bitcast.75) | data formatting | bytes 18874368 | tf_op jit(solution)/shard_map/dot_general | solution.py:19
  95.9 11.1 %fusion.47 = f32[16,2,96,768]{3,2,1,0:T(8,128)S(1)} fusion(bf16[16,2,96,1536]{3,2,1,0:T(8,128)(2,1)} %bitcast.78, bf16[1536,768,1,1]{1,0,3,2:T(8,128)(2,1)} %bitcast.81), kind=kOutput, calls=%fused_computation.89 | convolution fusion | flops 7247757312 | bytes 21233664 | tf_op jit(solution)/shard_map/dot_general | solution.py:19
  107.0 3.2 select_bitcast_fusion
  110.2 1.9 copy-done.5
  114.2 0.9 copy.75
  115.1 1.7 fusion.21
  116.8 2.0 reshape.198
  118.8 9.1 %reduce_sum.96 = f32[24,3072]{1,0:T(8,128)S(1)} reduce(f32[24,64,3072]{2,1,0:T(8,128)} %bitcast.74, f32[]{:T(128)} %constant.88.clone.1), dimensions={1}, to_apply=%region_6.7 | reduce | flops 4644864 | bytes 19169284 | tf_op jit(solution)/shard_map/reduce_sum | solution.py:127
  127.9 0.7 fusion.30
  128.6 3.1 fusion.23
  131.7 0.9 copy.74
  132.6 1.8 reshape.208
  134.5 1.2 copy.77
  135.7 3.3 reshape.206
  139.0 2.6 copy.76
  141.5 1.7 select_maximum_fusion
  143.3 1.9 copy.79
  145.2 1.1 pad_maximum_fusion
  146.2 1.6 all_to_all.16
  147.8 5.7 %all-to-all-start.2 = ((f32[128,1,1792]{2,1,0:T(1,128)}), f32[128,1,1792]{2,1,0:T(1,128)}, u32[]{:S(2)}, u32[]{:S(2)}) async-start(f32[128,1,1792]{2,1,0:T(1,128)} %all_to_all.16), calls=%async_computation.2 | async-start | bytes 1835008 | tf_op jit(solution)/shard_map/all_to_all | solution.py:154
  153.5 8.3 %fusion.12 = f32[16,96,768]{2,1,0:T(8,128)} fusion(f32[16,96,768]{2,1,0:T(8,128)} %collective-permute-done.1, f32[16,2,96,768]{3,2,1,0:T(8,128)} %copy-done.5, pred[]{:T(512)S(6)} %eq.51), kind=kLoop, calls=%fused_computation.17 | loop fusion | flops 2359296 | bytes 18874368 | tf_op jit(solution)/shard_map/add | solution.py:174
  161.8 8.9 %all-to-all-done.2 = f32[128,1,1792]{2,1,0:T(1,128)} async-done(((f32[128,1,1792]{2,1,0:T(1,128)}), f32[128,1,1792]{2,1,0:T(1,128)}, u32[]{:S(2)}, u32[]{:S(2)}) %all-to-all-start.2) | async-done | bytes 917536 | tf_op jit(solution)/shard_map/all_to_all | solution.py:154
  170.7 5.9 %all-to-all-start.1 = ((f32[64,24,768]{2,1,0:T(8,128)}), f32[64,24,768]{2,1,0:T(8,128)}, u32[]{:S(2)}, u32[]{:S(2)}) async-start(f32[64,24,768]{2,1,0:T(8,128)} %bitcast.77), calls=%async_computation.1 | async-start | bytes 9437184 | tf_op jit(solution)/shard_map/all_to_all | solution.py:175
  176.6 13.8 %multiply_reduce_fusion = (f32[768]{0:T(1024)S(1)}, f32[1536]{0:T(1024)S(1)}, f32[1536]{0:T(1024)S(1)}, f32[1536,768]{1,0:T(8,128)}) fusion(bf16[24,64,768]{2,1,0:T(8,128)(2,1)S(1)} %copy-done.4, f32[1536]{0:T(1024)S(1)} %div.71, f32[1536]{0:T(1024)S(1)} %rsqrt.16, f32[768]{0:T(1024)S(1)} %copy-done.9, bf16[1536,3072]{1,0:T(8,128)(2,1)} %get-tuple-element.19, ...), kind=kOutput, calls=%fused_computation.20 | convolution fusion | flops 7258370048 | bytes 21264384 | tf_op jit(solution)/shard_map/dot_general | solution.py:25
  190.5 105.1 %all-gather.2 = f32[128,1,768]{2,1,0:T(1,128)S(1)} all-gather(f32[1,1,768]{2,1,0:T(1,128)S(1)} %reshape.221), channel_id=2, replica_groups=mesh['z'=4,'y'=4,'c'=2,'x'=4] {'z','y','c','x'}, dimensions={0}, use_global_device_ids=true | all-gather | bytes 396288 | tf_op jit(solution)/shard_map/all_gather | solution.py:187
  296.4 3.9 %subtract_multiply_fusion = f32[1536,768]{1,0:T(8,128)S(1)} fusion(bf16[24,64,768]{2,1,0:T(8,128)(2,1)S(1)} %copy-done.4, f32[1536,768]{1,0:T(8,128)} %get-tuple-element.20, f32[1536]{0:T(1024)S(1)} %get-tuple-element.23, f32[1536]{0:T(1024)S(1)} %get-tuple-element.24, f32[768]{0:T(1024)S(1)} %copy-done.9, f32[1536]{0:T(1024)S(1)} %div.71, f32[1536]{0:T(1024)S(1)} %rsqrt.16), kind=kLoop, calls=%fused_computation.24 | loop fusion | flops 9437184 | bytes 11824128 | tf_op jit(solution)/shard_map/mul | solution.py:192
  300.3 2.0 add_convert_fusion
  302.3 2.4 copy.80
  306.0 4.7 %scatter_custom_fusion = f32[2048,256]{1,0:T(8,128)} fusion(s32[512]{0:T(512)S(1)} %reshape.211, f32[512,256]{1,0:T(8,128)S(1)} %reshape.213, f32[]{:T(128)} %constant.88.clone.1), kind=kCustom, calls=%fused_computation.44 | custom fusion | flops 131072 | bytes 2097156 | tf_op jit(solution)/shard_map/scatter-add | solution.py:158
  310.7 5.3 %multiply_subtract_fusion = (f32[2048,256]{1,0:T(8,128)}, f32[2048,256]{1,0:T(8,128)}) fusion(f32[2048,256]{1,0:T(8,128)} %param.20, f32[2048,256]{1,0:T(8,128)} %scatter_custom_fusion, f32[2048,256]{1,0:T(8,128)} %param.21), kind=kLoop, calls=%fused_computation.37 | loop fusion | flops 2621440 | bytes 10485760 | tf_op jit(solution)/shard_map/sub | solution.py:160
  316.1 1.9 copy-done.2
  318.0 3.0 shard_map.162
  320.9 11.9 %all-gather.1 = f32[4,6,256]{2,1,0:T(8,128)S(1)} all-gather(f32[1,6,256]{2,1,0:T(8,128)S(1)} %bitcast.73), channel_id=1, replica_groups=mesh['z'=4,'y'=4,'c'=2,'x'=4] {'x'}, dimensions={0}, use_global_device_ids=true | all-gather | bytes 30720 | tf_op jit(solution)/shard_map/all_gather | solution.py:183
  333.5 12.7 %all_gather.20 = f32[96,768]{1,0:T(8,128)S(1)} all-gather(f32[24,768]{1,0:T(8,128)S(1)} %get-tuple-element.9), channel_id=1, replica_groups=mesh['z'=4,'y'=4,'c'=2,'x'=4] {'x'}, dimensions={0}, use_global_device_ids=true | all-gather | bytes 368640 | tf_op jit(solution)/shard_map/all_gather | solution.py:182
  346.1 2.6 reduce_sum.95
  348.7 12.3 %all_gather.18 = f32[96,768]{1,0:T(8,128)S(1)} all-gather(f32[24,768]{1,0:T(8,128)S(1)} %reduce_sum.95), channel_id=1, replica_groups=mesh['z'=4,'y'=4,'c'=2,'x'=4] {'x'}, dimensions={0}, use_global_device_ids=true | all-gather | bytes 368640 | tf_op jit(solution)/shard_map/all_gather | solution.py:176
  (59 shorter events, 7.4 us)
Async XLA Ops:
  7.2 1.1 copy-start
  7.2 3.9 %copy-start.4 = (bf16[24,64,768]{2,1,0:T(8,128)(2,1)S(1)}, bf16[24,64,768]{2,1,0:T(8,128)(2,1)}, u32[]{:S(2)}) copy-start(bf16[24,64,768]{2,1,0:T(8,128)(2,1)} %param.11) | copy-start | bytes 7077892
  8.2 6.2 %copy-start.11 = (s32[1024]{0:T(1024)S(1)}, s32[1024]{0:T(1024)}, u32[]{:S(2)}) copy-start(s32[1024]{0:T(1024)} %param.17) | copy-start | bytes 12292
  11.0 3.5 collective-permute-start
  17.6 13.3 %copy-start.9 = (f32[768]{0:T(1024)S(1)}, f32[768]{0:T(1024)}, u32[]{:S(2)}) copy-start(f32[768]{0:T(1024)} %param.12) | copy-start | bytes 9220
  17.6 36.5 %all-to-all-start = ((f32[64,24,256]{2,1,0:T(8,128)}), f32[64,24,256]{2,1,0:T(8,128)}, u32[]{:S(2)}, u32[]{:S(2)}) async-start(f32[64,24,256]{2,1,0:T(8,128)} %bitcast.83), calls=%async_computation | async-start | bytes 3145728 | tf_op jit(solution)/shard_map/all_to_all | solution.py:117
  29.4 286.6 %all-gather.5.cloned.1.call-start = ((), (), s32[]{:S(2)}) async-start(), calls=%async_computation.3 | async-start | bytes 3170304 | tf_op jit(solution)/shard_map/all_gather | solution.py:178
  30.9 24.7 %copy-start.3 = (bf16[768,256]{1,0:T(8,128)(2,1)S(1)}, bf16[768,256]{1,0:T(8,128)(2,1)}, u32[]{:S(2)}) copy-start(bf16[768,256]{1,0:T(8,128)(2,1)} %proj_ref.1) | copy-start | bytes 1179652
  55.6 27.6 %copy-start.8 = (f32[24,256]{1,0:T(8,128)}, f32[24,256]{1,0:T(8,128)S(1)}, u32[]{:S(2)}) copy-start(f32[24,256]{1,0:T(8,128)S(1)} %reduce_sum.92) | copy-start | bytes 73732
  55.6 4.1 %copy-start.6 = (bf16[1536,768]{1,0:T(8,128)(2,1)S(1)}, bf16[1536,768]{1,0:T(8,128)(2,1)}, u32[]{:S(2)}) copy-start(bf16[1536,768]{1,0:T(8,128)(2,1)} %multiply_convert_fusion.1) | copy-start | bytes 7077892
  107.0 5.1 %copy-start.5 = (f32[16,2,96,768]{3,2,1,0:T(8,128)}, f32[16,2,96,768]{3,2,1,0:T(8,128)S(1)}, u32[]{:S(2)}) copy-start(f32[16,2,96,768]{3,2,1,0:T(8,128)S(1)} %fusion.47) | copy-start | bytes 28311556
  107.0 5.8 %copy-start.10 = (s32[1,512]{1,0:T(1,128)S(1)}, s32[1,512]{1,0:T(1,128)}, u32[]{:S(2)}) copy-start(s32[1,512]{1,0:T(1,128)} %param.19) | copy-start | bytes 6148
  107.0 8.1 %copy-start.12 = (s32[1024]{0:T(1024)S(1)}, s32[1024]{0:T(1024)}, u32[]{:S(2)}) copy-start(s32[1024]{0:T(1024)} %param.18) | copy-start | bytes 12292
  112.1 41.4 %collective-permute-start.1 = (f32[16,96,768]{2,1,0:T(8,128)}, f32[16,96,768]{2,1,0:T(8,128)}, u32[]{:S(2)}, u32[]{:S(2)}) collective-permute-start(f32[16,96,768]{2,1,0:T(8,128)} %select_bitcast_fusion), channel_id=1, source_target_pairs={{0,4},{4,0},{1,5},{5,1},{2,6},{6,2},{3,7},{7,3},{8,12},{12,8},{9,1... | collective-permute-start | bytes 14155784 | tf_op jit(solution)/shard_map/ppermute | solution.py:41
  131.7 13.5 %copy-start.7 = (f32[128,1024]{1,0:T(8,128)S(1)}, f32[128,1024]{1,0:T(8,128)}, u32[]{:S(2)}) copy-start(f32[128,1024]{1,0:T(8,128)} %reshape.198) | copy-start | bytes 1572868
  147.8 22.9 %all-to-all-start.2 = ((f32[128,1,1792]{2,1,0:T(1,128)}), f32[128,1,1792]{2,1,0:T(1,128)}, u32[]{:S(2)}, u32[]{:S(2)}) async-start(f32[128,1,1792]{2,1,0:T(1,128)} %all_to_all.16), calls=%async_computation.2 | async-start | bytes 1835008 | tf_op jit(solution)/shard_map/all_to_all | solution.py:154
  170.7 175.5 %all-to-all-start.1 = ((f32[64,24,768]{2,1,0:T(8,128)}), f32[64,24,768]{2,1,0:T(8,128)}, u32[]{:S(2)}, u32[]{:S(2)}) async-start(f32[64,24,768]{2,1,0:T(8,128)} %bitcast.77), calls=%async_computation.1 | async-start | bytes 9437184 | tf_op jit(solution)/shard_map/all_to_all | solution.py:175
  310.7 51.7 %copy-start.1 = (bf16[1024,256]{1,0:T(8,128)(2,1)S(1)}, bf16[1024,256]{1,0:T(8,128)(2,1)}, u32[]{:S(2)}) copy-start(bf16[1024,256]{1,0:T(8,128)(2,1)} %param.16) | copy-start | bytes 1572868
  316.1 1.9 copy-start.2
Sparse Core Ops, SparseCore 0:
  119.0 72.3 all-gather.4

commit v2 on v1

v2 whole, which is shorter than its diff:
```python
import functools
import math

import jax
import jax.numpy as jnp
from jax import lax
from jax.experimental import pallas as pl
from jax.experimental.pallas import tpu as pltpu
from jax.sharding import Mesh
from jax.sharding import PartitionSpec as P

GELU_C = 0.7978845608028654
GELU_K = 0.044715
NORM_EPS = 1e-05
LEARN_RATE = 0.1
CHIPS = ("z", "y", "x")
GROUP = ("z", "y", "c")
DEVICES = ("z", "y", "c", "x")
VMEM = 48 << 20


def contract_first(left, right):
    return lax.dot_general(
        left, right, (((0,), (0,)), ((), ())), preferred_element_type=jnp.float32
    )


def contract_last(left, right):
    return lax.dot_general(
        left, right, (((1,), (1,)), ((), ())), preferred_element_type=jnp.float32
    )


def cost(flops, moved, transcendentals=0):
    return pl.CostEstimate(flops=flops, bytes_accessed=moved, transcendentals=transcendentals)


def swap_cores(block):
    return lax.ppermute(block, "c", [(0, 1), (1, 0)])


def along(block, name, step):
    size = lax.axis_size(name)
    return lax.ppermute(block, name, [(i, i ^ step) for i in range(size)])


def partners(name, second):
    sizes = [lax.axis_size(n) for n in DEVICES]
    at = DEVICES.index(name)
    pairs = []
    for index in range(math.prod(sizes)):
        place, rest = [], index
        for size in reversed(sizes):
            place.insert(0, rest % size)
            rest //= size
        place[at] ^= 1 if (place[DEVICES.index("c")] == 1) == second else 3
        to = 0
        for size, p in zip(sizes, place):
            to = to * size + p
        pairs.append((index, to))
    return pairs


def slot_of(core, here, size):
    block = lax.iota(jnp.int32, size) ^ here
    one = jnp.where(block == 0, 0, jnp.where(block == 1, 2, jnp.where(block == 2, 3, 1)))
    two = jnp.where(block < 2, block, 5 - block)
    return jnp.where(core == 0, one, two)


def halve(parts, names, second, also=()):
    kept, sent = [], []
    for part, name in zip(parts, names):
        dim = ("z", "y", "x").index(name)
        middle = part.shape[dim] // 2
        kept.append(lax.slice_in_dim(part, 0, middle, axis=dim))
        sent.append(
            lax.ppermute(
                lax.slice_in_dim(part, middle, None, axis=dim), DEVICES, partners(name, second)
            )
        )
    if also:
        sent, also = lax.optimization_barrier((sent, also))
    return [k + s for k, s in zip(kept, sent)], also


def layer_norm(rows):
    center = jnp.mean(rows, axis=1, keepdims=True)
    offset = rows - center
    inv_scale = lax.rsqrt(jnp.mean(offset * offset, axis=1, keepdims=True) + NORM_EPS)
    return offset * inv_scale, inv_scale


def forward_kernel(units, titles_ref, gain_ref, w_ref, normed_ref, slope_ref, act_ref, mean_ref):
    rows, width = titles_ref.shape
    length = rows // units
    step = 8 * length

    @pl.when(pl.program_id(0) == 0)
    def _():
        for r in range(units // 8):
            block = titles_ref[r * step : (r + 1) * step, :].astype(jnp.float32)
            normed, _ = layer_norm(block)
            normed_ref[r * step : (r + 1) * step, :] = (normed * gain_ref[...]).astype(jnp.bfloat16)
            mean_ref[r * 8 : (r + 1) * 8, :] = jnp.mean(block.reshape(8, length, width), axis=1)

    for r in range(units // 8):
        pre = jnp.dot(
            normed_ref[r * step : (r + 1) * step, :],
            w_ref[...],
            preferred_element_type=jnp.float32,
        )
        square = pre * pre
        tangent = jnp.tanh(pre * (GELU_C + (GELU_C * GELU_K) * square))
        half = 0.5 + 0.5 * tangent
        value = pre * half
        slope = half + value * (1.0 - tangent) * (GELU_C + (3.0 * GELU_C * GELU_K) * square)
        slope_ref[r * step : (r + 1) * step, :] = slope.astype(jnp.bfloat16)
        act_ref[r * 8 : (r + 1) * 8, :] = jnp.mean(value.reshape(8, length, -1), axis=1)


def forward(titles, ln_gain, w_up):
    units, length, width = titles.shape
    rows, hidden = units * length, w_up.shape[1]
    block = 512
    return pl.pallas_call(
        functools.partial(forward_kernel, units),
        grid=(hidden // block,),
        in_specs=[
            pl.BlockSpec((rows, width), lambda i: (0, 0)),
            pl.BlockSpec((1, width), lambda i: (0, 0)),
            pl.BlockSpec((width, block), lambda i: (0, i)),
        ],
        out_specs=[
            pl.BlockSpec((rows, width), lambda i: (0, 0)),
            pl.BlockSpec((rows, block), lambda i: (0, i)),
            pl.BlockSpec((units, block), lambda i: (0, i)),
            pl.BlockSpec((units, width), lambda i: (0, 0)),
        ],
        out_shape=[
            jax.ShapeDtypeStruct((rows, width), jnp.bfloat16),
            jax.ShapeDtypeStruct((rows, hidden), jnp.bfloat16),
            jax.ShapeDtypeStruct((units, hidden), jnp.float32),
            jax.ShapeDtypeStruct((units, width), jnp.float32),
        ],
        compiler_params=pltpu.CompilerParams(vmem_limit_bytes=VMEM),
        cost_estimate=cost(8 * rows * width * hidden, 4 * rows * hidden, rows * hidden),
        name="forward",
    )(titles.reshape(rows, width), ln_gain.reshape(1, width), w_up)


def up_kernel(
    units, slots, core_ref, keep_at, send_at, slope_ref, act_ref, normed_ref, mean_ref, pool_ref,
    grad_ref, pre_ref, *out_refs
):
    rows, block = slope_ref.shape
    length, step = rows // units, rows // units * 8
    part = block // slots
    for r in range(units // 8):
        slope = slope_ref[r * step : (r + 1) * step, :].astype(jnp.float32)
        d_pre = slope.reshape(8, length, block) * act_ref[r * 8 : (r + 1) * 8, :][:, None, :]
        pre_ref[r * step : (r + 1) * step, :] = d_pre.reshape(step, block).astype(jnp.bfloat16)
    up = contract_first(pre_ref[...], normed_ref[...])
    down = contract_first(mean_ref[...], grad_ref[...])
    proj = contract_first(pool_ref[...], grad_ref[...])
    first = core_ref[0] == 0
    half = slots // 2
    n_x = half // 4
    for q in range(half):
        y, x = q // n_x, q % n_x
        even, odd = (y * 2 * n_x + x, (y * 2 + 1) * n_x + x)

        def pieces(k):
            rows_f = up[k * part : (k + 1) * part]
            rows_d = down[k * part : (k + 1) * part]
            out = []
            for p in range(3):
                out.append(rows_f[:, p * 256 : (p + 1) * 256])
                out.append(rows_d[p * 8 : (p + 1) * 8])
            return out + [proj[k * 8 : (k + 1) * 8]]

        a, b = pieces(even), pieces(odd)
        keep = [jnp.where(first, u, v) for u, v in zip(a, b)]
        send = [jnp.where(first, v, u) for u, v in zip(a, b)]
        for values, at, refs in ((keep, keep_at, out_refs[:3]), (send, send_at, out_refs[3:])):
            place = at[1, y] * n_x + at[2, x]
            for p in range(3):
                refs[p][place, :part, :] = values[2 * p]
                refs[p][place, part : part + 8, :] = values[2 * p + 1]
            refs[0][place, part + 8 :, :] = values[6]


def up_products(core, keep_at, send_at, slope, d_act, normed_b, mean_act_b, pooled_b, grad_b):
    rows, hidden = slope.shape
    units, width = d_act.shape[0], normed_b.shape[1]
    width_e = grad_b.shape[1]
    sides = keep_at.shape[1]
    block = hidden // sides
    slots = 2 * sides * sides
    part = block // slots
    tall = (part + 16, part + 8, part + 8)

    def whole(array):
        return pl.BlockSpec(array.shape, lambda i, c, k, s: (0, 0))

    def columns(array):
        return pl.BlockSpec((array.shape[0], array.shape[1] // sides), lambda i, c, k, s: (0, i))

    return pl.pallas_call(
        functools.partial(up_kernel, units, slots),
        grid_spec=pltpu.PrefetchScalarGridSpec(
            num_scalar_prefetch=3,
            grid=(sides,),
            in_specs=[
                columns(slope),
                columns(d_act),
                whole(normed_b),
                columns(mean_act_b),
                columns(pooled_b),
                whole(grad_b),
            ],
            out_specs=[columns(slope)]
            + [
                pl.BlockSpec((slots // 2, h, width_e), lambda i, c, k, s: (k[0, i], 0, 0))
                for h in tall
            ]
            + [
                pl.BlockSpec((slots // 2, h, width_e), lambda i, c, k, s: (s[0, i], 0, 0))
                for h in tall
            ],
        ),
        out_shape=[jax.ShapeDtypeStruct((rows, hidden), jnp.bfloat16)]
        + [jax.ShapeDtypeStruct((sides * slots // 2, h, width_e), jnp.float32) for h in tall * 2],
        compiler_params=pltpu.CompilerParams(vmem_limit_bytes=VMEM),
        cost_estimate=cost(2 * rows * width * hidden, 4 * rows * hidden),
        name="up_products",
    )(core, keep_at, send_at, slope, d_act, normed_b, mean_act_b, pooled_b, grad_b)


def titles_kernel(pre_ref, w_ref, titles_ref, gain_ref, pool_ref, out_ref, gain_out):
    rows, width = titles_ref.shape
    units = pool_ref.shape[0]
    length = rows // units
    d_normed = contract_last(pre_ref[...], w_ref[...])
    normed, inv_scale = layer_norm(titles_ref[...].astype(jnp.float32))
    product = d_normed * normed

    @pl.when(pl.program_id(0) == 0)
    def _():
        gain_out[...] = jnp.zeros_like(gain_out)

    gain_out[...] += jnp.sum(product.reshape(rows // 8, 8, width), axis=0)
    d_hat = d_normed * gain_ref[...]
    d_flat = inv_scale * (
        d_hat
        - jnp.mean(d_hat, axis=1, keepdims=True)
        - normed * jnp.mean(d_hat * normed, axis=1, keepdims=True)
    )
    d_block = d_flat.reshape(units, length, width) + (pool_ref[...] * (1.0 / length))[:, None, :]
    out_ref[...] = d_block.reshape(rows, width).astype(jnp.bfloat16)


def title_grads(d_pre, w_up, titles, ln_gain, d_pooled):
    units, length, width = titles.shape
    rows, hidden = d_pre.shape
    step = 8 * length
    return pl.pallas_call(
        titles_kernel,
        grid=(rows // step,),
        in_specs=[
            pl.BlockSpec((step, hidden), lambda i: (i, 0)),
            pl.BlockSpec((width, hidden), lambda i: (0, 0)),
            pl.BlockSpec((step, width), lambda i: (i, 0)),
            pl.BlockSpec((1, width), lambda i: (0, 0)),
            pl.BlockSpec((8, width), lambda i: (i, 0)),
        ],
        out_specs=[
            pl.BlockSpec((step, width), lambda i: (i, 0)),
            pl.BlockSpec((8, width), lambda i: (0, 0)),
        ],
        out_shape=[
            jax.ShapeDtypeStruct((rows, width), jnp.bfloat16),
            jax.ShapeDtypeStruct((8, width), jnp.float32),
        ],
        compiler_params=pltpu.CompilerParams(vmem_limit_bytes=VMEM),
        cost_estimate=cost(2 * rows * width * hidden, 2 * rows * hidden),
        name="title_grads",
    )(d_pre, w_up, titles.reshape(rows, width), ln_gain.reshape(1, width), d_pooled)


def rows_kernel(arrived_ref, table_ref, accum_ref, table_out, accum_out):
    step, width_e = table_ref.shape
    slots = arrived_ref.shape[0]
    grads = arrived_ref[:, :width_e]
    ids = arrived_ref[:, width_e : width_e + 1].astype(jnp.int32)
    here = lax.broadcasted_iota(jnp.int32, (slots, step), 1) + pl.program_id(0) * step
    onehot = jnp.where(here == ids, 1.0, 0.0).astype(jnp.bfloat16)
    high = grads.astype(jnp.bfloat16)
    low = (grads - high.astype(jnp.float32)).astype(jnp.bfloat16)
    row_grad = contract_first(onehot, high) + contract_first(onehot, low)
    new_accum = accum_ref[...] + row_grad * row_grad
    accum_out[...] = new_accum
    table_out[...] = table_ref[...] - LEARN_RATE * row_grad * lax.rsqrt(new_accum)


def row_update(arrived, table, accum):
    rows, width_e = table.shape
    step = 512
    tile = pl.BlockSpec((step, width_e), lambda i: (i, 0))
    return pl.pallas_call(
        rows_kernel,
        grid=(rows // step,),
        in_specs=[pl.BlockSpec(arrived.shape, lambda i: (0, 0)), tile, tile],
        out_specs=[tile, tile],
        out_shape=[jax.ShapeDtypeStruct((rows, width_e), jnp.float32)] * 2,
        compiler_params=pltpu.CompilerParams(vmem_limit_bytes=VMEM),
        cost_estimate=cost(4 * rows * width_e * arrived.shape[0], 16 * rows * width_e),
        name="row_update",
    )(arrived, table, accum)


def per_device(
    titles,
    ln_gain,
    w_up,
    w_down,
    w_proj,
    sample_grad,
    sample_item,
    sample_row,
    row_ids,
    table,
    accum,
):
    n_z, n_y, n_c, n_x = (lax.axis_size(name) for name in DEVICES)
    chips, groups = n_z * n_y * n_x, n_z * n_y * n_c
    devices = chips * n_c
    core, my_x = lax.axis_index("c"), lax.axis_index("x")
    units, length, width = titles.shape
    hidden = w_up.shape[1]
    width_e = sample_grad.shape[1]
    share_f, share_d = hidden // devices, width // devices

    place = lax.iota(jnp.int32, chips * units)
    chip, unit = place // units, place % units

    def item_part(of_core):
        wanted = (((chip // n_x) * n_c + of_core) * n_x + chip % n_x) * units + unit
        onehot = (sample_item[:, None] == wanted[None, :]).astype(jnp.bfloat16)
        return contract_first(onehot, sample_grad)

    got = swap_cores(item_part(1 - core))
    mine = (item_part(core) + got).reshape(chips, units, width_e)
    item_all = lax.all_to_all(mine, CHIPS, 0, 0, tiled=True)

    slot_count = row_ids.shape[1]
    rows_here = table.shape[0]
    slot_hot = (sample_row[:, None] == lax.iota(jnp.int32, slot_count)[None, :]).astype(
        jnp.bfloat16
    )
    local_rows = (row_ids[0] % rows_here).astype(jnp.float32)
    row_part = jnp.concatenate(
        [
            contract_first(slot_hot, sample_grad),
            jnp.broadcast_to(local_rows[:, None], (slot_count, 128)),
        ],
        axis=1,
    )
    row_all = lax.all_to_all(
        row_part.reshape(devices, slot_count // devices, width_e + 128), DEVICES, 0, 0, tiled=True
    )

    normed_b, slope, mean_act, mean_title = forward(titles, ln_gain, w_up)
    mean_act_b = mean_act.astype(jnp.bfloat16)
    pooled = mean_title + jnp.dot(mean_act_b, w_down, preferred_element_type=jnp.float32)
    lane = lax.iota(jnp.int32, devices * 8)
    source = jnp.where(lane % 8 < share_d, lane // 8 * share_d + lane % 8, -1)
    spread = (lax.iota(jnp.int32, width)[:, None] == source[None, :]).astype(jnp.bfloat16)
    pooled_b = jnp.dot(
        pooled.astype(jnp.bfloat16), spread, preferred_element_type=jnp.float32
    ).astype(jnp.bfloat16)
    item_all, pooled_b = lax.optimization_barrier((item_all, pooled_b))

    item_grad = jnp.sum(item_all, axis=0)
    grad_b = item_grad.astype(jnp.bfloat16)
    d_pooled = contract_last(grad_b, w_proj)
    d_act = contract_last(d_pooled.astype(jnp.bfloat16), w_down) / length

    here = [(lax.axis_index(name), lax.axis_size(name)) for name in CHIPS]
    keep_at = jnp.stack([slot_of(core, at, size) for at, size in here])
    send_at = jnp.stack([slot_of(1 - core, at, size) for at, size in here])
    d_pre, *sums = up_products(
        core.reshape(1), keep_at, send_at, slope, d_act, normed_b, mean_act_b, pooled_b, grad_b
    )
    parts = [
        (keep + swap_cores(send)).reshape(n_z, n_y, n_x, -1, width_e)
        for keep, send in zip(sums[:3], sums[3:])
    ]

    beside = title_grads(d_pre, w_up, titles, ln_gain, d_pooled)
    parts, (d_titles, gain_term) = halve(parts, "xyz", False, tuple(beside))
    beside = row_update(row_all.reshape(slot_count, width_e + 128), table, accum)
    parts, (new_table, new_accum) = halve(parts, "xyz", True, tuple(beside))
    gain_term = gain_term + swap_cores(gain_term)
    for name in ("y", "z"):
        gain_term = gain_term + along(gain_term, name, 1)
        gain_term = gain_term + along(gain_term, name, 2)
    for names in ("yzx", "zxy"):
        parts, _ = halve(parts, names, False)
        parts, _ = halve(parts, names, True)

    flat = [part.reshape(-1, width_e) for part in parts]
    last = jnp.concatenate(
        flat + [gain_term[:, p * width_e : (p + 1) * width_e] for p in range(3)], axis=0
    )
    blocks = jnp.stack([last, along(last, "x", 1), along(last, "x", 2), along(last, "x", 3)])
    ordered = jnp.stack(
        [lax.dynamic_index_in_dim(blocks, my_x ^ j, 0, keepdims=False) for j in range(n_x)]
    )
    starts = [0, share_f + 16, 2 * share_f + 24]
    end = 3 * share_f + 32
    grad_up = jnp.concatenate([ordered[:, at : at + share_f] for at in starts], axis=2)
    grad_up = grad_up.reshape(-1, width).T
    outer = jnp.concatenate(
        [ordered[:, at + share_f : at + share_f + 8] for at in starts], axis=1
    ).reshape(-1, width_e)
    high = outer.astype(jnp.bfloat16)
    low = (outer - high.astype(jnp.float32)).astype(jnp.bfloat16)
    grad_down = contract_last(high, w_proj) + contract_last(low, w_proj)
    grad_proj = ordered[:, share_f + 8 : share_f + 8 + share_d].reshape(-1, width_e)
    gains = jnp.sum(ordered[:, end:].reshape(n_x, 3, 8, width_e), axis=(0, 2)).reshape(width)
    mine_at = (lax.axis_index("z") * n_y + lax.axis_index("y")) * n_c + core
    grad_gain = lax.dynamic_slice_in_dim(gains, mine_at * (width // groups), width // groups, 0)
    return (
        d_titles.reshape(units, length, width),
        grad_up,
        grad_down,
        grad_proj,
        grad_gain,
        new_table,
        new_accum,
    )


def solution(mesh):
    n_table, n_rep = mesh.devices.shape
    side = n_rep
    fine = Mesh(mesh.devices.reshape(n_table // (2 * side), side, 2, n_rep), DEVICES)
    split, tab = P(DEVICES), P(GROUP)
    return jax.shard_map(
        per_device,
        mesh=fine,
        in_specs=(split, P(), P(), P(), P(), split, split, split, split, split, split),
        out_specs=(split, P(None, GROUP), tab, tab, tab, split, split),
        check_vma=False,
    )
```

time: 376 us -> 202 us (0.54); the launches traced: 370 us -> 201 us
  blocking collectives: 142 us -> 0 us
  Pallas kernels: 2.96 us -> 53.8 us
  matrix products: 63.1 us -> 16.4 us
  other arithmetic: 51.4 us -> 13 us
  starting transfers between devices: 23.8 us -> 53.9 us
  local copies, waits for them, and re-layouts: 40.7 us -> 21.1 us
  between operations: 14.8 us -> 1.27 us
  waiting for transfers between devices: 31 us -> 41.8 us
    all_gather x4 -> x0, blocking collectives: 142 us -> none  [the longest x1 105 us: per_device(): gains = lax.all_gather(gain_term, DEVICES, axis=0)]
    pallas_call x1 -> x4, Pallas kernels: 2.96 us -> 53.8 us  [the longest x1 19.7 us: forward(): pl.pallas_call(functools.partial(forward_kernel, units), grid=(hidden //...]
    ppermute x0 -> x25, starting transfers between devices: none -> 31.7 us  [the longest x18 25.1 us: halve(): lax.ppermute(lax.slice_in_dim(part, middle, None, axis=dim), DEVICES, par...]
    ppermute x0 -> x25, waiting for transfers between devices: none -> 29.7 us  [the longest x18 15.4 us: halve(): lax.ppermute(lax.slice_in_dim(part, middle, None, axis=dim), DEVICES, par...]
    all_to_all x3 -> x2, waiting for transfers between devices: 28 us -> 0.01 us  [the longest x1 0.01 us: per_device(): item_all = lax.all_to_all(mine, CHIPS, 0, 0, tiled=True)]
    dot_general x2 -> x1, matrix products: 26.6 us -> 3.76 us  [per_device(): jnp.dot(pooled.astype(jnp.bfloat16), spread, preferred_element_type=jnp.f...]
    reduce_sum x6 -> x3, other arithmetic: 15.1 us -> 1.58 us  [the longest x1 1.54 us: per_device(): item_grad = jnp.sum(item_all, axis=0)]
    dot_general x1 -> x0, local copies, waits for them, and re-layouts: 12.7 us -> none  [contract_first(): lax.dot_general(left, right, (((0,), (0,)), ((), ())), preferred_element_...]
  transfers between devices with their start and end apart: 6 -> 32, of which waited for: 3 -> 18; matrix products, arithmetic and copies ran while one was open for 22% -> 13% of each run, Pallas kernels for 1% -> 19%
where the time goes in v2:
time: 202 us; the launch traced here: 201 us
  starting transfers between devices  53.9 us (27%)
  Pallas kernels  53.8 us (27%)
  waiting for transfers between devices  41.8 us (21%)
  local copies, waits for them, and re-layouts  21.1 us (10%)
  matrix products  16.4 us (8%)
  other arithmetic  13 us (6%)
    ppermute x18, starting transfers between devices, halve(): lax.ppermute(lax.slice_in_dim(part, middle, None, axis=dim), DEVICES, par...  25.1 us
    pallas_call x1, Pallas kernels, forward(): pl.pallas_call(functools.partial(forward_kernel, units), grid=(hidden //...  19.7 us
    pallas_call x1, Pallas kernels, up_products(): pl.pallas_call(functools.partial(up_kernel, units, slots), grid_spec=pltp...  15.6 us
    ppermute x18, waiting for transfers between devices, halve(): lax.ppermute(lax.slice_in_dim(part, middle, None, axis=dim), DEVICES, par...  15.4 us
    pallas_call x1, Pallas kernels, title_grads(): pl.pallas_call(titles_kernel, grid=(rows // step,), in_specs=[pl.BlockSpe...  14.9 us
    ppermute x7, waiting for transfers between devices, along(): return lax.ppermute(block, name, [(i, i ^ step) for i in range(size)])  14.3 us
    ppermute x5, waiting for transfers between devices, swap_cores(): return lax.ppermute(block, 'c', [(0, 1), (1, 0)])  12.1 us
    all_to_all x1, starting transfers between devices, per_device(): item_all = lax.all_to_all(mine, CHIPS, 0, 0, tiled=True)  12 us
  transfers between devices with their start and end apart: 32, of which 18 were waited for; matrix products, arithmetic and copies ran while one was open for 13% of the time, Pallas kernels for 19%

profile of v2, /device:TPU:0, one launch (start us, length us, event | category | flops | bytes accessed | tf_op | source)
XLA Modules:
  0.0 201.3 jit_solution(7996118976953768542)
XLA Ops:
  1.7 2.7 %fusion = f32[1536,256]{1,0:T(8,128)S(1)} fusion(bf16[1024,256]{1,0:T(8,128)(2,1)S(1)} %copy-done, s32[1536]{0:T(1024)S(1)} %fusion.35, s32[1024]{0:T(1024)} %param.17), kind=kOutput, calls=%fused_computation | convolution fusion | flops 806879232 | bytes 2107392 | tf_op jit(solution)/shard_map/dot_general | solution.py:23
  4.6 3.3 %collective-permute-done = f32[1536,256]{1,0:T(8,128)S(1)} collective-permute-done((f32[1536,256]{1,0:T(8,128)S(1)}, f32[1536,256]{1,0:T(8,128)S(1)}, u32[]{:S(2)}, u32[]{:S(2)}) %collective-permute-start) | collective-permute-done | bytes 1572896 | tf_op jit(solution)/shard_map/ppermute | solution.py:39
  7.9 3.1 %fusion.9 = f32[1536,256]{1,0:T(8,128)} fusion(f32[1536,256]{1,0:T(8,128)S(1)} %collective-permute-done, bf16[1024,256]{1,0:T(8,128)(2,1)S(1)} %copy-done, s32[1536]{0:T(1024)S(1)} %fusion.36, s32[1024]{0:T(1024)S(1)} %copy-done.20), kind=kOutput, calls=%fused_computation.11 | convolution fusion | flops 807272448 | bytes 3680256 | tf_op jit(solution)/shard_map/dot_general | solution.py:23
  11.0 12.0 %all-to-all-start = ((f32[64,24,256]{2,1,0:T(8,128)}), f32[64,24,256]{2,1,0:T(8,128)}, u32[]{:S(2)}, u32[]{:S(2)}) async-start(f32[64,24,256]{2,1,0:T(8,128)} %bitcast.55), calls=%async_computation | async-start | bytes 3145728 | tf_op jit(solution)/shard_map/all_to_all | solution.py:354
  23.1 19.7 %forward.1 = (bf16[1536,768]{1,0:T(8,128)(2,1)S(1)}, bf16[1536,3072]{1,0:T(8,128)(2,1)}, f32[24,3072]{1,0:T(8,128)S(1)}, f32[24,768]{1,0:T(8,128)S(1)}) custom-call(bf16[1536,768]{1,0:T(8,128)(2,1)S(1)} %bitcast.48, f32[1,768]{1,0:T(1,128)S(1)} %reshape.298.gain_ref, bf16[768,3072]{1,0:T(8,128)(2,1)} %w_ref.3), custom_call_target="tpu_custom_call" | custom-call | flops 28991029248 | bytes 18874368 | tf_op jit(solution)/shard_map/forward/pallas_call | solution.py:126
  42.8 1.4 copy-done.4
  44.3 3.8 %fusion.14.pool_ref = bf16[24,1024]{1,0:T(8,128)(2,1)S(1)} fusion(s32[1024]{0:T(1024)S(1)} %fusion.48, f32[24,768]{1,0:T(8,128)S(1)} %get-tuple-element.35, bf16[24,3072]{1,0:T(8,128)(2,1)S(1)} %convert_element_type.35.mean_ref, bf16[3072,768]{1,0:T(8,128)(2,1)} %param.14), kind=kOutput, calls=%fused_computation.17 | convolution fusion | flops 151842816 | bytes 4993024 | tf_op jit(solution)/shard_map/dot_general | solution.py:379
  48.1 1.5 reduce_sum.21.grad_ref
  49.6 1.2 fusion.55.pool_ref
  50.8 3.7 %convolution_multiply_fusion.act_ref = f32[24,3072]{1,0:T(8,128)S(1)} fusion(bf16[3072,768]{1,0:T(8,128)(2,1)} %param.14, f32[24,768]{1,0:T(8,128)S(1)} %fusion.55.pool_ref), kind=kOutput, calls=%fused_computation.4 | convolution fusion | flops 113338368 | bytes 5087232 | tf_op jit(solution)/shard_map/dot_general | solution.py:29
  54.5 15.6 %up_products.1 = (bf16[1536,3072]{1,0:T(8,128)(2,1)}, f32[64,40,256]{2,1,0:T(8,128)}, f32[64,32,256]{2,1,0:T(8,128)S(1)}, f32[64,32,256]{2,1,0:T(8,128)S(1)}, f3...) custom-call(s32[1]{0:T(128)} %bitcast.core_ref, s32[3,4]{1,0:T(4,128)S(1)} %pad_add_fusion.keep_at, ...), custom_call_target="tpu_custom_call" | custom-call | flops 7247757312 | bytes 18874368 | tf_op jit(solution)/shard_map/up_products/pallas_call | solution.py:209
  70.7 7.6 %collective-permute-done.5 = f32[64,32,256]{2,1,0:T(8,128)S(1)} collective-permute-done((f32[64,32,256]{2,1,0:T(8,128)}, f32[64,32,256]{2,1,0:T(8,128)S(1)}, u32[]{:S(2)}, u32[]{:S(2)}) %collective-permute-start.5) | collective-permute-done | bytes 2097184 | tf_op jit(solution)/shard_map/ppermute | solution.py:39
  80.3 1.3 slice.196
  81.6 1.3 collective-permute-start.2
  82.9 1.6 fusion.53
  84.6 1.5 collective-permute-start.6
  86.5 1.3 copy-done.7
  88.8 1.5 collective-permute-start.4
  92.0 2.3 %copy.20 = f32[512,384]{1,0:T(8,128)} copy(f32[512,384]{0,1:T(8,128)} %pad_maximum_fusion) | data formatting | bytes 1572864 | tf_op jit(solution)/shard_map/concatenate | solution.py:362
  94.3 2.3 %reshape.303 = f32[128,4,384]{2,1,0:T(4,128)} reshape(f32[512,384]{1,0:T(8,128)} %copy.20) | data formatting | bytes 1572864 | tf_op jit(solution)/shard_map/reshape | solution.py:370
  96.5 9.6 %all-to-all-start.1 = ((f32[128,4,384]{2,1,0:T(4,128)}), f32[128,4,384]{2,1,0:T(4,128)}, u32[]{:S(2)}, u32[]{:S(2)}) async-start(f32[128,4,384]{2,1,0:T(4,128)} %reshape.303), calls=%async_computation.1 | async-start | bytes 1572864 | tf_op jit(solution)/shard_map/all_to_all | solution.py:369
  106.1 14.9 %title_grads.1 = (bf16[1536,768]{1,0:T(8,128)(2,1)}, f32[8,768]{1,0:T(8,128)S(1)}) custom-call(bf16[1536,3072]{1,0:T(8,128)(2,1)} %get-tuple-element.46.pre_ref, bf16[768,3072]{1,0:T(8,128)(2,1)} %w_ref.3, bf16[1536,768]{1,0:T(8,128)(2,1)S(1)} %bitcast.49, f32[1,768]{1,0:T(1,128)S(1)} %reshape.298.gain_ref, f32[24,768]{1,0:T(8,128)S(1)} %fusion.55.pool_ref), custom_call_target="tpu_custom_call" | custom-call | flops 7247757312 | bytes 9437184 | tf_op jit(solution)/shard_map/title_grads/pallas_call | solution.py:267
  121.0 1.5 add.256
  123.7 2.8 %collective-permute-start.9 = (f32[1,4,4,32,256]{4,3,2,1,0:T(8,128)}, f32[1,4,4,32,256]{4,3,2,1,0:T(8,128)}, u32[]{:S(2)}, u32[]{:S(2)}) collective-permute-start(f32[1,4,4,32,256]{4,3,2,1,0:T(8,128)} %slice.205), channel_id=1, source_target_pairs={{0,96},{1,97},{2,98},{3,99},{4,36},{5,37},{6,38},{7,39},{8,104},{9... | collective-permute-start | bytes 1572872 | tf_op jit(solution)/shard_map/ppermute | solution.py:78
  126.5 1.5 slice_add_fusion
  129.0 2.7 %collective-permute-start.7 = (f32[4,4,1,40,256]{4,3,2,1,0:T(8,128)}, f32[4,4,1,40,256]{4,3,2,1,0:T(8,128)}, u32[]{:S(2)}, u32[]{:S(2)}) collective-permute-start(f32[4,4,1,40,256]{4,3,2,1,0:T(8,128)} %slice.201), channel_id=1, source_target_pairs={{0,3},{1,2},{2,1},{3,0},{4,5},{5,4},{6,7},{7,6},{8,11},{9,10},{10,... | collective-permute-start | bytes 1966088 | tf_op jit(solution)/shard_map/ppermute | solution.py:78
  131.7 1.4 slice_add_fusion.1
  134.0 2.9 %collective-permute-start.8 = (f32[4,1,4,32,256]{4,3,2,1,0:T(8,128)}, f32[4,1,4,32,256]{4,3,2,1,0:T(8,128)}, u32[]{:S(2)}, u32[]{:S(2)}) collective-permute-start(f32[4,1,4,32,256]{4,3,2,1,0:T(8,128)} %slice.203), channel_id=1, source_target_pairs={{0,24},{1,25},{2,26},{3,27},{4,12},{5,13},{6,14},{7,15},{8,16},{9,... | collective-permute-start | bytes 1572872 | tf_op jit(solution)/shard_map/ppermute | solution.py:78
  138.3 3.6 %collective-permute-done.23 = f32[8,768]{1,0:T(8,128)S(1)} collective-permute-done((f32[8,768]{1,0:T(8,128)S(1)}, f32[8,768]{1,0:T(8,128)S(1)}, u32[]{:S(2)}, u32[]{:S(2)}) %collective-permute-start.23) | collective-permute-done | bytes 24608 | tf_op jit(solution)/shard_map/ppermute | solution.py:44
  142.7 4.6 %collective-permute-done.24 = f32[8,768]{1,0:T(8,128)S(1)} collective-permute-done((f32[8,768]{1,0:T(8,128)S(1)}, f32[8,768]{1,0:T(8,128)S(1)}, u32[]{:S(2)}, u32[]{:S(2)}) %collective-permute-start.24) | collective-permute-done | bytes 24608 | tf_op jit(solution)/shard_map/ppermute | solution.py:44
  147.3 1.4 reshape.304.arrived_ref
  148.7 2.4 %collective-permute-done.25 = f32[8,768]{1,0:T(8,128)S(1)} collective-permute-done((f32[8,768]{1,0:T(8,128)S(1)}, f32[8,768]{1,0:T(8,128)S(1)}, u32[]{:S(2)}, u32[]{:S(2)}) %collective-permute-start.25) | collective-permute-done | bytes 24608 | tf_op jit(solution)/shard_map/ppermute | solution.py:44
  151.9 1.6 copy-done.2
  153.5 3.7 %row_update.1 = (f32[2048,256]{1,0:T(8,128)}, f32[2048,256]{1,0:T(8,128)}) custom-call(f32[512,384]{1,0:T(8,128)S(1)} %reshape.304.arrived_ref, f32[2048,256]{1,0:T(8,128)S(1)} %copy-done.1, f32[2048,256]{1,0:T(8,128)S(1)} %copy-done.2), custom_call_target="tpu_custom_call" | custom-call | flops 1073741824 | bytes 8388608 | tf_op jit(solution)/shard_map/row_update/pallas_call | solution.py:310
  157.2 1.3 slice_add_fusion.3
  162.1 2.9 %collective-permute-done.18 = f32[1,4,2,32,256]{4,3,2,1,0:T(8,128)S(1)} collective-permute-done((f32[1,4,2,32,256]{4,3,2,1,0:T(8,128)S(1)}, f32[1,4,2,32,256]{4,3,2,1,0:T(8,128)S(1)}, u32[]{:S(2)}, u32[]{:S(2)}) %collective-permute-start.18) | collective-permute-done | bytes 262176 | tf_op jit(solution)/shard_map/ppermute | solution.py:78
  166.5 2.0 collective-permute-start.15
  169.5 1.8 collective-permute-done.19
  172.8 1.9 collective-permute-start.16
  175.6 1.7 collective-permute-start.12
  177.8 2.7 %collective-permute-done.12 = f32[2,1,1,40,256]{4,3,2,1,0:T(8,128)S(1)} collective-permute-done((f32[2,1,1,40,256]{4,3,2,1,0:T(8,128)S(1)}, f32[2,1,1,40,256]{4,3,2,1,0:T(8,128)S(1)}, u32[]{:S(2)}, u32[]{:S(2)}) %collective-permute-start.12) | collective-permute-done | bytes 81952 | tf_op jit(solution)/shard_map/ppermute | solution.py:78
  180.6 3.1 %collective-permute-start.13 = (f32[1,1,1,40,256]{4,3,2,1,0:T(8,128)S(1)}, f32[1,1,1,40,256]{4,3,2,1,0:T(8,128)S(1)}, u32[]{:S(2)}, u32[]{:S(2)}) collective-permute-start(f32[1,1,1,40,256]{4,3,2,1,0:T(8,128)S(1)} %slice.213), channel_id=1, source_target_pairs={{0,96},{1,97},{2,98},{3,99},{4,36},{5,37},{6,38},{7,39},{8,104},{9... | collective-permute-start | bytes 122888 | tf_op jit(solution)/shard_map/ppermute | solution.py:78
  184.4 1.5 collective-permute-done.13
  185.9 3.3 %collective-permute-done.17 = f32[1,1,1,32,256]{4,3,2,1,0:T(8,128)S(1)} collective-permute-done((f32[1,1,1,32,256]{4,3,2,1,0:T(8,128)S(1)}, f32[1,1,1,32,256]{4,3,2,1,0:T(8,128)S(1)}, u32[]{:S(2)}, u32[]{:S(2)}) %collective-permute-start.17) | collective-permute-done | bytes 32800 | tf_op jit(solution)/shard_map/ppermute | solution.py:78
  189.3 2.1 %collective-permute-start.28 = (f32[128,256]{1,0:T(8,128)S(1)}, f32[128,256]{1,0:T(8,128)S(1)}, u32[]{:S(2)}, u32[]{:S(2)}) collective-permute-start(f32[128,256]{1,0:T(8,128)S(1)} %constant_dynamic-update-slice_fusion), channel_id=1, source_target_pairs={{0,2},{1,3},{2,0},{3,1},{4,6},{5,7},{6,4},{7,5},{8,10},{9,11},{10,... | collective-permute-start | bytes 393224 | tf_op jit(solution)/shard_map/ppermute | solution.py:44
  191.4 2.5 %collective-permute-start.29 = (f32[128,256]{1,0:T(8,128)S(1)}, f32[128,256]{1,0:T(8,128)S(1)}, u32[]{:S(2)}, u32[]{:S(2)}) collective-permute-start(f32[128,256]{1,0:T(8,128)S(1)} %constant_dynamic-update-slice_fusion), channel_id=1, source_target_pairs={{0,3},{1,2},{2,1},{3,0},{4,7},{5,6},{6,5},{7,4},{8,11},{9,10},{10,... | collective-permute-start | bytes 393224 | tf_op jit(solution)/shard_map/ppermute | solution.py:44
  194.3 1.6 collective-permute-done.28
  195.9 1.8 collective-permute-done.29
  (148 shorter events, 26.7 us)
Async XLA Ops:
  1.7 2.8 %copy-start.18 = (f32[768]{0:T(1024)S(1)}, f32[768]{0:T(1024)}, u32[]{:S(2)}) copy-start(f32[768]{0:T(1024)} %param.12) | copy-start | bytes 9220
  1.7 6.2 %copy-start.20 = (s32[1024]{0:T(1024)S(1)}, s32[1024]{0:T(1024)}, u32[]{:S(2)}) copy-start(s32[1024]{0:T(1024)} %param.17) | copy-start | bytes 12292
  4.4 3.5 %collective-permute-start = (f32[1536,256]{1,0:T(8,128)S(1)}, f32[1536,256]{1,0:T(8,128)S(1)}, u32[]{:S(2)}, u32[]{:S(2)}) collective-permute-start(f32[1536,256]{1,0:T(8,128)S(1)} %fusion), channel_id=1, source_target_pairs={{0,4},{4,0},{1,5},{5,1},{2,6},{6,2},{3,7},{7,3},{8,12},{12,8},{9,1... | collective-permute-start | bytes 4718600 | tf_op jit(solution)/shard_map/ppermute | solution.py:39
  11.0 12.1 %copy-start.3 = (bf16[24,64,768]{2,1,0:T(8,128)(2,1)S(1)}, bf16[24,64,768]{2,1,0:T(8,128)(2,1)}, u32[]{:S(2)}) copy-start(bf16[24,64,768]{2,1,0:T(8,128)(2,1)} %param.11) | copy-start | bytes 7077892
  11.0 37.0 %all-to-all-start = ((f32[64,24,256]{2,1,0:T(8,128)}), f32[64,24,256]{2,1,0:T(8,128)}, u32[]{:S(2)}, u32[]{:S(2)}) async-start(f32[64,24,256]{2,1,0:T(8,128)} %bitcast.55), calls=%async_computation | async-start | bytes 3145728 | tf_op jit(solution)/shard_map/all_to_all | solution.py:354
  70.1 8.7 %collective-permute-start.1 = (f32[64,40,256]{2,1,0:T(8,128)}, f32[64,40,256]{2,1,0:T(8,128)S(1)}, u32[]{:S(2)}, u32[]{:S(2)}) collective-permute-start(f32[64,40,256]{2,1,0:T(8,128)} %get-tuple-element.41), channel_id=1, source_target_pairs={{0,4},{4,0},{1,5},{5,1},{2,6},{6,2},{3,7},{7,3},{8,12},{12,8},{9,1... | collective-permute-start | bytes 7864328 | tf_op jit(solution)/shard_map/ppermute | solution.py:39
  70.1 8.1 %collective-permute-start.5 = (f32[64,32,256]{2,1,0:T(8,128)}, f32[64,32,256]{2,1,0:T(8,128)S(1)}, u32[]{:S(2)}, u32[]{:S(2)}) collective-permute-start(f32[64,32,256]{2,1,0:T(8,128)} %get-tuple-element.45), channel_id=1, source_target_pairs={{0,4},{4,0},{1,5},{5,1},{2,6},{6,2},{3,7},{7,3},{8,12},{12,8},{9,1... | collective-permute-start | bytes 6291464 | tf_op jit(solution)/shard_map/ppermute | solution.py:39
  70.6 15.4 %collective-permute-start.3 = (f32[64,32,256]{2,1,0:T(8,128)}, f32[64,32,256]{2,1,0:T(8,128)S(1)}, u32[]{:S(2)}, u32[]{:S(2)}) collective-permute-start(f32[64,32,256]{2,1,0:T(8,128)} %get-tuple-element.43), channel_id=1, source_target_pairs={{0,4},{4,0},{1,5},{5,1},{2,6},{6,2},{3,7},{7,3},{8,12},{12,8},{9,1... | collective-permute-start | bytes 6291464 | tf_op jit(solution)/shard_map/ppermute | solution.py:39
  78.2 1.7 copy-start.17
  80.3 4.2 %copy-start.5 = (f32[64,40,256]{2,1,0:T(8,128)}, f32[64,40,256]{2,1,0:T(8,128)S(1)}, u32[]{:S(2)}) copy-start(f32[64,40,256]{2,1,0:T(8,128)S(1)} %add.251) | copy-start | bytes 7864324
  81.6 39.4 %collective-permute-start.2 = (f32[4,4,2,40,256]{4,3,2,1,0:T(8,128)}, f32[4,4,2,40,256]{4,3,2,1,0:T(8,128)}, u32[]{:S(2)}, u32[]{:S(2)}) collective-permute-start(f32[4,4,2,40,256]{4,3,2,1,0:T(8,128)} %slice.196), channel_id=1, source_target_pairs={{0,1},{1,0},{2,3},{3,2},{4,7},{5,6},{6,5},{7,4},{8,9},{9,8},{10,11... | collective-permute-start | bytes 3932168 | tf_op jit(solution)/shard_map/ppermute | solution.py:78
  84.6 36.4 %collective-permute-start.6 = (f32[2,4,4,32,256]{4,3,2,1,0:T(8,128)}, f32[2,4,4,32,256]{4,3,2,1,0:T(8,128)}, u32[]{:S(2)}, u32[]{:S(2)}) collective-permute-start(f32[2,4,4,32,256]{4,3,2,1,0:T(8,128)} %bitcast.5), channel_id=1, source_target_pairs={{0,32},{1,33},{2,34},{3,35},{4,100},{5,101},{6,102},{7,103},{8,40}... | collective-permute-start | bytes 3145736 | tf_op jit(solution)/shard_map/ppermute | solution.py:78
  86.4 3.9 %copy-start.21 = (s32[1024]{0:T(1024)S(1)}, s32[1024]{0:T(1024)}, u32[]{:S(2)}) copy-start(s32[1024]{0:T(1024)} %param.18) | copy-start | bytes 12292
  86.4 4.5 %copy-start.19 = (s32[1,512]{1,0:T(1,128)S(1)}, s32[1,512]{1,0:T(1,128)}, u32[]{:S(2)}) copy-start(s32[1,512]{1,0:T(1,128)} %param.19) | copy-start | bytes 6148
  88.8 32.2 %collective-permute-start.4 = (f32[4,2,4,32,256]{4,3,2,1,0:T(8,128)}, f32[4,2,4,32,256]{4,3,2,1,0:T(8,128)}, u32[]{:S(2)}, u32[]{:S(2)}) collective-permute-start(f32[4,2,4,32,256]{4,3,2,1,0:T(8,128)} %slice.197), channel_id=1, source_target_pairs={{0,8},{1,9},{2,10},{3,11},{4,28},{5,29},{6,30},{7,31},{8,0},{9,1},... | collective-permute-start | bytes 3145736 | tf_op jit(solution)/shard_map/ppermute | solution.py:78
  96.5 50.8 %all-to-all-start.1 = ((f32[128,4,384]{2,1,0:T(4,128)}), f32[128,4,384]{2,1,0:T(4,128)}, u32[]{:S(2)}, u32[]{:S(2)}) async-start(f32[128,4,384]{2,1,0:T(4,128)} %reshape.303), calls=%async_computation.1 | async-start | bytes 1572864 | tf_op jit(solution)/shard_map/all_to_all | solution.py:369
  106.1 14.9 %copy-start.15 = (f32[32,32,256]{2,1,0:T(8,128)S(1)}, f32[32,32,256]{2,1,0:T(8,128)}, u32[]{:S(2)}) copy-start(f32[32,32,256]{2,1,0:T(8,128)} %get-tuple-element.63) | copy-start | bytes 3145732
  121.0 5.5 %copy-start.6 = (f32[64,40,256]{2,1,0:T(8,128)S(1)}, f32[64,40,256]{2,1,0:T(8,128)}, u32[]{:S(2)}) copy-start(f32[64,40,256]{2,1,0:T(8,128)} %copy-done.5) | copy-start | bytes 7864324
  123.7 8.0 %copy-start.8 = (f32[64,32,256]{2,1,0:T(8,128)S(1)}, f32[64,32,256]{2,1,0:T(8,128)}, u32[]{:S(2)}) copy-start(f32[64,32,256]{2,1,0:T(8,128)} %copy-done.7) | copy-start | bytes 6291460
  123.7 33.4 %collective-permute-start.9 = (f32[1,4,4,32,256]{4,3,2,1,0:T(8,128)}, f32[1,4,4,32,256]{4,3,2,1,0:T(8,128)}, u32[]{:S(2)}, u32[]{:S(2)}) collective-permute-start(f32[1,4,4,32,256]{4,3,2,1,0:T(8,128)} %slice.205), channel_id=1, source_target_pairs={{0,96},{1,97},{2,98},{3,99},{4,36},{5,37},{6,38},{7,39},{8,104},{9... | collective-permute-start | bytes 1572872 | tf_op jit(solution)/shard_map/ppermute | solution.py:78
  128.0 5.1 %copy-start.9 = (f32[4,4,2,40,256]{4,3,2,1,0:T(8,128)}, f32[4,4,2,40,256]{4,3,2,1,0:T(8,128)S(1)}, u32[]{:S(2)}) copy-start(f32[4,4,2,40,256]{4,3,2,1,0:T(8,128)S(1)} %slice_add_fusion) | copy-start | bytes 3932164
  129.0 28.2 %collective-permute-start.7 = (f32[4,4,1,40,256]{4,3,2,1,0:T(8,128)}, f32[4,4,1,40,256]{4,3,2,1,0:T(8,128)}, u32[]{:S(2)}, u32[]{:S(2)}) collective-permute-start(f32[4,4,1,40,256]{4,3,2,1,0:T(8,128)} %slice.201), channel_id=1, source_target_pairs={{0,3},{1,2},{2,1},{3,0},{4,5},{5,4},{6,7},{7,6},{8,11},{9,10},{10,... | collective-permute-start | bytes 1966088 | tf_op jit(solution)/shard_map/ppermute | solution.py:78
  133.1 4.9 %copy-start.13 = (f32[4,2,4,32,256]{4,3,2,1,0:T(8,128)}, f32[4,2,4,32,256]{4,3,2,1,0:T(8,128)S(1)}, u32[]{:S(2)}) copy-start(f32[4,2,4,32,256]{4,3,2,1,0:T(8,128)S(1)} %slice_add_fusion.1) | copy-start | bytes 3145732
  133.1 18.8 %copy-start.1 = (f32[2048,256]{1,0:T(8,128)S(1)}, f32[2048,256]{1,0:T(8,128)}, u32[]{:S(2)}) copy-start(f32[2048,256]{1,0:T(8,128)} %table_ref.1) | copy-start | bytes 6291460
  134.0 23.2 %collective-permute-start.8 = (f32[4,1,4,32,256]{4,3,2,1,0:T(8,128)}, f32[4,1,4,32,256]{4,3,2,1,0:T(8,128)}, u32[]{:S(2)}, u32[]{:S(2)}) collective-permute-start(f32[4,1,4,32,256]{4,3,2,1,0:T(8,128)} %slice.203), channel_id=1, source_target_pairs={{0,24},{1,25},{2,26},{3,27},{4,12},{5,13},{6,14},{7,15},{8,16},{9,... | collective-permute-start | bytes 1572872 | tf_op jit(solution)/shard_map/ppermute | solution.py:78
  136.9 1.2 collective-permute-start.22
  138.1 3.9 %collective-permute-start.23 = (f32[8,768]{1,0:T(8,128)S(1)}, f32[8,768]{1,0:T(8,128)S(1)}, u32[]{:S(2)}, u32[]{:S(2)}) collective-permute-start(f32[8,768]{1,0:T(8,128)S(1)} %add.273), channel_id=1, source_target_pairs={{0,8},{8,0},{16,24},{24,16},{1,9},{9,1},{17,25},{25,17},{2,10},{10... | collective-permute-start | bytes 73736 | tf_op jit(solution)/shard_map/ppermute | solution.py:44
  142.0 5.3 %collective-permute-start.24 = (f32[8,768]{1,0:T(8,128)S(1)}, f32[8,768]{1,0:T(8,128)S(1)}, u32[]{:S(2)}, u32[]{:S(2)}) collective-permute-start(f32[8,768]{1,0:T(8,128)S(1)} %add.274), channel_id=1, source_target_pairs={{0,16},{8,24},{16,0},{24,8},{1,17},{9,25},{17,1},{25,9},{2,18},{10... | collective-permute-start | bytes 73736 | tf_op jit(solution)/shard_map/ppermute | solution.py:44
  147.3 3.8 %collective-permute-start.25 = (f32[8,768]{1,0:T(8,128)S(1)}, f32[8,768]{1,0:T(8,128)S(1)}, u32[]{:S(2)}, u32[]{:S(2)}) collective-permute-start(f32[8,768]{1,0:T(8,128)S(1)} %add.275), channel_id=1, source_target_pairs={{0,32},{32,0},{64,96},{96,64},{1,33},{33,1},{65,97},{97,65},{2,34}... | collective-permute-start | bytes 73736 | tf_op jit(solution)/shard_map/ppermute | solution.py:44
  151.1 6.0 %collective-permute-start.26 = (f32[8,768]{1,0:T(8,128)S(1)}, f32[8,768]{1,0:T(8,128)S(1)}, u32[]{:S(2)}, u32[]{:S(2)}) collective-permute-start(f32[8,768]{1,0:T(8,128)S(1)} %add.276), channel_id=1, source_target_pairs={{0,64},{32,96},{64,0},{96,32},{1,65},{33,97},{65,1},{97,33},{2,66}... | collective-permute-start | bytes 73736 | tf_op jit(solution)/shard_map/ppermute | solution.py:44
  153.5 3.7 %copy-start.12 = (f32[2,4,4,32,256]{4,3,2,1,0:T(8,128)S(1)}, f32[2,4,4,32,256]{4,3,2,1,0:T(8,128)}, u32[]{:S(2)}) copy-start(f32[2,4,4,32,256]{4,3,2,1,0:T(8,128)} %copy-done.11) | copy-start | bytes 3145732
  157.2 1.7 copy-start.14
  157.2 3.3 %copy-start.10 = (f32[4,4,2,40,256]{4,3,2,1,0:T(8,128)S(1)}, f32[4,4,2,40,256]{4,3,2,1,0:T(8,128)}, u32[]{:S(2)}) copy-start(f32[4,4,2,40,256]{4,3,2,1,0:T(8,128)} %copy-done.9) | copy-start | bytes 3932164
  158.5 6.5 %collective-permute-start.18 = (f32[1,4,2,32,256]{4,3,2,1,0:T(8,128)S(1)}, f32[1,4,2,32,256]{4,3,2,1,0:T(8,128)S(1)}, u32[]{:S(2)}, u32[]{:S(2)}) collective-permute-start(f32[1,4,2,32,256]{4,3,2,1,0:T(8,128)S(1)} %slice.225), channel_id=1, source_target_pairs={{0,1},{1,0},{2,3},{3,2},{4,7},{5,6},{6,5},{7,4},{8,9},{9,8},{10,11... | collective-permute-start | bytes 786440 | tf_op jit(solution)/shard_map/ppermute | solution.py:78
  160.0 6.5 %collective-permute-start.14 = (f32[2,1,4,32,256]{4,3,2,1,0:T(8,128)S(1)}, f32[2,1,4,32,256]{4,3,2,1,0:T(8,128)S(1)}, u32[]{:S(2)}, u32[]{:S(2)}) collective-permute-start(f32[2,1,4,32,256]{4,3,2,1,0:T(8,128)S(1)} %slice.216), channel_id=1, source_target_pairs={{0,32},{1,33},{2,34},{3,35},{4,100},{5,101},{6,102},{7,103},{8,40}... | collective-permute-start | bytes 786440 | tf_op jit(solution)/shard_map/ppermute | solution.py:78
  161.7 7.2 %collective-permute-start.10 = (f32[4,2,1,40,256]{4,3,2,1,0:T(8,128)S(1)}, f32[4,2,1,40,256]{4,3,2,1,0:T(8,128)S(1)}, u32[]{:S(2)}, u32[]{:S(2)}) collective-permute-start(f32[4,2,1,40,256]{4,3,2,1,0:T(8,128)S(1)} %slice.207), channel_id=1, source_target_pairs={{0,8},{1,9},{2,10},{3,11},{4,28},{5,29},{6,30},{7,31},{8,0},{9,1},... | collective-permute-start | bytes 983048 | tf_op jit(solution)/shard_map/ppermute | solution.py:78
  165.0 6.3 %collective-permute-start.19 = (f32[1,4,1,32,256]{4,3,2,1,0:T(8,128)S(1)}, f32[1,4,1,32,256]{4,3,2,1,0:T(8,128)S(1)}, u32[]{:S(2)}, u32[]{:S(2)}) collective-permute-start(f32[1,4,1,32,256]{4,3,2,1,0:T(8,128)S(1)} %slice.227), channel_id=1, source_target_pairs={{0,3},{1,2},{2,1},{3,0},{4,5},{5,4},{6,7},{7,6},{8,11},{9,10},{10,... | collective-permute-start | bytes 393224 | tf_op jit(solution)/shard_map/ppermute | solution.py:78
  166.5 6.3 %collective-permute-start.15 = (f32[1,1,4,32,256]{4,3,2,1,0:T(8,128)S(1)}, f32[1,1,4,32,256]{4,3,2,1,0:T(8,128)S(1)}, u32[]{:S(2)}, u32[]{:S(2)}) collective-permute-start(f32[1,1,4,32,256]{4,3,2,1,0:T(8,128)S(1)} %slice.218), channel_id=1, source_target_pairs={{0,96},{1,97},{2,98},{3,99},{4,36},{5,37},{6,38},{7,39},{8,104},{9... | collective-permute-start | bytes 393224 | tf_op jit(solution)/shard_map/ppermute | solution.py:78
  168.9 6.6 %collective-permute-start.11 = (f32[4,1,1,40,256]{4,3,2,1,0:T(8,128)S(1)}, f32[4,1,1,40,256]{4,3,2,1,0:T(8,128)S(1)}, u32[]{:S(2)}, u32[]{:S(2)}) collective-permute-start(f32[4,1,1,40,256]{4,3,2,1,0:T(8,128)S(1)} %slice.209), channel_id=1, source_target_pairs={{0,24},{1,25},{2,26},{3,27},{4,12},{5,13},{6,14},{7,15},{8,16},{9,... | collective-permute-start | bytes 491528 | tf_op jit(solution)/shard_map/ppermute | solution.py:78
  171.3 5.9 %collective-permute-start.20 = (f32[1,2,1,32,256]{4,3,2,1,0:T(8,128)S(1)}, f32[1,2,1,32,256]{4,3,2,1,0:T(8,128)S(1)}, u32[]{:S(2)}, u32[]{:S(2)}) collective-permute-start(f32[1,2,1,32,256]{4,3,2,1,0:T(8,128)S(1)} %slice.229), channel_id=1, source_target_pairs={{0,8},{1,9},{2,10},{3,11},{4,28},{5,29},{6,30},{7,31},{8,0},{9,1},... | collective-permute-start | bytes 196616 | tf_op jit(solution)/shard_map/ppermute | solution.py:78
  172.8 10.8 %collective-permute-start.16 = (f32[1,1,2,32,256]{4,3,2,1,0:T(8,128)S(1)}, f32[1,1,2,32,256]{4,3,2,1,0:T(8,128)S(1)}, u32[]{:S(2)}, u32[]{:S(2)}) collective-permute-start(f32[1,1,2,32,256]{4,3,2,1,0:T(8,128)S(1)} %slice.220), channel_id=1, source_target_pairs={{0,1},{1,0},{2,3},{3,2},{4,7},{5,6},{6,5},{7,4},{8,9},{9,8},{10,11... | collective-permute-start | bytes 196616 | tf_op jit(solution)/shard_map/ppermute | solution.py:78
  175.6 5.0 %collective-permute-start.12 = (f32[2,1,1,40,256]{4,3,2,1,0:T(8,128)S(1)}, f32[2,1,1,40,256]{4,3,2,1,0:T(8,128)S(1)}, u32[]{:S(2)}, u32[]{:S(2)}) collective-permute-start(f32[2,1,1,40,256]{4,3,2,1,0:T(8,128)S(1)} %slice.211), channel_id=1, source_target_pairs={{0,32},{1,33},{2,34},{3,35},{4,100},{5,101},{6,102},{7,103},{8,40}... | collective-permute-start | bytes 245768 | tf_op jit(solution)/shard_map/ppermute | solution.py:78
  177.3 11.9 %collective-permute-start.21 = (f32[1,1,1,32,256]{4,3,2,1,0:T(8,128)S(1)}, f32[1,1,1,32,256]{4,3,2,1,0:T(8,128)S(1)}, u32[]{:S(2)}, u32[]{:S(2)}) collective-permute-start(f32[1,1,1,32,256]{4,3,2,1,0:T(8,128)S(1)} %slice.231), channel_id=1, source_target_pairs={{0,24},{1,25},{2,26},{3,27},{4,12},{5,13},{6,14},{7,15},{8,16},{9,... | collective-permute-start | bytes 98312 | tf_op jit(solution)/shard_map/ppermute | solution.py:78
  180.6 5.3 %collective-permute-start.13 = (f32[1,1,1,40,256]{4,3,2,1,0:T(8,128)S(1)}, f32[1,1,1,40,256]{4,3,2,1,0:T(8,128)S(1)}, u32[]{:S(2)}, u32[]{:S(2)}) collective-permute-start(f32[1,1,1,40,256]{4,3,2,1,0:T(8,128)S(1)} %slice.213), channel_id=1, source_target_pairs={{0,96},{1,97},{2,98},{3,99},{4,36},{5,37},{6,38},{7,39},{8,104},{9... | collective-permute-start | bytes 122888 | tf_op jit(solution)/shard_map/ppermute | solution.py:78
  183.7 5.5 %collective-permute-start.17 = (f32[1,1,1,32,256]{4,3,2,1,0:T(8,128)S(1)}, f32[1,1,1,32,256]{4,3,2,1,0:T(8,128)S(1)}, u32[]{:S(2)}, u32[]{:S(2)}) collective-permute-start(f32[1,1,1,32,256]{4,3,2,1,0:T(8,128)S(1)} %slice.222), channel_id=1, source_target_pairs={{0,3},{1,2},{2,1},{3,0},{4,5},{5,4},{6,7},{7,6},{8,11},{9,10},{10,... | collective-permute-start | bytes 98312 | tf_op jit(solution)/shard_map/ppermute | solution.py:78
  189.2 5.0 %collective-permute-start.27 = (f32[128,256]{1,0:T(8,128)S(1)}, f32[128,256]{1,0:T(8,128)S(1)}, u32[]{:S(2)}, u32[]{:S(2)}) collective-permute-start(f32[128,256]{1,0:T(8,128)S(1)} %constant_dynamic-update-slice_fusion), channel_id=1, source_target_pairs={{0,1},{1,0},{2,3},{3,2},{4,5},{5,4},{6,7},{7,6},{8,9},{9,8},{10,11... | collective-permute-start | bytes 393224 | tf_op jit(solution)/shard_map/ppermute | solution.py:44
  189.3 6.5 %collective-permute-start.28 = (f32[128,256]{1,0:T(8,128)S(1)}, f32[128,256]{1,0:T(8,128)S(1)}, u32[]{:S(2)}, u32[]{:S(2)}) collective-permute-start(f32[128,256]{1,0:T(8,128)S(1)} %constant_dynamic-update-slice_fusion), channel_id=1, source_target_pairs={{0,2},{1,3},{2,0},{3,1},{4,6},{5,7},{6,4},{7,5},{8,10},{9,11},{10,... | collective-permute-start | bytes 393224 | tf_op jit(solution)/shard_map/ppermute | solution.py:44
  191.4 6.2 %collective-permute-start.29 = (f32[128,256]{1,0:T(8,128)S(1)}, f32[128,256]{1,0:T(8,128)S(1)}, u32[]{:S(2)}, u32[]{:S(2)}) collective-permute-start(f32[128,256]{1,0:T(8,128)S(1)} %constant_dynamic-update-slice_fusion), channel_id=1, source_target_pairs={{0,3},{1,2},{2,1},{3,0},{4,7},{5,6},{6,5},{7,4},{8,11},{9,10},{10,... | collective-permute-start | bytes 393224 | tf_op jit(solution)/shard_map/ppermute | solution.py:44
  (6 other events, 7.5 us)

commit v3 on v2

--- a/solution.py
+++ b/solution.py
@@ -149,13 +149,36 @@
     )(titles.reshape(rows, width), ln_gain.reshape(1, width), w_up)
 
 
-def up_kernel(
-    units, slots, core_ref, keep_at, send_at, slope_ref, act_ref, normed_ref, mean_ref, pool_ref,
-    grad_ref, pre_ref, *out_refs
+def place_sums(core_ref, keep_at, send_at, ups, down, proj, out_refs):
+    slots = proj.shape[0] // 8
+    part = down.shape[0] // slots
+    n_x = slots // 8
+    first = core_ref[0] == 0
+    for q in range(slots // 2):
+        y, x = q // n_x, q % n_x
+        spots = [at[1, y] * n_x + at[2, x] for at in (keep_at, send_at)]
+        pair = (y * 2 * n_x + x, (y * 2 + 1) * n_x + x)
+
+        def store(refs, top, rows):
+            even, odd = (rows(k) for k in pair)
+            end = top + even.shape[0]
+            refs[0][spots[0], top:end, :] = jnp.where(first, even, odd)
+            refs[1][spots[1], top:end, :] = jnp.where(first, odd, even)
+
+        for index, up, refs in zip(*ups, zip(out_refs[::2], out_refs[1::2])):
+            store(refs, 0, lambda k: up[k * part : (k + 1) * part])
+            low = index * 8
+            store(refs, part, lambda k: down[k * part + low : k * part + low + 8])
+            if index == 0:
+                store(refs, part + 8, lambda k: proj[k * 8 : (k + 1) * 8])
+
+
+def first_kernel(
+    units, core_ref, keep_at, send_at, slope_ref, act_ref, mean_ref, pool_ref, grad_ref,
+    normed_ref, pre_ref, *out_refs
 ):
     rows, block = slope_ref.shape
     length, step = rows // units, rows // units * 8
-    part = block // slots
     for r in range(units // 8):
         slope = slope_ref[r * step : (r + 1) * step, :].astype(jnp.float32)
         d_pre = slope.reshape(8, length, block) * act_ref[r * 8 : (r + 1) * 8, :][:, None, :]
@@ -163,78 +186,66 @@
     up = contract_first(pre_ref[...], normed_ref[...])
     down = contract_first(mean_ref[...], grad_ref[...])
     proj = contract_first(pool_ref[...], grad_ref[...])
-    first = core_ref[0] == 0
-    half = slots // 2
-    n_x = half // 4
-    for q in range(half):
-        y, x = q // n_x, q % n_x
-        even, odd = (y * 2 * n_x + x, (y * 2 + 1) * n_x + x)
-
-        def pieces(k):
-            rows_f = up[k * part : (k + 1) * part]
-            rows_d = down[k * part : (k + 1) * part]
-            out = []
-            for p in range(3):
-                out.append(rows_f[:, p * 256 : (p + 1) * 256])
-                out.append(rows_d[p * 8 : (p + 1) * 8])
-            return out + [proj[k * 8 : (k + 1) * 8]]
-
-        a, b = pieces(even), pieces(odd)
-        keep = [jnp.where(first, u, v) for u, v in zip(a, b)]
-        send = [jnp.where(first, v, u) for u, v in zip(a, b)]
-        for values, at, refs in ((keep, keep_at, out_refs[:3]), (send, send_at, out_refs[3:])):
-            place = at[1, y] * n_x + at[2, x]
-            for p in range(3):
-                refs[p][place, :part, :] = values[2 * p]
-                refs[p][place, part : part + 8, :] = values[2 * p + 1]
-            refs[0][place, part + 8 :, :] = values[6]
-
-
-def up_products(core, keep_at, send_at, slope, d_act, normed_b, mean_act_b, pooled_b, grad_b):
-    rows, hidden = slope.shape
-    units, width = d_act.shape[0], normed_b.shape[1]
-    width_e = grad_b.shape[1]
-    sides = keep_at.shape[1]
-    block = hidden // sides
+    place_sums(core_ref, keep_at, send_at, ((0,), (up,)), down, proj, out_refs)
+
+
+def other_kernel(
+    indices, core_ref, keep_at, send_at, pre_ref, mean_ref, pool_ref, grad_ref, *refs
+):
+    count = len(indices)
+    normed = jnp.concatenate([ref[...] for ref in refs[:count]], axis=1)
+    up = contract_first(pre_ref[...], normed)
+    down = contract_first(mean_ref[...], grad_ref[...])
+    wide = grad_ref.shape[1]
+    ups = [up[:, p * wide : (p + 1) * wide] for p in range(count)]
+    empty = jnp.zeros((pool_ref.shape[1], 1), jnp.float32)
+    place_sums(core_ref, keep_at, send_at, (indices, ups), down, empty, refs[count:])
+
+
+def up_products(tables, indices, left, normed_b, mean_act_b, pooled_b, grad_b):
+    rows, hidden = left[0].shape
+    units, width_e = grad_b.shape
+    sides = tables[1].shape[1]
     slots = 2 * sides * sides
-    part = block // slots
-    tall = (part + 16, part + 8, part + 8)
-
-    def whole(array):
-        return pl.BlockSpec(array.shape, lambda i, c, k, s: (0, 0))
+    part = hidden // sides // slots
+    tall = [part + 8 + 8 * (index == 0) for index in indices for _ in range(2)]
+    first = len(left) == 2
 
     def columns(array):
         return pl.BlockSpec((array.shape[0], array.shape[1] // sides), lambda i, c, k, s: (0, i))
 
+    def lanes(index):
+        return pl.BlockSpec((rows, width_e), lambda i, c, k, s: (0, index))
+
+    def sums(height, table):
+        return pl.BlockSpec(
+            (slots // 2, height, width_e), lambda i, *tables: (tables[table][0, i], 0, 0)
+        )
+
+    out_specs = [sums(h, 1 + n % 2) for n, h in enumerate(tall)]
+    out_shape = [jax.ShapeDtypeStruct((sides * slots // 2, h, width_e), jnp.float32) for h in tall]
+    if first:
+        kernel = functools.partial(first_kernel, units)
+        out_specs.insert(0, columns(left[0]))
+        out_shape.insert(0, jax.ShapeDtypeStruct((rows, hidden), jnp.bfloat16))
+    else:
+        kernel = functools.partial(other_kernel, indices)
     return pl.pallas_call(
-        functools.partial(up_kernel, units, slots),
+        kernel,
         grid_spec=pltpu.PrefetchScalarGridSpec(
             num_scalar_prefetch=3,
             grid=(sides,),
-            in_specs=[
-                columns(slope),
-                columns(d_act),
-                whole(normed_b),
-                columns(mean_act_b),
-                columns(pooled_b),
-                whole(grad_b),
-            ],
-            out_specs=[columns(slope)]
-            + [
-                pl.BlockSpec((slots // 2, h, width_e), lambda i, c, k, s: (k[0, i], 0, 0))
-                for h in tall
-            ]
-            + [
-                pl.BlockSpec((slots // 2, h, width_e), lambda i, c, k, s: (s[0, i], 0, 0))
-                for h in tall
-            ],
+            in_specs=[columns(array) for array in left]
+            + [columns(mean_act_b), columns(pooled_b)]
+            + [pl.BlockSpec(grad_b.shape, lambda i, c, k, s: (0, 0))]
+            + [lanes(index) for index in indices],
+            out_specs=out_specs,
         ),
-        out_shape=[jax.ShapeDtypeStruct((rows, hidden), jnp.bfloat16)]
-        + [jax.ShapeDtypeStruct((sides * slots // 2, h, width_e), jnp.float32) for h in tall * 2],
+        out_shape=out_shape,
         compiler_params=pltpu.CompilerParams(vmem_limit_bytes=VMEM),
-        cost_estimate=cost(2 * rows * width * hidden, 4 * rows * hidden),
-        name="up_products",
-    )(core, keep_at, send_at, slope, d_act, normed_b, mean_act_b, pooled_b, grad_b)
+        cost_estimate=cost(2 * rows * width_e * len(indices) * hidden, 4 * rows * hidden),
+        name="first_products" if first else "other_products",
+    )(*tables, *left, mean_act_b, pooled_b, grad_b, *[normed_b] * len(indices))
 
 
 def titles_kernel(pre_ref, w_ref, titles_ref, gain_ref, pool_ref, out_ref, gain_out):
@@ -351,6 +362,7 @@
 
     got = swap_cores(item_part(1 - core))
     mine = (item_part(core) + got).reshape(chips, units, width_e)
+    mine, ln_gain = lax.optimization_barrier((mine, ln_gain))
     item_all = lax.all_to_all(mine, CHIPS, 0, 0, tiled=True)
 
     slot_count = row_ids.shape[1]
@@ -366,9 +378,7 @@
         ],
         axis=1,
     )
-    row_all = lax.all_to_all(
-        row_part.reshape(devices, slot_count // devices, width_e + 128), DEVICES, 0, 0, tiled=True
-    )
+    row_part = row_part.reshape(devices, slot_count // devices, width_e + 128)
 
     normed_b, slope, mean_act, mean_title = forward(titles, ln_gain, w_up)
     mean_act_b = mean_act.astype(jnp.bfloat16)
@@ -379,7 +389,7 @@
     pooled_b = jnp.dot(
         pooled.astype(jnp.bfloat16), spread, preferred_element_type=jnp.float32
     ).astype(jnp.bfloat16)
-    item_all, pooled_b = lax.optimization_barrier((item_all, pooled_b))
+    item_all, pooled_b, row_part = lax.optimization_barrier((item_all, pooled_b, row_part))
 
     item_grad = jnp.sum(item_all, axis=0)
     grad_b = item_grad.astype(jnp.bfloat16)
@@ -389,36 +399,37 @@
     here = [(lax.axis_index(name), lax.axis_size(name)) for name in CHIPS]
     keep_at = jnp.stack([slot_of(core, at, size) for at, size in here])
     send_at = jnp.stack([slot_of(1 - core, at, size) for at, size in here])
-    d_pre, *sums = up_products(
-        core.reshape(1), keep_at, send_at, slope, d_act, normed_b, mean_act_b, pooled_b, grad_b
-    )
+    tables = (core.reshape(1), keep_at, send_at)
+    items = (normed_b, mean_act_b, pooled_b, grad_b)
+    d_pre, *sums = up_products(tables, (0,), (slope, d_act), *items)
+    sums += up_products(tables, (1, 2), (d_pre,), *items)
     parts = [
         (keep + swap_cores(send)).reshape(n_z, n_y, n_x, -1, width_e)
-        for keep, send in zip(sums[:3], sums[3:])
+        for keep, send in zip(sums[::2], sums[1::2])
     ]
 
     beside = title_grads(d_pre, w_up, titles, ln_gain, d_pooled)
     parts, (d_titles, gain_term) = halve(parts, "xyz", False, tuple(beside))
+    parts, row_part = lax.optimization_barrier((parts, row_part))
+    row_all = lax.all_to_all(row_part, DEVICES, 0, 0, tiled=True)
+    gain_term = (gain_term + swap_cores(gain_term)).reshape(8, 3, width_e)
+    gain_term = jnp.pad(jnp.sum(gain_term, axis=0), ((0, 5), (0, 0)))
+    parts, (gain_term,) = halve(parts, "xyz", True, (gain_term,))
+    gain_term = jnp.broadcast_to(gain_term, parts[0].shape[:3] + gain_term.shape)
+    parts[0] = jnp.concatenate([parts[0], gain_term], axis=3)
+    parts, _ = halve(parts, "yzx", False)
+    parts, (row_all,) = halve(parts, "yzx", True, (row_all,))
     beside = row_update(row_all.reshape(slot_count, width_e + 128), table, accum)
-    parts, (new_table, new_accum) = halve(parts, "xyz", True, tuple(beside))
-    gain_term = gain_term + swap_cores(gain_term)
-    for name in ("y", "z"):
-        gain_term = gain_term + along(gain_term, name, 1)
-        gain_term = gain_term + along(gain_term, name, 2)
-    for names in ("yzx", "zxy"):
-        parts, _ = halve(parts, names, False)
-        parts, _ = halve(parts, names, True)
+    parts, (new_table, new_accum) = halve(parts, "zxy", False, tuple(beside))
+    parts, _ = halve(parts, "zxy", True)
 
     flat = [part.reshape(-1, width_e) for part in parts]
-    last = jnp.concatenate(
-        flat + [gain_term[:, p * width_e : (p + 1) * width_e] for p in range(3)], axis=0
-    )
+    last = jnp.concatenate(flat, axis=0)
     blocks = jnp.stack([last, along(last, "x", 1), along(last, "x", 2), along(last, "x", 3)])
     ordered = jnp.stack(
         [lax.dynamic_index_in_dim(blocks, my_x ^ j, 0, keepdims=False) for j in range(n_x)]
     )
-    starts = [0, share_f + 16, 2 * share_f + 24]
-    end = 3 * share_f + 32
+    starts = [0, share_f + 24, 2 * share_f + 32]
     grad_up = jnp.concatenate([ordered[:, at : at + share_f] for at in starts], axis=2)
     grad_up = grad_up.reshape(-1, width).T
     outer = jnp.concatenate(
@@ -428,7 +439,7 @@
     low = (outer - high.astype(jnp.float32)).astype(jnp.bfloat16)
     grad_down = contract_last(high, w_proj) + contract_last(low, w_proj)
     grad_proj = ordered[:, share_f + 8 : share_f + 8 + share_d].reshape(-1, width_e)
-    gains = jnp.sum(ordered[:, end:].reshape(n_x, 3, 8, width_e), axis=(0, 2)).reshape(width)
+    gains = jnp.sum(ordered[:, share_f + 16 : share_f + 19], axis=0).reshape(width)
     mine_at = (lax.axis_index("z") * n_y + lax.axis_index("y")) * n_c + core
     grad_gain = lax.dynamic_slice_in_dim(gains, mine_at * (width // groups), width // groups, 0)
     return (

time: 202 us -> 186 us (0.921)
  waiting for transfers between devices: 41.8 us -> 29.2 us
  local copies, waits for them, and re-layouts: 21.1 us -> 14.2 us
  Pallas kernels: 53.8 us -> 59.1 us
  starting transfers between devices: 53.9 us -> 49.8 us
  matrix products: 16.4 us -> 18.8 us
    ppermute x7 -> x3, waiting for transfers between devices: 14.3 us -> 5.26 us  [along(): return lax.ppermute(block, name, [(i, i ^ step) for i in range(size)])]
    pallas_call x1 -> x2, Pallas kernels: 15.6 us -> 21 us  [up_products(): pl.pallas_call(kernel, grid_spec=pltpu.PrefetchScalarGridSpec(num_scalar_...]
    all_to_all x1, starting transfers between devices: 9.58 us -> 5.68 us  [per_device(): row_all = lax.all_to_all(row_part, DEVICES, 0, 0, tiled=True)]
    ppermute x5, waiting for transfers between devices: 12.1 us -> 8.42 us  [swap_cores(): return lax.ppermute(block, 'c', [(0, 1), (1, 0)])]
    slice x17 -> x16, local copies, waits for them, and re-layouts: 5.23 us -> 2.07 us  [halve(): lax.slice_in_dim(part, middle, None, axis=dim)]
    dot_general x3, matrix products: 6.5 us -> 9 us  [contract_first(): lax.dot_general(left, right, (((0,), (0,)), ((), ())), preferred_element_...]
    concatenate x1, local copies, waits for them, and re-layouts: 2.31 us -> 0.26 us  [per_device(): jnp.concatenate([contract_first(slot_hot, sample_grad), jnp.broadcast_to(...]
    ppermute x7 -> x3, starting transfers between devices: 6.54 us -> 4.78 us  [along(): return lax.ppermute(block, name, [(i, i ^ step) for i in range(size)])]
  transfers between devices with their start and end apart: 32 -> 28, of which waited for: 18 -> 11; matrix products, arithmetic and copies ran while one was open for 13% -> 9% of each run, Pallas kernels for 19% -> 26%
where the time goes in v3:
time: 186 us; the launch traced here: 185 us
  Pallas kernels  59.1 us (32%)
  starting transfers between devices  49.8 us (27%)
  waiting for transfers between devices  29.2 us (16%)
  matrix products  18.8 us (10%)
  local copies, waits for them, and re-layouts  14.2 us (8%)
  other arithmetic  12.4 us (7%)
    ppermute x18, starting transfers between devices, halve(): lax.ppermute(lax.slice_in_dim(part, middle, None, axis=dim), DEVICES, par...  26.9 us
    pallas_call x2, Pallas kernels, up_products(): pl.pallas_call(kernel, grid_spec=pltpu.PrefetchScalarGridSpec(num_scalar_...  21 us
    pallas_call x1, Pallas kernels, forward(): pl.pallas_call(functools.partial(forward_kernel, units), grid=(hidden //...  19.7 us
    ppermute x18, waiting for transfers between devices, halve(): lax.ppermute(lax.slice_in_dim(part, middle, None, axis=dim), DEVICES, par...  15.6 us
    pallas_call x1, Pallas kernels, title_grads(): pl.pallas_call(titles_kernel, grid=(rows // step,), in_specs=[pl.BlockSpe...  14.7 us
    all_to_all x1, starting transfers between devices, per_device(): item_all = lax.all_to_all(mine, CHIPS, 0, 0, tiled=True)  11.9 us
    dot_general x3, matrix products, contract_first(): lax.dot_general(left, right, (((0,), (0,)), ((), ())), preferred_element_...  9 us
    ppermute x5, waiting for transfers between devices, swap_cores(): return lax.ppermute(block, 'c', [(0, 1), (1, 0)])  8.42 us
  transfers between devices with their start and end apart: 28, of which 11 were waited for; matrix products, arithmetic and copies ran while one was open for 9% of the time, Pallas kernels for 26%

profile of v3, /device:TPU:0, one launch (start us, length us, event | category | flops | bytes accessed | tf_op | source)
XLA Modules:
  0.0 184.8 jit_solution(15674296953254480973)
XLA Ops:
  0.7 1.0 copy-done
  1.7 3.8 %fusion = f32[1536,256]{1,0:T(8,128)} fusion(bf16[1024,256]{1,0:T(8,128)(2,1)S(1)} %copy-done, s32[1536]{0:T(1024)S(1)} %fusion.34, s32[1024]{0:T(1024)} %param.17), kind=kOutput, calls=%fused_computation | convolution fusion | flops 806879232 | bytes 2107392 | tf_op jit(solution)/shard_map/dot_general | solution.py:23
  6.6 1.1 reshape.300
  7.8 1.4 collective-permute-done
  9.3 4.5 %fusion.9 = f32[1536,256]{1,0:T(8,128)} fusion(f32[1536,256]{1,0:T(8,128)} %collective-permute-done, bf16[1024,256]{1,0:T(8,128)(2,1)S(1)} %copy-done, s32[1536]{0:T(1024)S(1)} %fusion.35, s32[1024]{0:T(1024)S(1)} %copy-done.20), kind=kOutput, calls=%fused_computation.11 | convolution fusion | flops 807272448 | bytes 3680256 | tf_op jit(solution)/shard_map/dot_general | solution.py:23
  13.8 11.9 %all-to-all-start = ((f32[64,24,256]{2,1,0:T(8,128)}), f32[64,24,256]{2,1,0:T(8,128)}, u32[]{:S(2)}, u32[]{:S(2)}) async-start(f32[64,24,256]{2,1,0:T(8,128)} %bitcast.2), calls=%async_computation | async-start | bytes 3145728 | tf_op jit(solution)/shard_map/all_to_all | solution.py:366
  25.7 1.7 copy-done.5
  27.4 19.7 %forward.1 = (bf16[1536,768]{1,0:T(8,128)(2,1)S(1)}, bf16[1536,3072]{1,0:T(8,128)(2,1)}, f32[24,3072]{1,0:T(8,128)S(1)}, f32[24,768]{1,0:T(8,128)S(1)}) custom-call(bf16[1536,768]{1,0:T(8,128)(2,1)S(1)} %bitcast.41, f32[1,768]{1,0:T(1,128)S(1)} %reshape.299.gain_ref, bf16[768,3072]{1,0:T(8,128)(2,1)} %w_ref.3), custom_call_target="tpu_custom_call" | custom-call | flops 28991029248 | bytes 18874368 | tf_op jit(solution)/shard_map/forward/pallas_call | solution.py:126
  47.1 4.6 %fusion.14.pool_ref = bf16[24,1024]{1,0:T(8,128)(2,1)S(1)} fusion(s32[1024]{0:T(1024)S(1)} %fusion.47, f32[24,768]{1,0:T(8,128)S(1)} %get-tuple-element.52, bf16[24,3072]{1,0:T(8,128)(2,1)S(1)} %convert_element_type.37.mean_ref, bf16[3072,768]{1,0:T(8,128)(2,1)} %param.14), kind=kOutput, calls=%fused_computation.17 | convolution fusion | flops 151842816 | bytes 4993024 | tf_op jit(solution)/shard_map/dot_general | solution.py:389
  51.7 1.5 reduce_sum.29.grad_ref
  53.5 3.7 %convolution_multiply_fusion.act_ref = f32[24,3072]{1,0:T(8,128)S(1)} fusion(bf16[3072,768]{1,0:T(8,128)(2,1)} %param.14, f32[24,768]{1,0:T(8,128)S(1)} %fusion.55.pool_ref), kind=kOutput, calls=%fused_computation.4 | convolution fusion | flops 113338368 | bytes 5087232 | tf_op jit(solution)/shard_map/dot_general | solution.py:29
  57.2 10.5 %first_products.1 = (bf16[1536,3072]{1,0:T(8,128)(2,1)}, f32[64,40,256]{2,1,0:T(8,128)S(1)}, f32[64,40,256]{2,1,0:T(8,128)}) custom-call(s32[1]{0:T(128)} %bitcast.core_ref, s32[3,4]{1,0:T(4,128)S(1)} %pad_add_fusion.keep_at, s32[3,4]{1,0:T(4,128)S(1)} %pad_add_fusion.1.send_at, bf16[1536,3072]{1,0:T(8,128)(2,1)} %get-tuple-element.50.slope_ref, ...), custom_call_target="tpu_custom_call" | custom-call | flops 2415919104 | bytes 18874368 | tf_op jit(solution)/shard_map/first_products/pallas_call | solution.py:233
  67.7 10.5 %other_products.1 = (f32[64,32,256]{2,1,0:T(8,128)S(1)}, f32[64,32,256]{2,1,0:T(8,128)S(1)}, f32[64,32,256]{2,1,0:T(8,128)}, f32[64,32,256]{2,1,0:T(8,128)}) custom-call(s32[1]{0:T(128)} %bitcast.core_ref, s32[3,4]{1,0:T(4,128)S(1)} %pad_add_fusion.keep_at, s32[3,4]{1,0:T(4,128)S(1)} %pad_add_fusion.1.send_at, bf16[1536,3072]{1,0:T(8,128)(2,1)} %get-tuple-element.59.pre_ref, ...), custom_call_target="tpu_custom_call" | custom-call | flops 4831838208 | bytes 18874368 | tf_op jit(solution)/shard_map/other_products/pallas_call | solution.py:233
  78.8 7.0 %collective-permute-done.5 = f32[64,32,256]{2,1,0:T(8,128)S(1)} collective-permute-done((f32[64,32,256]{2,1,0:T(8,128)}, f32[64,32,256]{2,1,0:T(8,128)S(1)}, u32[]{:S(2)}, u32[]{:S(2)}) %collective-permute-start.5) | collective-permute-done | bytes 2097184 | tf_op jit(solution)/shard_map/ppermute | solution.py:39
  85.7 2.0 %add.244 = f32[64,32,256]{2,1,0:T(8,128)S(1)} add(f32[64,32,256]{2,1,0:T(8,128)} %get-tuple-element.62, f32[64,32,256]{2,1,0:T(8,128)S(1)} %collective-permute-done.5) | non-fusion elementwise | flops 524288 | bytes 6291456 | tf_op jit(solution)/shard_map/add | solution.py:407
  88.2 1.4 collective-permute-start.2
  89.8 1.5 collective-permute-start.6
  91.8 1.8 collective-permute-start.4
  93.6 14.7 %title_grads.1 = (bf16[1536,768]{1,0:T(8,128)(2,1)}, f32[8,768]{1,0:T(8,128)S(1)}) custom-call(bf16[1536,3072]{1,0:T(8,128)(2,1)} %get-tuple-element.59.pre_ref, bf16[768,3072]{1,0:T(8,128)(2,1)} %w_ref.3, bf16[1536,768]{1,0:T(8,128)(2,1)S(1)} %bitcast.42, f32[1,768]{1,0:T(1,128)S(1)} %reshape.299.gain_ref, f32[24,768]{1,0:T(8,128)S(1)} %fusion.55.pool_ref), custom_call_target="tpu_custom_call" | custom-call | flops 7247757312 | bytes 9437184 | tf_op jit(solution)/shard_map/title_grads/pallas_call | solution.py:278
  108.3 1.0 copy-done.12
  109.6 1.0 copy-done.13
  110.9 2.1 %collective-permute-start.7 = (f32[4,4,1,40,256]{4,3,2,1,0:T(8,128)S(1)}, f32[4,4,1,40,256]{4,3,2,1,0:T(8,128)}, u32[]{:S(2)}, u32[]{:S(2)}) collective-permute-start(f32[4,4,1,40,256]{4,3,2,1,0:T(8,128)S(1)} %slice.147), channel_id=1, source_target_pairs={{0,3},{1,2},{2,1},{3,0},{4,5},{5,4},{6,7},{7,6},{8,11},{9,10},{10,... | collective-permute-start | bytes 1966088 | tf_op jit(solution)/shard_map/ppermute | solution.py:78
  113.9 2.1 %collective-permute-start.8 = (f32[4,1,4,32,256]{4,3,2,1,0:T(8,128)}, f32[4,1,4,32,256]{4,3,2,1,0:T(8,128)}, u32[]{:S(2)}, u32[]{:S(2)}) collective-permute-start(f32[4,1,4,32,256]{4,3,2,1,0:T(8,128)} %slice.148), channel_id=1, source_target_pairs={{0,24},{1,25},{2,26},{3,27},{4,12},{5,13},{6,14},{7,15},{8,16},{9,... | collective-permute-start | bytes 1572872 | tf_op jit(solution)/shard_map/ppermute | solution.py:78
  116.9 2.2 %collective-permute-start.9 = (f32[1,4,4,32,256]{4,3,2,1,0:T(8,128)}, f32[1,4,4,32,256]{4,3,2,1,0:T(8,128)}, u32[]{:S(2)}, u32[]{:S(2)}) collective-permute-start(f32[1,4,4,32,256]{4,3,2,1,0:T(8,128)} %slice.149), channel_id=1, source_target_pairs={{0,96},{1,97},{2,98},{3,99},{4,36},{5,37},{6,38},{7,39},{8,104},{9... | collective-permute-start | bytes 1572872 | tf_op jit(solution)/shard_map/ppermute | solution.py:78
  119.1 5.7 %all-to-all-start.1 = ((f32[128,4,384]{2,1,0:T(4,128)}), f32[128,4,384]{2,1,0:T(4,128)}, u32[]{:S(2)}, u32[]{:S(2)}) async-start(f32[128,4,384]{2,1,0:T(4,128)} %reshape.300), calls=%async_computation.1 | async-start | bytes 1572864 | tf_op jit(solution)/shard_map/all_to_all | solution.py:414
  124.9 3.8 %collective-permute-done.9 = f32[1,4,4,32,256]{4,3,2,1,0:T(8,128)} collective-permute-done((f32[1,4,4,32,256]{4,3,2,1,0:T(8,128)}, f32[1,4,4,32,256]{4,3,2,1,0:T(8,128)}, u32[]{:S(2)}, u32[]{:S(2)}) %collective-permute-start.9) | collective-permute-done | bytes 524320 | tf_op jit(solution)/shard_map/ppermute | solution.py:78
  128.7 1.3 slice_add_fusion.3
  130.1 1.2 slice_add_fusion.2
  131.4 1.1 slice_add_fusion.4
  132.8 3.9 %collective-permute-done.15 = f32[1,4,2,32,256]{4,3,2,1,0:T(8,128)S(1)} collective-permute-done((f32[1,4,2,32,256]{4,3,2,1,0:T(8,128)S(1)}, f32[1,4,2,32,256]{4,3,2,1,0:T(8,128)S(1)}, u32[]{:S(2)}, u32[]{:S(2)}) %collective-permute-start.15) | collective-permute-done | bytes 262176 | tf_op jit(solution)/shard_map/ppermute | solution.py:78
  136.8 2.2 %collective-permute-start.16 = (f32[1,4,1,32,256]{4,3,2,1,0:T(8,128)S(1)}, f32[1,4,1,32,256]{4,3,2,1,0:T(8,128)S(1)}, u32[]{:S(2)}, u32[]{:S(2)}) collective-permute-start(f32[1,4,1,32,256]{4,3,2,1,0:T(8,128)S(1)} %slice.199), channel_id=1, source_target_pairs={{0,3},{1,2},{2,1},{3,0},{4,5},{5,4},{6,7},{7,6},{8,11},{9,10},{10,... | collective-permute-start | bytes 393224 | tf_op jit(solution)/shard_map/ppermute | solution.py:78
  140.0 2.1 %collective-permute-start.12 = (f32[4,1,1,48,256]{4,3,2,1,0:T(8,128)S(1)}, f32[4,1,1,48,256]{4,3,2,1,0:T(8,128)}, u32[]{:S(2)}, u32[]{:S(2)}) collective-permute-start(f32[4,1,1,48,256]{4,3,2,1,0:T(8,128)S(1)} %slice.193), channel_id=1, source_target_pairs={{0,24},{1,25},{2,26},{3,27},{4,12},{5,13},{6,14},{7,15},{8,16},{9,... | collective-permute-start | bytes 589832 | tf_op jit(solution)/shard_map/ppermute | solution.py:78
  142.8 3.5 %collective-permute-start.14 = (f32[1,1,4,32,256]{4,3,2,1,0:T(8,128)S(1)}, f32[1,1,4,32,256]{4,3,2,1,0:T(8,128)S(1)}, u32[]{:S(2)}, u32[]{:S(2)}) collective-permute-start(f32[1,1,4,32,256]{4,3,2,1,0:T(8,128)S(1)} %slice.196), channel_id=1, source_target_pairs={{0,96},{1,97},{2,98},{3,99},{4,36},{5,37},{6,38},{7,39},{8,104},{9... | collective-permute-start | bytes 393224 | tf_op jit(solution)/shard_map/ppermute | solution.py:78
  146.3 2.9 %collective-permute-done.14 = f32[1,1,4,32,256]{4,3,2,1,0:T(8,128)S(1)} collective-permute-done((f32[1,1,4,32,256]{4,3,2,1,0:T(8,128)S(1)}, f32[1,1,4,32,256]{4,3,2,1,0:T(8,128)S(1)}, u32[]{:S(2)}, u32[]{:S(2)}) %collective-permute-start.14) | collective-permute-done | bytes 131104 | tf_op jit(solution)/shard_map/ppermute | solution.py:78
  149.9 1.4 reshape.304.arrived_ref
  151.3 0.9 slice_add_fusion.8
  152.5 1.0 slice_add_fusion.9
  153.5 1.8 collective-permute-start.18
  155.3 1.0 slice_add_fusion.7
  156.4 1.6 copy-done.4
  158.0 3.7 %row_update.1 = (f32[2048,256]{1,0:T(8,128)}, f32[2048,256]{1,0:T(8,128)}) custom-call(f32[512,384]{1,0:T(8,128)S(1)} %reshape.304.arrived_ref, f32[2048,256]{1,0:T(8,128)S(1)} %copy-done.3, f32[2048,256]{1,0:T(8,128)S(1)} %copy-done.4), custom_call_target="tpu_custom_call" | custom-call | flops 1073741824 | bytes 8388608 | tf_op jit(solution)/shard_map/row_update/pallas_call | solution.py:321
  161.7 3.3 %collective-permute-start.20 = (f32[1,1,1,48,256]{4,3,2,1,0:T(8,128)S(1)}, f32[1,1,1,48,256]{4,3,2,1,0:T(8,128)S(1)}, u32[]{:S(2)}, u32[]{:S(2)}) collective-permute-start(f32[1,1,1,48,256]{4,3,2,1,0:T(8,128)S(1)} %slice.207), channel_id=1, source_target_pairs={{0,96},{1,97},{2,98},{3,99},{4,36},{5,37},{6,38},{7,39},{8,104},{9... | collective-permute-start | bytes 147464 | tf_op jit(solution)/shard_map/ppermute | solution.py:78
  165.9 1.2 collective-permute-start.22
  167.1 3.1 %collective-permute-done.21 = f32[1,1,1,32,256]{4,3,2,1,0:T(8,128)S(1)} collective-permute-done((f32[1,1,1,32,256]{4,3,2,1,0:T(8,128)S(1)}, f32[1,1,1,32,256]{4,3,2,1,0:T(8,128)S(1)}, u32[]{:S(2)}, u32[]{:S(2)}) %collective-permute-start.21) | collective-permute-done | bytes 32800 | tf_op jit(solution)/shard_map/ppermute | solution.py:78
  171.7 3.4 %collective-permute-start.24 = (f32[112,256]{1,0:T(8,128)S(1)}, f32[112,256]{1,0:T(8,128)S(1)}, u32[]{:S(2)}, u32[]{:S(2)}) collective-permute-start(f32[112,256]{1,0:T(8,128)S(1)} %get-tuple-element.103), channel_id=1, source_target_pairs={{0,2},{1,3},{2,0},{3,1},{4,6},{5,7},{6,4},{7,5},{8,10},{9,11},{10,... | collective-permute-start | bytes 344072 | tf_op jit(solution)/shard_map/ppermute | solution.py:44
  176.0 3.2 %collective-permute-done.24 = f32[112,256]{1,0:T(8,128)S(1)} collective-permute-done((f32[112,256]{1,0:T(8,128)S(1)}, f32[112,256]{1,0:T(8,128)S(1)}, u32[]{:S(2)}, u32[]{:S(2)}) %collective-permute-start.24) | collective-permute-done | bytes 114720 | tf_op jit(solution)/shard_map/ppermute | solution.py:44
  179.2 2.0 %collective-permute-done.25 = f32[112,256]{1,0:T(8,128)S(1)} collective-permute-done((f32[112,256]{1,0:T(8,128)S(1)}, f32[112,256]{1,0:T(8,128)S(1)}, u32[]{:S(2)}, u32[]{:S(2)}) %collective-permute-start.25) | collective-permute-done | bytes 114720 | tf_op jit(solution)/shard_map/ppermute | solution.py:44
  183.1 1.0 convolution_add_fusion
  (136 shorter events, 14.4 us)
Async XLA Ops:
  0.6 1.1 copy-start
  1.7 3.8 %copy-start.18 = (s32[1,512]{1,0:T(1,128)S(1)}, s32[1,512]{1,0:T(1,128)}, u32[]{:S(2)}) copy-start(s32[1,512]{1,0:T(1,128)} %param.19) | copy-start | bytes 6148
  1.7 3.8 %copy-start.19 = (s32[1024]{0:T(1024)S(1)}, s32[1024]{0:T(1024)}, u32[]{:S(2)}) copy-start(s32[1024]{0:T(1024)} %param.18) | copy-start | bytes 12292
  5.5 3.8 %collective-permute-start = (f32[1536,256]{1,0:T(8,128)}, f32[1536,256]{1,0:T(8,128)}, u32[]{:S(2)}, u32[]{:S(2)}) collective-permute-start(f32[1536,256]{1,0:T(8,128)} %fusion), channel_id=1, source_target_pairs={{0,4},{4,0},{1,5},{5,1},{2,6},{6,2},{3,7},{7,3},{8,12},{12,8},{9,1... | collective-permute-start | bytes 4718600 | tf_op jit(solution)/shard_map/ppermute | solution.py:39
  6.2 3.0 %copy-start.20 = (s32[1024]{0:T(1024)S(1)}, s32[1024]{0:T(1024)}, u32[]{:S(2)}) copy-start(s32[1024]{0:T(1024)} %param.17) | copy-start | bytes 12292
  7.8 6.0 %copy-start.17 = (f32[768]{0:T(1024)S(1)}, f32[768]{0:T(1024)}, u32[]{:S(2)}) copy-start(f32[768]{0:T(1024)} %param.12) | copy-start | bytes 9220
  13.8 38.0 %all-to-all-start = ((f32[64,24,256]{2,1,0:T(8,128)}), f32[64,24,256]{2,1,0:T(8,128)}, u32[]{:S(2)}, u32[]{:S(2)}) async-start(f32[64,24,256]{2,1,0:T(8,128)} %bitcast.2), calls=%async_computation | async-start | bytes 3145728 | tf_op jit(solution)/shard_map/all_to_all | solution.py:366
  25.7 1.7 copy-start.5
  47.1 10.1 %copy-start.2 = (bf16[1536,768]{1,0:T(8,128)(2,1)}, bf16[1536,768]{1,0:T(8,128)(2,1)S(1)}, u32[]{:S(2)}) copy-start(bf16[1536,768]{1,0:T(8,128)(2,1)S(1)} %get-tuple-element.56.normed_ref.refs_0_.refs_1_) | copy-start | bytes 7077892
  47.1 6.2 %copy-start.8 = (bf16[768,256]{1,0:T(8,128)(2,1)S(1)}, bf16[768,256]{1,0:T(8,128)(2,1)}, u32[]{:S(2)}) copy-start(bf16[768,256]{1,0:T(8,128)(2,1)} %param.15) | copy-start | bytes 1179652
  67.7 20.0 %collective-permute-start.1 = (f32[64,40,256]{2,1,0:T(8,128)}, f32[64,40,256]{2,1,0:T(8,128)S(1)}, u32[]{:S(2)}, u32[]{:S(2)}) collective-permute-start(f32[64,40,256]{2,1,0:T(8,128)} %get-tuple-element.58), channel_id=1, source_target_pairs={{0,4},{4,0},{1,5},{5,1},{2,6},{6,2},{3,7},{7,3},{8,12},{12,8},{9,1... | collective-permute-start | bytes 7864328 | tf_op jit(solution)/shard_map/ppermute | solution.py:39
  78.3 7.5 %collective-permute-start.5 = (f32[64,32,256]{2,1,0:T(8,128)}, f32[64,32,256]{2,1,0:T(8,128)S(1)}, u32[]{:S(2)}, u32[]{:S(2)}) collective-permute-start(f32[64,32,256]{2,1,0:T(8,128)} %get-tuple-element.63), channel_id=1, source_target_pairs={{0,4},{4,0},{1,5},{5,1},{2,6},{6,2},{3,7},{7,3},{8,12},{12,8},{9,1... | collective-permute-start | bytes 6291464 | tf_op jit(solution)/shard_map/ppermute | solution.py:39
  78.8 12.5 %collective-permute-start.3 = (f32[64,32,256]{2,1,0:T(8,128)S(1)}, f32[64,32,256]{2,1,0:T(8,128)S(1)}, u32[]{:S(2)}, u32[]{:S(2)}) collective-permute-start(f32[64,32,256]{2,1,0:T(8,128)S(1)} %get-tuple-element.61), channel_id=1, source_target_pairs={{0,4},{4,0},{1,5},{5,1},{2,6},{6,2},{3,7},{7,3},{8,12},{12,8},{9,1... | collective-permute-start | bytes 6291464 | tf_op jit(solution)/shard_map/ppermute | solution.py:39
  88.2 20.1 %collective-permute-start.2 = (f32[4,4,2,40,256]{4,3,2,1,0:T(8,128)S(1)}, f32[4,4,2,40,256]{4,3,2,1,0:T(8,128)S(1)}, u32[]{:S(2)}, u32[]{:S(2)}) collective-permute-start(f32[4,4,2,40,256]{4,3,2,1,0:T(8,128)S(1)} %slice.184), channel_id=1, source_target_pairs={{0,1},{1,0},{2,3},{3,2},{4,7},{5,6},{6,5},{7,4},{8,9},{9,8},{10,11... | collective-permute-start | bytes 3932168 | tf_op jit(solution)/shard_map/ppermute | solution.py:78
  89.8 18.5 %collective-permute-start.6 = (f32[2,4,4,32,256]{4,3,2,1,0:T(8,128)S(1)}, f32[2,4,4,32,256]{4,3,2,1,0:T(8,128)S(1)}, u32[]{:S(2)}, u32[]{:S(2)}) collective-permute-start(f32[2,4,4,32,256]{4,3,2,1,0:T(8,128)S(1)} %bitcast.48), channel_id=1, source_target_pairs={{0,32},{1,33},{2,34},{3,35},{4,100},{5,101},{6,102},{7,103},{8,40}... | collective-permute-start | bytes 3145736 | tf_op jit(solution)/shard_map/ppermute | solution.py:78
  91.3 2.3 %copy-start.6 = (bf16[24,64,768]{2,1,0:T(8,128)(2,1)S(1)}, bf16[24,64,768]{2,1,0:T(8,128)(2,1)}, u32[]{:S(2)}) copy-start(bf16[24,64,768]{2,1,0:T(8,128)(2,1)} %param.11) | copy-start | bytes 7077892
  91.8 16.5 %collective-permute-start.4 = (f32[4,2,4,32,256]{4,3,2,1,0:T(8,128)S(1)}, f32[4,2,4,32,256]{4,3,2,1,0:T(8,128)S(1)}, u32[]{:S(2)}, u32[]{:S(2)}) collective-permute-start(f32[4,2,4,32,256]{4,3,2,1,0:T(8,128)S(1)} %slice.185), channel_id=1, source_target_pairs={{0,8},{1,9},{2,10},{3,11},{4,28},{5,29},{6,30},{7,31},{8,0},{9,1},... | collective-permute-start | bytes 3145736 | tf_op jit(solution)/shard_map/ppermute | solution.py:78
  108.3 1.0 copy-start.12
  109.4 1.2 copy-start.13
  110.8 6.1 %copy-start.7 = (f32[2,4,4,32,256]{4,3,2,1,0:T(8,128)}, f32[2,4,4,32,256]{4,3,2,1,0:T(8,128)S(1)}, u32[]{:S(2)}) copy-start(f32[2,4,4,32,256]{4,3,2,1,0:T(8,128)S(1)} %add.247) | copy-start | bytes 3145732
  110.9 17.8 %collective-permute-start.7 = (f32[4,4,1,40,256]{4,3,2,1,0:T(8,128)S(1)}, f32[4,4,1,40,256]{4,3,2,1,0:T(8,128)}, u32[]{:S(2)}, u32[]{:S(2)}) collective-permute-start(f32[4,4,1,40,256]{4,3,2,1,0:T(8,128)S(1)} %slice.147), channel_id=1, source_target_pairs={{0,3},{1,2},{2,1},{3,0},{4,5},{5,4},{6,7},{7,6},{8,11},{9,10},{10,... | collective-permute-start | bytes 1966088 | tf_op jit(solution)/shard_map/ppermute | solution.py:78
  113.9 10.9 %collective-permute-start.8 = (f32[4,1,4,32,256]{4,3,2,1,0:T(8,128)}, f32[4,1,4,32,256]{4,3,2,1,0:T(8,128)}, u32[]{:S(2)}, u32[]{:S(2)}) collective-permute-start(f32[4,1,4,32,256]{4,3,2,1,0:T(8,128)} %slice.148), channel_id=1, source_target_pairs={{0,24},{1,25},{2,26},{3,27},{4,12},{5,13},{6,14},{7,15},{8,16},{9,... | collective-permute-start | bytes 1572872 | tf_op jit(solution)/shard_map/ppermute | solution.py:78
  116.9 11.8 %collective-permute-start.9 = (f32[1,4,4,32,256]{4,3,2,1,0:T(8,128)}, f32[1,4,4,32,256]{4,3,2,1,0:T(8,128)}, u32[]{:S(2)}, u32[]{:S(2)}) collective-permute-start(f32[1,4,4,32,256]{4,3,2,1,0:T(8,128)} %slice.149), channel_id=1, source_target_pairs={{0,96},{1,97},{2,98},{3,99},{4,36},{5,37},{6,38},{7,39},{8,104},{9... | collective-permute-start | bytes 1572872 | tf_op jit(solution)/shard_map/ppermute | solution.py:78
  119.1 5.7 %collective-permute-start.10 = (f32[8,768]{1,0:T(8,128)S(1)}, f32[8,768]{1,0:T(8,128)S(1)}, u32[]{:S(2)}, u32[]{:S(2)}) collective-permute-start(f32[8,768]{1,0:T(8,128)S(1)} %get-tuple-element.74), channel_id=1, source_target_pairs={{0,4},{4,0},{1,5},{5,1},{2,6},{6,2},{3,7},{7,3},{8,12},{12,8},{9,1... | collective-permute-start | bytes 73736 | tf_op jit(solution)/shard_map/ppermute | solution.py:39
  119.1 27.2 %all-to-all-start.1 = ((f32[128,4,384]{2,1,0:T(4,128)}), f32[128,4,384]{2,1,0:T(4,128)}, u32[]{:S(2)}, u32[]{:S(2)}) async-start(f32[128,4,384]{2,1,0:T(4,128)} %reshape.300), calls=%async_computation.1 | async-start | bytes 1572864 | tf_op jit(solution)/shard_map/all_to_all | solution.py:414
  130.0 6.7 %collective-permute-start.15 = (f32[1,4,2,32,256]{4,3,2,1,0:T(8,128)S(1)}, f32[1,4,2,32,256]{4,3,2,1,0:T(8,128)S(1)}, u32[]{:S(2)}, u32[]{:S(2)}) collective-permute-start(f32[1,4,2,32,256]{4,3,2,1,0:T(8,128)S(1)} %slice.198), channel_id=1, source_target_pairs={{0,1},{1,0},{2,3},{3,2},{4,7},{5,6},{6,5},{7,4},{8,9},{9,8},{10,11... | collective-permute-start | bytes 786440 | tf_op jit(solution)/shard_map/ppermute | solution.py:78
  131.3 8.5 %collective-permute-start.11 = (f32[4,2,1,48,256]{4,3,2,1,0:T(8,128)S(1)}, f32[4,2,1,48,256]{4,3,2,1,0:T(8,128)S(1)}, u32[]{:S(2)}, u32[]{:S(2)}) collective-permute-start(f32[4,2,1,48,256]{4,3,2,1,0:T(8,128)S(1)} %pad_maximum_fusion.3), channel_id=1, source_target_pairs={{0,8},{1,9},{2,10},{3,11},{4,28},{5,29},{6,30},{7,31},{8,0},{9,1},... | collective-permute-start | bytes 1179656 | tf_op jit(solution)/shard_map/ppermute | solution.py:78
  132.6 9.4 %collective-permute-start.13 = (f32[2,1,4,32,256]{4,3,2,1,0:T(8,128)S(1)}, f32[2,1,4,32,256]{4,3,2,1,0:T(8,128)S(1)}, u32[]{:S(2)}, u32[]{:S(2)}) collective-permute-start(f32[2,1,4,32,256]{4,3,2,1,0:T(8,128)S(1)} %slice.195), channel_id=1, source_target_pairs={{0,32},{1,33},{2,34},{3,35},{4,100},{5,101},{6,102},{7,103},{8,40}... | collective-permute-start | bytes 786440 | tf_op jit(solution)/shard_map/ppermute | solution.py:78
  136.8 2.2 %copy-start.14 = (f32[1,4,2,32,256]{4,3,2,1,0:T(8,128)}, f32[1,4,2,32,256]{4,3,2,1,0:T(8,128)S(1)}, u32[]{:S(2)}) copy-start(f32[1,4,2,32,256]{4,3,2,1,0:T(8,128)S(1)} %slice_add_fusion.5) | copy-start | bytes 786436
  136.8 9.5 %collective-permute-start.16 = (f32[1,4,1,32,256]{4,3,2,1,0:T(8,128)S(1)}, f32[1,4,1,32,256]{4,3,2,1,0:T(8,128)S(1)}, u32[]{:S(2)}, u32[]{:S(2)}) collective-permute-start(f32[1,4,1,32,256]{4,3,2,1,0:T(8,128)S(1)} %slice.199), channel_id=1, source_target_pairs={{0,3},{1,2},{2,1},{3,0},{4,5},{5,4},{6,7},{7,6},{8,11},{9,10},{10,... | collective-permute-start | bytes 393224 | tf_op jit(solution)/shard_map/ppermute | solution.py:78
  139.9 2.2 %copy-start.10 = (f32[4,2,1,48,256]{4,3,2,1,0:T(8,128)}, f32[4,2,1,48,256]{4,3,2,1,0:T(8,128)S(1)}, u32[]{:S(2)}) copy-start(f32[4,2,1,48,256]{4,3,2,1,0:T(8,128)S(1)} %fusion.18) | copy-start | bytes 1179652
  139.9 16.4 %copy-start.3 = (f32[2048,256]{1,0:T(8,128)S(1)}, f32[2048,256]{1,0:T(8,128)}, u32[]{:S(2)}) copy-start(f32[2048,256]{1,0:T(8,128)} %table_ref.1) | copy-start | bytes 6291460
  140.0 9.3 %collective-permute-start.12 = (f32[4,1,1,48,256]{4,3,2,1,0:T(8,128)S(1)}, f32[4,1,1,48,256]{4,3,2,1,0:T(8,128)}, u32[]{:S(2)}, u32[]{:S(2)}) collective-permute-start(f32[4,1,1,48,256]{4,3,2,1,0:T(8,128)S(1)} %slice.193), channel_id=1, source_target_pairs={{0,24},{1,25},{2,26},{3,27},{4,12},{5,13},{6,14},{7,15},{8,16},{9,... | collective-permute-start | bytes 589832 | tf_op jit(solution)/shard_map/ppermute | solution.py:78
  142.1 0.7 copy-start.15
  142.8 12.5 %copy-start.11 = (f32[4,2,1,48,256]{4,3,2,1,0:T(8,128)S(1)}, f32[4,2,1,48,256]{4,3,2,1,0:T(8,128)}, u32[]{:S(2)}) copy-start(f32[4,2,1,48,256]{4,3,2,1,0:T(8,128)} %copy-done.10) | copy-start | bytes 1179652
  142.8 6.4 %collective-permute-start.14 = (f32[1,1,4,32,256]{4,3,2,1,0:T(8,128)S(1)}, f32[1,1,4,32,256]{4,3,2,1,0:T(8,128)S(1)}, u32[]{:S(2)}, u32[]{:S(2)}) collective-permute-start(f32[1,1,4,32,256]{4,3,2,1,0:T(8,128)S(1)} %slice.196), channel_id=1, source_target_pairs={{0,96},{1,97},{2,98},{3,99},{4,36},{5,37},{6,38},{7,39},{8,104},{9... | collective-permute-start | bytes 393224 | tf_op jit(solution)/shard_map/ppermute | solution.py:78
  152.2 9.4 %collective-permute-start.19 = (f32[1,2,1,32,256]{4,3,2,1,0:T(8,128)S(1)}, f32[1,2,1,32,256]{4,3,2,1,0:T(8,128)S(1)}, u32[]{:S(2)}, u32[]{:S(2)}) collective-permute-start(f32[1,2,1,32,256]{4,3,2,1,0:T(8,128)S(1)} %slice.205), channel_id=1, source_target_pairs={{0,8},{1,9},{2,10},{3,11},{4,28},{5,29},{6,30},{7,31},{8,0},{9,1},... | collective-permute-start | bytes 196616 | tf_op jit(solution)/shard_map/ppermute | solution.py:78
  153.5 8.2 %collective-permute-start.18 = (f32[1,1,2,32,256]{4,3,2,1,0:T(8,128)S(1)}, f32[1,1,2,32,256]{4,3,2,1,0:T(8,128)S(1)}, u32[]{:S(2)}, u32[]{:S(2)}) collective-permute-start(f32[1,1,2,32,256]{4,3,2,1,0:T(8,128)S(1)} %slice.203), channel_id=1, source_target_pairs={{0,1},{1,0},{2,3},{3,2},{4,7},{5,6},{6,5},{7,4},{8,9},{9,8},{10,11... | collective-permute-start | bytes 196616 | tf_op jit(solution)/shard_map/ppermute | solution.py:78
  156.3 5.4 %collective-permute-start.17 = (f32[2,1,1,48,256]{4,3,2,1,0:T(8,128)S(1)}, f32[2,1,1,48,256]{4,3,2,1,0:T(8,128)S(1)}, u32[]{:S(2)}, u32[]{:S(2)}) collective-permute-start(f32[2,1,1,48,256]{4,3,2,1,0:T(8,128)S(1)} %slice.201), channel_id=1, source_target_pairs={{0,32},{1,33},{2,34},{3,35},{4,100},{5,101},{6,102},{7,103},{8,40}... | collective-permute-start | bytes 294920 | tf_op jit(solution)/shard_map/ppermute | solution.py:78
  156.4 1.6 copy-start.4
  161.7 9.4 %collective-permute-start.20 = (f32[1,1,1,48,256]{4,3,2,1,0:T(8,128)S(1)}, f32[1,1,1,48,256]{4,3,2,1,0:T(8,128)S(1)}, u32[]{:S(2)}, u32[]{:S(2)}) collective-permute-start(f32[1,1,1,48,256]{4,3,2,1,0:T(8,128)S(1)} %slice.207), channel_id=1, source_target_pairs={{0,96},{1,97},{2,98},{3,99},{4,36},{5,37},{6,38},{7,39},{8,104},{9... | collective-permute-start | bytes 147464 | tf_op jit(solution)/shard_map/ppermute | solution.py:78
  165.0 5.2 %collective-permute-start.21 = (f32[1,1,1,32,256]{4,3,2,1,0:T(8,128)S(1)}, f32[1,1,1,32,256]{4,3,2,1,0:T(8,128)S(1)}, u32[]{:S(2)}, u32[]{:S(2)}) collective-permute-start(f32[1,1,1,32,256]{4,3,2,1,0:T(8,128)S(1)} %slice.210), channel_id=1, source_target_pairs={{0,3},{1,2},{2,1},{3,0},{4,5},{5,4},{6,7},{7,6},{8,11},{9,10},{10,... | collective-permute-start | bytes 98312 | tf_op jit(solution)/shard_map/ppermute | solution.py:78
  165.9 5.2 %collective-permute-start.22 = (f32[1,1,1,32,256]{4,3,2,1,0:T(8,128)S(1)}, f32[1,1,1,32,256]{4,3,2,1,0:T(8,128)S(1)}, u32[]{:S(2)}, u32[]{:S(2)}) collective-permute-start(f32[1,1,1,32,256]{4,3,2,1,0:T(8,128)S(1)} %slice.213), channel_id=1, source_target_pairs={{0,24},{1,25},{2,26},{3,27},{4,12},{5,13},{6,14},{7,15},{8,16},{9,... | collective-permute-start | bytes 98312 | tf_op jit(solution)/shard_map/ppermute | solution.py:78
  171.1 4.9 %collective-permute-start.23 = (f32[112,256]{1,0:T(8,128)S(1)}, f32[112,256]{1,0:T(8,128)S(1)}, u32[]{:S(2)}, u32[]{:S(2)}) collective-permute-start(f32[112,256]{1,0:T(8,128)S(1)} %get-tuple-element.103), channel_id=1, source_target_pairs={{0,1},{1,0},{2,3},{3,2},{4,5},{5,4},{6,7},{7,6},{8,9},{9,8},{10,11... | collective-permute-start | bytes 344072 | tf_op jit(solution)/shard_map/ppermute | solution.py:44
  171.7 7.4 %collective-permute-start.24 = (f32[112,256]{1,0:T(8,128)S(1)}, f32[112,256]{1,0:T(8,128)S(1)}, u32[]{:S(2)}, u32[]{:S(2)}) collective-permute-start(f32[112,256]{1,0:T(8,128)S(1)} %get-tuple-element.103), channel_id=1, source_target_pairs={{0,2},{1,3},{2,0},{3,1},{4,6},{5,7},{6,4},{7,5},{8,10},{9,11},{10,... | collective-permute-start | bytes 344072 | tf_op jit(solution)/shard_map/ppermute | solution.py:44
  175.2 6.0 %collective-permute-start.25 = (f32[112,256]{1,0:T(8,128)S(1)}, f32[112,256]{1,0:T(8,128)S(1)}, u32[]{:S(2)}, u32[]{:S(2)}) collective-permute-start(f32[112,256]{1,0:T(8,128)S(1)} %get-tuple-element.103), channel_id=1, source_target_pairs={{0,3},{1,2},{2,1},{3,0},{4,7},{5,6},{6,5},{7,4},{8,11},{9,10},{10,... | collective-permute-start | bytes 344072 | tf_op jit(solution)/shard_map/ppermute | solution.py:44
  181.2 1.0 copy-start.9
  181.3 3.5 %copy-start.1 = (bf16[1024,256]{1,0:T(8,128)(2,1)S(1)}, bf16[1024,256]{1,0:T(8,128)(2,1)}, u32[]{:S(2)}) copy-start(bf16[1024,256]{1,0:T(8,128)(2,1)} %param.16) | copy-start | bytes 1572868
  (1 other events, 0.7 us)

commit v4 on v3

--- a/solution.py
+++ b/solution.py
@@ -16,7 +16,7 @@
 CHIPS = ("z", "y", "x")
 GROUP = ("z", "y", "c")
 DEVICES = ("z", "y", "c", "x")
-VMEM = 48 << 20
+VMEM = 30 << 20
 
 
 def contract_first(left, right):
@@ -91,6 +91,36 @@
     return offset * inv_scale, inv_scale
 
 
+def item_kernel(key_ref, grad_ref, *refs):
+    out_ref = refs[-1]
+    rows = out_ref.shape[0]
+    place = lax.broadcasted_iota(jnp.int32, (rows, key_ref.shape[1]), 0) + pl.program_id(0) * rows
+    onehot = jnp.where(place == key_ref[...], 1.0, 0.0).astype(jnp.bfloat16)
+    total = jnp.dot(onehot, grad_ref[...], preferred_element_type=jnp.float32)
+    for ref in refs[:-1]:
+        total = total + ref[...]
+    out_ref[...] = total
+
+
+def segment_sums(key, sample_grad, count, *more):
+    samples, width_e = sample_grad.shape
+    step = 512
+    return pl.pallas_call(
+        item_kernel,
+        grid=(count // step,),
+        in_specs=[
+            pl.BlockSpec((1, samples), lambda i: (0, 0)),
+            pl.BlockSpec((samples, width_e), lambda i: (0, 0)),
+        ]
+        + [pl.BlockSpec((step, width_e), lambda i: (i, 0))] * len(more),
+        out_specs=pl.BlockSpec((step, width_e), lambda i: (i, 0)),
+        out_shape=jax.ShapeDtypeStruct((count, width_e), jnp.float32),
+        compiler_params=pltpu.CompilerParams(vmem_limit_bytes=24 << 20),
+        cost_estimate=cost(2 * samples * width_e * count, 4 * width_e * count),
+        name="segment_sums",
+    )(key.reshape(1, samples), sample_grad, *more)
+
+
 def forward_kernel(units, titles_ref, gain_ref, w_ref, normed_ref, slope_ref, act_ref, mean_ref):
     rows, width = titles_ref.shape
     length = rows // units
@@ -139,7 +169,7 @@
         ],
         out_shape=[
             jax.ShapeDtypeStruct((rows, width), jnp.bfloat16),
-            jax.ShapeDtypeStruct((rows, hidden), jnp.bfloat16),
+            pltpu.HBM((rows, hidden), jnp.bfloat16),
             jax.ShapeDtypeStruct((units, hidden), jnp.float32),
             jax.ShapeDtypeStruct((units, width), jnp.float32),
         ],
@@ -227,7 +257,7 @@
     if first:
         kernel = functools.partial(first_kernel, units)
         out_specs.insert(0, columns(left[0]))
-        out_shape.insert(0, jax.ShapeDtypeStruct((rows, hidden), jnp.bfloat16))
+        out_shape.insert(0, pltpu.VMEM((rows, hidden), jnp.bfloat16))
     else:
         kernel = functools.partial(other_kernel, indices)
     return pl.pallas_call(
@@ -324,7 +354,7 @@
         in_specs=[pl.BlockSpec(arrived.shape, lambda i: (0, 0)), tile, tile],
         out_specs=[tile, tile],
         out_shape=[jax.ShapeDtypeStruct((rows, width_e), jnp.float32)] * 2,
-        compiler_params=pltpu.CompilerParams(vmem_limit_bytes=VMEM),
+        compiler_params=pltpu.CompilerParams(vmem_limit_bytes=16 << 20),
         cost_estimate=cost(4 * rows * width_e * arrived.shape[0], 16 * rows * width_e),
         name="row_update",
     )(arrived, table, accum)
@@ -352,16 +382,13 @@
     width_e = sample_grad.shape[1]
     share_f, share_d = hidden // devices, width // devices
 
-    place = lax.iota(jnp.int32, chips * units)
-    chip, unit = place // units, place % units
-
-    def item_part(of_core):
-        wanted = (((chip // n_x) * n_c + of_core) * n_x + chip % n_x) * units + unit
-        onehot = (sample_item[:, None] == wanted[None, :]).astype(jnp.bfloat16)
-        return contract_first(onehot, sample_grad)
-
-    got = swap_cores(item_part(1 - core))
-    mine = (item_part(core) + got).reshape(chips, units, width_e)
+    owner = sample_item // units
+    spot = (owner // (n_c * n_x) * n_x + owner % n_x) * units + sample_item % units
+    of_core = owner // n_x % n_c
+    sent = segment_sums(jnp.where(of_core == core, -1, spot), sample_grad, chips * units)
+    got = swap_cores(sent)
+    mine = segment_sums(jnp.where(of_core == core, spot, -1), sample_grad, chips * units, got)
+    mine = mine.reshape(chips, units, width_e)
     mine, ln_gain = lax.optimization_barrier((mine, ln_gain))
     item_all = lax.all_to_all(mine, CHIPS, 0, 0, tiled=True)
 
@@ -401,8 +428,11 @@
     send_at = jnp.stack([slot_of(1 - core, at, size) for at, size in here])
     tables = (core.reshape(1), keep_at, send_at)
     items = (normed_b, mean_act_b, pooled_b, grad_b)
+    slope = pltpu.with_memory_space_constraint(slope, pltpu.HBM)
     d_pre, *sums = up_products(tables, (0,), (slope, d_act), *items)
-    sums += up_products(tables, (1, 2), (d_pre,), *items)
+    d_pre = pltpu.with_memory_space_constraint(d_pre, pltpu.VMEM)
+    for index in (1, 2):
+        sums += up_products(tables, (index,), (d_pre,), *items)
     parts = [
         (keep + swap_cores(send)).reshape(n_z, n_y, n_x, -1, width_e)
         for keep, send in zip(sums[::2], sums[1::2])

time: 186 us -> 171 us (0.919)
  matrix products: 18.8 us -> 9.58 us
  waiting for transfers between devices: 29.2 us -> 21.7 us
  local copies, waits for them, and re-layouts: 14.2 us -> 17 us
  Pallas kernels: 59.1 us -> 57.1 us
  starting transfers between devices: 49.8 us -> 51.7 us
    ppermute x5, waiting for transfers between devices: 8.42 us -> 0.01 us  [swap_cores(): return lax.ppermute(block, 'c', [(0, 1), (1, 0)])]
    dot_general x3 -> x1, matrix products: 9 us -> 0.67 us  [contract_first(): lax.dot_general(left, right, (((0,), (0,)), ((), ())), preferred_element_...]
    pallas_call x0 -> x2, Pallas kernels: none -> 4.98 us  [segment_sums(): pl.pallas_call(item_kernel, grid=(count // step,), in_specs=[pl.BlockSpec...]
    pallas_call x1, Pallas kernels: 14.7 us -> 11.5 us  [title_grads(): pl.pallas_call(titles_kernel, grid=(rows // step,), in_specs=[pl.BlockSpe...]
    pallas_call x2 -> x3, Pallas kernels: 21 us -> 18 us  [up_products(): pl.pallas_call(kernel, grid_spec=pltpu.PrefetchScalarGridSpec(num_scalar_...]
    unnamed x42 -> x34, local copies, waits for them, and re-layouts: 7.84 us -> 7.34 us
  transfers between devices with their start and end apart: 28 -> 28, of which waited for: 11 -> 10; matrix products, arithmetic and copies ran while one was open for 9% -> 11% of each run, Pallas kernels for 26% -> 26%
where the time goes in v4:
time: 171 us; the launch traced here: 170 us
  Pallas kernels  57.1 us (33%)
  starting transfers between devices  51.7 us (30%)
  waiting for transfers between devices  21.7 us (13%)
  local copies, waits for them, and re-layouts  17 us (10%)
  other arithmetic  11.8 us (7%)
  matrix products  9.58 us (6%)
    ppermute x18, starting transfers between devices, halve(): lax.ppermute(lax.slice_in_dim(part, middle, None, axis=dim), DEVICES, par...  28.3 us
    pallas_call x1, Pallas kernels, forward(): pl.pallas_call(functools.partial(forward_kernel, units), grid=(hidden //...  18.9 us
    pallas_call x3, Pallas kernels, up_products(): pl.pallas_call(kernel, grid_spec=pltpu.PrefetchScalarGridSpec(num_scalar_...  18 us
    ppermute x18, waiting for transfers between devices, halve(): lax.ppermute(lax.slice_in_dim(part, middle, None, axis=dim), DEVICES, par...  17 us
    all_to_all x1, starting transfers between devices, per_device(): item_all = lax.all_to_all(mine, CHIPS, 0, 0, tiled=True)  11.7 us
    pallas_call x1, Pallas kernels, title_grads(): pl.pallas_call(titles_kernel, grid=(rows // step,), in_specs=[pl.BlockSpe...  11.5 us
    unnamed x34, local copies, waits for them, and re-layouts  7.34 us
    add x15, other arithmetic, halve(): return ([k + s for k, s in zip(kept, sent)], also)  7.27 us
  transfers between devices with their start and end apart: 28, of which 10 were waited for; matrix products, arithmetic and copies ran while one was open for 11% of the time, Pallas kernels for 26%

profile of v4, /device:TPU:0, one launch (start us, length us, event | category | flops | bytes accessed | tf_op | source)
XLA Modules:
  0.0 170.0 jit_solution(2185296298699853332)
XLA Ops:
  1.4 1.0 copy-done.3
  2.5 2.5 %segment_sums.2 = f32[1536,256]{1,0:T(8,128)} custom-call(s32[1,1024]{1,0:T(1,128)S(1)} %bitcast.42, bf16[1024,256]{1,0:T(8,128)(2,1)S(1)} %copy-done.3), custom_call_target="tpu_custom_call" | custom-call | flops 805306368 | bytes 1572864 | tf_op jit(solution)/shard_map/segment_sums/pallas_call | solution.py:108
  5.8 1.1 copy.19
  6.9 2.3 %reshape.251 = f32[128,4,384]{2,1,0:T(4,128)} reshape(f32[512,384]{1,0:T(8,128)} %copy.19) | data formatting | bytes 1572864 | tf_op jit(solution)/shard_map/reshape | solution.py:408
  9.3 2.5 %segment_sums.3 = f32[1536,256]{1,0:T(8,128)} custom-call(s32[1,1024]{1,0:T(1,128)S(1)} %bitcast.41, bf16[1024,256]{1,0:T(8,128)(2,1)S(1)} %copy-done.4, f32[1536,256]{1,0:T(8,128)S(1)} %collective-permute-done.refs_0_), custom_call_target="tpu_custom_call" | custom-call | flops 805306368 | bytes 1572864 | tf_op jit(solution)/shard_map/segment_sums/pallas_call | solution.py:108
  11.8 11.7 %all-to-all-start = ((f32[64,24,256]{2,1,0:T(8,128)}), f32[64,24,256]{2,1,0:T(8,128)}, u32[]{:S(2)}, u32[]{:S(2)}) async-start(f32[64,24,256]{2,1,0:T(8,128)} %bitcast.4), calls=%async_computation | async-start | bytes 3145728 | tf_op jit(solution)/shard_map/all_to_all | solution.py:393
  23.5 2.3 %copy-done.5 = bf16[768,3072]{1,0:T(8,128)(2,1)S(1)} copy-done((bf16[768,3072]{1,0:T(8,128)(2,1)S(1)}, bf16[768,3072]{1,0:T(8,128)(2,1)}, u32[]{:S(2)}) %copy-start.5) | copy-done | bytes 4718616
  25.9 1.7 copy-done.6
  27.5 18.9 %forward.1 = (bf16[1536,768]{1,0:T(8,128)(2,1)S(1)}, bf16[1536,3072]{1,0:T(8,128)(2,1)}, f32[24,3072]{1,0:T(8,128)S(1)}, f32[24,768]{1,0:T(8,128)S(1)}) custom-call(bf16[1536,768]{1,0:T(8,128)(2,1)S(1)} %bitcast.45, f32[1,768]{1,0:T(1,128)S(1)} %reshape.250.gain_ref, bf16[768,3072]{1,0:T(8,128)(2,1)S(1)} %copy-done.5), custom_call_target="tpu_custom_call" | custom-call | flops 28991029248 | bytes 18874368 | tf_op jit(solution)/shard_map/forward/pallas_call | solution.py:156
  46.4 3.8 %fusion.3.pool_ref = bf16[24,1024]{1,0:T(8,128)(2,1)S(1)} fusion(s32[1024]{0:T(1024)S(1)} %fusion.31, f32[24,768]{1,0:T(8,128)S(1)} %get-tuple-element.52, bf16[24,3072]{1,0:T(8,128)(2,1)S(1)} %convert_element_type.35.mean_ref, bf16[3072,768]{1,0:T(8,128)(2,1)} %param.14), kind=kOutput, calls=%fused_computation.8 | convolution fusion | flops 151842816 | bytes 4993024 | tf_op jit(solution)/shard_map/dot_general | solution.py:416
  50.2 1.5 reduce_sum.29.grad_ref
  52.0 3.7 %convolution_multiply_fusion.act_ref = f32[24,3072]{1,0:T(8,128)S(1)} fusion(bf16[3072,768]{1,0:T(8,128)(2,1)} %param.14, f32[24,768]{1,0:T(8,128)S(1)} %fusion.46.pool_ref), kind=kOutput, calls=%fused_computation | convolution fusion | flops 113338368 | bytes 5087232 | tf_op jit(solution)/shard_map/dot_general | solution.py:29
  55.6 7.8 %first_products.1 = (bf16[1536,3072]{1,0:T(8,128)(2,1)S(1)}, f32[64,40,256]{2,1,0:T(8,128)S(1)}, f32[64,40,256]{2,1,0:T(8,128)S(1)}) custom-call(s32[1]{0:T(128)} %bitcast.core_ref, s32[3,4]{1,0:T(4,128)S(1)} %pad_add_fusion.keep_at, s32[3,4]{1,0:T(4,128)S(1)} %pad_add_fusion.1.send_at, bf16[1536,3072]{1,0:T(8,128)(2,1)} %get-tuple-element.50.slope_ref, ...), custom_call_target="tpu_custom_call" | custom-call | flops 2415919104 | bytes 18874368 | tf_op jit(solution)/shard_map/first_products/pallas_call | solution.py:263
  63.9 5.1 %other_products.3 = (f32[64,32,256]{2,1,0:T(8,128)S(1)}, f32[64,32,256]{2,1,0:T(8,128)S(1)}) custom-call(s32[1]{0:T(128)} %bitcast.core_ref, s32[3,4]{1,0:T(4,128)S(1)} %pad_add_fusion.keep_at, s32[3,4]{1,0:T(4,128)S(1)} %pad_add_fusion.1.send_at, bf16[1536,3072]{1,0:T(8,128)(2,1)S(1)} %get-tuple-element.59.pre_ref, ...), custom_call_target="tpu_custom_call" | custom-call | flops 2415919104 | bytes 18874368 | tf_op jit(solution)/shard_map/other_products/pallas_call | solution.py:263
  69.4 5.1 %other_products.2 = (f32[64,32,256]{2,1,0:T(8,128)S(1)}, f32[64,32,256]{2,1,0:T(8,128)S(1)}) custom-call(s32[1]{0:T(128)} %bitcast.core_ref, s32[3,4]{1,0:T(4,128)S(1)} %pad_add_fusion.keep_at, s32[3,4]{1,0:T(4,128)S(1)} %pad_add_fusion.1.send_at, bf16[1536,3072]{1,0:T(8,128)(2,1)S(1)} %get-tuple-element.59.pre_ref, ...), custom_call_target="tpu_custom_call" | custom-call | flops 2415919104 | bytes 18874368 | tf_op jit(solution)/shard_map/other_products/pallas_call | solution.py:263
  75.7 1.4 collective-permute-start.2
  77.2 1.6 collective-permute-start.6
  79.3 1.6 collective-permute-start.4
  80.9 11.5 %title_grads.1 = (bf16[1536,768]{1,0:T(8,128)(2,1)}, f32[8,768]{1,0:T(8,128)S(1)}) custom-call(bf16[1536,3072]{1,0:T(8,128)(2,1)S(1)} %get-tuple-element.59.pre_ref, bf16[768,3072]{1,0:T(8,128)(2,1)S(1)} %bitcast.44, bf16[1536,768]{1,0:T(8,128)(2,1)S(1)} %bitcast.46, f32[1,768]{1,0:T(1,128)S(1)} %reshape.250.gain_ref, f32[24,768]{1,0:T(8,128)S(1)} %fusion.46.pool_ref), custom_call_target="tpu_custom_call" | custom-call | flops 7247757312 | bytes 9437184 | tf_op jit(solution)/shard_map/title_grads/pallas_call | solution.py:308
  92.4 1.7 %collective-permute-done.4 = f32[4,2,4,32,256]{4,3,2,1,0:T(8,128)S(1)} collective-permute-done((f32[4,2,4,32,256]{4,3,2,1,0:T(8,128)S(1)}, f32[4,2,4,32,256]{4,3,2,1,0:T(8,128)S(1)}, u32[]{:S(2)}, u32[]{:S(2)}) %collective-permute-start.4) | collective-permute-done | bytes 1048608 | tf_op jit(solution)/shard_map/ppermute | solution.py:78
  94.8 2.8 %collective-permute-start.7 = (f32[4,4,1,40,256]{4,3,2,1,0:T(8,128)S(1)}, f32[4,4,1,40,256]{4,3,2,1,0:T(8,128)}, u32[]{:S(2)}, u32[]{:S(2)}) collective-permute-start(f32[4,4,1,40,256]{4,3,2,1,0:T(8,128)S(1)} %slice.147), channel_id=1, source_target_pairs={{0,3},{1,2},{2,1},{3,0},{4,5},{5,4},{6,7},{7,6},{8,11},{9,10},{10,... | collective-permute-start | bytes 1966088 | tf_op jit(solution)/shard_map/ppermute | solution.py:78
  98.4 2.7 %collective-permute-start.8 = (f32[4,1,4,32,256]{4,3,2,1,0:T(8,128)}, f32[4,1,4,32,256]{4,3,2,1,0:T(8,128)}, u32[]{:S(2)}, u32[]{:S(2)}) collective-permute-start(f32[4,1,4,32,256]{4,3,2,1,0:T(8,128)} %slice.148), channel_id=1, source_target_pairs={{0,24},{1,25},{2,26},{3,27},{4,12},{5,13},{6,14},{7,15},{8,16},{9,... | collective-permute-start | bytes 1572872 | tf_op jit(solution)/shard_map/ppermute | solution.py:78
  101.9 3.0 %collective-permute-start.9 = (f32[1,4,4,32,256]{4,3,2,1,0:T(8,128)}, f32[1,4,4,32,256]{4,3,2,1,0:T(8,128)}, u32[]{:S(2)}, u32[]{:S(2)}) collective-permute-start(f32[1,4,4,32,256]{4,3,2,1,0:T(8,128)} %slice.149), channel_id=1, source_target_pairs={{0,96},{1,97},{2,98},{3,99},{4,36},{5,37},{6,38},{7,39},{8,104},{9... | collective-permute-start | bytes 1572872 | tf_op jit(solution)/shard_map/ppermute | solution.py:78
  104.9 5.7 %all-to-all-start.1 = ((f32[128,4,384]{2,1,0:T(4,128)}), f32[128,4,384]{2,1,0:T(4,128)}, u32[]{:S(2)}, u32[]{:S(2)}) async-start(f32[128,4,384]{2,1,0:T(4,128)} %reshape.251), calls=%async_computation.1 | async-start | bytes 1572864 | tf_op jit(solution)/shard_map/all_to_all | solution.py:444
  110.7 3.8 %collective-permute-done.9 = f32[1,4,4,32,256]{4,3,2,1,0:T(8,128)} collective-permute-done((f32[1,4,4,32,256]{4,3,2,1,0:T(8,128)}, f32[1,4,4,32,256]{4,3,2,1,0:T(8,128)}, u32[]{:S(2)}, u32[]{:S(2)}) %collective-permute-start.9) | collective-permute-done | bytes 524320 | tf_op jit(solution)/shard_map/ppermute | solution.py:78
  114.5 1.3 slice_add_fusion.3
  115.9 1.2 slice_add_fusion.2
  117.3 1.1 slice_add_fusion.4
  118.7 3.8 %collective-permute-done.15 = f32[1,4,2,32,256]{4,3,2,1,0:T(8,128)S(1)} collective-permute-done((f32[1,4,2,32,256]{4,3,2,1,0:T(8,128)S(1)}, f32[1,4,2,32,256]{4,3,2,1,0:T(8,128)S(1)}, u32[]{:S(2)}, u32[]{:S(2)}) %collective-permute-start.15) | collective-permute-done | bytes 262176 | tf_op jit(solution)/shard_map/ppermute | solution.py:78
  123.3 2.1 %collective-permute-start.16 = (f32[1,4,1,32,256]{4,3,2,1,0:T(8,128)}, f32[1,4,1,32,256]{4,3,2,1,0:T(8,128)}, u32[]{:S(2)}, u32[]{:S(2)}) collective-permute-start(f32[1,4,1,32,256]{4,3,2,1,0:T(8,128)} %slice.199), channel_id=1, source_target_pairs={{0,3},{1,2},{2,1},{3,0},{4,5},{5,4},{6,7},{7,6},{8,11},{9,10},{10,... | collective-permute-start | bytes 393224 | tf_op jit(solution)/shard_map/ppermute | solution.py:78
  126.5 2.5 %collective-permute-start.12 = (f32[4,1,1,48,256]{4,3,2,1,0:T(8,128)}, f32[4,1,1,48,256]{4,3,2,1,0:T(8,128)}, u32[]{:S(2)}, u32[]{:S(2)}) collective-permute-start(f32[4,1,1,48,256]{4,3,2,1,0:T(8,128)} %slice.193), channel_id=1, source_target_pairs={{0,24},{1,25},{2,26},{3,27},{4,12},{5,13},{6,14},{7,15},{8,16},{9,... | collective-permute-start | bytes 589832 | tf_op jit(solution)/shard_map/ppermute | solution.py:78
  129.1 3.6 %collective-permute-start.14 = (f32[1,1,4,32,256]{4,3,2,1,0:T(8,128)S(1)}, f32[1,1,4,32,256]{4,3,2,1,0:T(8,128)S(1)}, u32[]{:S(2)}, u32[]{:S(2)}) collective-permute-start(f32[1,1,4,32,256]{4,3,2,1,0:T(8,128)S(1)} %slice.196), channel_id=1, source_target_pairs={{0,96},{1,97},{2,98},{3,99},{4,36},{5,37},{6,38},{7,39},{8,104},{9... | collective-permute-start | bytes 393224 | tf_op jit(solution)/shard_map/ppermute | solution.py:78
  132.7 2.9 %collective-permute-done.14 = f32[1,1,4,32,256]{4,3,2,1,0:T(8,128)S(1)} collective-permute-done((f32[1,1,4,32,256]{4,3,2,1,0:T(8,128)S(1)}, f32[1,1,4,32,256]{4,3,2,1,0:T(8,128)S(1)}, u32[]{:S(2)}, u32[]{:S(2)}) %collective-permute-start.14) | collective-permute-done | bytes 131104 | tf_op jit(solution)/shard_map/ppermute | solution.py:78
  136.3 1.4 reshape.255.arrived_ref
  138.9 1.0 slice_add_fusion.9
  140.6 1.0 slice_add_fusion.7
  142.0 1.6 copy-done.2
  143.6 3.7 %row_update.1 = (f32[2048,256]{1,0:T(8,128)}, f32[2048,256]{1,0:T(8,128)}) custom-call(f32[512,384]{1,0:T(8,128)S(1)} %reshape.255.arrived_ref, f32[2048,256]{1,0:T(8,128)S(1)} %copy-done.1, f32[2048,256]{1,0:T(8,128)S(1)} %copy-done.2), custom_call_target="tpu_custom_call" | custom-call | flops 1073741824 | bytes 8388608 | tf_op jit(solution)/shard_map/row_update/pallas_call | solution.py:351
  147.3 3.1 %collective-permute-start.20 = (f32[1,1,1,48,256]{4,3,2,1,0:T(8,128)S(1)}, f32[1,1,1,48,256]{4,3,2,1,0:T(8,128)S(1)}, u32[]{:S(2)}, u32[]{:S(2)}) collective-permute-start(f32[1,1,1,48,256]{4,3,2,1,0:T(8,128)S(1)} %slice.207), channel_id=1, source_target_pairs={{0,96},{1,97},{2,98},{3,99},{4,36},{5,37},{6,38},{7,39},{8,104},{9... | collective-permute-start | bytes 147464 | tf_op jit(solution)/shard_map/ppermute | solution.py:78
  150.4 1.4 collective-permute-start.21
  151.8 1.0 collective-permute-start.22
  152.8 2.8 %collective-permute-done.21 = f32[1,1,1,32,256]{4,3,2,1,0:T(8,128)S(1)} collective-permute-done((f32[1,1,1,32,256]{4,3,2,1,0:T(8,128)S(1)}, f32[1,1,1,32,256]{4,3,2,1,0:T(8,128)S(1)}, u32[]{:S(2)}, u32[]{:S(2)}) %collective-permute-start.21) | collective-permute-done | bytes 32800 | tf_op jit(solution)/shard_map/ppermute | solution.py:78
  155.6 1.4 collective-permute-done.22
  157.8 2.7 %collective-permute-start.24 = (f32[112,256]{1,0:T(8,128)S(1)}, f32[112,256]{1,0:T(8,128)S(1)}, u32[]{:S(2)}, u32[]{:S(2)}) collective-permute-start(f32[112,256]{1,0:T(8,128)S(1)} %get-tuple-element.106), channel_id=1, source_target_pairs={{0,2},{1,3},{2,0},{3,1},{4,6},{5,7},{6,4},{7,5},{8,10},{9,11},{10,... | collective-permute-start | bytes 344072 | tf_op jit(solution)/shard_map/ppermute | solution.py:44
  160.6 1.3 collective-permute-start.25
  162.0 2.6 %collective-permute-done.24 = f32[112,256]{1,0:T(8,128)S(1)} collective-permute-done((f32[112,256]{1,0:T(8,128)S(1)}, f32[112,256]{1,0:T(8,128)S(1)}, u32[]{:S(2)}, u32[]{:S(2)}) %collective-permute-start.24) | collective-permute-done | bytes 114720 | tf_op jit(solution)/shard_map/ppermute | solution.py:44
  164.6 2.0 %collective-permute-done.25 = f32[112,256]{1,0:T(8,128)S(1)} collective-permute-done((f32[112,256]{1,0:T(8,128)S(1)}, f32[112,256]{1,0:T(8,128)S(1)}, u32[]{:S(2)}, u32[]{:S(2)}) %collective-permute-start.25) | collective-permute-done | bytes 114720 | tf_op jit(solution)/shard_map/ppermute | solution.py:44
  168.3 1.0 convolution_add_fusion
  (130 shorter events, 15.4 us)
Async XLA Ops:
  0.6 51.1 %copy-start = (bf16[768,256]{1,0:T(8,128)(2,1)S(1)}, bf16[768,256]{1,0:T(8,128)(2,1)}, u32[]{:S(2)}) copy-start(bf16[768,256]{1,0:T(8,128)(2,1)} %param.15) | copy-start | bytes 1179652
  0.6 4.3 %copy-start.13 = (s32[1,512]{1,0:T(1,128)S(1)}, s32[1,512]{1,0:T(1,128)}, u32[]{:S(2)}) copy-start(s32[1,512]{1,0:T(1,128)} %param.19) | copy-start | bytes 6148
  0.7 4.3 %copy-start.14 = (s32[1024]{0:T(1024)S(1)}, s32[1024]{0:T(1024)}, u32[]{:S(2)}) copy-start(s32[1024]{0:T(1024)} %param.18) | copy-start | bytes 12292
  1.4 1.0 copy-start.3
  2.5 2.5 %copy-start.4 = (bf16[1024,256]{1,0:T(8,128)(2,1)S(1)}, bf16[1024,256]{1,0:T(8,128)(2,1)}, u32[]{:S(2)}) copy-start(bf16[1024,256]{1,0:T(8,128)(2,1)} %grad_ref.3) | copy-start | bytes 1572868
  5.0 4.3 %collective-permute-start = (f32[1536,256]{1,0:T(8,128)}, f32[1536,256]{1,0:T(8,128)S(1)}, u32[]{:S(2)}, u32[]{:S(2)}) collective-permute-start(f32[1536,256]{1,0:T(8,128)} %segment_sums.2), channel_id=1, source_target_pairs={{0,4},{4,0},{1,5},{5,1},{2,6},{6,2},{3,7},{7,3},{8,12},{12,8},{9,1... | collective-permute-start | bytes 4718600 | tf_op jit(solution)/shard_map/ppermute | solution.py:39
  9.2 2.6 %copy-start.12 = (f32[768]{0:T(1024)S(1)}, f32[768]{0:T(1024)}, u32[]{:S(2)}) copy-start(f32[768]{0:T(1024)} %param.12) | copy-start | bytes 9220
  11.8 38.4 %all-to-all-start = ((f32[64,24,256]{2,1,0:T(8,128)}), f32[64,24,256]{2,1,0:T(8,128)}, u32[]{:S(2)}, u32[]{:S(2)}) async-start(f32[64,24,256]{2,1,0:T(8,128)} %bitcast.4), calls=%async_computation | async-start | bytes 3145728 | tf_op jit(solution)/shard_map/all_to_all | solution.py:393
  23.5 2.3 %copy-start.5 = (bf16[768,3072]{1,0:T(8,128)(2,1)S(1)}, bf16[768,3072]{1,0:T(8,128)(2,1)}, u32[]{:S(2)}) copy-start(bf16[768,3072]{1,0:T(8,128)(2,1)} %w_ref.3) | copy-start | bytes 14155780
  25.9 1.7 copy-start.6
  63.5 11.8 %collective-permute-start.1 = (f32[64,40,256]{2,1,0:T(8,128)S(1)}, f32[64,40,256]{2,1,0:T(8,128)S(1)}, u32[]{:S(2)}, u32[]{:S(2)}) collective-permute-start(f32[64,40,256]{2,1,0:T(8,128)S(1)} %get-tuple-element.58), channel_id=1, source_target_pairs={{0,4},{4,0},{1,5},{5,1},{2,6},{6,2},{3,7},{7,3},{8,12},{12,8},{9,1... | collective-permute-start | bytes 7864328 | tf_op jit(solution)/shard_map/ppermute | solution.py:39
  69.1 5.8 %collective-permute-start.5 = (f32[64,32,256]{2,1,0:T(8,128)S(1)}, f32[64,32,256]{2,1,0:T(8,128)S(1)}, u32[]{:S(2)}, u32[]{:S(2)}) collective-permute-start(f32[64,32,256]{2,1,0:T(8,128)S(1)} %get-tuple-element.63), channel_id=1, source_target_pairs={{0,4},{4,0},{1,5},{5,1},{2,6},{6,2},{3,7},{7,3},{8,12},{12,8},{9,1... | collective-permute-start | bytes 6291464 | tf_op jit(solution)/shard_map/ppermute | solution.py:39
  74.5 4.2 %collective-permute-start.3 = (f32[64,32,256]{2,1,0:T(8,128)S(1)}, f32[64,32,256]{2,1,0:T(8,128)S(1)}, u32[]{:S(2)}, u32[]{:S(2)}) collective-permute-start(f32[64,32,256]{2,1,0:T(8,128)S(1)} %get-tuple-element.61), channel_id=1, source_target_pairs={{0,4},{4,0},{1,5},{5,1},{2,6},{6,2},{3,7},{7,3},{8,12},{12,8},{9,1... | collective-permute-start | bytes 6291464 | tf_op jit(solution)/shard_map/ppermute | solution.py:39
  75.7 18.5 %collective-permute-start.2 = (f32[4,4,2,40,256]{4,3,2,1,0:T(8,128)S(1)}, f32[4,4,2,40,256]{4,3,2,1,0:T(8,128)S(1)}, u32[]{:S(2)}, u32[]{:S(2)}) collective-permute-start(f32[4,4,2,40,256]{4,3,2,1,0:T(8,128)S(1)} %slice.184), channel_id=1, source_target_pairs={{0,1},{1,0},{2,3},{3,2},{4,7},{5,6},{6,5},{7,4},{8,9},{9,8},{10,11... | collective-permute-start | bytes 3932168 | tf_op jit(solution)/shard_map/ppermute | solution.py:78
  77.1 3.8 %slice-start = ((s8[4718592]{0:T(1024)(128)(4,1)}), s8[4194304]{0:T(1024)(128)(4,1)S(1)}, s32[]{:S(2)}) async-start(s8[4718592]{0:T(1024)(128)(4,1)} %bitcast.43), calls=%async_computation.2 | async-start | bytes 8388608
  77.2 15.2 %collective-permute-start.6 = (f32[2,4,4,32,256]{4,3,2,1,0:T(8,128)S(1)}, f32[2,4,4,32,256]{4,3,2,1,0:T(8,128)S(1)}, u32[]{:S(2)}, u32[]{:S(2)}) collective-permute-start(f32[2,4,4,32,256]{4,3,2,1,0:T(8,128)S(1)} %bitcast.52), channel_id=1, source_target_pairs={{0,32},{1,33},{2,34},{3,35},{4,100},{5,101},{6,102},{7,103},{8,40}... | collective-permute-start | bytes 3145736 | tf_op jit(solution)/shard_map/ppermute | solution.py:78
  78.8 2.1 %slice-start.1 = ((s8[4718592]{0:T(1024)(128)(4,1)}), s8[524288]{0:T(1024)(128)(4,1)S(1)}, s32[]{:S(2)}) async-start(s8[4718592]{0:T(1024)(128)(4,1)} %bitcast.43), calls=%async_computation.3 | async-start | bytes 1048576
  78.8 2.1 %copy-start.7 = (bf16[24,64,768]{2,1,0:T(8,128)(2,1)S(1)}, bf16[24,64,768]{2,1,0:T(8,128)(2,1)}, u32[]{:S(2)}) copy-start(bf16[24,64,768]{2,1,0:T(8,128)(2,1)} %param.11) | copy-start | bytes 7077892
  79.3 14.9 %collective-permute-start.4 = (f32[4,2,4,32,256]{4,3,2,1,0:T(8,128)S(1)}, f32[4,2,4,32,256]{4,3,2,1,0:T(8,128)S(1)}, u32[]{:S(2)}, u32[]{:S(2)}) collective-permute-start(f32[4,2,4,32,256]{4,3,2,1,0:T(8,128)S(1)} %slice.185), channel_id=1, source_target_pairs={{0,8},{1,9},{2,10},{3,11},{4,28},{5,29},{6,30},{7,31},{8,0},{9,1},... | collective-permute-start | bytes 3145736 | tf_op jit(solution)/shard_map/ppermute | solution.py:78
  94.7 7.2 %copy-start.8 = (f32[2,4,4,32,256]{4,3,2,1,0:T(8,128)}, f32[2,4,4,32,256]{4,3,2,1,0:T(8,128)S(1)}, u32[]{:S(2)}) copy-start(f32[2,4,4,32,256]{4,3,2,1,0:T(8,128)S(1)} %add.165) | copy-start | bytes 3145732
  94.8 19.8 %collective-permute-start.7 = (f32[4,4,1,40,256]{4,3,2,1,0:T(8,128)S(1)}, f32[4,4,1,40,256]{4,3,2,1,0:T(8,128)}, u32[]{:S(2)}, u32[]{:S(2)}) collective-permute-start(f32[4,4,1,40,256]{4,3,2,1,0:T(8,128)S(1)} %slice.147), channel_id=1, source_target_pairs={{0,3},{1,2},{2,1},{3,0},{4,5},{5,4},{6,7},{7,6},{8,11},{9,10},{10,... | collective-permute-start | bytes 1966088 | tf_op jit(solution)/shard_map/ppermute | solution.py:78
  98.4 12.2 %collective-permute-start.8 = (f32[4,1,4,32,256]{4,3,2,1,0:T(8,128)}, f32[4,1,4,32,256]{4,3,2,1,0:T(8,128)}, u32[]{:S(2)}, u32[]{:S(2)}) collective-permute-start(f32[4,1,4,32,256]{4,3,2,1,0:T(8,128)} %slice.148), channel_id=1, source_target_pairs={{0,24},{1,25},{2,26},{3,27},{4,12},{5,13},{6,14},{7,15},{8,16},{9,... | collective-permute-start | bytes 1572872 | tf_op jit(solution)/shard_map/ppermute | solution.py:78
  101.9 12.6 %collective-permute-start.9 = (f32[1,4,4,32,256]{4,3,2,1,0:T(8,128)}, f32[1,4,4,32,256]{4,3,2,1,0:T(8,128)}, u32[]{:S(2)}, u32[]{:S(2)}) collective-permute-start(f32[1,4,4,32,256]{4,3,2,1,0:T(8,128)} %slice.149), channel_id=1, source_target_pairs={{0,96},{1,97},{2,98},{3,99},{4,36},{5,37},{6,38},{7,39},{8,104},{9... | collective-permute-start | bytes 1572872 | tf_op jit(solution)/shard_map/ppermute | solution.py:78
  104.9 5.7 %collective-permute-start.10 = (f32[8,768]{1,0:T(8,128)S(1)}, f32[8,768]{1,0:T(8,128)S(1)}, u32[]{:S(2)}, u32[]{:S(2)}) collective-permute-start(f32[8,768]{1,0:T(8,128)S(1)} %get-tuple-element.74), channel_id=1, source_target_pairs={{0,4},{4,0},{1,5},{5,1},{2,6},{6,2},{3,7},{7,3},{8,12},{12,8},{9,1... | collective-permute-start | bytes 73736 | tf_op jit(solution)/shard_map/ppermute | solution.py:39
  104.9 27.8 %all-to-all-start.1 = ((f32[128,4,384]{2,1,0:T(4,128)}), f32[128,4,384]{2,1,0:T(4,128)}, u32[]{:S(2)}, u32[]{:S(2)}) async-start(f32[128,4,384]{2,1,0:T(4,128)} %reshape.251), calls=%async_computation.1 | async-start | bytes 1572864 | tf_op jit(solution)/shard_map/all_to_all | solution.py:444
  115.8 6.7 %collective-permute-start.15 = (f32[1,4,2,32,256]{4,3,2,1,0:T(8,128)S(1)}, f32[1,4,2,32,256]{4,3,2,1,0:T(8,128)S(1)}, u32[]{:S(2)}, u32[]{:S(2)}) collective-permute-start(f32[1,4,2,32,256]{4,3,2,1,0:T(8,128)S(1)} %slice.198), channel_id=1, source_target_pairs={{0,1},{1,0},{2,3},{3,2},{4,7},{5,6},{6,5},{7,4},{8,9},{9,8},{10,11... | collective-permute-start | bytes 786440 | tf_op jit(solution)/shard_map/ppermute | solution.py:78
  117.2 8.5 %collective-permute-start.11 = (f32[4,2,1,48,256]{4,3,2,1,0:T(8,128)S(1)}, f32[4,2,1,48,256]{4,3,2,1,0:T(8,128)S(1)}, u32[]{:S(2)}, u32[]{:S(2)}) collective-permute-start(f32[4,2,1,48,256]{4,3,2,1,0:T(8,128)S(1)} %pad_maximum_fusion.3), channel_id=1, source_target_pairs={{0,8},{1,9},{2,10},{3,11},{4,28},{5,29},{6,30},{7,31},{8,0},{9,1},... | collective-permute-start | bytes 1179656 | tf_op jit(solution)/shard_map/ppermute | solution.py:78
  118.5 10.6 %collective-permute-start.13 = (f32[2,1,4,32,256]{4,3,2,1,0:T(8,128)S(1)}, f32[2,1,4,32,256]{4,3,2,1,0:T(8,128)S(1)}, u32[]{:S(2)}, u32[]{:S(2)}) collective-permute-start(f32[2,1,4,32,256]{4,3,2,1,0:T(8,128)S(1)} %slice.195), channel_id=1, source_target_pairs={{0,32},{1,33},{2,34},{3,35},{4,100},{5,101},{6,102},{7,103},{8,40}... | collective-permute-start | bytes 786440 | tf_op jit(solution)/shard_map/ppermute | solution.py:78
  123.3 9.5 %collective-permute-start.16 = (f32[1,4,1,32,256]{4,3,2,1,0:T(8,128)}, f32[1,4,1,32,256]{4,3,2,1,0:T(8,128)}, u32[]{:S(2)}, u32[]{:S(2)}) collective-permute-start(f32[1,4,1,32,256]{4,3,2,1,0:T(8,128)} %slice.199), channel_id=1, source_target_pairs={{0,3},{1,2},{2,1},{3,0},{4,5},{5,4},{6,7},{7,6},{8,11},{9,10},{10,... | collective-permute-start | bytes 393224 | tf_op jit(solution)/shard_map/ppermute | solution.py:78
  125.8 3.3 %copy-start.9 = (f32[4,2,1,48,256]{4,3,2,1,0:T(8,128)}, f32[4,2,1,48,256]{4,3,2,1,0:T(8,128)S(1)}, u32[]{:S(2)}) copy-start(f32[4,2,1,48,256]{4,3,2,1,0:T(8,128)S(1)} %fusion.7) | copy-start | bytes 1179652
  126.5 15.5 %copy-start.1 = (f32[2048,256]{1,0:T(8,128)S(1)}, f32[2048,256]{1,0:T(8,128)}, u32[]{:S(2)}) copy-start(f32[2048,256]{1,0:T(8,128)} %table_ref.1) | copy-start | bytes 6291460
  126.5 9.8 %collective-permute-start.12 = (f32[4,1,1,48,256]{4,3,2,1,0:T(8,128)}, f32[4,1,1,48,256]{4,3,2,1,0:T(8,128)}, u32[]{:S(2)}, u32[]{:S(2)}) collective-permute-start(f32[4,1,1,48,256]{4,3,2,1,0:T(8,128)} %slice.193), channel_id=1, source_target_pairs={{0,24},{1,25},{2,26},{3,27},{4,12},{5,13},{6,14},{7,15},{8,16},{9,... | collective-permute-start | bytes 589832 | tf_op jit(solution)/shard_map/ppermute | solution.py:78
  129.1 6.5 %copy-start.10 = (f32[2,1,4,32,256]{4,3,2,1,0:T(8,128)}, f32[2,1,4,32,256]{4,3,2,1,0:T(8,128)S(1)}, u32[]{:S(2)}) copy-start(f32[2,1,4,32,256]{4,3,2,1,0:T(8,128)S(1)} %slice_add_fusion.6) | copy-start | bytes 786436
  129.1 6.5 %collective-permute-start.14 = (f32[1,1,4,32,256]{4,3,2,1,0:T(8,128)S(1)}, f32[1,1,4,32,256]{4,3,2,1,0:T(8,128)S(1)}, u32[]{:S(2)}, u32[]{:S(2)}) collective-permute-start(f32[1,1,4,32,256]{4,3,2,1,0:T(8,128)S(1)} %slice.196), channel_id=1, source_target_pairs={{0,96},{1,97},{2,98},{3,99},{4,36},{5,37},{6,38},{7,39},{8,104},{9... | collective-permute-start | bytes 393224 | tf_op jit(solution)/shard_map/ppermute | solution.py:78
  135.6 0.7 copy-start.11
  138.7 8.6 %collective-permute-start.19 = (f32[1,2,1,32,256]{4,3,2,1,0:T(8,128)S(1)}, f32[1,2,1,32,256]{4,3,2,1,0:T(8,128)S(1)}, u32[]{:S(2)}, u32[]{:S(2)}) collective-permute-start(f32[1,2,1,32,256]{4,3,2,1,0:T(8,128)S(1)} %slice.205), channel_id=1, source_target_pairs={{0,8},{1,9},{2,10},{3,11},{4,28},{5,29},{6,30},{7,31},{8,0},{9,1},... | collective-permute-start | bytes 196616 | tf_op jit(solution)/shard_map/ppermute | solution.py:78
  139.9 7.3 %collective-permute-start.18 = (f32[1,1,2,32,256]{4,3,2,1,0:T(8,128)S(1)}, f32[1,1,2,32,256]{4,3,2,1,0:T(8,128)S(1)}, u32[]{:S(2)}, u32[]{:S(2)}) collective-permute-start(f32[1,1,2,32,256]{4,3,2,1,0:T(8,128)S(1)} %slice.203), channel_id=1, source_target_pairs={{0,1},{1,0},{2,3},{3,2},{4,7},{5,6},{6,5},{7,4},{8,9},{9,8},{10,11... | collective-permute-start | bytes 196616 | tf_op jit(solution)/shard_map/ppermute | solution.py:78
  141.7 5.6 %collective-permute-start.17 = (f32[2,1,1,48,256]{4,3,2,1,0:T(8,128)S(1)}, f32[2,1,1,48,256]{4,3,2,1,0:T(8,128)S(1)}, u32[]{:S(2)}, u32[]{:S(2)}) collective-permute-start(f32[2,1,1,48,256]{4,3,2,1,0:T(8,128)S(1)} %slice.201), channel_id=1, source_target_pairs={{0,32},{1,33},{2,34},{3,35},{4,100},{5,101},{6,102},{7,103},{8,40}... | collective-permute-start | bytes 294920 | tf_op jit(solution)/shard_map/ppermute | solution.py:78
  142.0 1.6 copy-start.2
  147.3 9.8 %collective-permute-start.20 = (f32[1,1,1,48,256]{4,3,2,1,0:T(8,128)S(1)}, f32[1,1,1,48,256]{4,3,2,1,0:T(8,128)S(1)}, u32[]{:S(2)}, u32[]{:S(2)}) collective-permute-start(f32[1,1,1,48,256]{4,3,2,1,0:T(8,128)S(1)} %slice.207), channel_id=1, source_target_pairs={{0,96},{1,97},{2,98},{3,99},{4,36},{5,37},{6,38},{7,39},{8,104},{9... | collective-permute-start | bytes 147464 | tf_op jit(solution)/shard_map/ppermute | solution.py:78
  150.4 5.2 %collective-permute-start.21 = (f32[1,1,1,32,256]{4,3,2,1,0:T(8,128)S(1)}, f32[1,1,1,32,256]{4,3,2,1,0:T(8,128)S(1)}, u32[]{:S(2)}, u32[]{:S(2)}) collective-permute-start(f32[1,1,1,32,256]{4,3,2,1,0:T(8,128)S(1)} %slice.210), channel_id=1, source_target_pairs={{0,3},{1,2},{2,1},{3,0},{4,5},{5,4},{6,7},{7,6},{8,11},{9,10},{10,... | collective-permute-start | bytes 98312 | tf_op jit(solution)/shard_map/ppermute | solution.py:78
  151.8 5.2 %collective-permute-start.22 = (f32[1,1,1,32,256]{4,3,2,1,0:T(8,128)S(1)}, f32[1,1,1,32,256]{4,3,2,1,0:T(8,128)S(1)}, u32[]{:S(2)}, u32[]{:S(2)}) collective-permute-start(f32[1,1,1,32,256]{4,3,2,1,0:T(8,128)S(1)} %slice.213), channel_id=1, source_target_pairs={{0,24},{1,25},{2,26},{3,27},{4,12},{5,13},{6,14},{7,15},{8,16},{9,... | collective-permute-start | bytes 98312 | tf_op jit(solution)/shard_map/ppermute | solution.py:78
  157.1 4.9 %collective-permute-start.23 = (f32[112,256]{1,0:T(8,128)S(1)}, f32[112,256]{1,0:T(8,128)S(1)}, u32[]{:S(2)}, u32[]{:S(2)}) collective-permute-start(f32[112,256]{1,0:T(8,128)S(1)} %get-tuple-element.106), channel_id=1, source_target_pairs={{0,1},{1,0},{2,3},{3,2},{4,5},{5,4},{6,7},{7,6},{8,9},{9,8},{10,11... | collective-permute-start | bytes 344072 | tf_op jit(solution)/shard_map/ppermute | solution.py:44
  157.8 6.7 %collective-permute-start.24 = (f32[112,256]{1,0:T(8,128)S(1)}, f32[112,256]{1,0:T(8,128)S(1)}, u32[]{:S(2)}, u32[]{:S(2)}) collective-permute-start(f32[112,256]{1,0:T(8,128)S(1)} %get-tuple-element.106), channel_id=1, source_target_pairs={{0,2},{1,3},{2,0},{3,1},{4,6},{5,7},{6,4},{7,5},{8,10},{9,11},{10,... | collective-permute-start | bytes 344072 | tf_op jit(solution)/shard_map/ppermute | solution.py:44
  160.6 6.0 %collective-permute-start.25 = (f32[112,256]{1,0:T(8,128)S(1)}, f32[112,256]{1,0:T(8,128)S(1)}, u32[]{:S(2)}, u32[]{:S(2)}) collective-permute-start(f32[112,256]{1,0:T(8,128)S(1)} %get-tuple-element.106), channel_id=1, source_target_pairs={{0,3},{1,2},{2,1},{3,0},{4,7},{5,6},{6,5},{7,4},{8,11},{9,10},{10,... | collective-permute-start | bytes 344072 | tf_op jit(solution)/shard_map/ppermute | solution.py:44

commit v5 on v4

--- a/solution.py
+++ b/solution.py
@@ -179,9 +179,11 @@
     )(titles.reshape(rows, width), ln_gain.reshape(1, width), w_up)
 
 
-def place_sums(core_ref, keep_at, send_at, ups, down, proj, out_refs):
-    slots = proj.shape[0] // 8
-    part = down.shape[0] // slots
+def place_sums(core_ref, keep_at, send_at, index, up, down, proj, out_refs):
+    slots = 2 * keep_at.shape[1] * keep_at.shape[1]
+    part = up.shape[0] // slots
+    width_e, width = down.shape[1], up.shape[1]
+    half = width_e // 2
     n_x = slots // 8
     first = core_ref[0] == 0
     for q in range(slots // 2):
@@ -189,18 +191,22 @@
         spots = [at[1, y] * n_x + at[2, x] for at in (keep_at, send_at)]
         pair = (y * 2 * n_x + x, (y * 2 + 1) * n_x + x)
 
-        def store(refs, top, rows):
+        def store(top, left, rows):
             even, odd = (rows(k) for k in pair)
-            end = top + even.shape[0]
-            refs[0][spots[0], top:end, :] = jnp.where(first, even, odd)
-            refs[1][spots[1], top:end, :] = jnp.where(first, odd, even)
-
-        for index, up, refs in zip(*ups, zip(out_refs[::2], out_refs[1::2])):
-            store(refs, 0, lambda k: up[k * part : (k + 1) * part])
-            low = index * 8
-            store(refs, part, lambda k: down[k * part + low : k * part + low + 8])
-            if index == 0:
-                store(refs, part + 8, lambda k: proj[k * 8 : (k + 1) * 8])
+            end, right = top + even.shape[0], left + even.shape[1]
+            out_refs[0][spots[0], top:end, left:right] = jnp.where(first, even, odd)
+            out_refs[1][spots[1], top:end, left:right] = jnp.where(first, odd, even)
+
+        store(0, 0, lambda k: up[k * part : (k + 1) * part])
+        store(part, 0, lambda k: down[k * part + index * 8 : k * part + index * 8 + 8])
+        store(
+            part,
+            width_e,
+            lambda k: down[k * part + 16 : k * part + 24, index * half : (index + 1) * half],
+        )
+        if index == 0:
+            store(part + 8, 0, lambda k: proj[k * 8 : (k + 1) * 8])
+            store(part + 8, width_e, lambda k: jnp.zeros((8, width - width_e), jnp.float32))
 
 
 def first_kernel(
@@ -216,66 +222,56 @@
     up = contract_first(pre_ref[...], normed_ref[...])
     down = contract_first(mean_ref[...], grad_ref[...])
     proj = contract_first(pool_ref[...], grad_ref[...])
-    place_sums(core_ref, keep_at, send_at, ((0,), (up,)), down, proj, out_refs)
+    place_sums(core_ref, keep_at, send_at, 0, up, down, proj, out_refs)
 
 
 def other_kernel(
-    indices, core_ref, keep_at, send_at, pre_ref, mean_ref, pool_ref, grad_ref, *refs
+    core_ref, keep_at, send_at, pre_ref, mean_ref, grad_ref, normed_ref, *out_refs
 ):
-    count = len(indices)
-    normed = jnp.concatenate([ref[...] for ref in refs[:count]], axis=1)
-    up = contract_first(pre_ref[...], normed)
+    up = contract_first(pre_ref[...], normed_ref[...])
     down = contract_first(mean_ref[...], grad_ref[...])
-    wide = grad_ref.shape[1]
-    ups = [up[:, p * wide : (p + 1) * wide] for p in range(count)]
-    empty = jnp.zeros((pool_ref.shape[1], 1), jnp.float32)
-    place_sums(core_ref, keep_at, send_at, (indices, ups), down, empty, refs[count:])
-
-
-def up_products(tables, indices, left, normed_b, mean_act_b, pooled_b, grad_b):
+    place_sums(core_ref, keep_at, send_at, 1, up, down, None, out_refs)
+
+
+def up_products(tables, index, left, by_column, grad_b, normed_b):
     rows, hidden = left[0].shape
-    units, width_e = grad_b.shape
+    wide = normed_b.shape[1] // 2
     sides = tables[1].shape[1]
     slots = 2 * sides * sides
-    part = hidden // sides // slots
-    tall = [part + 8 + 8 * (index == 0) for index in indices for _ in range(2)]
-    first = len(left) == 2
+    height = hidden // sides // slots + (16, 8)[index]
 
     def columns(array):
         return pl.BlockSpec((array.shape[0], array.shape[1] // sides), lambda i, c, k, s: (0, i))
 
-    def lanes(index):
-        return pl.BlockSpec((rows, width_e), lambda i, c, k, s: (0, index))
-
-    def sums(height, table):
+    def sums(table):
         return pl.BlockSpec(
-            (slots // 2, height, width_e), lambda i, *tables: (tables[table][0, i], 0, 0)
+            (slots // 2, height, wide), lambda i, *tables: (tables[table][0, i], 0, 0)
         )
 
-    out_specs = [sums(h, 1 + n % 2) for n, h in enumerate(tall)]
-    out_shape = [jax.ShapeDtypeStruct((sides * slots // 2, h, width_e), jnp.float32) for h in tall]
-    if first:
-        kernel = functools.partial(first_kernel, units)
+    out_specs = [sums(1), sums(2)]
+    out_shape = [jax.ShapeDtypeStruct((sides * slots // 2, height, wide), jnp.float32)] * 2
+    kernel, name = other_kernel, "other_products"
+    if index == 0:
+        kernel, name = functools.partial(first_kernel, left[1].shape[0]), "first_products"
         out_specs.insert(0, columns(left[0]))
         out_shape.insert(0, pltpu.VMEM((rows, hidden), jnp.bfloat16))
-    else:
-        kernel = functools.partial(other_kernel, indices)
     return pl.pallas_call(
         kernel,
         grid_spec=pltpu.PrefetchScalarGridSpec(
             num_scalar_prefetch=3,
             grid=(sides,),
-            in_specs=[columns(array) for array in left]
-            + [columns(mean_act_b), columns(pooled_b)]
-            + [pl.BlockSpec(grad_b.shape, lambda i, c, k, s: (0, 0))]
-            + [lanes(index) for index in indices],
+            in_specs=[columns(array) for array in left + by_column]
+            + [
+                pl.BlockSpec(grad_b.shape, lambda i, c, k, s: (0, 0)),
+                pl.BlockSpec((rows, wide), lambda i, c, k, s: (0, index)),
+            ],
             out_specs=out_specs,
         ),
         out_shape=out_shape,
         compiler_params=pltpu.CompilerParams(vmem_limit_bytes=VMEM),
-        cost_estimate=cost(2 * rows * width_e * len(indices) * hidden, 4 * rows * hidden),
-        name="first_products" if first else "other_products",
-    )(*tables, *left, mean_act_b, pooled_b, grad_b, *[normed_b] * len(indices))
+        cost_estimate=cost(2 * rows * wide * hidden, 4 * rows * hidden),
+        name=name,
+    )(*tables, *left, *by_column, grad_b, normed_b)
 
 
 def titles_kernel(pre_ref, w_ref, titles_ref, gain_ref, pool_ref, out_ref, gain_out):
@@ -427,49 +423,51 @@
     keep_at = jnp.stack([slot_of(core, at, size) for at, size in here])
     send_at = jnp.stack([slot_of(1 - core, at, size) for at, size in here])
     tables = (core.reshape(1), keep_at, send_at)
-    items = (normed_b, mean_act_b, pooled_b, grad_b)
     slope = pltpu.with_memory_space_constraint(slope, pltpu.HBM)
-    d_pre, *sums = up_products(tables, (0,), (slope, d_act), *items)
+    d_pre, *sums = up_products(
+        tables, 0, (slope, d_act), (mean_act_b, pooled_b), grad_b, normed_b
+    )
     d_pre = pltpu.with_memory_space_constraint(d_pre, pltpu.VMEM)
-    for index in (1, 2):
-        sums += up_products(tables, (index,), (d_pre,), *items)
+    sums += up_products(tables, 1, (d_pre,), (mean_act_b,), grad_b, normed_b)
     parts = [
-        (keep + swap_cores(send)).reshape(n_z, n_y, n_x, -1, width_e)
+        (keep + swap_cores(send)).reshape(n_z, n_y, n_x, -1, width // 2)
         for keep, send in zip(sums[::2], sums[1::2])
     ]
 
-    beside = title_grads(d_pre, w_up, titles, ln_gain, d_pooled)
-    parts, (d_titles, gain_term) = halve(parts, "xyz", False, tuple(beside))
-    parts, row_part = lax.optimization_barrier((parts, row_part))
+    d_titles, gain_term = title_grads(d_pre, w_up, titles, ln_gain, d_pooled)
+    gain_term, row_part = lax.optimization_barrier((gain_term, row_part))
     row_all = lax.all_to_all(row_part, DEVICES, 0, 0, tiled=True)
-    gain_term = (gain_term + swap_cores(gain_term)).reshape(8, 3, width_e)
-    gain_term = jnp.pad(jnp.sum(gain_term, axis=0), ((0, 5), (0, 0)))
-    parts, (gain_term,) = halve(parts, "xyz", True, (gain_term,))
-    gain_term = jnp.broadcast_to(gain_term, parts[0].shape[:3] + gain_term.shape)
-    parts[0] = jnp.concatenate([parts[0], gain_term], axis=3)
-    parts, _ = halve(parts, "yzx", False)
-    parts, (row_all,) = halve(parts, "yzx", True, (row_all,))
+    parts, (d_titles, gain_term) = halve(parts, "xy", False, (d_titles, gain_term))
+    gain_term = (gain_term + swap_cores(gain_term)).reshape(8, -1, 128)
+    gain_term = jnp.sum(gain_term, axis=0)
+    gain_term = jnp.pad(
+        gain_term, ((share_f + 8, 8 - gain_term.shape[0]), (width // 2 - 128, 0))
+    )
+    parts, (gain_term,) = halve(parts, "xy", True, (gain_term,))
+    parts[0] = parts[0] + gain_term
+    parts, _ = halve(parts, "yx", False)
+    parts, (row_all,) = halve(parts, "yx", True, (row_all,))
+    both = [jnp.concatenate(parts, axis=3)]
     beside = row_update(row_all.reshape(slot_count, width_e + 128), table, accum)
-    parts, (new_table, new_accum) = halve(parts, "zxy", False, tuple(beside))
-    parts, _ = halve(parts, "zxy", True)
-
-    flat = [part.reshape(-1, width_e) for part in parts]
-    last = jnp.concatenate(flat, axis=0)
+    both, (new_table, new_accum) = halve(both, "z", False, tuple(beside))
+    both, _ = halve(both, "z", True)
+
+    last = both[0].reshape(-1, width // 2)
     blocks = jnp.stack([last, along(last, "x", 1), along(last, "x", 2), along(last, "x", 3)])
     ordered = jnp.stack(
         [lax.dynamic_index_in_dim(blocks, my_x ^ j, 0, keepdims=False) for j in range(n_x)]
     )
-    starts = [0, share_f + 24, 2 * share_f + 32]
-    grad_up = jnp.concatenate([ordered[:, at : at + share_f] for at in starts], axis=2)
-    grad_up = grad_up.reshape(-1, width).T
-    outer = jnp.concatenate(
-        [ordered[:, at + share_f : at + share_f + 8] for at in starts], axis=1
-    ).reshape(-1, width_e)
+    one, two = ordered[:, : share_f + 16], ordered[:, share_f + 16 :]
+    grad_up = jnp.concatenate([one[:, :share_f], two[:, :share_f]], axis=2).reshape(-1, width).T
+    one, two, tail = one[:, share_f : share_f + 8], two[:, share_f:], one[:, share_f + 8 :]
+    third = jnp.concatenate([one[:, :, width_e:], two[:, :, width_e:]], axis=2)
+    outer = jnp.concatenate([one[:, :, :width_e], two[:, :, :width_e], third], axis=1)
+    outer = outer.reshape(-1, width_e)
     high = outer.astype(jnp.bfloat16)
     low = (outer - high.astype(jnp.float32)).astype(jnp.bfloat16)
     grad_down = contract_last(high, w_proj) + contract_last(low, w_proj)
-    grad_proj = ordered[:, share_f + 8 : share_f + 8 + share_d].reshape(-1, width_e)
-    gains = jnp.sum(ordered[:, share_f + 16 : share_f + 19], axis=0).reshape(width)
+    grad_proj = tail[:, :share_d, :width_e].reshape(-1, width_e)
+    gains = jnp.sum(tail[:, : width // 128, width_e:], axis=0).reshape(width)
     mine_at = (lax.axis_index("z") * n_y + lax.axis_index("y")) * n_c + core
     grad_gain = lax.dynamic_slice_in_dim(gains, mine_at * (width // groups), width // groups, 0)
     return (

time: 171 us -> 186 us (1.088)
  waiting for transfers between devices: 21.7 us -> 35.4 us
  local copies, waits for them, and re-layouts: 17 us -> 29 us
  starting transfers between devices: 51.7 us -> 43.7 us
  other arithmetic: 11.8 us -> 9.79 us
    unnamed x34 -> x46, local copies, waits for them, and re-layouts: 7.34 us -> 19.9 us
    ppermute x18 -> x10, starting transfers between devices: 28.3 us -> 16.3 us  [halve(): lax.ppermute(lax.slice_in_dim(part, middle, None, axis=dim), DEVICES, par...]
    all_to_all x1, waiting for transfers between devices: 0.01 us -> 8.24 us  [per_device(): row_all = lax.all_to_all(row_part, DEVICES, 0, 0, tiled=True)]
    all_to_all x1, starting transfers between devices: 5.68 us -> 10.5 us  [per_device(): row_all = lax.all_to_all(row_part, DEVICES, 0, 0, tiled=True)]
    ppermute x5 -> x4, waiting for transfers between devices: 0.01 us -> 4.37 us  [swap_cores(): return lax.ppermute(block, 'c', [(0, 1), (1, 0)])]
    add x15 -> x8, other arithmetic: 7.27 us -> 6.02 us  [halve(): return ([k + s for k, s in zip(kept, sent)], also)]
    ppermute x18 -> x10, waiting for transfers between devices: 17 us -> 18.2 us  [halve(): lax.ppermute(lax.slice_in_dim(part, middle, None, axis=dim), DEVICES, par...]
    pallas_call x3 -> x2, Pallas kernels: 18 us -> 17.2 us  [up_products(): pl.pallas_call(kernel, grid_spec=pltpu.PrefetchScalarGridSpec(num_scalar_...]
  transfers between devices with their start and end apart: 28 -> 19, of which waited for: 10 -> 8; matrix products, arithmetic and copies ran while one was open for 11% -> 8% of each run, Pallas kernels for 26% -> 23%
where the time goes in v5:
time: 186 us; the launch traced here: 185 us
  Pallas kernels  56.2 us (30%)
  starting transfers between devices  43.7 us (23%)
  waiting for transfers between devices  35.4 us (19%)
  local copies, waits for them, and re-layouts  29 us (16%)
  other arithmetic  9.79 us (5%)
  matrix products  9.73 us (5%)
    unnamed x46, local copies, waits for them, and re-layouts  19.9 us
    pallas_call x1, Pallas kernels, forward(): pl.pallas_call(functools.partial(forward_kernel, units), grid=(hidden //...  18.9 us
    ppermute x10, waiting for transfers between devices, halve(): lax.ppermute(lax.slice_in_dim(part, middle, None, axis=dim), DEVICES, par...  18.2 us
    pallas_call x2, Pallas kernels, up_products(): pl.pallas_call(kernel, grid_spec=pltpu.PrefetchScalarGridSpec(num_scalar_...  17.2 us
    ppermute x10, starting transfers between devices, halve(): lax.ppermute(lax.slice_in_dim(part, middle, None, axis=dim), DEVICES, par...  16.3 us
    pallas_call x1, Pallas kernels, title_grads(): pl.pallas_call(titles_kernel, grid=(rows // step,), in_specs=[pl.BlockSpe...  11.5 us
    all_to_all x1, starting transfers between devices, per_device(): item_all = lax.all_to_all(mine, CHIPS, 0, 0, tiled=True)  11.5 us
    all_to_all x1, starting transfers between devices, per_device(): row_all = lax.all_to_all(row_part, DEVICES, 0, 0, tiled=True)  10.5 us
  transfers between devices with their start and end apart: 19, of which 8 were waited for; matrix products, arithmetic and copies ran while one was open for 8% of the time, Pallas kernels for 23%

profile of v5, /device:TPU:0, one launch (start us, length us, event | category | flops | bytes accessed | tf_op | source)
XLA Modules:
  0.0 184.9 jit_solution(6272379755996209251)
XLA Ops:
  1.4 1.0 copy-done.3
  2.5 2.5 %segment_sums.2 = f32[1536,256]{1,0:T(8,128)} custom-call(s32[1,1024]{1,0:T(1,128)S(1)} %bitcast.38, bf16[1024,256]{1,0:T(8,128)(2,1)S(1)} %copy-done.3), custom_call_target="tpu_custom_call" | custom-call | flops 805306368 | bytes 1572864 | tf_op jit(solution)/shard_map/segment_sums/pallas_call | solution.py:108
  5.8 1.1 copy.19
  6.9 2.3 %reshape.245 = f32[128,4,384]{2,1,0:T(4,128)} reshape(f32[512,384]{1,0:T(8,128)} %copy.19) | data formatting | bytes 1572864 | tf_op jit(solution)/shard_map/reshape | solution.py:404
  9.3 2.5 %segment_sums.3 = f32[1536,256]{1,0:T(8,128)} custom-call(s32[1,1024]{1,0:T(1,128)S(1)} %bitcast.37, bf16[1024,256]{1,0:T(8,128)(2,1)S(1)} %copy-done.4, f32[1536,256]{1,0:T(8,128)S(1)} %collective-permute-done.refs_0_), custom_call_target="tpu_custom_call" | custom-call | flops 805306368 | bytes 1572864 | tf_op jit(solution)/shard_map/segment_sums/pallas_call | solution.py:108
  11.8 11.5 %all-to-all-start = ((f32[64,24,256]{2,1,0:T(8,128)}), f32[64,24,256]{2,1,0:T(8,128)S(1)}, u32[]{:S(2)}, u32[]{:S(2)}) async-start(f32[64,24,256]{2,1,0:T(8,128)} %bitcast.4), calls=%async_computation | async-start | bytes 3145728 | tf_op jit(solution)/shard_map/all_to_all | solution.py:389
  23.3 2.3 %copy-done.5 = bf16[768,3072]{1,0:T(8,128)(2,1)S(1)} copy-done((bf16[768,3072]{1,0:T(8,128)(2,1)S(1)}, bf16[768,3072]{1,0:T(8,128)(2,1)}, u32[]{:S(2)}) %copy-start.5) | copy-done | bytes 4718616
  25.6 1.7 copy-done.6
  27.3 18.9 %forward.1 = (bf16[1536,768]{1,0:T(8,128)(2,1)S(1)}, bf16[1536,3072]{1,0:T(8,128)(2,1)}, f32[24,3072]{1,0:T(8,128)S(1)}, f32[24,768]{1,0:T(8,128)S(1)}) custom-call(bf16[1536,768]{1,0:T(8,128)(2,1)S(1)} %bitcast.41, f32[1,768]{1,0:T(1,128)S(1)} %reshape.244.gain_ref, bf16[768,3072]{1,0:T(8,128)(2,1)S(1)} %copy-done.5), custom_call_target="tpu_custom_call" | custom-call | flops 28991029248 | bytes 18874368 | tf_op jit(solution)/shard_map/forward/pallas_call | solution.py:156
  46.2 1.4 copy-done.11
  47.6 3.8 %fusion.3.pool_ref = bf16[24,1024]{1,0:T(8,128)(2,1)S(1)} fusion(s32[1024]{0:T(1024)S(1)} %fusion.32, f32[24,768]{1,0:T(8,128)S(1)} %get-tuple-element.43, bf16[24,3072]{1,0:T(8,128)(2,1)S(1)} %convert_element_type.35.mean_ref, bf16[3072,768]{1,0:T(8,128)(2,1)} %param.14), kind=kOutput, calls=%fused_computation.9 | convolution fusion | flops 151842816 | bytes 4993024 | tf_op jit(solution)/shard_map/dot_general | solution.py:412
  51.7 3.8 %convolution_multiply_fusion.act_ref = f32[24,3072]{1,0:T(8,128)S(1)} fusion(bf16[3072,768]{1,0:T(8,128)(2,1)} %param.14, f32[24,768]{1,0:T(8,128)S(1)} %fusion.45.pool_ref), kind=kOutput, calls=%fused_computation | convolution fusion | flops 113338368 | bytes 5087232 | tf_op jit(solution)/shard_map/dot_general | solution.py:29
  55.6 9.6 %first_products.1 = (bf16[1536,3072]{1,0:T(8,128)(2,1)S(1)}, f32[64,40,384]{2,1,0:T(8,128)S(1)}, f32[64,40,384]{2,1,0:T(8,128)S(1)}) custom-call(s32[1]{0:T(128)} %bitcast.core_ref, s32[3,4]{1,0:T(4,128)S(1)} %pad_add_fusion.keep_at, s32[3,4]{1,0:T(4,128)S(1)} %pad_add_fusion.1.send_at, bf16[1536,3072]{1,0:T(8,128)(2,1)} %get-tuple-element.41.slope_ref, ...), custom_call_target="tpu_custom_call" | custom-call | flops 3623878656 | bytes 18874368 | tf_op jit(solution)/shard_map/first_products/pallas_call | solution.py:258
  65.2 3.7 %copy-done.8 = bf16[1536,3072]{1,0:T(8,128)(2,1)} copy-done((bf16[1536,3072]{1,0:T(8,128)(2,1)}, bf16[1536,3072]{1,0:T(8,128)(2,1)S(1)}, u32[]{:S(2)}) %copy-start.8) | copy-done | bytes 9437208
  69.1 3.7 %copy-done.9 = bf16[1536,3072]{1,0:T(8,128)(2,1)S(1)} copy-done((bf16[1536,3072]{1,0:T(8,128)(2,1)S(1)}, bf16[1536,3072]{1,0:T(8,128)(2,1)}, u32[]{:S(2)}) %copy-start.9) | copy-done | bytes 9437208
  72.7 7.6 %other_products.1 = (f32[64,32,384]{2,1,0:T(8,128)S(1)}, f32[64,32,384]{2,1,0:T(8,128)S(1)}) custom-call(s32[1]{0:T(128)} %bitcast.core_ref, s32[3,4]{1,0:T(4,128)S(1)} %pad_add_fusion.keep_at, s32[3,4]{1,0:T(4,128)S(1)} %pad_add_fusion.1.send_at, bf16[1536,3072]{1,0:T(8,128)(2,1)S(1)} %copy-done.9, bf16[24,3072]{1,0:T(8,128)(2,1)S(1)} %convert_element_type.35.mean_ref, ...), custom_call_target="tpu_custom_call" | custom-call | flops 3623878656 | bytes 18874368 | tf_op jit(solution)/shard_map/other_products/pallas_call | solution.py:258
  81.3 1.7 collective-permute-start.2
  82.9 3.2 %collective-permute-done.3 = f32[64,32,384]{2,1,0:T(8,128)S(1)} collective-permute-done((f32[64,32,384]{2,1,0:T(8,128)S(1)}, f32[64,32,384]{2,1,0:T(8,128)S(1)}, u32[]{:S(2)}, u32[]{:S(2)}) %collective-permute-start.3) | collective-permute-done | bytes 3145760 | tf_op jit(solution)/shard_map/ppermute | solution.py:39
  86.8 1.6 collective-permute-start.4
  88.4 3.7 %copy-done.10 = bf16[1536,3072]{1,0:T(8,128)(2,1)S(1)} copy-done((bf16[1536,3072]{1,0:T(8,128)(2,1)S(1)}, bf16[1536,3072]{1,0:T(8,128)(2,1)}, u32[]{:S(2)}) %copy-start.10) | copy-done | bytes 9437208
  92.1 11.5 %title_grads.1 = (bf16[1536,768]{1,0:T(8,128)(2,1)}, f32[8,768]{1,0:T(8,128)S(1)}) custom-call(bf16[1536,3072]{1,0:T(8,128)(2,1)S(1)} %copy-done.10, bf16[768,3072]{1,0:T(8,128)(2,1)S(1)} %bitcast.40, bf16[1536,768]{1,0:T(8,128)(2,1)S(1)} %bitcast.42, f32[1,768]{1,0:T(1,128)S(1)} %reshape.244.gain_ref, f32[24,768]{1,0:T(8,128)S(1)} %fusion.45.pool_ref), custom_call_target="tpu_custom_call" | custom-call | flops 7247757312 | bytes 9437184 | tf_op jit(solution)/shard_map/title_grads/pallas_call | solution.py:304
  103.6 3.7 %collective-permute-done.4 = f32[4,2,4,32,384]{4,3,2,1,0:T(8,128)S(1)} collective-permute-done((f32[4,2,4,32,384]{4,3,2,1,0:T(8,128)S(1)}, f32[4,2,4,32,384]{4,3,2,1,0:T(8,128)S(1)}, u32[]{:S(2)}, u32[]{:S(2)}) %collective-permute-start.4) | collective-permute-done | bytes 1572896 | tf_op jit(solution)/shard_map/ppermute | solution.py:78
  107.6 2.8 %collective-permute-start.5 = (f32[4,4,1,40,384]{4,3,2,1,0:T(8,128)S(1)}, f32[4,4,1,40,384]{4,3,2,1,0:T(8,128)S(1)}, u32[]{:S(2)}, u32[]{:S(2)}) collective-permute-start(f32[4,4,1,40,384]{4,3,2,1,0:T(8,128)S(1)} %slice.132), channel_id=1, source_target_pairs={{0,3},{1,2},{2,1},{3,0},{4,5},{5,4},{6,7},{7,6},{8,11},{9,10},{10,... | collective-permute-start | bytes 2949128 | tf_op jit(solution)/shard_map/ppermute | solution.py:78
  110.7 2.8 %collective-permute-start.6 = (f32[4,1,4,32,384]{4,3,2,1,0:T(8,128)S(1)}, f32[4,1,4,32,384]{4,3,2,1,0:T(8,128)S(1)}, u32[]{:S(2)}, u32[]{:S(2)}) collective-permute-start(f32[4,1,4,32,384]{4,3,2,1,0:T(8,128)S(1)} %slice.134), channel_id=1, source_target_pairs={{0,24},{1,25},{2,26},{3,27},{4,12},{5,13},{6,14},{7,15},{8,16},{9,... | collective-permute-start | bytes 2359304 | tf_op jit(solution)/shard_map/ppermute | solution.py:78
  113.5 1.2 collective-permute-done.7
  114.7 9.3 %collective-permute-done.6 = f32[4,1,4,32,384]{4,3,2,1,0:T(8,128)S(1)} collective-permute-done((f32[4,1,4,32,384]{4,3,2,1,0:T(8,128)S(1)}, f32[4,1,4,32,384]{4,3,2,1,0:T(8,128)S(1)}, u32[]{:S(2)}, u32[]{:S(2)}) %collective-permute-start.6) | collective-permute-done | bytes 786464 | tf_op jit(solution)/shard_map/ppermute | solution.py:78
  124.7 1.0 slice_add_fusion.3
  125.7 1.8 slice.141
  127.7 10.5 %all-to-all-start.1 = ((f32[128,4,384]{2,1,0:T(4,128)}), f32[128,4,384]{2,1,0:T(4,128)S(1)}, u32[]{:S(2)}, u32[]{:S(2)}) async-start(f32[128,4,384]{2,1,0:T(4,128)} %reshape.245), calls=%async_computation.1 | async-start | bytes 1572864 | tf_op jit(solution)/shard_map/all_to_all | solution.py:439
  138.3 0.8 copy-done.14
  139.1 2.3 %collective-permute-start.9 = (f32[4,1,1,40,384]{4,3,2,1,0:T(8,128)S(1)}, f32[4,1,1,40,384]{4,3,2,1,0:T(8,128)}, u32[]{:S(2)}, u32[]{:S(2)}) collective-permute-start(f32[4,1,1,40,384]{4,3,2,1,0:T(8,128)S(1)} %slice.138), channel_id=1, source_target_pairs={{0,24},{1,25},{2,26},{3,27},{4,12},{5,13},{6,14},{7,15},{8,16},{9,... | collective-permute-start | bytes 737288 | tf_op jit(solution)/shard_map/ppermute | solution.py:78
  141.4 1.2 slice_add_fusion.5
  143.4 2.7 %collective-permute-start.11 = (f32[4,1,1,32,384]{4,3,2,1,0:T(8,128)}, f32[4,1,1,32,384]{4,3,2,1,0:T(8,128)}, u32[]{:S(2)}, u32[]{:S(2)}) collective-permute-start(f32[4,1,1,32,384]{4,3,2,1,0:T(8,128)} %slice.142), channel_id=1, source_target_pairs={{0,3},{1,2},{2,1},{3,0},{4,5},{5,4},{6,7},{7,6},{8,11},{9,10},{10,... | collective-permute-start | bytes 589832 | tf_op jit(solution)/shard_map/ppermute | solution.py:78
  146.1 8.2 %all-to-all-done.1 = f32[128,4,384]{2,1,0:T(4,128)S(1)} async-done(((f32[128,4,384]{2,1,0:T(4,128)}), f32[128,4,384]{2,1,0:T(4,128)S(1)}, u32[]{:S(2)}, u32[]{:S(2)}) %all-to-all-start.1) | async-done | bytes 786464 | tf_op jit(solution)/shard_map/all_to_all | solution.py:439
  154.4 1.4 slice_add_fusion.6
  155.8 1.0 slice_add_fusion.7
  157.6 0.8 collective-permute-start.12
  158.4 1.4 reshape.249.arrived_ref
  159.8 1.6 copy-done.2
  161.4 3.6 %row_update.1 = (f32[2048,256]{1,0:T(8,128)}, f32[2048,256]{1,0:T(8,128)}) custom-call(f32[512,384]{1,0:T(8,128)S(1)} %reshape.249.arrived_ref, f32[2048,256]{1,0:T(8,128)S(1)} %copy-done.1, f32[2048,256]{1,0:T(8,128)S(1)} %copy-done.2), custom_call_target="tpu_custom_call" | custom-call | flops 1073741824 | bytes 8388608 | tf_op jit(solution)/shard_map/row_update/pallas_call | solution.py:347
  165.1 1.0 fusion.8
  166.1 0.9 collective-permute-start.13
  167.0 5.2 %collective-permute-done.13 = f32[1,1,1,72,384]{4,3,2,1,0:T(8,128)S(1)} collective-permute-done((f32[1,1,1,72,384]{4,3,2,1,0:T(8,128)S(1)}, f32[1,1,1,72,384]{4,3,2,1,0:T(8,128)S(1)}, u32[]{:S(2)}, u32[]{:S(2)}) %collective-permute-start.13) | collective-permute-done | bytes 110624 | tf_op jit(solution)/shard_map/ppermute | solution.py:78
  172.8 2.8 %collective-permute-start.15 = (f32[72,384]{1,0:T(8,128)S(1)}, f32[72,384]{1,0:T(8,128)S(1)}, u32[]{:S(2)}, u32[]{:S(2)}) collective-permute-start(f32[72,384]{1,0:T(8,128)S(1)} %get-tuple-element.85), channel_id=1, source_target_pairs={{0,2},{1,3},{2,0},{3,1},{4,6},{5,7},{6,4},{7,5},{8,10},{9,11},{10,... | collective-permute-start | bytes 331784 | tf_op jit(solution)/shard_map/ppermute | solution.py:44
  175.6 1.4 collective-permute-start.16
  177.0 2.5 %collective-permute-done.15 = f32[72,384]{1,0:T(8,128)S(1)} collective-permute-done((f32[72,384]{1,0:T(8,128)S(1)}, f32[72,384]{1,0:T(8,128)S(1)}, u32[]{:S(2)}, u32[]{:S(2)}) %collective-permute-start.15) | collective-permute-done | bytes 110624 | tf_op jit(solution)/shard_map/ppermute | solution.py:44
  179.5 2.1 %collective-permute-done.16 = f32[72,384]{1,0:T(8,128)S(1)} collective-permute-done((f32[72,384]{1,0:T(8,128)S(1)}, f32[72,384]{1,0:T(8,128)S(1)}, u32[]{:S(2)}, u32[]{:S(2)}) %collective-permute-start.16) | collective-permute-done | bytes 110624 | tf_op jit(solution)/shard_map/ppermute | solution.py:44
  183.2 1.0 convolution_add_fusion
  (102 shorter events, 10.2 us)
Async XLA Ops:
  0.6 50.9 %copy-start = (bf16[768,256]{1,0:T(8,128)(2,1)S(1)}, bf16[768,256]{1,0:T(8,128)(2,1)}, u32[]{:S(2)}) copy-start(bf16[768,256]{1,0:T(8,128)(2,1)} %param.15) | copy-start | bytes 1179652
  0.6 4.3 %copy-start.19 = (s32[1,512]{1,0:T(1,128)S(1)}, s32[1,512]{1,0:T(1,128)}, u32[]{:S(2)}) copy-start(s32[1,512]{1,0:T(1,128)} %param.19) | copy-start | bytes 6148
  0.7 4.3 %copy-start.20 = (s32[1024]{0:T(1024)S(1)}, s32[1024]{0:T(1024)}, u32[]{:S(2)}) copy-start(s32[1024]{0:T(1024)} %param.18) | copy-start | bytes 12292
  1.4 1.0 copy-start.3
  2.5 2.5 %copy-start.4 = (bf16[1024,256]{1,0:T(8,128)(2,1)S(1)}, bf16[1024,256]{1,0:T(8,128)(2,1)}, u32[]{:S(2)}) copy-start(bf16[1024,256]{1,0:T(8,128)(2,1)} %grad_ref.3) | copy-start | bytes 1572868
  5.0 4.3 %collective-permute-start = (f32[1536,256]{1,0:T(8,128)}, f32[1536,256]{1,0:T(8,128)S(1)}, u32[]{:S(2)}, u32[]{:S(2)}) collective-permute-start(f32[1536,256]{1,0:T(8,128)} %segment_sums.2), channel_id=1, source_target_pairs={{0,4},{4,0},{1,5},{5,1},{2,6},{6,2},{3,7},{7,3},{8,12},{12,8},{9,1... | collective-permute-start | bytes 4718600 | tf_op jit(solution)/shard_map/ppermute | solution.py:39
  6.9 4.9 %copy-start.18 = (f32[768]{0:T(1024)S(1)}, f32[768]{0:T(1024)}, u32[]{:S(2)}) copy-start(f32[768]{0:T(1024)} %param.12) | copy-start | bytes 9220
  11.8 39.6 %all-to-all-start = ((f32[64,24,256]{2,1,0:T(8,128)}), f32[64,24,256]{2,1,0:T(8,128)S(1)}, u32[]{:S(2)}, u32[]{:S(2)}) async-start(f32[64,24,256]{2,1,0:T(8,128)} %bitcast.4), calls=%async_computation | async-start | bytes 3145728 | tf_op jit(solution)/shard_map/all_to_all | solution.py:389
  23.3 2.3 %copy-start.5 = (bf16[768,3072]{1,0:T(8,128)(2,1)S(1)}, bf16[768,3072]{1,0:T(8,128)(2,1)}, u32[]{:S(2)}) copy-start(bf16[768,3072]{1,0:T(8,128)(2,1)} %w_ref.3) | copy-start | bytes 14155780
  25.6 1.7 copy-start.6
  46.2 1.4 copy-start.11
  51.7 3.8 %copy-start.12 = (bf16[1536,768]{1,0:T(8,128)(2,1)S(1)}, bf16[1536,768]{1,0:T(8,128)(2,1)}, u32[]{:S(2)}) copy-start(bf16[1536,768]{1,0:T(8,128)(2,1)} %copy-done.11) | copy-start | bytes 7077892
  65.2 3.7 %copy-start.8 = (bf16[1536,3072]{1,0:T(8,128)(2,1)}, bf16[1536,3072]{1,0:T(8,128)(2,1)S(1)}, u32[]{:S(2)}) copy-start(bf16[1536,3072]{1,0:T(8,128)(2,1)S(1)} %get-tuple-element.50.pre_ref) | copy-start | bytes 28311556
  68.8 11.9 %collective-permute-start.1 = (f32[64,40,384]{2,1,0:T(8,128)S(1)}, f32[64,40,384]{2,1,0:T(8,128)S(1)}, u32[]{:S(2)}, u32[]{:S(2)}) collective-permute-start(f32[64,40,384]{2,1,0:T(8,128)S(1)} %get-tuple-element.49), channel_id=1, source_target_pairs={{0,4},{4,0},{1,5},{5,1},{2,6},{6,2},{3,7},{7,3},{8,12},{12,8},{9,1... | collective-permute-start | bytes 11796488 | tf_op jit(solution)/shard_map/ppermute | solution.py:39
  69.1 3.7 %copy-start.9 = (bf16[1536,3072]{1,0:T(8,128)(2,1)S(1)}, bf16[1536,3072]{1,0:T(8,128)(2,1)}, u32[]{:S(2)}) copy-start(bf16[1536,3072]{1,0:T(8,128)(2,1)} %copy-done.8) | copy-start | bytes 28311556
  80.3 5.7 %collective-permute-start.3 = (f32[64,32,384]{2,1,0:T(8,128)S(1)}, f32[64,32,384]{2,1,0:T(8,128)S(1)}, u32[]{:S(2)}, u32[]{:S(2)}) collective-permute-start(f32[64,32,384]{2,1,0:T(8,128)S(1)} %get-tuple-element.52), channel_id=1, source_target_pairs={{0,4},{4,0},{1,5},{5,1},{2,6},{6,2},{3,7},{7,3},{8,12},{12,8},{9,1... | collective-permute-start | bytes 9437192 | tf_op jit(solution)/shard_map/ppermute | solution.py:39
  81.1 7.3 %slice-start = ((s8[4718592]{0:T(1024)(128)(4,1)}), s8[4194304]{0:T(1024)(128)(4,1)S(1)}, s32[]{:S(2)}) async-start(s8[4718592]{0:T(1024)(128)(4,1)} %bitcast.39), calls=%async_computation.2 | async-start | bytes 8388608
  81.3 26.1 %collective-permute-start.2 = (f32[4,4,2,40,384]{4,3,2,1,0:T(8,128)S(1)}, f32[4,4,2,40,384]{4,3,2,1,0:T(8,128)S(1)}, u32[]{:S(2)}, u32[]{:S(2)}) collective-permute-start(f32[4,4,2,40,384]{4,3,2,1,0:T(8,128)S(1)} %slice.128), channel_id=1, source_target_pairs={{0,1},{1,0},{2,3},{3,2},{4,7},{5,6},{6,5},{7,4},{8,9},{9,8},{10,11... | collective-permute-start | bytes 5898248 | tf_op jit(solution)/shard_map/ppermute | solution.py:78
  86.1 2.3 %slice-start.1 = ((s8[4718592]{0:T(1024)(128)(4,1)}), s8[524288]{0:T(1024)(128)(4,1)S(1)}, s32[]{:S(2)}) async-start(s8[4718592]{0:T(1024)(128)(4,1)} %bitcast.39), calls=%async_computation.3 | async-start | bytes 1048576
  86.7 1.7 copy-start.7
  86.8 20.5 %collective-permute-start.4 = (f32[4,2,4,32,384]{4,3,2,1,0:T(8,128)S(1)}, f32[4,2,4,32,384]{4,3,2,1,0:T(8,128)S(1)}, u32[]{:S(2)}, u32[]{:S(2)}) collective-permute-start(f32[4,2,4,32,384]{4,3,2,1,0:T(8,128)S(1)} %slice.129), channel_id=1, source_target_pairs={{0,8},{1,9},{2,10},{3,11},{4,28},{5,29},{6,30},{7,31},{8,0},{9,1},... | collective-permute-start | bytes 4718600 | tf_op jit(solution)/shard_map/ppermute | solution.py:78
  88.4 3.7 %copy-start.10 = (bf16[1536,3072]{1,0:T(8,128)(2,1)S(1)}, bf16[1536,3072]{1,0:T(8,128)(2,1)}, u32[]{:S(2)}) copy-start(bf16[1536,3072]{1,0:T(8,128)(2,1)} %copy-done.8) | copy-start | bytes 28311556
  107.6 16.4 %collective-permute-start.5 = (f32[4,4,1,40,384]{4,3,2,1,0:T(8,128)S(1)}, f32[4,4,1,40,384]{4,3,2,1,0:T(8,128)S(1)}, u32[]{:S(2)}, u32[]{:S(2)}) collective-permute-start(f32[4,4,1,40,384]{4,3,2,1,0:T(8,128)S(1)} %slice.132), channel_id=1, source_target_pairs={{0,3},{1,2},{2,1},{3,0},{4,5},{5,4},{6,7},{7,6},{8,11},{9,10},{10,... | collective-permute-start | bytes 2949128 | tf_op jit(solution)/shard_map/ppermute | solution.py:78
  110.7 13.3 %collective-permute-start.6 = (f32[4,1,4,32,384]{4,3,2,1,0:T(8,128)S(1)}, f32[4,1,4,32,384]{4,3,2,1,0:T(8,128)S(1)}, u32[]{:S(2)}, u32[]{:S(2)}) collective-permute-start(f32[4,1,4,32,384]{4,3,2,1,0:T(8,128)S(1)} %slice.134), channel_id=1, source_target_pairs={{0,24},{1,25},{2,26},{3,27},{4,12},{5,13},{6,14},{7,15},{8,16},{9,... | collective-permute-start | bytes 2359304 | tf_op jit(solution)/shard_map/ppermute | solution.py:78
  113.5 1.2 collective-permute-start.7
  124.1 14.1 %collective-permute-start.8 = (f32[4,2,1,40,384]{4,3,2,1,0:T(8,128)S(1)}, f32[4,2,1,40,384]{4,3,2,1,0:T(8,128)S(1)}, u32[]{:S(2)}, u32[]{:S(2)}) collective-permute-start(f32[4,2,1,40,384]{4,3,2,1,0:T(8,128)S(1)} %slice.136), channel_id=1, source_target_pairs={{0,8},{1,9},{2,10},{3,11},{4,28},{5,29},{6,30},{7,31},{8,0},{9,1},... | collective-permute-start | bytes 1474568 | tf_op jit(solution)/shard_map/ppermute | solution.py:78
  127.5 14.0 %collective-permute-start.10 = (f32[4,1,2,32,384]{4,3,2,1,0:T(8,128)}, f32[4,1,2,32,384]{4,3,2,1,0:T(8,128)}, u32[]{:S(2)}, u32[]{:S(2)}) collective-permute-start(f32[4,1,2,32,384]{4,3,2,1,0:T(8,128)} %slice.141), channel_id=1, source_target_pairs={{0,1},{1,0},{2,3},{3,2},{4,7},{5,6},{6,5},{7,4},{8,9},{9,8},{10,11... | collective-permute-start | bytes 1179656 | tf_op jit(solution)/shard_map/ppermute | solution.py:78
  127.7 26.7 %all-to-all-start.1 = ((f32[128,4,384]{2,1,0:T(4,128)}), f32[128,4,384]{2,1,0:T(4,128)S(1)}, u32[]{:S(2)}, u32[]{:S(2)}) async-start(f32[128,4,384]{2,1,0:T(4,128)} %reshape.245), calls=%async_computation.1 | async-start | bytes 1572864 | tf_op jit(solution)/shard_map/all_to_all | solution.py:439
  138.3 0.8 copy-start.14
  139.1 20.7 %copy-start.1 = (f32[2048,256]{1,0:T(8,128)S(1)}, f32[2048,256]{1,0:T(8,128)}, u32[]{:S(2)}) copy-start(f32[2048,256]{1,0:T(8,128)} %table_ref.1) | copy-start | bytes 6291460
  139.1 15.3 %collective-permute-start.9 = (f32[4,1,1,40,384]{4,3,2,1,0:T(8,128)S(1)}, f32[4,1,1,40,384]{4,3,2,1,0:T(8,128)}, u32[]{:S(2)}, u32[]{:S(2)}) collective-permute-start(f32[4,1,1,40,384]{4,3,2,1,0:T(8,128)S(1)} %slice.138), channel_id=1, source_target_pairs={{0,24},{1,25},{2,26},{3,27},{4,12},{5,13},{6,14},{7,15},{8,16},{9,... | collective-permute-start | bytes 737288 | tf_op jit(solution)/shard_map/ppermute | solution.py:78
  142.6 0.8 copy-start.17
  143.4 11.0 %collective-permute-start.11 = (f32[4,1,1,32,384]{4,3,2,1,0:T(8,128)}, f32[4,1,1,32,384]{4,3,2,1,0:T(8,128)}, u32[]{:S(2)}, u32[]{:S(2)}) collective-permute-start(f32[4,1,1,32,384]{4,3,2,1,0:T(8,128)} %slice.142), channel_id=1, source_target_pairs={{0,3},{1,2},{2,1},{3,0},{4,5},{5,4},{6,7},{7,6},{8,11},{9,10},{10,... | collective-permute-start | bytes 589832 | tf_op jit(solution)/shard_map/ppermute | solution.py:78
  154.4 3.2 %copy-start.13 = (f32[128,4,384]{2,1,0:T(4,128)}, f32[128,4,384]{2,1,0:T(4,128)S(1)}, u32[]{:S(2)}) copy-start(f32[128,4,384]{2,1,0:T(4,128)S(1)} %all-to-all-done.1) | copy-start | bytes 2359300
  156.8 0.8 copy-start.15
  157.6 7.5 %collective-permute-start.12 = (f32[2,1,1,72,384]{4,3,2,1,0:T(8,128)}, f32[2,1,1,72,384]{4,3,2,1,0:T(8,128)}, u32[]{:S(2)}, u32[]{:S(2)}) collective-permute-start(f32[2,1,1,72,384]{4,3,2,1,0:T(8,128)} %pad_maximum_fusion.4), channel_id=1, source_target_pairs={{0,32},{1,33},{2,34},{3,35},{4,100},{5,101},{6,102},{7,103},{8,40}... | collective-permute-start | bytes 663560 | tf_op jit(solution)/shard_map/ppermute | solution.py:78
  159.8 1.6 copy-start.2
  161.4 3.7 %copy-start.16 = (f32[4,1,1,32,384]{4,3,2,1,0:T(8,128)S(1)}, f32[4,1,1,32,384]{4,3,2,1,0:T(8,128)}, u32[]{:S(2)}) copy-start(f32[4,1,1,32,384]{4,3,2,1,0:T(8,128)} %copy-done.15) | copy-start | bytes 589828
  166.1 6.0 %collective-permute-start.13 = (f32[1,1,1,72,384]{4,3,2,1,0:T(8,128)S(1)}, f32[1,1,1,72,384]{4,3,2,1,0:T(8,128)S(1)}, u32[]{:S(2)}, u32[]{:S(2)}) collective-permute-start(f32[1,1,1,72,384]{4,3,2,1,0:T(8,128)S(1)} %slice.147), channel_id=1, source_target_pairs={{0,96},{1,97},{2,98},{3,99},{4,36},{5,37},{6,38},{7,39},{8,104},{9... | collective-permute-start | bytes 331784 | tf_op jit(solution)/shard_map/ppermute | solution.py:78
  172.1 4.8 %collective-permute-start.14 = (f32[72,384]{1,0:T(8,128)S(1)}, f32[72,384]{1,0:T(8,128)S(1)}, u32[]{:S(2)}, u32[]{:S(2)}) collective-permute-start(f32[72,384]{1,0:T(8,128)S(1)} %get-tuple-element.85), channel_id=1, source_target_pairs={{0,1},{1,0},{2,3},{3,2},{4,5},{5,4},{6,7},{7,6},{8,9},{9,8},{10,11... | collective-permute-start | bytes 331784 | tf_op jit(solution)/shard_map/ppermute | solution.py:44
  172.8 6.7 %collective-permute-start.15 = (f32[72,384]{1,0:T(8,128)S(1)}, f32[72,384]{1,0:T(8,128)S(1)}, u32[]{:S(2)}, u32[]{:S(2)}) collective-permute-start(f32[72,384]{1,0:T(8,128)S(1)} %get-tuple-element.85), channel_id=1, source_target_pairs={{0,2},{1,3},{2,0},{3,1},{4,6},{5,7},{6,4},{7,5},{8,10},{9,11},{10,... | collective-permute-start | bytes 331784 | tf_op jit(solution)/shard_map/ppermute | solution.py:44
  175.6 6.0 %collective-permute-start.16 = (f32[72,384]{1,0:T(8,128)S(1)}, f32[72,384]{1,0:T(8,128)S(1)}, u32[]{:S(2)}, u32[]{:S(2)}) collective-permute-start(f32[72,384]{1,0:T(8,128)S(1)} %get-tuple-element.85), channel_id=1, source_target_pairs={{0,3},{1,2},{2,1},{3,0},{4,7},{5,6},{6,5},{7,4},{8,11},{9,10},{10,... | collective-permute-start | bytes 331784 | tf_op jit(solution)/shard_map/ppermute | solution.py:44

commit v6 on v5

--- a/solution.py
+++ b/solution.py
@@ -16,7 +16,7 @@
 CHIPS = ("z", "y", "x")
 GROUP = ("z", "y", "c")
 DEVICES = ("z", "y", "c", "x")
-VMEM = 30 << 20
+VMEM = 26 << 20
 
 
 def contract_first(left, right):
@@ -173,7 +173,7 @@
             jax.ShapeDtypeStruct((units, hidden), jnp.float32),
             jax.ShapeDtypeStruct((units, width), jnp.float32),
         ],
-        compiler_params=pltpu.CompilerParams(vmem_limit_bytes=VMEM),
+        compiler_params=pltpu.CompilerParams(vmem_limit_bytes=24 << 20),
         cost_estimate=cost(8 * rows * width * hidden, 4 * rows * hidden, rows * hidden),
         name="forward",
     )(titles.reshape(rows, width), ln_gain.reshape(1, width), w_up)
@@ -268,7 +268,7 @@
             out_specs=out_specs,
         ),
         out_shape=out_shape,
-        compiler_params=pltpu.CompilerParams(vmem_limit_bytes=VMEM),
+        compiler_params=pltpu.CompilerParams(vmem_limit_bytes=14 << 20),
         cost_estimate=cost(2 * rows * wide * hidden, 4 * rows * hidden),
         name=name,
     )(*tables, *left, *by_column, grad_b, normed_b)
@@ -429,15 +429,18 @@
     )
     d_pre = pltpu.with_memory_space_constraint(d_pre, pltpu.VMEM)
     sums += up_products(tables, 1, (d_pre,), (mean_act_b,), grad_b, normed_b)
+    row_all = lax.all_to_all(row_part, DEVICES, 0, 0, tiled=True)
+    sums[3], row_all = lax.optimization_barrier((sums[3], row_all))
     parts = [
         (keep + swap_cores(send)).reshape(n_z, n_y, n_x, -1, width // 2)
         for keep, send in zip(sums[::2], sums[1::2])
     ]
 
     d_titles, gain_term = title_grads(d_pre, w_up, titles, ln_gain, d_pooled)
-    gain_term, row_part = lax.optimization_barrier((gain_term, row_part))
-    row_all = lax.all_to_all(row_part, DEVICES, 0, 0, tiled=True)
-    parts, (d_titles, gain_term) = halve(parts, "xy", False, (d_titles, gain_term))
+    beside = row_update(row_all.reshape(slot_count, width_e + 128), table, accum)
+    parts, (d_titles, gain_term, new_table, new_accum) = halve(
+        parts, "xy", False, (d_titles, gain_term, *beside)
+    )
     gain_term = (gain_term + swap_cores(gain_term)).reshape(8, -1, 128)
     gain_term = jnp.sum(gain_term, axis=0)
     gain_term = jnp.pad(
@@ -446,10 +449,9 @@
     parts, (gain_term,) = halve(parts, "xy", True, (gain_term,))
     parts[0] = parts[0] + gain_term
     parts, _ = halve(parts, "yx", False)
-    parts, (row_all,) = halve(parts, "yx", True, (row_all,))
+    parts, _ = halve(parts, "yx", True)
     both = [jnp.concatenate(parts, axis=3)]
-    beside = row_update(row_all.reshape(slot_count, width_e + 128), table, accum)
-    both, (new_table, new_accum) = halve(both, "z", False, tuple(beside))
+    both, _ = halve(both, "z", False)
     both, _ = halve(both, "z", True)
 
     last = both[0].reshape(-1, width // 2)

time: 186 us -> 197 us (1.059)
  local copies, waits for them, and re-layouts: 29 us -> 35.3 us
  other arithmetic: 9.79 us -> 11.8 us
    ppermute x10, waiting for transfers between devices: 18.2 us -> 30.5 us  [halve(): lax.ppermute(lax.slice_in_dim(part, middle, None, axis=dim), DEVICES, par...]
    all_to_all x1, waiting for transfers between devices: 8.24 us -> 0.01 us  [per_device(): row_all = lax.all_to_all(row_part, DEVICES, 0, 0, tiled=True)]
    unnamed x46 -> x70, local copies, waits for them, and re-layouts: 19.9 us -> 26.3 us
    add x2, other arithmetic: 1.02 us -> 4.46 us  [per_device(): keep + swap_cores(send)]
    ppermute x4, waiting for transfers between devices: 4.37 us -> 1.2 us  [swap_cores(): return lax.ppermute(block, 'c', [(0, 1), (1, 0)])]
    add x8, other arithmetic: 6.02 us -> 3.93 us  [halve(): return ([k + s for k, s in zip(kept, sent)], also)]
  transfers between devices with their start and end apart: 19 -> 19, of which waited for: 8 -> 11; matrix products, arithmetic and copies ran while one was open for 8% -> 9% of each run, Pallas kernels for 23% -> 21%
where the time goes in v6:
time: 197 us
  Pallas kernels  57.5 us (29%)
  starting transfers between devices  44.1 us (22%)
  waiting for transfers between devices  36.9 us (19%)
  local copies, waits for them, and re-layouts  35.3 us (18%)
  other arithmetic  11.8 us (6%)
  matrix products  9.78 us (5%)
    ppermute x10, waiting for transfers between devices, halve(): lax.ppermute(lax.slice_in_dim(part, middle, None, axis=dim), DEVICES, par...  30.5 us
    unnamed x70, local copies, waits for them, and re-layouts  26.3 us
    pallas_call x1, Pallas kernels, forward(): pl.pallas_call(functools.partial(forward_kernel, units), grid=(hidden //...  18.9 us
    pallas_call x2, Pallas kernels, up_products(): pl.pallas_call(kernel, grid_spec=pltpu.PrefetchScalarGridSpec(num_scalar_...  18.4 us
    ppermute x10, starting transfers between devices, halve(): lax.ppermute(lax.slice_in_dim(part, middle, None, axis=dim), DEVICES, par...  17.2 us
    all_to_all x1, starting transfers between devices, per_device(): item_all = lax.all_to_all(mine, CHIPS, 0, 0, tiled=True)  11.7 us
    pallas_call x1, Pallas kernels, title_grads(): pl.pallas_call(titles_kernel, grid=(rows // step,), in_specs=[pl.BlockSpe...  11.5 us
    all_to_all x1, starting transfers between devices, per_device(): row_all = lax.all_to_all(row_part, DEVICES, 0, 0, tiled=True)  10.3 us
  transfers between devices with their start and end apart: 19, of which 11 were waited for; matrix products, arithmetic and copies ran while one was open for 9% of the time, Pallas kernels for 21%

profile of v6, /device:TPU:0, one launch (start us, length us, event | category | flops | bytes accessed | tf_op | source)
XLA Modules:
  0.0 196.5 jit_solution(3231807348060591877)
XLA Ops:
  1.4 1.0 copy-done.6
  2.5 2.5 %segment_sums.2 = f32[1536,256]{1,0:T(8,128)} custom-call(s32[1,1024]{1,0:T(1,128)S(1)} %bitcast.38, bf16[1024,256]{1,0:T(8,128)(2,1)S(1)} %copy-done.6), custom_call_target="tpu_custom_call" | custom-call | flops 805306368 | bytes 1572864 | tf_op jit(solution)/shard_map/segment_sums/pallas_call | solution.py:108
  5.8 1.1 copy.19
  6.9 2.3 %reshape.245 = f32[128,4,384]{2,1,0:T(4,128)} reshape(f32[512,384]{1,0:T(8,128)} %copy.19) | data formatting | bytes 1572864 | tf_op jit(solution)/shard_map/reshape | solution.py:404
  9.3 2.5 %segment_sums.3 = f32[1536,256]{1,0:T(8,128)} custom-call(s32[1,1024]{1,0:T(1,128)S(1)} %bitcast.37, bf16[1024,256]{1,0:T(8,128)(2,1)S(1)} %copy-done.7, f32[1536,256]{1,0:T(8,128)S(1)} %collective-permute-done.refs_0_), custom_call_target="tpu_custom_call" | custom-call | flops 805306368 | bytes 1572864 | tf_op jit(solution)/shard_map/segment_sums/pallas_call | solution.py:108
  11.8 11.7 %all-to-all-start = ((f32[64,24,256]{2,1,0:T(8,128)}), f32[64,24,256]{2,1,0:T(8,128)}, u32[]{:S(2)}, u32[]{:S(2)}) async-start(f32[64,24,256]{2,1,0:T(8,128)} %bitcast.4), calls=%async_computation | async-start | bytes 3145728 | tf_op jit(solution)/shard_map/all_to_all | solution.py:389
  23.6 2.3 %copy-done.14 = bf16[768,3072]{1,0:T(8,128)(2,1)S(1)} copy-done((bf16[768,3072]{1,0:T(8,128)(2,1)S(1)}, bf16[768,3072]{1,0:T(8,128)(2,1)}, u32[]{:S(2)}) %copy-start.14) | copy-done | bytes 4718616
  25.9 1.7 copy-done.16
  27.5 18.9 %forward.1 = (bf16[1536,768]{1,0:T(8,128)(2,1)S(1)}, bf16[1536,3072]{1,0:T(8,128)(2,1)}, f32[24,3072]{1,0:T(8,128)S(1)}, f32[24,768]{1,0:T(8,128)S(1)}) custom-call(bf16[1536,768]{1,0:T(8,128)(2,1)S(1)} %bitcast.41, f32[1,768]{1,0:T(1,128)S(1)} %reshape.244.gain_ref, bf16[768,3072]{1,0:T(8,128)(2,1)S(1)} %copy-done.14), custom_call_target="tpu_custom_call" | custom-call | flops 28991029248 | bytes 18874368 | tf_op jit(solution)/shard_map/forward/pallas_call | solution.py:156
  46.4 1.4 copy-done.20
  47.8 3.8 %fusion.3.pool_ref = bf16[24,1024]{1,0:T(8,128)(2,1)S(1)} fusion(s32[1024]{0:T(1024)S(1)} %fusion.32, f32[24,768]{1,0:T(8,128)S(1)} %get-tuple-element.39, bf16[24,3072]{1,0:T(8,128)(2,1)S(1)} %convert_element_type.35.mean_ref, bf16[3072,768]{1,0:T(8,128)(2,1)} %param.14), kind=kOutput, calls=%fused_computation.9 | convolution fusion | flops 151842816 | bytes 4993024 | tf_op jit(solution)/shard_map/dot_general | solution.py:412
  51.7 1.5 reduce_sum.29.grad_ref
  53.4 3.8 %convolution_multiply_fusion.act_ref = f32[24,3072]{1,0:T(8,128)S(1)} fusion(bf16[3072,768]{1,0:T(8,128)(2,1)} %param.14, f32[24,768]{1,0:T(8,128)S(1)} %fusion.45.pool_ref), kind=kOutput, calls=%fused_computation | convolution fusion | flops 113338368 | bytes 5087232 | tf_op jit(solution)/shard_map/dot_general | solution.py:29
  57.3 10.8 %first_products.1 = (bf16[1536,3072]{1,0:T(8,128)(2,1)S(1)}, f32[64,40,384]{2,1,0:T(8,128)S(1)}, f32[64,40,384]{2,1,0:T(8,128)}) custom-call(s32[1]{0:T(128)} %bitcast.core_ref, s32[3,4]{1,0:T(4,128)S(1)} %pad_add_fusion.keep_at, s32[3,4]{1,0:T(4,128)S(1)} %pad_add_fusion.1.send_at, bf16[1536,3072]{1,0:T(8,128)(2,1)} %get-tuple-element.37.slope_ref, ...), custom_call_target="tpu_custom_call" | custom-call | flops 3623878656 | bytes 18874368 | tf_op jit(solution)/shard_map/first_products/pallas_call | solution.py:258
  68.1 1.9 copy-done.1
  70.0 3.7 %copy-done.18 = bf16[1536,3072]{1,0:T(8,128)(2,1)} copy-done((bf16[1536,3072]{1,0:T(8,128)(2,1)}, bf16[1536,3072]{1,0:T(8,128)(2,1)S(1)}, u32[]{:S(2)}) %copy-start.18) | copy-done | bytes 9437208
  73.8 10.3 %all-to-all-start.1 = ((f32[128,4,384]{2,1,0:T(4,128)}), f32[128,4,384]{2,1,0:T(4,128)}, u32[]{:S(2)}, u32[]{:S(2)}) async-start(f32[128,4,384]{2,1,0:T(4,128)} %reshape.245), calls=%async_computation.1 | async-start | bytes 1572864 | tf_op jit(solution)/shard_map/all_to_all | solution.py:432
  86.4 3.7 %copy-done.19 = bf16[1536,3072]{1,0:T(8,128)(2,1)S(1)} copy-done((bf16[1536,3072]{1,0:T(8,128)(2,1)S(1)}, bf16[1536,3072]{1,0:T(8,128)(2,1)}, u32[]{:S(2)}) %copy-start.19) | copy-done | bytes 9437208
  90.1 1.7 copy-done.22
  91.7 7.6 %other_products.1 = (f32[64,32,384]{2,1,0:T(8,128)S(1)}, f32[64,32,384]{2,1,0:T(8,128)S(1)}) custom-call(s32[1]{0:T(128)} %bitcast.core_ref, s32[3,4]{1,0:T(4,128)S(1)} %copy-done.13, s32[3,4]{1,0:T(4,128)S(1)} %copy-done.11, bf16[1536,3072]{1,0:T(8,128)(2,1)S(1)} %copy-done.19, bf16[24,3072]{1,0:T(8,128)(2,1)S(1)} %copy-done.5, ...), custom_call_target="tpu_custom_call" | custom-call | flops 3623878656 | bytes 18874368 | tf_op jit(solution)/shard_map/other_products/pallas_call | solution.py:258
  99.3 1.7 copy-done.15
  101.0 3.8 %add.141 = f32[64,40,384]{2,1,0:T(8,128)S(1)} add(f32[64,40,384]{2,1,0:T(8,128)} %copy-done.1, f32[64,40,384]{2,1,0:T(8,128)} %collective-permute-done.1) | non-fusion elementwise | flops 983040 | bytes 11796480 | tf_op jit(solution)/shard_map/add | solution.py:435
  104.9 2.0 %copy-done.23 = f32[64,40,384]{2,1,0:T(8,128)} copy-done((f32[64,40,384]{2,1,0:T(8,128)}, f32[64,40,384]{2,1,0:T(8,128)S(1)}, u32[]{:S(2)}) %copy-start.23) | copy-done | bytes 3932184
  106.9 1.4 slice.128
  110.0 1.3 slice.129
  111.2 1.5 collective-permute-start.4
  114.1 11.5 %title_grads.1 = (bf16[1536,768]{1,0:T(8,128)(2,1)}, f32[8,768]{1,0:T(8,128)S(1)}) custom-call(bf16[1536,3072]{1,0:T(8,128)(2,1)S(1)} %bitcast.44, bf16[768,3072]{1,0:T(8,128)(2,1)S(1)} %bitcast.40, bf16[1536,768]{1,0:T(8,128)(2,1)S(1)} %bitcast.42, f32[1,768]{1,0:T(1,128)S(1)} %reshape.244.gain_ref, f32[24,768]{1,0:T(8,128)S(1)} %copy-done.9), custom_call_target="tpu_custom_call" | custom-call | flops 7247757312 | bytes 9437184 | tf_op jit(solution)/shard_map/title_grads/pallas_call | solution.py:304
  125.6 1.4 reshape.248.arrived_ref
  127.0 1.6 copy-done.3
  128.6 3.7 %row_update.1 = (f32[2048,256]{1,0:T(8,128)}, f32[2048,256]{1,0:T(8,128)}) custom-call(f32[512,384]{1,0:T(8,128)S(1)} %reshape.248.arrived_ref, f32[2048,256]{1,0:T(8,128)S(1)} %copy-done.2, f32[2048,256]{1,0:T(8,128)S(1)} %copy-done.3), custom_call_target="tpu_custom_call" | custom-call | flops 1073741824 | bytes 8388608 | tf_op jit(solution)/shard_map/row_update/pallas_call | solution.py:347
  133.2 2.0 %slice_add_fusion = f32[4,4,2,40,384]{4,3,2,1,0:T(8,128)S(1)} fusion(f32[4,4,2,40,384]{4,3,2,1,0:T(8,128)} %collective-permute-done.2, f32[4,4,4,40,384]{4,3,2,1,0:T(8,128)S(1)} %bitcast.46), kind=kLoop, calls=%fused_computation.5 | loop fusion | flops 491520 | bytes 5898240 | tf_op jit(solution)/shard_map/add | solution.py:84
  135.3 2.3 %collective-permute-start.5 = (f32[4,4,1,40,384]{4,3,2,1,0:T(8,128)S(1)}, f32[4,4,1,40,384]{4,3,2,1,0:T(8,128)S(1)}, u32[]{:S(2)}, u32[]{:S(2)}) collective-permute-start(f32[4,4,1,40,384]{4,3,2,1,0:T(8,128)S(1)} %slice.132), channel_id=1, source_target_pairs={{0,3},{1,2},{2,1},{3,0},{4,5},{5,4},{6,7},{7,6},{8,11},{9,10},{10,... | collective-permute-start | bytes 2949128 | tf_op jit(solution)/shard_map/ppermute | solution.py:78
  137.6 1.7 slice_add_fusion.1
  139.3 2.9 %collective-permute-start.6 = (f32[4,1,4,32,384]{4,3,2,1,0:T(8,128)S(1)}, f32[4,1,4,32,384]{4,3,2,1,0:T(8,128)S(1)}, u32[]{:S(2)}, u32[]{:S(2)}) collective-permute-start(f32[4,1,4,32,384]{4,3,2,1,0:T(8,128)S(1)} %slice.134), channel_id=1, source_target_pairs={{0,24},{1,25},{2,26},{3,27},{4,12},{5,13},{6,14},{7,15},{8,16},{9,... | collective-permute-start | bytes 2359304 | tf_op jit(solution)/shard_map/ppermute | solution.py:78
  142.2 1.2 collective-permute-done.7
  143.4 9.2 %collective-permute-done.6 = f32[4,1,4,32,384]{4,3,2,1,0:T(8,128)S(1)} collective-permute-done((f32[4,1,4,32,384]{4,3,2,1,0:T(8,128)S(1)}, f32[4,1,4,32,384]{4,3,2,1,0:T(8,128)S(1)}, u32[]{:S(2)}, u32[]{:S(2)}) %collective-permute-start.6) | collective-permute-done | bytes 786464 | tf_op jit(solution)/shard_map/ppermute | solution.py:78
  153.5 7.6 %collective-permute-done.10 = f32[4,1,2,32,384]{4,3,2,1,0:T(8,128)S(1)} collective-permute-done((f32[4,1,2,32,384]{4,3,2,1,0:T(8,128)S(1)}, f32[4,1,2,32,384]{4,3,2,1,0:T(8,128)S(1)}, u32[]{:S(2)}, u32[]{:S(2)}) %collective-permute-start.10) | collective-permute-done | bytes 393248 | tf_op jit(solution)/shard_map/ppermute | solution.py:78
  162.2 2.8 %collective-permute-start.9 = (f32[4,1,1,40,384]{4,3,2,1,0:T(8,128)S(1)}, f32[4,1,1,40,384]{4,3,2,1,0:T(8,128)S(1)}, u32[]{:S(2)}, u32[]{:S(2)}) collective-permute-start(f32[4,1,1,40,384]{4,3,2,1,0:T(8,128)S(1)} %slice.138), channel_id=1, source_target_pairs={{0,24},{1,25},{2,26},{3,27},{4,12},{5,13},{6,14},{7,15},{8,16},{9,... | collective-permute-start | bytes 737288 | tf_op jit(solution)/shard_map/ppermute | solution.py:78
  165.1 3.1 %collective-permute-done.11 = f32[4,1,1,32,384]{4,3,2,1,0:T(8,128)S(1)} collective-permute-done((f32[4,1,1,32,384]{4,3,2,1,0:T(8,128)S(1)}, f32[4,1,1,32,384]{4,3,2,1,0:T(8,128)S(1)}, u32[]{:S(2)}, u32[]{:S(2)}) %collective-permute-start.11) | collective-permute-done | bytes 196640 | tf_op jit(solution)/shard_map/ppermute | solution.py:78
  168.2 1.5 collective-permute-done.9
  169.8 1.7 collective-permute-start.12
  171.5 5.2 %collective-permute-done.12 = f32[2,1,1,72,384]{4,3,2,1,0:T(8,128)S(1)} collective-permute-done((f32[2,1,1,72,384]{4,3,2,1,0:T(8,128)S(1)}, f32[2,1,1,72,384]{4,3,2,1,0:T(8,128)S(1)}, u32[]{:S(2)}, u32[]{:S(2)}) %collective-permute-start.12) | collective-permute-done | bytes 221216 | tf_op jit(solution)/shard_map/ppermute | solution.py:78
  176.7 3.8 %collective-permute-start.13 = (f32[1,1,1,72,384]{4,3,2,1,0:T(8,128)S(1)}, f32[1,1,1,72,384]{4,3,2,1,0:T(8,128)S(1)}, u32[]{:S(2)}, u32[]{:S(2)}) collective-permute-start(f32[1,1,1,72,384]{4,3,2,1,0:T(8,128)S(1)} %slice.147), channel_id=1, source_target_pairs={{0,96},{1,97},{2,98},{3,99},{4,36},{5,37},{6,38},{7,39},{8,104},{9... | collective-permute-start | bytes 331784 | tf_op jit(solution)/shard_map/ppermute | solution.py:78
  180.5 2.7 %collective-permute-done.13 = f32[1,1,1,72,384]{4,3,2,1,0:T(8,128)S(1)} collective-permute-done((f32[1,1,1,72,384]{4,3,2,1,0:T(8,128)S(1)}, f32[1,1,1,72,384]{4,3,2,1,0:T(8,128)S(1)}, u32[]{:S(2)}, u32[]{:S(2)}) %collective-permute-start.13) | collective-permute-done | bytes 110624 | tf_op jit(solution)/shard_map/ppermute | solution.py:78
  183.2 1.9 collective-permute-start.14
  185.1 2.1 %collective-permute-start.15 = (f32[72,384]{1,0:T(8,128)S(1)}, f32[72,384]{1,0:T(8,128)S(1)}, u32[]{:S(2)}, u32[]{:S(2)}) collective-permute-start(f32[72,384]{1,0:T(8,128)S(1)} %get-tuple-element.77), channel_id=1, source_target_pairs={{0,2},{1,3},{2,0},{3,1},{4,6},{5,7},{6,4},{7,5},{8,10},{9,11},{10,... | collective-permute-start | bytes 331784 | tf_op jit(solution)/shard_map/ppermute | solution.py:44
  188.0 3.3 %collective-permute-done.15 = f32[72,384]{1,0:T(8,128)S(1)} collective-permute-done((f32[72,384]{1,0:T(8,128)S(1)}, f32[72,384]{1,0:T(8,128)S(1)}, u32[]{:S(2)}, u32[]{:S(2)}) %collective-permute-start.15) | collective-permute-done | bytes 110624 | tf_op jit(solution)/shard_map/ppermute | solution.py:44
  191.3 1.8 collective-permute-done.16
  (127 shorter events, 14.8 us)
Async XLA Ops:
  0.6 52.6 %copy-start = (bf16[768,256]{1,0:T(8,128)(2,1)S(1)}, bf16[768,256]{1,0:T(8,128)(2,1)}, u32[]{:S(2)}) copy-start(bf16[768,256]{1,0:T(8,128)(2,1)} %param.15) | copy-start | bytes 1179652
  0.6 4.3 %copy-start.28 = (s32[1,512]{1,0:T(1,128)S(1)}, s32[1,512]{1,0:T(1,128)}, u32[]{:S(2)}) copy-start(s32[1,512]{1,0:T(1,128)} %param.19) | copy-start | bytes 6148
  0.7 4.3 %copy-start.29 = (s32[1024]{0:T(1024)S(1)}, s32[1024]{0:T(1024)}, u32[]{:S(2)}) copy-start(s32[1024]{0:T(1024)} %param.18) | copy-start | bytes 12292
  2.5 2.5 %copy-start.7 = (bf16[1024,256]{1,0:T(8,128)(2,1)S(1)}, bf16[1024,256]{1,0:T(8,128)(2,1)}, u32[]{:S(2)}) copy-start(bf16[1024,256]{1,0:T(8,128)(2,1)} %grad_ref.3) | copy-start | bytes 1572868
  5.0 4.3 %collective-permute-start = (f32[1536,256]{1,0:T(8,128)}, f32[1536,256]{1,0:T(8,128)S(1)}, u32[]{:S(2)}, u32[]{:S(2)}) collective-permute-start(f32[1536,256]{1,0:T(8,128)} %segment_sums.2), channel_id=1, source_target_pairs={{0,4},{4,0},{1,5},{5,1},{2,6},{6,2},{3,7},{7,3},{8,12},{12,8},{9,1... | collective-permute-start | bytes 4718600 | tf_op jit(solution)/shard_map/ppermute | solution.py:39
  6.9 4.9 %copy-start.27 = (f32[768]{0:T(1024)S(1)}, f32[768]{0:T(1024)}, u32[]{:S(2)}) copy-start(f32[768]{0:T(1024)} %param.12) | copy-start | bytes 9220
  9.2 48.1 %copy-start.10 = (s32[3,4]{1,0:T(4,128)}, s32[3,4]{1,0:T(4,128)S(1)}, u32[]{:S(2)}) copy-start(s32[3,4]{1,0:T(4,128)S(1)} %pad_add_fusion.1.send_at) | copy-start | bytes 148
  9.2 48.1 %copy-start.12 = (s32[3,4]{1,0:T(4,128)}, s32[3,4]{1,0:T(4,128)S(1)}, u32[]{:S(2)}) copy-start(s32[3,4]{1,0:T(4,128)S(1)} %pad_add_fusion.keep_at) | copy-start | bytes 148
  11.8 39.8 %all-to-all-start = ((f32[64,24,256]{2,1,0:T(8,128)}), f32[64,24,256]{2,1,0:T(8,128)}, u32[]{:S(2)}, u32[]{:S(2)}) async-start(f32[64,24,256]{2,1,0:T(8,128)} %bitcast.4), calls=%async_computation | async-start | bytes 3145728 | tf_op jit(solution)/shard_map/all_to_all | solution.py:389
  23.5 2.3 %copy-start.14 = (bf16[768,3072]{1,0:T(8,128)(2,1)S(1)}, bf16[768,3072]{1,0:T(8,128)(2,1)}, u32[]{:S(2)}) copy-start(bf16[768,3072]{1,0:T(8,128)(2,1)} %w_ref.3) | copy-start | bytes 14155780
  25.9 1.7 copy-start.16
  47.8 9.5 %copy-start.4 = (bf16[24,3072]{1,0:T(8,128)(2,1)}, bf16[24,3072]{1,0:T(8,128)(2,1)S(1)}, u32[]{:S(2)}) copy-start(bf16[24,3072]{1,0:T(8,128)(2,1)S(1)} %convert_element_type.35.mean_ref) | copy-start | bytes 442372
  53.4 3.8 %copy-start.8 = (f32[24,768]{1,0:T(8,128)}, f32[24,768]{1,0:T(8,128)S(1)}, u32[]{:S(2)}) copy-start(f32[24,768]{1,0:T(8,128)S(1)} %fusion.45.pool_ref) | copy-start | bytes 221188
  53.4 3.9 %copy-start.21 = (bf16[1536,768]{1,0:T(8,128)(2,1)S(1)}, bf16[1536,768]{1,0:T(8,128)(2,1)}, u32[]{:S(2)}) copy-start(bf16[1536,768]{1,0:T(8,128)(2,1)} %copy-done.20) | copy-start | bytes 7077892
  68.1 1.9 copy-start.1
  70.0 3.7 %copy-start.18 = (bf16[1536,3072]{1,0:T(8,128)(2,1)}, bf16[1536,3072]{1,0:T(8,128)(2,1)S(1)}, u32[]{:S(2)}) copy-start(bf16[1536,3072]{1,0:T(8,128)(2,1)S(1)} %get-tuple-element.46.pre_ref) | copy-start | bytes 28311556
  73.7 27.3 %collective-permute-start.1 = (f32[64,40,384]{2,1,0:T(8,128)}, f32[64,40,384]{2,1,0:T(8,128)}, u32[]{:S(2)}, u32[]{:S(2)}) collective-permute-start(f32[64,40,384]{2,1,0:T(8,128)} %get-tuple-element.45), channel_id=1, source_target_pairs={{0,4},{4,0},{1,5},{5,1},{2,6},{6,2},{3,7},{7,3},{8,12},{12,8},{9,1... | collective-permute-start | bytes 11796488 | tf_op jit(solution)/shard_map/ppermute | solution.py:39
  73.8 27.2 %all-to-all-start.1 = ((f32[128,4,384]{2,1,0:T(4,128)}), f32[128,4,384]{2,1,0:T(4,128)}, u32[]{:S(2)}, u32[]{:S(2)}) async-start(f32[128,4,384]{2,1,0:T(4,128)} %reshape.245), calls=%async_computation.1 | async-start | bytes 1572864 | tf_op jit(solution)/shard_map/all_to_all | solution.py:432
  86.4 3.7 %copy-start.19 = (bf16[1536,3072]{1,0:T(8,128)(2,1)S(1)}, bf16[1536,3072]{1,0:T(8,128)(2,1)}, u32[]{:S(2)}) copy-start(bf16[1536,3072]{1,0:T(8,128)(2,1)} %copy-done.18) | copy-start | bytes 28311556
  90.1 1.7 copy-start.22
  99.3 1.7 copy-start.15
  101.0 8.3 %collective-permute-start.3 = (f32[64,32,384]{2,1,0:T(8,128)}, f32[64,32,384]{2,1,0:T(8,128)S(1)}, u32[]{:S(2)}, u32[]{:S(2)}) collective-permute-start(f32[64,32,384]{2,1,0:T(8,128)} %copy-done.15), channel_id=1, source_target_pairs={{0,4},{4,0},{1,5},{5,1},{2,6},{6,2},{3,7},{7,3},{8,12},{12,8},{9,1... | collective-permute-start | bytes 9437192 | tf_op jit(solution)/shard_map/ppermute | solution.py:39
  101.0 11.7 %slice-start.2 = ((s8[9437184]{0:T(1024)(128)(4,1)}), s8[4194304]{0:T(1024)(128)(4,1)S(1)}, s32[]{:S(2)}) async-start(s8[9437184]{0:T(1024)(128)(4,1)} %bitcast.43), calls=%async_computation.4 | async-start | bytes 8388608
  101.0 11.7 %slice-start.3 = ((s8[9437184]{0:T(1024)(128)(4,1)}), s8[1048576]{0:T(1024)(128)(4,1)S(1)}, s32[]{:S(2)}) async-start(s8[9437184]{0:T(1024)(128)(4,1)} %bitcast.43), calls=%async_computation.5 | async-start | bytes 2097152
  104.9 2.0 %copy-start.23 = (f32[64,40,384]{2,1,0:T(8,128)}, f32[64,40,384]{2,1,0:T(8,128)S(1)}, u32[]{:S(2)}) copy-start(f32[64,40,384]{2,1,0:T(8,128)S(1)} %add.141) | copy-start | bytes 11796484
  106.9 5.8 %slice-start = ((s8[4718592]{0:T(1024)(128)(4,1)}), s8[4194304]{0:T(1024)(128)(4,1)S(1)}, s32[]{:S(2)}) async-start(s8[4718592]{0:T(1024)(128)(4,1)} %bitcast.39), calls=%async_computation.2 | async-start | bytes 8388608
  108.3 24.9 %collective-permute-start.2 = (f32[4,4,2,40,384]{4,3,2,1,0:T(8,128)}, f32[4,4,2,40,384]{4,3,2,1,0:T(8,128)}, u32[]{:S(2)}, u32[]{:S(2)}) collective-permute-start(f32[4,4,2,40,384]{4,3,2,1,0:T(8,128)} %slice.128), channel_id=1, source_target_pairs={{0,1},{1,0},{2,3},{3,2},{4,7},{5,6},{6,5},{7,4},{8,9},{9,8},{10,11... | collective-permute-start | bytes 5898248 | tf_op jit(solution)/shard_map/ppermute | solution.py:78
  109.3 3.4 %slice-start.1 = ((s8[4718592]{0:T(1024)(128)(4,1)}), s8[524288]{0:T(1024)(128)(4,1)S(1)}, s32[]{:S(2)}) async-start(s8[4718592]{0:T(1024)(128)(4,1)} %bitcast.39), calls=%async_computation.3 | async-start | bytes 1048576
  109.3 4.2 %slice-start.4 = ((s8[9437184]{0:T(1024)(128)(4,1)}), s8[4194304]{0:T(1024)(128)(4,1)S(1)}, s32[]{:S(2)}) async-start(s8[9437184]{0:T(1024)(128)(4,1)} %bitcast.43), calls=%async_computation.6 | async-start | bytes 8388608
  109.9 2.8 %copy-start.25 = (f32[64,32,384]{2,1,0:T(8,128)}, f32[64,32,384]{2,1,0:T(8,128)S(1)}, u32[]{:S(2)}) copy-start(f32[64,32,384]{2,1,0:T(8,128)S(1)} %add.142) | copy-start | bytes 9437188
  109.9 3.5 %copy-start.9 = (f32[24,768]{1,0:T(8,128)S(1)}, f32[24,768]{1,0:T(8,128)}, u32[]{:S(2)}) copy-start(f32[24,768]{1,0:T(8,128)} %copy-done.8) | copy-start | bytes 221188
  109.9 4.1 %copy-start.17 = (bf16[24,64,768]{2,1,0:T(8,128)(2,1)S(1)}, bf16[24,64,768]{2,1,0:T(8,128)(2,1)}, u32[]{:S(2)}) copy-start(bf16[24,64,768]{2,1,0:T(8,128)(2,1)} %param.11) | copy-start | bytes 7077892
  111.2 21.1 %collective-permute-start.4 = (f32[4,2,4,32,384]{4,3,2,1,0:T(8,128)}, f32[4,2,4,32,384]{4,3,2,1,0:T(8,128)}, u32[]{:S(2)}, u32[]{:S(2)}) collective-permute-start(f32[4,2,4,32,384]{4,3,2,1,0:T(8,128)} %slice.129), channel_id=1, source_target_pairs={{0,8},{1,9},{2,10},{3,11},{4,28},{5,29},{6,30},{7,31},{8,0},{9,1},... | collective-permute-start | bytes 4718600 | tf_op jit(solution)/shard_map/ppermute | solution.py:78
  114.1 12.9 %copy-start.2 = (f32[2048,256]{1,0:T(8,128)S(1)}, f32[2048,256]{1,0:T(8,128)}, u32[]{:S(2)}) copy-start(f32[2048,256]{1,0:T(8,128)} %table_ref.1) | copy-start | bytes 6291460
  128.6 4.6 %copy-start.24 = (f32[64,40,384]{2,1,0:T(8,128)S(1)}, f32[64,40,384]{2,1,0:T(8,128)}, u32[]{:S(2)}) copy-start(f32[64,40,384]{2,1,0:T(8,128)} %copy-done.23) | copy-start | bytes 11796484
  133.2 4.4 %copy-start.26 = (f32[64,32,384]{2,1,0:T(8,128)S(1)}, f32[64,32,384]{2,1,0:T(8,128)}, u32[]{:S(2)}) copy-start(f32[64,32,384]{2,1,0:T(8,128)} %copy-done.25) | copy-start | bytes 9437188
  135.3 17.3 %collective-permute-start.5 = (f32[4,4,1,40,384]{4,3,2,1,0:T(8,128)S(1)}, f32[4,4,1,40,384]{4,3,2,1,0:T(8,128)S(1)}, u32[]{:S(2)}, u32[]{:S(2)}) collective-permute-start(f32[4,4,1,40,384]{4,3,2,1,0:T(8,128)S(1)} %slice.132), channel_id=1, source_target_pairs={{0,3},{1,2},{2,1},{3,0},{4,5},{5,4},{6,7},{7,6},{8,11},{9,10},{10,... | collective-permute-start | bytes 2949128 | tf_op jit(solution)/shard_map/ppermute | solution.py:78
  139.3 13.3 %collective-permute-start.6 = (f32[4,1,4,32,384]{4,3,2,1,0:T(8,128)S(1)}, f32[4,1,4,32,384]{4,3,2,1,0:T(8,128)S(1)}, u32[]{:S(2)}, u32[]{:S(2)}) collective-permute-start(f32[4,1,4,32,384]{4,3,2,1,0:T(8,128)S(1)} %slice.134), channel_id=1, source_target_pairs={{0,24},{1,25},{2,26},{3,27},{4,12},{5,13},{6,14},{7,15},{8,16},{9,... | collective-permute-start | bytes 2359304 | tf_op jit(solution)/shard_map/ppermute | solution.py:78
  142.2 1.2 collective-permute-start.7
  152.7 8.4 %collective-permute-start.10 = (f32[4,1,2,32,384]{4,3,2,1,0:T(8,128)S(1)}, f32[4,1,2,32,384]{4,3,2,1,0:T(8,128)S(1)}, u32[]{:S(2)}, u32[]{:S(2)}) collective-permute-start(f32[4,1,2,32,384]{4,3,2,1,0:T(8,128)S(1)} %slice.141), channel_id=1, source_target_pairs={{0,1},{1,0},{2,3},{3,2},{4,7},{5,6},{6,5},{7,4},{8,9},{9,8},{10,11... | collective-permute-start | bytes 1179656 | tf_op jit(solution)/shard_map/ppermute | solution.py:78
  153.2 8.9 %collective-permute-start.8 = (f32[4,2,1,40,384]{4,3,2,1,0:T(8,128)S(1)}, f32[4,2,1,40,384]{4,3,2,1,0:T(8,128)S(1)}, u32[]{:S(2)}, u32[]{:S(2)}) collective-permute-start(f32[4,2,1,40,384]{4,3,2,1,0:T(8,128)S(1)} %slice.136), channel_id=1, source_target_pairs={{0,8},{1,9},{2,10},{3,11},{4,28},{5,29},{6,30},{7,31},{8,0},{9,1},... | collective-permute-start | bytes 1474568 | tf_op jit(solution)/shard_map/ppermute | solution.py:78
  161.2 7.0 %collective-permute-start.11 = (f32[4,1,1,32,384]{4,3,2,1,0:T(8,128)S(1)}, f32[4,1,1,32,384]{4,3,2,1,0:T(8,128)S(1)}, u32[]{:S(2)}, u32[]{:S(2)}) collective-permute-start(f32[4,1,1,32,384]{4,3,2,1,0:T(8,128)S(1)} %slice.143), channel_id=1, source_target_pairs={{0,3},{1,2},{2,1},{3,0},{4,5},{5,4},{6,7},{7,6},{8,11},{9,10},{10,... | collective-permute-start | bytes 589832 | tf_op jit(solution)/shard_map/ppermute | solution.py:78
  162.2 7.5 %collective-permute-start.9 = (f32[4,1,1,40,384]{4,3,2,1,0:T(8,128)S(1)}, f32[4,1,1,40,384]{4,3,2,1,0:T(8,128)S(1)}, u32[]{:S(2)}, u32[]{:S(2)}) collective-permute-start(f32[4,1,1,40,384]{4,3,2,1,0:T(8,128)S(1)} %slice.138), channel_id=1, source_target_pairs={{0,24},{1,25},{2,26},{3,27},{4,12},{5,13},{6,14},{7,15},{8,16},{9,... | collective-permute-start | bytes 737288 | tf_op jit(solution)/shard_map/ppermute | solution.py:78
  169.8 6.9 %collective-permute-start.12 = (f32[2,1,1,72,384]{4,3,2,1,0:T(8,128)S(1)}, f32[2,1,1,72,384]{4,3,2,1,0:T(8,128)S(1)}, u32[]{:S(2)}, u32[]{:S(2)}) collective-permute-start(f32[2,1,1,72,384]{4,3,2,1,0:T(8,128)S(1)} %pad_maximum_fusion.4), channel_id=1, source_target_pairs={{0,32},{1,33},{2,34},{3,35},{4,100},{5,101},{6,102},{7,103},{8,40}... | collective-permute-start | bytes 663560 | tf_op jit(solution)/shard_map/ppermute | solution.py:78
  176.7 6.5 %collective-permute-start.13 = (f32[1,1,1,72,384]{4,3,2,1,0:T(8,128)S(1)}, f32[1,1,1,72,384]{4,3,2,1,0:T(8,128)S(1)}, u32[]{:S(2)}, u32[]{:S(2)}) collective-permute-start(f32[1,1,1,72,384]{4,3,2,1,0:T(8,128)S(1)} %slice.147), channel_id=1, source_target_pairs={{0,96},{1,97},{2,98},{3,99},{4,36},{5,37},{6,38},{7,39},{8,104},{9... | collective-permute-start | bytes 331784 | tf_op jit(solution)/shard_map/ppermute | solution.py:78
  183.2 4.8 %collective-permute-start.14 = (f32[72,384]{1,0:T(8,128)S(1)}, f32[72,384]{1,0:T(8,128)S(1)}, u32[]{:S(2)}, u32[]{:S(2)}) collective-permute-start(f32[72,384]{1,0:T(8,128)S(1)} %get-tuple-element.77), channel_id=1, source_target_pairs={{0,1},{1,0},{2,3},{3,2},{4,5},{5,4},{6,7},{7,6},{8,9},{9,8},{10,11... | collective-permute-start | bytes 331784 | tf_op jit(solution)/shard_map/ppermute | solution.py:44
  185.1 6.3 %collective-permute-start.15 = (f32[72,384]{1,0:T(8,128)S(1)}, f32[72,384]{1,0:T(8,128)S(1)}, u32[]{:S(2)}, u32[]{:S(2)}) collective-permute-start(f32[72,384]{1,0:T(8,128)S(1)} %get-tuple-element.77), channel_id=1, source_target_pairs={{0,2},{1,3},{2,0},{3,1},{4,6},{5,7},{6,4},{7,5},{8,10},{9,11},{10,... | collective-permute-start | bytes 331784 | tf_op jit(solution)/shard_map/ppermute | solution.py:44
  187.2 6.0 %collective-permute-start.16 = (f32[72,384]{1,0:T(8,128)S(1)}, f32[72,384]{1,0:T(8,128)S(1)}, u32[]{:S(2)}, u32[]{:S(2)}) collective-permute-start(f32[72,384]{1,0:T(8,128)S(1)} %get-tuple-element.77), channel_id=1, source_target_pairs={{0,3},{1,2},{2,1},{3,0},{4,7},{5,6},{6,5},{7,4},{8,11},{9,10},{10,... | collective-permute-start | bytes 331784 | tf_op jit(solution)/shard_map/ppermute | solution.py:44
  (6 other events, 6.3 us)

commit v7 on v4

--- a/solution.py
+++ b/solution.py
@@ -70,18 +70,15 @@
 
 def halve(parts, names, second, also=()):
     kept, sent = [], []
-    for part, name in zip(parts, names):
+    for terms, name in zip(parts, names):
         dim = ("z", "y", "x").index(name)
-        middle = part.shape[dim] // 2
-        kept.append(lax.slice_in_dim(part, 0, middle, axis=dim))
-        sent.append(
-            lax.ppermute(
-                lax.slice_in_dim(part, middle, None, axis=dim), DEVICES, partners(name, second)
-            )
-        )
+        size = terms[0].shape[dim]
+        kept.append(tuple(lax.slice_in_dim(term, 0, size // 2, axis=dim) for term in terms))
+        later = [lax.slice_in_dim(term, size // 2, size, axis=dim) for term in terms]
+        sent.append(lax.ppermute(sum(later[1:], later[0]), DEVICES, partners(name, second)))
     if also:
         sent, also = lax.optimization_barrier((sent, also))
-    return [k + s for k, s in zip(kept, sent)], also
+    return [terms + (got,) for terms, got in zip(kept, sent)], also
 
 
 def layer_norm(rows):
@@ -176,7 +173,11 @@
         compiler_params=pltpu.CompilerParams(vmem_limit_bytes=VMEM),
         cost_estimate=cost(8 * rows * width * hidden, 4 * rows * hidden, rows * hidden),
         name="forward",
-    )(titles.reshape(rows, width), ln_gain.reshape(1, width), w_up)
+    )(
+        pltpu.with_memory_space_constraint(titles.reshape(rows, width), pltpu.HBM),
+        ln_gain.reshape(1, width),
+        pltpu.with_memory_space_constraint(w_up, pltpu.HBM),
+    )
 
 
 def place_sums(core_ref, keep_at, send_at, ups, down, proj, out_refs):
@@ -433,27 +434,30 @@
     d_pre = pltpu.with_memory_space_constraint(d_pre, pltpu.VMEM)
     for index in (1, 2):
         sums += up_products(tables, (index,), (d_pre,), *items)
+    shape = (n_z, n_y, n_x, -1, width_e)
     parts = [
-        (keep + swap_cores(send)).reshape(n_z, n_y, n_x, -1, width_e)
+        (keep.reshape(shape), swap_cores(send).reshape(shape))
         for keep, send in zip(sums[::2], sums[1::2])
     ]
 
     beside = title_grads(d_pre, w_up, titles, ln_gain, d_pooled)
     parts, (d_titles, gain_term) = halve(parts, "xyz", False, tuple(beside))
-    parts, row_part = lax.optimization_barrier((parts, row_part))
+    (got, row_part) = lax.optimization_barrier((parts[0][-1], row_part))
+    parts[0] = parts[0][:-1] + (got,)
     row_all = lax.all_to_all(row_part, DEVICES, 0, 0, tiled=True)
     gain_term = (gain_term + swap_cores(gain_term)).reshape(8, 3, width_e)
     gain_term = jnp.pad(jnp.sum(gain_term, axis=0), ((0, 5), (0, 0)))
     parts, (gain_term,) = halve(parts, "xyz", True, (gain_term,))
-    gain_term = jnp.broadcast_to(gain_term, parts[0].shape[:3] + gain_term.shape)
-    parts[0] = jnp.concatenate([parts[0], gain_term], axis=3)
+    total = sum(parts[0][1:], parts[0][0])
+    gain_term = jnp.broadcast_to(gain_term, total.shape[:3] + gain_term.shape)
+    parts[0] = (jnp.concatenate([total, gain_term], axis=3),)
     parts, _ = halve(parts, "yzx", False)
     parts, (row_all,) = halve(parts, "yzx", True, (row_all,))
     beside = row_update(row_all.reshape(slot_count, width_e + 128), table, accum)
     parts, (new_table, new_accum) = halve(parts, "zxy", False, tuple(beside))
     parts, _ = halve(parts, "zxy", True)
 
-    flat = [part.reshape(-1, width_e) for part in parts]
+    flat = [sum(terms[1:], terms[0]).reshape(-1, width_e) for terms in parts]
     last = jnp.concatenate(flat, axis=0)
     blocks = jnp.stack([last, along(last, "x", 1), along(last, "x", 2), along(last, "x", 3)])
     ordered = jnp.stack(

time: 171 us -> 179 us (1.047)
  other arithmetic: 11.8 us -> 29.1 us
  local copies, waits for them, and re-layouts: 17 us -> 9.62 us
  starting transfers between devices: 51.7 us -> 46.7 us
  Pallas kernels: 57.1 us -> 58.9 us
    add x18 -> x19, other arithmetic: 8.4 us -> 23.2 us  [the longest x18 21.5 us: halve(): sum(later[1:], later[0])]
    ppermute x18, starting transfers between devices: 28.3 us -> 24.2 us  [halve(): lax.ppermute(sum(later[1:], later[0]), DEVICES, partners(name, second))]
    unnamed x34 -> x52, local copies, waits for them, and re-layouts: 7.34 us -> 3.47 us
    slice x17 -> x0, local copies, waits for them, and re-layouts: 3.56 us -> none  [the longest x16 3.42 us: halve(): lax.slice_in_dim(part, middle, None, axis=dim)]
    reshape x3, other arithmetic: 0.02 us -> 2.58 us  [per_device(): flat = [sum(terms[1:], terms[0]).reshape(-1, width_e) for terms in parts]]
  transfers between devices with their start and end apart: 28 -> 28, of which waited for: 10 -> 10; matrix products, arithmetic and copies ran while one was open for 11% -> 17% of each run, Pallas kernels for 26% -> 26%
where the time goes in v7:
time: 179 us; the launch traced here: 178 us
  Pallas kernels  58.9 us (33%)
  starting transfers between devices  46.7 us (26%)
  other arithmetic  29.1 us (16%)
  waiting for transfers between devices  22.8 us (13%)
  local copies, waits for them, and re-layouts  9.62 us (5%)
  matrix products  9.58 us (5%)
    ppermute x18, starting transfers between devices, halve(): lax.ppermute(sum(later[1:], later[0]), DEVICES, partners(name, second))  24.2 us
    add x18, other arithmetic, halve(): sum(later[1:], later[0])  21.5 us
    pallas_call x1, Pallas kernels, forward(): pl.pallas_call(functools.partial(forward_kernel, units), grid=(hidden //...  20.6 us
    pallas_call x3, Pallas kernels, up_products(): pl.pallas_call(kernel, grid_spec=pltpu.PrefetchScalarGridSpec(num_scalar_...  18 us
    ppermute x18, waiting for transfers between devices, halve(): lax.ppermute(sum(later[1:], later[0]), DEVICES, partners(name, second))  17.8 us
    all_to_all x1, starting transfers between devices, per_device(): item_all = lax.all_to_all(mine, CHIPS, 0, 0, tiled=True)  11.7 us
    pallas_call x1, Pallas kernels, title_grads(): pl.pallas_call(titles_kernel, grid=(rows // step,), in_specs=[pl.BlockSpe...  11.7 us
    all_to_all x1, starting transfers between devices, per_device(): row_all = lax.all_to_all(row_part, DEVICES, 0, 0, tiled=True)  5.68 us
  transfers between devices with their start and end apart: 28, of which 10 were waited for; matrix products, arithmetic and copies ran while one was open for 17% of the time, Pallas kernels for 26%

profile of v7, /device:TPU:0, one launch (start us, length us, event | category | flops | bytes accessed | tf_op | source)
XLA Modules:
  0.0 177.7 jit_solution(10146414565501370344)
XLA Ops:
  2.5 2.5 %segment_sums.2 = f32[1536,256]{1,0:T(8,128)} custom-call(s32[1,1024]{1,0:T(1,128)S(1)} %bitcast.56, bf16[1024,256]{1,0:T(8,128)(2,1)S(1)} %copy-done.5), custom_call_target="tpu_custom_call" | custom-call | flops 805306368 | bytes 1572864 | tf_op jit(solution)/shard_map/segment_sums/pallas_call | solution.py:105
  5.8 1.1 copy.19
  6.9 2.3 %reshape.286 = f32[128,4,384]{2,1,0:T(4,128)} reshape(f32[512,384]{1,0:T(8,128)} %copy.19) | data formatting | bytes 1572864 | tf_op jit(solution)/shard_map/reshape | solution.py:409
  9.3 2.5 %segment_sums.3 = f32[1536,256]{1,0:T(8,128)} custom-call(s32[1,1024]{1,0:T(1,128)S(1)} %bitcast.55, bf16[1024,256]{1,0:T(8,128)(2,1)S(1)} %copy-done.6, f32[1536,256]{1,0:T(8,128)S(1)} %collective-permute-done.refs_0_), custom_call_target="tpu_custom_call" | custom-call | flops 805306368 | bytes 1572864 | tf_op jit(solution)/shard_map/segment_sums/pallas_call | solution.py:105
  11.8 11.7 %all-to-all-start = ((f32[64,24,256]{2,1,0:T(8,128)}), f32[64,24,256]{2,1,0:T(8,128)}, u32[]{:S(2)}, u32[]{:S(2)}) async-start(f32[64,24,256]{2,1,0:T(8,128)} %bitcast.4), calls=%async_computation | async-start | bytes 3145728 | tf_op jit(solution)/shard_map/all_to_all | solution.py:394
  23.5 20.6 %forward.1 = (bf16[1536,768]{1,0:T(8,128)(2,1)S(1)}, bf16[1536,3072]{1,0:T(8,128)(2,1)}, f32[24,3072]{1,0:T(8,128)S(1)}, f32[24,768]{1,0:T(8,128)S(1)}) custom-call(bf16[1536,768]{1,0:T(8,128)(2,1)} %bitcast.59, f32[1,768]{1,0:T(1,128)S(1)} %reshape.285.gain_ref, bf16[768,3072]{1,0:T(8,128)(2,1)} %w_ref.3), custom_call_target="tpu_custom_call" | custom-call | flops 28991029248 | bytes 18874368 | tf_op jit(solution)/shard_map/forward/pallas_call | solution.py:153
  44.1 3.8 %fusion.3.pool_ref = bf16[24,1024]{1,0:T(8,128)(2,1)S(1)} fusion(s32[1024]{0:T(1024)S(1)} %fusion.76, f32[24,768]{1,0:T(8,128)S(1)} %get-tuple-element.50, bf16[24,3072]{1,0:T(8,128)(2,1)S(1)} %convert_element_type.35.mean_ref, bf16[3072,768]{1,0:T(8,128)(2,1)} %param.14), kind=kOutput, calls=%fused_computation.11 | convolution fusion | flops 151842816 | bytes 4993024 | tf_op jit(solution)/shard_map/dot_general | solution.py:417
  48.5 1.5 reduce_sum.29.grad_ref
  50.3 3.7 %convolution_multiply_fusion.act_ref = f32[24,3072]{1,0:T(8,128)S(1)} fusion(bf16[3072,768]{1,0:T(8,128)(2,1)} %param.14, f32[24,768]{1,0:T(8,128)S(1)} %fusion.90.pool_ref), kind=kOutput, calls=%fused_computation | convolution fusion | flops 113338368 | bytes 5087232 | tf_op jit(solution)/shard_map/dot_general | solution.py:29
  54.0 7.8 %first_products.1 = (bf16[1536,3072]{1,0:T(8,128)(2,1)S(1)}, f32[64,40,256]{2,1,0:T(8,128)S(1)}, f32[64,40,256]{2,1,0:T(8,128)S(1)}) custom-call(s32[1]{0:T(128)} %bitcast.core_ref, s32[3,4]{1,0:T(4,128)S(1)} %pad_add_fusion.keep_at, s32[3,4]{1,0:T(4,128)S(1)} %pad_add_fusion.1.send_at, bf16[1536,3072]{1,0:T(8,128)(2,1)} %get-tuple-element.48.slope_ref, ...), custom_call_target="tpu_custom_call" | custom-call | flops 2415919104 | bytes 18874368 | tf_op jit(solution)/shard_map/first_products/pallas_call | solution.py:264
  62.1 5.1 %other_products.2 = (f32[64,32,256]{2,1,0:T(8,128)S(1)}, f32[64,32,256]{2,1,0:T(8,128)S(1)}) custom-call(s32[1]{0:T(128)} %bitcast.core_ref, s32[3,4]{1,0:T(4,128)S(1)} %pad_add_fusion.keep_at, s32[3,4]{1,0:T(4,128)S(1)} %pad_add_fusion.1.send_at, bf16[1536,3072]{1,0:T(8,128)(2,1)S(1)} %get-tuple-element.57.pre_ref, ...), custom_call_target="tpu_custom_call" | custom-call | flops 2415919104 | bytes 18874368 | tf_op jit(solution)/shard_map/other_products/pallas_call | solution.py:264
  67.8 5.1 %other_products.3 = (f32[64,32,256]{2,1,0:T(8,128)S(1)}, f32[64,32,256]{2,1,0:T(8,128)S(1)}) custom-call(s32[1]{0:T(128)} %bitcast.core_ref, s32[3,4]{1,0:T(4,128)S(1)} %pad_add_fusion.keep_at, s32[3,4]{1,0:T(4,128)S(1)} %pad_add_fusion.1.send_at, bf16[1536,3072]{1,0:T(8,128)(2,1)S(1)} %get-tuple-element.57.pre_ref, ...), custom_call_target="tpu_custom_call" | custom-call | flops 2415919104 | bytes 18874368 | tf_op jit(solution)/shard_map/other_products/pallas_call | solution.py:264
  73.0 2.3 %slice_add_fusion.2 = f32[4,2,4,32,256]{4,3,2,1,0:T(8,128)} fusion(f32[4,4,4,32,256]{4,3,2,1,0:T(8,128)} %bitcast.9, f32[4,4,4,32,256]{4,3,2,1,0:T(8,128)S(1)} %bitcast.48), kind=kLoop, calls=%fused_computation.15 | loop fusion | flops 262144 | bytes 3145728 | tf_op jit(solution)/shard_map/add | solution.py:78
  76.5 1.5 collective-permute-start.2
  78.2 1.6 collective-permute-start.6
  79.8 11.7 %title_grads.1 = (bf16[1536,768]{1,0:T(8,128)(2,1)}, f32[8,768]{1,0:T(8,128)S(1)}) custom-call(bf16[1536,3072]{1,0:T(8,128)(2,1)S(1)} %get-tuple-element.57.pre_ref, bf16[768,3072]{1,0:T(8,128)(2,1)S(1)} %bitcast.58, bf16[1536,768]{1,0:T(8,128)(2,1)S(1)} %bitcast.60, f32[1,768]{1,0:T(1,128)S(1)} %reshape.285.gain_ref, f32[24,768]{1,0:T(8,128)S(1)} %fusion.90.pool_ref), custom_call_target="tpu_custom_call" | custom-call | flops 7247757312 | bytes 9437184 | tf_op jit(solution)/shard_map/title_grads/pallas_call | solution.py:309
  93.1 1.1 collective-permute-done.2
  94.2 1.1 fusion.6
  95.3 2.7 %collective-permute-start.7 = (f32[4,4,1,40,256]{4,3,2,1,0:T(8,128)}, f32[4,4,1,40,256]{4,3,2,1,0:T(8,128)}, u32[]{:S(2)}, u32[]{:S(2)}) collective-permute-start(f32[4,4,1,40,256]{4,3,2,1,0:T(8,128)} %fusion.6), channel_id=1, source_target_pairs={{0,3},{1,2},{2,1},{3,0},{4,5},{5,4},{6,7},{7,6},{8,11},{9,10},{10,... | collective-permute-start | bytes 1966088 | tf_op jit(solution)/shard_map/ppermute | solution.py:78
  98.0 2.1 %fusion.9 = f32[4,1,4,32,256]{4,3,2,1,0:T(8,128)} fusion(f32[4,4,4,32,256]{4,3,2,1,0:T(8,128)} %bitcast.9, f32[4,4,4,32,256]{4,3,2,1,0:T(8,128)S(1)} %bitcast.49, f32[4,2,4,32,256]{4,3,2,1,0:T(8,128)} %collective-permute-done.4), kind=kLoop, calls=%fused_computation.28 | loop fusion | flops 262144 | bytes 2097152 | tf_op jit(solution)/shard_map/add | solution.py:78
  100.1 2.1 %collective-permute-start.8 = (f32[4,1,4,32,256]{4,3,2,1,0:T(8,128)}, f32[4,1,4,32,256]{4,3,2,1,0:T(8,128)}, u32[]{:S(2)}, u32[]{:S(2)}) collective-permute-start(f32[4,1,4,32,256]{4,3,2,1,0:T(8,128)} %fusion.9), channel_id=1, source_target_pairs={{0,24},{1,25},{2,26},{3,27},{4,12},{5,13},{6,14},{7,15},{8,16},{9,... | collective-permute-start | bytes 1572872 | tf_op jit(solution)/shard_map/ppermute | solution.py:78
  102.3 3.0 %collective-permute-start.9 = (f32[1,4,4,32,256]{4,3,2,1,0:T(8,128)S(1)}, f32[1,4,4,32,256]{4,3,2,1,0:T(8,128)}, u32[]{:S(2)}, u32[]{:S(2)}) collective-permute-start(f32[1,4,4,32,256]{4,3,2,1,0:T(8,128)S(1)} %slice_add_fusion.7), channel_id=1, source_target_pairs={{0,96},{1,97},{2,98},{3,99},{4,36},{5,37},{6,38},{7,39},{8,104},{9... | collective-permute-start | bytes 1572872 | tf_op jit(solution)/shard_map/ppermute | solution.py:78
  105.3 5.7 %all-to-all-start.1 = ((f32[128,4,384]{2,1,0:T(4,128)}), f32[128,4,384]{2,1,0:T(4,128)}, u32[]{:S(2)}, u32[]{:S(2)}) async-start(f32[128,4,384]{2,1,0:T(4,128)} %reshape.286), calls=%async_computation.1 | async-start | bytes 1572864 | tf_op jit(solution)/shard_map/all_to_all | solution.py:447
  111.1 2.5 %collective-permute-done.9 = f32[1,4,4,32,256]{4,3,2,1,0:T(8,128)} collective-permute-done((f32[1,4,4,32,256]{4,3,2,1,0:T(8,128)S(1)}, f32[1,4,4,32,256]{4,3,2,1,0:T(8,128)}, u32[]{:S(2)}, u32[]{:S(2)}) %collective-permute-start.9) | collective-permute-done | bytes 524320 | tf_op jit(solution)/shard_map/ppermute | solution.py:78
  113.6 1.7 fusion.8
  115.3 1.5 fusion.14
  117.2 1.1 fusion.12
  118.3 1.4 collective-permute-start.15
  119.7 5.9 %collective-permute-done.13 = f32[2,1,4,32,256]{4,3,2,1,0:T(8,128)S(1)} collective-permute-done((f32[2,1,4,32,256]{4,3,2,1,0:T(8,128)S(1)}, f32[2,1,4,32,256]{4,3,2,1,0:T(8,128)S(1)}, u32[]{:S(2)}, u32[]{:S(2)}) %collective-permute-start.13) | collective-permute-done | bytes 262176 | tf_op jit(solution)/shard_map/ppermute | solution.py:78
  125.6 1.9 %slice_add_fusion.12 = f32[1,1,4,32,256]{4,3,2,1,0:T(8,128)} fusion(f32[2,1,4,32,256]{4,3,2,1,0:T(8,128)S(1)} %collective-permute-done.13, f32[4,4,4,32,256]{4,3,2,1,0:T(8,128)} %bitcast.9, f32[4,4,4,32,256]{4,3,2,1,0:T(8,128)} %bitcast.51, f32[4,1,4,32,256]{4,3,2,1,0:T(8,128)} %collective-permute-done.8, f32[4,2,4,32,256]{4,3,2,1,0:T(8,128)} %collective-permute-done.4), kind=kLoop, calls=%fused_computation.48 | loop fusion | flops 131072 | bytes 786432 | tf_op jit(solution)/shard_map/add | solution.py:78
  127.5 3.1 %collective-permute-start.14 = (f32[1,1,4,32,256]{4,3,2,1,0:T(8,128)}, f32[1,1,4,32,256]{4,3,2,1,0:T(8,128)S(1)}, u32[]{:S(2)}, u32[]{:S(2)}) collective-permute-start(f32[1,1,4,32,256]{4,3,2,1,0:T(8,128)} %slice_add_fusion.12), channel_id=1, source_target_pairs={{0,96},{1,97},{2,98},{3,99},{4,36},{5,37},{6,38},{7,39},{8,104},{9... | collective-permute-start | bytes 393224 | tf_op jit(solution)/shard_map/ppermute | solution.py:78
  132.9 1.8 %slice_add_fusion.10 = f32[1,4,1,32,256]{4,3,2,1,0:T(8,128)} fusion(f32[1,4,2,32,256]{4,3,2,1,0:T(8,128)S(1)} %collective-permute-done.15, f32[1,4,4,32,256]{4,3,2,1,0:T(8,128)S(1)} %bitcast.74, f32[1,4,4,32,256]{4,3,2,1,0:T(8,128)} %bitcast.66, f32[1,4,4,32,256]{4,3,2,1,0:T(8,128)} %collective-permute-done.9, f32[2,4,4,32,256]{4,3,2,1,0:T(8,128)} %copy-done.15), kind=kLoop, calls=%fused_computation.44 | loop fusion | flops 131072 | bytes 786432 | tf_op jit(solution)/shard_map/add | solution.py:78
  134.8 1.8 collective-permute-start.16
  136.5 4.6 %collective-permute-done.16 = f32[1,4,1,32,256]{4,3,2,1,0:T(8,128)S(1)} collective-permute-done((f32[1,4,1,32,256]{4,3,2,1,0:T(8,128)}, f32[1,4,1,32,256]{4,3,2,1,0:T(8,128)S(1)}, u32[]{:S(2)}, u32[]{:S(2)}) %collective-permute-start.16) | collective-permute-done | bytes 131104 | tf_op jit(solution)/shard_map/ppermute | solution.py:78
  141.2 1.7 fusion.23
  143.4 1.6 fusion.31
  145.0 1.6 fusion.28
  146.6 1.4 reshape.292.arrived_ref
  148.1 1.6 copy-done.4
  149.7 3.7 %row_update.1 = (f32[2048,256]{1,0:T(8,128)}, f32[2048,256]{1,0:T(8,128)}) custom-call(f32[512,384]{1,0:T(8,128)S(1)} %reshape.292.arrived_ref, f32[2048,256]{1,0:T(8,128)S(1)} %copy-done.3, f32[2048,256]{1,0:T(8,128)S(1)} %copy-done.4), custom_call_target="tpu_custom_call" | custom-call | flops 1073741824 | bytes 8388608 | tf_op jit(solution)/shard_map/row_update/pallas_call | solution.py:352
  154.2 2.4 %collective-permute-start.22 = (f32[1,1,1,32,256]{4,3,2,1,0:T(8,128)S(1)}, f32[1,1,1,32,256]{4,3,2,1,0:T(8,128)S(1)}, u32[]{:S(2)}, u32[]{:S(2)}) collective-permute-start(f32[1,1,1,32,256]{4,3,2,1,0:T(8,128)S(1)} %fusion.42), channel_id=1, source_target_pairs={{0,24},{1,25},{2,26},{3,27},{4,12},{5,13},{6,14},{7,15},{8,16},{9,... | collective-permute-start | bytes 98312 | tf_op jit(solution)/shard_map/ppermute | solution.py:78
  157.5 1.2 collective-permute-start.21
  161.1 1.6 collective-permute-done.21
  163.5 1.4 collective-permute-done.20
  165.8 2.2 %collective-permute-start.25 = (f32[112,256]{1,0:T(8,128)S(1)}, f32[112,256]{1,0:T(8,128)S(1)}, u32[]{:S(2)}, u32[]{:S(2)}) collective-permute-start(f32[112,256]{1,0:T(8,128)S(1)} %get-tuple-element.103), channel_id=1, source_target_pairs={{0,3},{1,2},{2,1},{3,0},{4,7},{5,6},{6,5},{7,4},{8,11},{9,10},{10,... | collective-permute-start | bytes 344072 | tf_op jit(solution)/shard_map/ppermute | solution.py:44
  168.0 1.4 collective-permute-start.24
  170.0 1.9 %collective-permute-done.25 = f32[112,256]{1,0:T(8,128)S(1)} collective-permute-done((f32[112,256]{1,0:T(8,128)S(1)}, f32[112,256]{1,0:T(8,128)S(1)}, u32[]{:S(2)}, u32[]{:S(2)}) %collective-permute-start.25) | collective-permute-done | bytes 114720 | tf_op jit(solution)/shard_map/ppermute | solution.py:44
  171.9 2.4 %collective-permute-done.24 = f32[112,256]{1,0:T(8,128)S(1)} collective-permute-done((f32[112,256]{1,0:T(8,128)S(1)}, f32[112,256]{1,0:T(8,128)S(1)}, u32[]{:S(2)}, u32[]{:S(2)}) %collective-permute-start.24) | collective-permute-done | bytes 114720 | tf_op jit(solution)/shard_map/ppermute | solution.py:44
  (132 shorter events, 20.6 us)
Async XLA Ops:
  0.6 49.4 %copy-start = (bf16[768,256]{1,0:T(8,128)(2,1)S(1)}, bf16[768,256]{1,0:T(8,128)(2,1)}, u32[]{:S(2)}) copy-start(bf16[768,256]{1,0:T(8,128)(2,1)} %param.15) | copy-start | bytes 1179652
  0.6 4.3 %copy-start.22 = (s32[1,512]{1,0:T(1,128)S(1)}, s32[1,512]{1,0:T(1,128)}, u32[]{:S(2)}) copy-start(s32[1,512]{1,0:T(1,128)} %param.19) | copy-start | bytes 6148
  0.7 4.3 %copy-start.23 = (s32[1024]{0:T(1024)S(1)}, s32[1024]{0:T(1024)}, u32[]{:S(2)}) copy-start(s32[1024]{0:T(1024)} %param.18) | copy-start | bytes 12292
  5.0 4.3 %collective-permute-start = (f32[1536,256]{1,0:T(8,128)}, f32[1536,256]{1,0:T(8,128)S(1)}, u32[]{:S(2)}, u32[]{:S(2)}) collective-permute-start(f32[1536,256]{1,0:T(8,128)} %segment_sums.2), channel_id=1, source_target_pairs={{0,4},{4,0},{1,5},{5,1},{2,6},{6,2},{3,7},{7,3},{8,12},{12,8},{9,1... | collective-permute-start | bytes 4718600 | tf_op jit(solution)/shard_map/ppermute | solution.py:39
  9.2 2.6 %copy-start.21 = (f32[768]{0:T(1024)S(1)}, f32[768]{0:T(1024)}, u32[]{:S(2)}) copy-start(f32[768]{0:T(1024)} %param.12) | copy-start | bytes 9220
  11.8 36.7 %all-to-all-start = ((f32[64,24,256]{2,1,0:T(8,128)}), f32[64,24,256]{2,1,0:T(8,128)}, u32[]{:S(2)}, u32[]{:S(2)}) async-start(f32[64,24,256]{2,1,0:T(8,128)} %bitcast.4), calls=%async_computation | async-start | bytes 3145728 | tf_op jit(solution)/shard_map/all_to_all | solution.py:394
  61.8 32.4 %copy-start.1 = (f32[64,40,256]{2,1,0:T(8,128)}, f32[64,40,256]{2,1,0:T(8,128)S(1)}, u32[]{:S(2)}) copy-start(f32[64,40,256]{2,1,0:T(8,128)S(1)} %get-tuple-element.55) | copy-start | bytes 7864324
  61.8 14.4 %collective-permute-start.1 = (f32[64,40,256]{2,1,0:T(8,128)S(1)}, f32[64,40,256]{2,1,0:T(8,128)S(1)}, u32[]{:S(2)}, u32[]{:S(2)}) collective-permute-start(f32[64,40,256]{2,1,0:T(8,128)S(1)} %get-tuple-element.56), channel_id=1, source_target_pairs={{0,4},{4,0},{1,5},{5,1},{2,6},{6,2},{3,7},{7,3},{8,12},{12,8},{9,1... | collective-permute-start | bytes 7864328 | tf_op jit(solution)/shard_map/ppermute | solution.py:39
  62.1 17.7 %slice-start = ((s8[4718592]{0:T(1024)(128)(4,1)}), s8[4194304]{0:T(1024)(128)(4,1)S(1)}, s32[]{:S(2)}) async-start(s8[4718592]{0:T(1024)(128)(4,1)} %bitcast.57), calls=%async_computation.2 | async-start | bytes 8388608
  67.2 30.8 %copy-start.2 = (f32[64,32,256]{2,1,0:T(8,128)}, f32[64,32,256]{2,1,0:T(8,128)S(1)}, u32[]{:S(2)}) copy-start(f32[64,32,256]{2,1,0:T(8,128)S(1)} %get-tuple-element.58) | copy-start | bytes 6291460
  67.2 12.5 %slice-start.1 = ((s8[4718592]{0:T(1024)(128)(4,1)}), s8[524288]{0:T(1024)(128)(4,1)S(1)}, s32[]{:S(2)}) async-start(s8[4718592]{0:T(1024)(128)(4,1)} %bitcast.57), calls=%async_computation.3 | async-start | bytes 1048576
  67.2 5.8 %collective-permute-start.3 = (f32[64,32,256]{2,1,0:T(8,128)S(1)}, f32[64,32,256]{2,1,0:T(8,128)}, u32[]{:S(2)}, u32[]{:S(2)}) collective-permute-start(f32[64,32,256]{2,1,0:T(8,128)S(1)} %get-tuple-element.59), channel_id=1, source_target_pairs={{0,4},{4,0},{1,5},{5,1},{2,6},{6,2},{3,7},{7,3},{8,12},{12,8},{9,1... | collective-permute-start | bytes 6291464 | tf_op jit(solution)/shard_map/ppermute | solution.py:39
  72.9 5.1 %collective-permute-start.5 = (f32[64,32,256]{2,1,0:T(8,128)S(1)}, f32[64,32,256]{2,1,0:T(8,128)S(1)}, u32[]{:S(2)}, u32[]{:S(2)}) collective-permute-start(f32[64,32,256]{2,1,0:T(8,128)S(1)} %get-tuple-element.61), channel_id=1, source_target_pairs={{0,4},{4,0},{1,5},{5,1},{2,6},{6,2},{3,7},{7,3},{8,12},{12,8},{9,1... | collective-permute-start | bytes 6291464 | tf_op jit(solution)/shard_map/ppermute | solution.py:39
  75.4 17.0 %collective-permute-start.4 = (f32[4,2,4,32,256]{4,3,2,1,0:T(8,128)}, f32[4,2,4,32,256]{4,3,2,1,0:T(8,128)}, u32[]{:S(2)}, u32[]{:S(2)}) collective-permute-start(f32[4,2,4,32,256]{4,3,2,1,0:T(8,128)} %slice_add_fusion.2), channel_id=1, source_target_pairs={{0,8},{1,9},{2,10},{3,11},{4,28},{5,29},{6,30},{7,31},{8,0},{9,1},... | collective-permute-start | bytes 3145736 | tf_op jit(solution)/shard_map/ppermute | solution.py:78
  76.3 17.9 %copy-start.10 = (f32[64,40,256]{2,1,0:T(8,128)}, f32[64,40,256]{2,1,0:T(8,128)S(1)}, u32[]{:S(2)}) copy-start(f32[64,40,256]{2,1,0:T(8,128)S(1)} %collective-permute-done.1) | copy-start | bytes 7864324
  76.5 3.3 %copy-start.7 = (bf16[24,64,768]{2,1,0:T(8,128)(2,1)S(1)}, bf16[24,64,768]{2,1,0:T(8,128)(2,1)}, u32[]{:S(2)}) copy-start(bf16[24,64,768]{2,1,0:T(8,128)(2,1)} %param.11) | copy-start | bytes 7077892
  76.5 17.7 %collective-permute-start.2 = (f32[4,4,2,40,256]{4,3,2,1,0:T(8,128)S(1)}, f32[4,4,2,40,256]{4,3,2,1,0:T(8,128)S(1)}, u32[]{:S(2)}, u32[]{:S(2)}) collective-permute-start(f32[4,4,2,40,256]{4,3,2,1,0:T(8,128)S(1)} %slice_add_fusion), channel_id=1, source_target_pairs={{0,1},{1,0},{2,3},{3,2},{4,7},{5,6},{6,5},{7,4},{8,9},{9,8},{10,11... | collective-permute-start | bytes 3932168 | tf_op jit(solution)/shard_map/ppermute | solution.py:78
  78.2 14.9 %collective-permute-start.6 = (f32[2,4,4,32,256]{4,3,2,1,0:T(8,128)S(1)}, f32[2,4,4,32,256]{4,3,2,1,0:T(8,128)S(1)}, u32[]{:S(2)}, u32[]{:S(2)}) collective-permute-start(f32[2,4,4,32,256]{4,3,2,1,0:T(8,128)S(1)} %bitcast.75), channel_id=1, source_target_pairs={{0,32},{1,33},{2,34},{3,35},{4,100},{5,101},{6,102},{7,103},{8,40}... | collective-permute-start | bytes 3145736 | tf_op jit(solution)/shard_map/ppermute | solution.py:78
  92.4 24.8 %copy-start.11 = (f32[16,32,256]{2,1,0:T(8,128)}, f32[16,32,256]{2,1,0:T(8,128)S(1)}, u32[]{:S(2)}) copy-start(f32[16,32,256]{2,1,0:T(8,128)S(1)} %get-tuple-element.93) | copy-start | bytes 1572868
  93.1 9.1 %copy-start.15 = (f32[2,4,4,32,256]{4,3,2,1,0:T(8,128)}, f32[2,4,4,32,256]{4,3,2,1,0:T(8,128)S(1)}, u32[]{:S(2)}) copy-start(f32[2,4,4,32,256]{4,3,2,1,0:T(8,128)S(1)} %collective-permute-done.6) | copy-start | bytes 3145732
  94.2 6.0 %copy-start.13 = (f32[4,4,2,40,256]{4,3,2,1,0:T(8,128)}, f32[4,4,2,40,256]{4,3,2,1,0:T(8,128)S(1)}, u32[]{:S(2)}) copy-start(f32[4,4,2,40,256]{4,3,2,1,0:T(8,128)S(1)} %collective-permute-done.2) | copy-start | bytes 3932164
  95.3 18.3 %collective-permute-start.7 = (f32[4,4,1,40,256]{4,3,2,1,0:T(8,128)}, f32[4,4,1,40,256]{4,3,2,1,0:T(8,128)}, u32[]{:S(2)}, u32[]{:S(2)}) collective-permute-start(f32[4,4,1,40,256]{4,3,2,1,0:T(8,128)} %fusion.6), channel_id=1, source_target_pairs={{0,3},{1,2},{2,1},{3,0},{4,5},{5,4},{6,7},{7,6},{8,11},{9,10},{10,... | collective-permute-start | bytes 1966088 | tf_op jit(solution)/shard_map/ppermute | solution.py:78
  100.1 10.9 %collective-permute-start.8 = (f32[4,1,4,32,256]{4,3,2,1,0:T(8,128)}, f32[4,1,4,32,256]{4,3,2,1,0:T(8,128)}, u32[]{:S(2)}, u32[]{:S(2)}) collective-permute-start(f32[4,1,4,32,256]{4,3,2,1,0:T(8,128)} %fusion.9), channel_id=1, source_target_pairs={{0,24},{1,25},{2,26},{3,27},{4,12},{5,13},{6,14},{7,15},{8,16},{9,... | collective-permute-start | bytes 1572872 | tf_op jit(solution)/shard_map/ppermute | solution.py:78
  102.2 11.4 %copy-start.14 = (f32[4,4,2,40,256]{4,3,2,1,0:T(8,128)S(1)}, f32[4,4,2,40,256]{4,3,2,1,0:T(8,128)}, u32[]{:S(2)}) copy-start(f32[4,4,2,40,256]{4,3,2,1,0:T(8,128)} %copy-done.13) | copy-start | bytes 3932164
  102.3 11.3 %collective-permute-start.9 = (f32[1,4,4,32,256]{4,3,2,1,0:T(8,128)S(1)}, f32[1,4,4,32,256]{4,3,2,1,0:T(8,128)}, u32[]{:S(2)}, u32[]{:S(2)}) collective-permute-start(f32[1,4,4,32,256]{4,3,2,1,0:T(8,128)S(1)} %slice_add_fusion.7), channel_id=1, source_target_pairs={{0,96},{1,97},{2,98},{3,99},{4,36},{5,37},{6,38},{7,39},{8,104},{9... | collective-permute-start | bytes 1572872 | tf_op jit(solution)/shard_map/ppermute | solution.py:78
  105.3 5.7 %collective-permute-start.10 = (f32[8,768]{1,0:T(8,128)S(1)}, f32[8,768]{1,0:T(8,128)S(1)}, u32[]{:S(2)}, u32[]{:S(2)}) collective-permute-start(f32[8,768]{1,0:T(8,128)S(1)} %get-tuple-element.70), channel_id=1, source_target_pairs={{0,4},{4,0},{1,5},{5,1},{2,6},{6,2},{3,7},{7,3},{8,12},{12,8},{9,1... | collective-permute-start | bytes 73736 | tf_op jit(solution)/shard_map/ppermute | solution.py:39
  105.3 31.2 %all-to-all-start.1 = ((f32[128,4,384]{2,1,0:T(4,128)}), f32[128,4,384]{2,1,0:T(4,128)}, u32[]{:S(2)}, u32[]{:S(2)}) async-start(f32[128,4,384]{2,1,0:T(4,128)} %reshape.286), calls=%async_computation.1 | async-start | bytes 1572864 | tf_op jit(solution)/shard_map/all_to_all | solution.py:447
  115.2 25.9 %copy-start.8 = (f32[4,4,1,40,256]{4,3,2,1,0:T(8,128)}, f32[4,4,1,40,256]{4,3,2,1,0:T(8,128)S(1)}, u32[]{:S(2)}) copy-start(f32[4,4,1,40,256]{4,3,2,1,0:T(8,128)S(1)} %fusion.8) | copy-start | bytes 1966084
  116.8 8.9 %collective-permute-start.13 = (f32[2,1,4,32,256]{4,3,2,1,0:T(8,128)S(1)}, f32[2,1,4,32,256]{4,3,2,1,0:T(8,128)S(1)}, u32[]{:S(2)}, u32[]{:S(2)}) collective-permute-start(f32[2,1,4,32,256]{4,3,2,1,0:T(8,128)S(1)} %fusion.14), channel_id=1, source_target_pairs={{0,32},{1,33},{2,34},{3,35},{4,100},{5,101},{6,102},{7,103},{8,40}... | collective-permute-start | bytes 786440 | tf_op jit(solution)/shard_map/ppermute | solution.py:78
  116.9 13.7 %collective-permute-start.11 = (f32[4,2,1,48,256]{4,3,2,1,0:T(8,128)S(1)}, f32[4,2,1,48,256]{4,3,2,1,0:T(8,128)S(1)}, u32[]{:S(2)}, u32[]{:S(2)}) collective-permute-start(f32[4,2,1,48,256]{4,3,2,1,0:T(8,128)S(1)} %fusion.10), channel_id=1, source_target_pairs={{0,8},{1,9},{2,10},{3,11},{4,28},{5,29},{6,30},{7,31},{8,0},{9,1},... | collective-permute-start | bytes 1179656 | tf_op jit(solution)/shard_map/ppermute | solution.py:78
  118.3 14.6 %collective-permute-start.15 = (f32[1,4,2,32,256]{4,3,2,1,0:T(8,128)S(1)}, f32[1,4,2,32,256]{4,3,2,1,0:T(8,128)S(1)}, u32[]{:S(2)}, u32[]{:S(2)}) collective-permute-start(f32[1,4,2,32,256]{4,3,2,1,0:T(8,128)S(1)} %fusion.12), channel_id=1, source_target_pairs={{0,1},{1,0},{2,3},{3,2},{4,7},{5,6},{6,5},{7,4},{8,9},{9,8},{10,11... | collective-permute-start | bytes 786440 | tf_op jit(solution)/shard_map/ppermute | solution.py:78
  125.6 5.0 %copy-start.17 = (f32[2,1,4,32,256]{4,3,2,1,0:T(8,128)}, f32[2,1,4,32,256]{4,3,2,1,0:T(8,128)S(1)}, u32[]{:S(2)}) copy-start(f32[2,1,4,32,256]{4,3,2,1,0:T(8,128)S(1)} %collective-permute-done.13) | copy-start | bytes 786436
  127.5 9.0 %collective-permute-start.14 = (f32[1,1,4,32,256]{4,3,2,1,0:T(8,128)}, f32[1,1,4,32,256]{4,3,2,1,0:T(8,128)S(1)}, u32[]{:S(2)}, u32[]{:S(2)}) collective-permute-start(f32[1,1,4,32,256]{4,3,2,1,0:T(8,128)} %slice_add_fusion.12), channel_id=1, source_target_pairs={{0,96},{1,97},{2,98},{3,99},{4,36},{5,37},{6,38},{7,39},{8,104},{9... | collective-permute-start | bytes 393224 | tf_op jit(solution)/shard_map/ppermute | solution.py:78
  132.1 15.9 %copy-start.3 = (f32[2048,256]{1,0:T(8,128)S(1)}, f32[2048,256]{1,0:T(8,128)}, u32[]{:S(2)}) copy-start(f32[2048,256]{1,0:T(8,128)} %table_ref.1) | copy-start | bytes 6291460
  132.1 9.0 %collective-permute-start.12 = (f32[4,1,1,48,256]{4,3,2,1,0:T(8,128)}, f32[4,1,1,48,256]{4,3,2,1,0:T(8,128)}, u32[]{:S(2)}, u32[]{:S(2)}) collective-permute-start(f32[4,1,1,48,256]{4,3,2,1,0:T(8,128)} %fusion.16), channel_id=1, source_target_pairs={{0,24},{1,25},{2,26},{3,27},{4,12},{5,13},{6,14},{7,15},{8,16},{9,... | collective-permute-start | bytes 589832 | tf_op jit(solution)/shard_map/ppermute | solution.py:78
  134.8 6.4 %collective-permute-start.16 = (f32[1,4,1,32,256]{4,3,2,1,0:T(8,128)}, f32[1,4,1,32,256]{4,3,2,1,0:T(8,128)S(1)}, u32[]{:S(2)}, u32[]{:S(2)}) collective-permute-start(f32[1,4,1,32,256]{4,3,2,1,0:T(8,128)} %slice_add_fusion.10), channel_id=1, source_target_pairs={{0,3},{1,2},{2,1},{3,0},{4,5},{5,4},{6,7},{7,6},{8,11},{9,10},{10,... | collective-permute-start | bytes 393224 | tf_op jit(solution)/shard_map/ppermute | solution.py:78
  141.1 5.5 %copy-start.19 = (f32[1,4,1,32,256]{4,3,2,1,0:T(8,128)}, f32[1,4,1,32,256]{4,3,2,1,0:T(8,128)S(1)}, u32[]{:S(2)}) copy-start(f32[1,4,1,32,256]{4,3,2,1,0:T(8,128)S(1)} %collective-permute-done.16) | copy-start | bytes 393220
  142.8 10.5 %collective-permute-start.17 = (f32[2,1,1,48,256]{4,3,2,1,0:T(8,128)}, f32[2,1,1,48,256]{4,3,2,1,0:T(8,128)}, u32[]{:S(2)}, u32[]{:S(2)}) collective-permute-start(f32[2,1,1,48,256]{4,3,2,1,0:T(8,128)} %fusion.23), channel_id=1, source_target_pairs={{0,32},{1,33},{2,34},{3,35},{4,100},{5,101},{6,102},{7,103},{8,40}... | collective-permute-start | bytes 294920 | tf_op jit(solution)/shard_map/ppermute | solution.py:78
  145.0 8.3 %collective-permute-start.18 = (f32[1,1,2,32,256]{4,3,2,1,0:T(8,128)}, f32[1,1,2,32,256]{4,3,2,1,0:T(8,128)}, u32[]{:S(2)}, u32[]{:S(2)}) collective-permute-start(f32[1,1,2,32,256]{4,3,2,1,0:T(8,128)} %fusion.31), channel_id=1, source_target_pairs={{0,1},{1,0},{2,3},{3,2},{4,7},{5,6},{6,5},{7,4},{8,9},{9,8},{10,11... | collective-permute-start | bytes 196616 | tf_op jit(solution)/shard_map/ppermute | solution.py:78
  146.6 6.7 %collective-permute-start.19 = (f32[1,2,1,32,256]{4,3,2,1,0:T(8,128)}, f32[1,2,1,32,256]{4,3,2,1,0:T(8,128)}, u32[]{:S(2)}, u32[]{:S(2)}) collective-permute-start(f32[1,2,1,32,256]{4,3,2,1,0:T(8,128)} %fusion.28), channel_id=1, source_target_pairs={{0,8},{1,9},{2,10},{3,11},{4,28},{5,29},{6,30},{7,31},{8,0},{9,1},... | collective-permute-start | bytes 196616 | tf_op jit(solution)/shard_map/ppermute | solution.py:78
  149.6 3.7 %copy-start.20 = (f32[1,4,1,32,256]{4,3,2,1,0:T(8,128)S(1)}, f32[1,4,1,32,256]{4,3,2,1,0:T(8,128)}, u32[]{:S(2)}) copy-start(f32[1,4,1,32,256]{4,3,2,1,0:T(8,128)} %copy-done.19) | copy-start | bytes 393220
  149.6 9.1 %copy-start.9 = (f32[4,4,1,40,256]{4,3,2,1,0:T(8,128)S(1)}, f32[4,4,1,40,256]{4,3,2,1,0:T(8,128)}, u32[]{:S(2)}) copy-start(f32[4,4,1,40,256]{4,3,2,1,0:T(8,128)} %copy-done.8) | copy-start | bytes 1966084
  154.2 6.1 %collective-permute-start.22 = (f32[1,1,1,32,256]{4,3,2,1,0:T(8,128)S(1)}, f32[1,1,1,32,256]{4,3,2,1,0:T(8,128)S(1)}, u32[]{:S(2)}, u32[]{:S(2)}) collective-permute-start(f32[1,1,1,32,256]{4,3,2,1,0:T(8,128)S(1)} %fusion.42), channel_id=1, source_target_pairs={{0,24},{1,25},{2,26},{3,27},{4,12},{5,13},{6,14},{7,15},{8,16},{9,... | collective-permute-start | bytes 98312 | tf_op jit(solution)/shard_map/ppermute | solution.py:78
  157.5 5.2 %collective-permute-start.21 = (f32[1,1,1,32,256]{4,3,2,1,0:T(8,128)S(1)}, f32[1,1,1,32,256]{4,3,2,1,0:T(8,128)S(1)}, u32[]{:S(2)}, u32[]{:S(2)}) collective-permute-start(f32[1,1,1,32,256]{4,3,2,1,0:T(8,128)S(1)} %fusion.52), channel_id=1, source_target_pairs={{0,3},{1,2},{2,1},{3,0},{4,5},{5,4},{6,7},{7,6},{8,11},{9,10},{10,... | collective-permute-start | bytes 98312 | tf_op jit(solution)/shard_map/ppermute | solution.py:78
  159.6 5.4 %collective-permute-start.20 = (f32[1,1,1,48,256]{4,3,2,1,0:T(8,128)S(1)}, f32[1,1,1,48,256]{4,3,2,1,0:T(8,128)S(1)}, u32[]{:S(2)}, u32[]{:S(2)}) collective-permute-start(f32[1,1,1,48,256]{4,3,2,1,0:T(8,128)S(1)} %fusion.35), channel_id=1, source_target_pairs={{0,96},{1,97},{2,98},{3,99},{4,36},{5,37},{6,38},{7,39},{8,104},{9... | collective-permute-start | bytes 147464 | tf_op jit(solution)/shard_map/ppermute | solution.py:78
  165.8 6.1 %collective-permute-start.25 = (f32[112,256]{1,0:T(8,128)S(1)}, f32[112,256]{1,0:T(8,128)S(1)}, u32[]{:S(2)}, u32[]{:S(2)}) collective-permute-start(f32[112,256]{1,0:T(8,128)S(1)} %get-tuple-element.103), channel_id=1, source_target_pairs={{0,3},{1,2},{2,1},{3,0},{4,7},{5,6},{6,5},{7,4},{8,11},{9,10},{10,... | collective-permute-start | bytes 344072 | tf_op jit(solution)/shard_map/ppermute | solution.py:44
  168.0 6.3 %collective-permute-start.24 = (f32[112,256]{1,0:T(8,128)S(1)}, f32[112,256]{1,0:T(8,128)S(1)}, u32[]{:S(2)}, u32[]{:S(2)}) collective-permute-start(f32[112,256]{1,0:T(8,128)S(1)} %get-tuple-element.103), channel_id=1, source_target_pairs={{0,2},{1,3},{2,0},{3,1},{4,6},{5,7},{6,4},{7,5},{8,10},{9,11},{10,... | collective-permute-start | bytes 344072 | tf_op jit(solution)/shard_map/ppermute | solution.py:44
  169.4 4.9 %collective-permute-start.23 = (f32[112,256]{1,0:T(8,128)S(1)}, f32[112,256]{1,0:T(8,128)S(1)}, u32[]{:S(2)}, u32[]{:S(2)}) collective-permute-start(f32[112,256]{1,0:T(8,128)S(1)} %get-tuple-element.103), channel_id=1, source_target_pairs={{0,1},{1,0},{2,3},{3,2},{4,5},{5,4},{6,7},{7,6},{8,9},{9,8},{10,11... | collective-permute-start | bytes 344072 | tf_op jit(solution)/shard_map/ppermute | solution.py:44
  (6 other events, 9.6 us)

commit v8 on v4

--- a/solution.py
+++ b/solution.py
@@ -176,7 +176,11 @@
         compiler_params=pltpu.CompilerParams(vmem_limit_bytes=VMEM),
         cost_estimate=cost(8 * rows * width * hidden, 4 * rows * hidden, rows * hidden),
         name="forward",
-    )(titles.reshape(rows, width), ln_gain.reshape(1, width), w_up)
+    )(
+        pltpu.with_memory_space_constraint(titles.reshape(rows, width), pltpu.HBM),
+        ln_gain.reshape(1, width),
+        pltpu.with_memory_space_constraint(w_up, pltpu.HBM),
+    )
 
 
 def place_sums(core_ref, keep_at, send_at, ups, down, proj, out_refs):
@@ -357,7 +361,11 @@
         compiler_params=pltpu.CompilerParams(vmem_limit_bytes=16 << 20),
         cost_estimate=cost(4 * rows * width_e * arrived.shape[0], 16 * rows * width_e),
         name="row_update",
-    )(arrived, table, accum)
+    )(
+        arrived,
+        pltpu.with_memory_space_constraint(table, pltpu.HBM),
+        pltpu.with_memory_space_constraint(accum, pltpu.HBM),
+    )
 
 
 def per_device(
@@ -449,8 +457,10 @@
     parts[0] = jnp.concatenate([parts[0], gain_term], axis=3)
     parts, _ = halve(parts, "yzx", False)
     parts, (row_all,) = halve(parts, "yzx", True, (row_all,))
-    beside = row_update(row_all.reshape(slot_count, width_e + 128), table, accum)
-    parts, (new_table, new_accum) = halve(parts, "zxy", False, tuple(beside))
+    new_table, new_accum = row_update(
+        row_all.reshape(slot_count, width_e + 128), table, accum
+    )
+    parts, _ = halve(parts, "zxy", False)
     parts, _ = halve(parts, "zxy", True)
 
     flat = [part.reshape(-1, width_e) for part in parts]

time: 171 us -> 162 us (0.947)
  local copies, waits for them, and re-layouts: 17 us -> 9.74 us
  Pallas kernels: 57.1 us -> 60.8 us
  other arithmetic: 11.8 us -> 8.83 us
  waiting for transfers between devices: 21.7 us -> 19.3 us
    unnamed x34 -> x20, local copies, waits for them, and re-layouts: 7.34 us -> 1.45 us
    ppermute x3, waiting for transfers between devices: 4.67 us -> 0.01 us  [along(): return lax.ppermute(block, name, [(i, i ^ step) for i in range(size)])]
    add x15, other arithmetic: 7.27 us -> 4.35 us  [halve(): return ([k + s for k, s in zip(kept, sent)], also)]
    pallas_call x1, Pallas kernels: 3.65 us -> 5.76 us  [row_update(): pl.pallas_call(rows_kernel, grid=(rows // step,), in_specs=[pl.BlockSpec(...]
  transfers between devices with their start and end apart: 28 -> 28, of which waited for: 10 -> 9; matrix products, arithmetic and copies ran while one was open for 11% -> 10% of each run, Pallas kernels for 26% -> 30%
where the time goes in v8:
time: 162 us; the launch traced here: 161 us
  Pallas kernels  60.8 us (38%)
  starting transfers between devices  51.8 us (32%)
  waiting for transfers between devices  19.3 us (12%)
  local copies, waits for them, and re-layouts  9.74 us (6%)
  matrix products  9.58 us (6%)
  other arithmetic  8.83 us (5%)
    ppermute x18, starting transfers between devices, halve(): lax.ppermute(lax.slice_in_dim(part, middle, None, axis=dim), DEVICES, par...  28.7 us
    pallas_call x1, Pallas kernels, forward(): pl.pallas_call(functools.partial(forward_kernel, units), grid=(hidden //...  20.5 us
    pallas_call x3, Pallas kernels, up_products(): pl.pallas_call(kernel, grid_spec=pltpu.PrefetchScalarGridSpec(num_scalar_...  18.1 us
    ppermute x18, waiting for transfers between devices, halve(): lax.ppermute(lax.slice_in_dim(part, middle, None, axis=dim), DEVICES, par...  18 us
    all_to_all x1, starting transfers between devices, per_device(): item_all = lax.all_to_all(mine, CHIPS, 0, 0, tiled=True)  11.7 us
    pallas_call x1, Pallas kernels, title_grads(): pl.pallas_call(titles_kernel, grid=(rows // step,), in_specs=[pl.BlockSpe...  11.5 us
    pallas_call x1, Pallas kernels, row_update(): pl.pallas_call(rows_kernel, grid=(rows // step,), in_specs=[pl.BlockSpec(...  5.76 us
    all_to_all x1, starting transfers between devices, per_device(): row_all = lax.all_to_all(row_part, DEVICES, 0, 0, tiled=True)  5.69 us
  transfers between devices with their start and end apart: 28, of which 9 were waited for; matrix products, arithmetic and copies ran while one was open for 10% of the time, Pallas kernels for 30%

profile of v8, /device:TPU:0, one launch (start us, length us, event | category | flops | bytes accessed | tf_op | source)
XLA Modules:
  0.0 161.4 jit_solution(16180309939998192110)
XLA Ops:
  0.7 0.8 broadcast_select_fusion
  1.4 1.0 copy-done.1
  2.5 2.5 %segment_sums.2 = f32[1536,256]{1,0:T(8,128)} custom-call(s32[1,1024]{1,0:T(1,128)S(1)} %bitcast.42, bf16[1024,256]{1,0:T(8,128)(2,1)S(1)} %copy-done.1), custom_call_target="tpu_custom_call" | custom-call | flops 805306368 | bytes 1572864 | tf_op jit(solution)/shard_map/segment_sums/pallas_call | solution.py:108
  5.0 0.7 fusion.1
  5.8 1.1 copy.19
  6.9 2.3 %reshape.251 = f32[128,4,384]{2,1,0:T(4,128)} reshape(f32[512,384]{1,0:T(8,128)} %copy.19) | data formatting | bytes 1572864 | tf_op jit(solution)/shard_map/reshape | solution.py:416
  9.3 2.5 %segment_sums.3 = f32[1536,256]{1,0:T(8,128)} custom-call(s32[1,1024]{1,0:T(1,128)S(1)} %bitcast.41, bf16[1024,256]{1,0:T(8,128)(2,1)S(1)} %copy-done.2, f32[1536,256]{1,0:T(8,128)S(1)} %collective-permute-done.refs_0_), custom_call_target="tpu_custom_call" | custom-call | flops 805306368 | bytes 1572864 | tf_op jit(solution)/shard_map/segment_sums/pallas_call | solution.py:108
  11.8 11.7 %all-to-all-start = ((f32[64,24,256]{2,1,0:T(8,128)}), f32[64,24,256]{2,1,0:T(8,128)}, u32[]{:S(2)}, u32[]{:S(2)}) async-start(f32[64,24,256]{2,1,0:T(8,128)} %bitcast.4), calls=%async_computation | async-start | bytes 3145728 | tf_op jit(solution)/shard_map/all_to_all | solution.py:401
  23.5 20.5 %forward.1 = (bf16[1536,768]{1,0:T(8,128)(2,1)S(1)}, bf16[1536,3072]{1,0:T(8,128)(2,1)}, f32[24,3072]{1,0:T(8,128)S(1)}, f32[24,768]{1,0:T(8,128)S(1)}) custom-call(bf16[1536,768]{1,0:T(8,128)(2,1)} %bitcast.45, f32[1,768]{1,0:T(1,128)S(1)} %reshape.250.gain_ref, bf16[768,3072]{1,0:T(8,128)(2,1)} %w_ref.3), custom_call_target="tpu_custom_call" | custom-call | flops 28991029248 | bytes 18874368 | tf_op jit(solution)/shard_map/forward/pallas_call | solution.py:156
  44.1 3.8 %fusion.3.pool_ref = bf16[24,1024]{1,0:T(8,128)(2,1)S(1)} fusion(s32[1024]{0:T(1024)S(1)} %fusion.31, f32[24,768]{1,0:T(8,128)S(1)} %get-tuple-element.47, bf16[24,3072]{1,0:T(8,128)(2,1)S(1)} %convert_element_type.35.mean_ref, bf16[3072,768]{1,0:T(8,128)(2,1)} %param.14), kind=kOutput, calls=%fused_computation.8 | convolution fusion | flops 151842816 | bytes 4993024 | tf_op jit(solution)/shard_map/dot_general | solution.py:424
  48.5 1.5 reduce_sum.29.grad_ref
  50.3 3.7 %convolution_multiply_fusion.act_ref = f32[24,3072]{1,0:T(8,128)S(1)} fusion(bf16[3072,768]{1,0:T(8,128)(2,1)} %param.14, f32[24,768]{1,0:T(8,128)S(1)} %fusion.46.pool_ref), kind=kOutput, calls=%fused_computation | convolution fusion | flops 113338368 | bytes 5087232 | tf_op jit(solution)/shard_map/dot_general | solution.py:29
  53.9 7.8 %first_products.1 = (bf16[1536,3072]{1,0:T(8,128)(2,1)S(1)}, f32[64,40,256]{2,1,0:T(8,128)S(1)}, f32[64,40,256]{2,1,0:T(8,128)S(1)}) custom-call(s32[1]{0:T(128)} %bitcast.core_ref, s32[3,4]{1,0:T(4,128)S(1)} %pad_add_fusion.keep_at, s32[3,4]{1,0:T(4,128)S(1)} %pad_add_fusion.1.send_at, bf16[1536,3072]{1,0:T(8,128)(2,1)} %get-tuple-element.45.slope_ref, ...), custom_call_target="tpu_custom_call" | custom-call | flops 2415919104 | bytes 18874368 | tf_op jit(solution)/shard_map/first_products/pallas_call | solution.py:267
  62.1 5.1 %other_products.3 = (f32[64,32,256]{2,1,0:T(8,128)S(1)}, f32[64,32,256]{2,1,0:T(8,128)S(1)}) custom-call(s32[1]{0:T(128)} %bitcast.core_ref, s32[3,4]{1,0:T(4,128)S(1)} %pad_add_fusion.keep_at, s32[3,4]{1,0:T(4,128)S(1)} %pad_add_fusion.1.send_at, bf16[1536,3072]{1,0:T(8,128)(2,1)S(1)} %get-tuple-element.54.pre_ref, ...), custom_call_target="tpu_custom_call" | custom-call | flops 2415919104 | bytes 18874368 | tf_op jit(solution)/shard_map/other_products/pallas_call | solution.py:267
  67.7 5.1 %other_products.2 = (f32[64,32,256]{2,1,0:T(8,128)S(1)}, f32[64,32,256]{2,1,0:T(8,128)S(1)}) custom-call(s32[1]{0:T(128)} %bitcast.core_ref, s32[3,4]{1,0:T(4,128)S(1)} %pad_add_fusion.keep_at, s32[3,4]{1,0:T(4,128)S(1)} %pad_add_fusion.1.send_at, bf16[1536,3072]{1,0:T(8,128)(2,1)S(1)} %get-tuple-element.54.pre_ref, ...), custom_call_target="tpu_custom_call" | custom-call | flops 2415919104 | bytes 18874368 | tf_op jit(solution)/shard_map/other_products/pallas_call | solution.py:267
  73.8 1.0 collective-permute-start.2
  74.9 1.5 collective-permute-start.6
  77.6 0.9 collective-permute-start.4
  78.9 11.5 %title_grads.1 = (bf16[1536,768]{1,0:T(8,128)(2,1)}, f32[8,768]{1,0:T(8,128)S(1)}) custom-call(bf16[1536,3072]{1,0:T(8,128)(2,1)S(1)} %get-tuple-element.54.pre_ref, bf16[768,3072]{1,0:T(8,128)(2,1)S(1)} %bitcast.44, bf16[1536,768]{1,0:T(8,128)(2,1)S(1)} %bitcast.46, f32[1,768]{1,0:T(1,128)S(1)} %reshape.250.gain_ref, f32[24,768]{1,0:T(8,128)S(1)} %fusion.46.pool_ref), custom_call_target="tpu_custom_call" | custom-call | flops 7247757312 | bytes 9437184 | tf_op jit(solution)/shard_map/title_grads/pallas_call | solution.py:312
  90.5 2.0 %collective-permute-done.4 = f32[4,2,4,32,256]{4,3,2,1,0:T(8,128)S(1)} collective-permute-done((f32[4,2,4,32,256]{4,3,2,1,0:T(8,128)S(1)}, f32[4,2,4,32,256]{4,3,2,1,0:T(8,128)S(1)}, u32[]{:S(2)}, u32[]{:S(2)}) %collective-permute-start.4) | collective-permute-done | bytes 1048608 | tf_op jit(solution)/shard_map/ppermute | solution.py:78
  93.1 2.2 %collective-permute-start.7 = (f32[4,4,1,40,256]{4,3,2,1,0:T(8,128)S(1)}, f32[4,4,1,40,256]{4,3,2,1,0:T(8,128)}, u32[]{:S(2)}, u32[]{:S(2)}) collective-permute-start(f32[4,4,1,40,256]{4,3,2,1,0:T(8,128)S(1)} %slice.147), channel_id=1, source_target_pairs={{0,3},{1,2},{2,1},{3,0},{4,5},{5,4},{6,7},{7,6},{8,11},{9,10},{10,... | collective-permute-start | bytes 1966088 | tf_op jit(solution)/shard_map/ppermute | solution.py:78
  95.3 0.8 slice.148
  96.1 2.7 %collective-permute-start.8 = (f32[4,1,4,32,256]{4,3,2,1,0:T(8,128)}, f32[4,1,4,32,256]{4,3,2,1,0:T(8,128)}, u32[]{:S(2)}, u32[]{:S(2)}) collective-permute-start(f32[4,1,4,32,256]{4,3,2,1,0:T(8,128)} %slice.148), channel_id=1, source_target_pairs={{0,24},{1,25},{2,26},{3,27},{4,12},{5,13},{6,14},{7,15},{8,16},{9,... | collective-permute-start | bytes 1572872 | tf_op jit(solution)/shard_map/ppermute | solution.py:78
  98.8 0.8 slice.149
  99.6 3.0 %collective-permute-start.9 = (f32[1,4,4,32,256]{4,3,2,1,0:T(8,128)}, f32[1,4,4,32,256]{4,3,2,1,0:T(8,128)}, u32[]{:S(2)}, u32[]{:S(2)}) collective-permute-start(f32[1,4,4,32,256]{4,3,2,1,0:T(8,128)} %slice.149), channel_id=1, source_target_pairs={{0,96},{1,97},{2,98},{3,99},{4,36},{5,37},{6,38},{7,39},{8,104},{9... | collective-permute-start | bytes 1572872 | tf_op jit(solution)/shard_map/ppermute | solution.py:78
  102.6 5.7 %all-to-all-start.1 = ((f32[128,4,384]{2,1,0:T(4,128)}), f32[128,4,384]{2,1,0:T(4,128)}, u32[]{:S(2)}, u32[]{:S(2)}) async-start(f32[128,4,384]{2,1,0:T(4,128)} %reshape.251), calls=%async_computation.1 | async-start | bytes 1572864 | tf_op jit(solution)/shard_map/all_to_all | solution.py:452
  108.4 3.8 %collective-permute-done.9 = f32[1,4,4,32,256]{4,3,2,1,0:T(8,128)} collective-permute-done((f32[1,4,4,32,256]{4,3,2,1,0:T(8,128)}, f32[1,4,4,32,256]{4,3,2,1,0:T(8,128)}, u32[]{:S(2)}, u32[]{:S(2)}) %collective-permute-start.9) | collective-permute-done | bytes 524320 | tf_op jit(solution)/shard_map/ppermute | solution.py:78
  112.2 1.3 slice_add_fusion.3
  113.6 1.2 slice_add_fusion.2
  115.0 1.1 slice_add_fusion.4
  116.4 3.8 %collective-permute-done.15 = f32[1,4,2,32,256]{4,3,2,1,0:T(8,128)S(1)} collective-permute-done((f32[1,4,2,32,256]{4,3,2,1,0:T(8,128)S(1)}, f32[1,4,2,32,256]{4,3,2,1,0:T(8,128)S(1)}, u32[]{:S(2)}, u32[]{:S(2)}) %collective-permute-start.15) | collective-permute-done | bytes 262176 | tf_op jit(solution)/shard_map/ppermute | solution.py:78
  120.3 2.4 %collective-permute-start.16 = (f32[1,4,1,32,256]{4,3,2,1,0:T(8,128)S(1)}, f32[1,4,1,32,256]{4,3,2,1,0:T(8,128)S(1)}, u32[]{:S(2)}, u32[]{:S(2)}) collective-permute-start(f32[1,4,1,32,256]{4,3,2,1,0:T(8,128)S(1)} %slice.199), channel_id=1, source_target_pairs={{0,3},{1,2},{2,1},{3,0},{4,5},{5,4},{6,7},{7,6},{8,11},{9,10},{10,... | collective-permute-start | bytes 393224 | tf_op jit(solution)/shard_map/ppermute | solution.py:78
  122.7 0.7 collective-permute-done.11
  123.5 2.3 %collective-permute-start.12 = (f32[4,1,1,48,256]{4,3,2,1,0:T(8,128)S(1)}, f32[4,1,1,48,256]{4,3,2,1,0:T(8,128)S(1)}, u32[]{:S(2)}, u32[]{:S(2)}) collective-permute-start(f32[4,1,1,48,256]{4,3,2,1,0:T(8,128)S(1)} %slice.193), channel_id=1, source_target_pairs={{0,24},{1,25},{2,26},{3,27},{4,12},{5,13},{6,14},{7,15},{8,16},{9,... | collective-permute-start | bytes 589832 | tf_op jit(solution)/shard_map/ppermute | solution.py:78
  125.8 3.6 %collective-permute-start.14 = (f32[1,1,4,32,256]{4,3,2,1,0:T(8,128)S(1)}, f32[1,1,4,32,256]{4,3,2,1,0:T(8,128)S(1)}, u32[]{:S(2)}, u32[]{:S(2)}) collective-permute-start(f32[1,1,4,32,256]{4,3,2,1,0:T(8,128)S(1)} %slice.196), channel_id=1, source_target_pairs={{0,96},{1,97},{2,98},{3,99},{4,36},{5,37},{6,38},{7,39},{8,104},{9... | collective-permute-start | bytes 393224 | tf_op jit(solution)/shard_map/ppermute | solution.py:78
  129.3 2.9 %collective-permute-done.14 = f32[1,1,4,32,256]{4,3,2,1,0:T(8,128)S(1)} collective-permute-done((f32[1,1,4,32,256]{4,3,2,1,0:T(8,128)S(1)}, f32[1,1,4,32,256]{4,3,2,1,0:T(8,128)S(1)}, u32[]{:S(2)}, u32[]{:S(2)}) %collective-permute-start.14) | collective-permute-done | bytes 131104 | tf_op jit(solution)/shard_map/ppermute | solution.py:78
  133.4 1.1 collective-permute-start.21
  134.5 2.6 %collective-permute-done.19 = f32[1,1,2,32,256]{4,3,2,1,0:T(8,128)S(1)} collective-permute-done((f32[1,1,2,32,256]{4,3,2,1,0:T(8,128)S(1)}, f32[1,1,2,32,256]{4,3,2,1,0:T(8,128)S(1)}, u32[]{:S(2)}, u32[]{:S(2)}) %collective-permute-start.19) | collective-permute-done | bytes 65568 | tf_op jit(solution)/shard_map/ppermute | solution.py:78
  137.1 1.2 collective-permute-start.20
  138.4 2.0 %collective-permute-start.22 = (f32[1,1,1,32,256]{4,3,2,1,0:T(8,128)S(1)}, f32[1,1,1,32,256]{4,3,2,1,0:T(8,128)S(1)}, u32[]{:S(2)}, u32[]{:S(2)}) collective-permute-start(f32[1,1,1,32,256]{4,3,2,1,0:T(8,128)S(1)} %slice.213), channel_id=1, source_target_pairs={{0,24},{1,25},{2,26},{3,27},{4,12},{5,13},{6,14},{7,15},{8,16},{9,... | collective-permute-start | bytes 98312 | tf_op jit(solution)/shard_map/ppermute | solution.py:78
  140.4 3.5 %collective-permute-start.18 = (f32[1,1,1,48,256]{4,3,2,1,0:T(8,128)S(1)}, f32[1,1,1,48,256]{4,3,2,1,0:T(8,128)S(1)}, u32[]{:S(2)}, u32[]{:S(2)}) collective-permute-start(f32[1,1,1,48,256]{4,3,2,1,0:T(8,128)S(1)} %slice.203), channel_id=1, source_target_pairs={{0,96},{1,97},{2,98},{3,99},{4,36},{5,37},{6,38},{7,39},{8,104},{9... | collective-permute-start | bytes 147464 | tf_op jit(solution)/shard_map/ppermute | solution.py:78
  143.9 2.0 %collective-permute-done.18 = f32[1,1,1,48,256]{4,3,2,1,0:T(8,128)S(1)} collective-permute-done((f32[1,1,1,48,256]{4,3,2,1,0:T(8,128)S(1)}, f32[1,1,1,48,256]{4,3,2,1,0:T(8,128)S(1)}, u32[]{:S(2)}, u32[]{:S(2)}) %collective-permute-start.18) | collective-permute-done | bytes 49184 | tf_op jit(solution)/shard_map/ppermute | solution.py:78
  146.6 2.7 %collective-permute-start.24 = (f32[112,256]{1,0:T(8,128)S(1)}, f32[112,256]{1,0:T(8,128)S(1)}, u32[]{:S(2)}, u32[]{:S(2)}) collective-permute-start(f32[112,256]{1,0:T(8,128)S(1)} %get-tuple-element.96), channel_id=1, source_target_pairs={{0,2},{1,3},{2,0},{3,1},{4,6},{5,7},{6,4},{7,5},{8,10},{9,11},{10,... | collective-permute-start | bytes 344072 | tf_op jit(solution)/shard_map/ppermute | solution.py:44
  149.3 1.5 collective-permute-start.25
  150.8 1.4 reshape.262.arrived_ref
  152.2 5.8 %row_update.1 = (f32[2048,256]{1,0:T(8,128)}, f32[2048,256]{1,0:T(8,128)}) custom-call(f32[512,384]{1,0:T(8,128)S(1)} %reshape.262.arrived_ref, f32[2048,256]{1,0:T(8,128)} %table_ref.1, f32[2048,256]{1,0:T(8,128)} %accum_ref.1), custom_call_target="tpu_custom_call" | custom-call | flops 1073741824 | bytes 8388608 | tf_op jit(solution)/shard_map/row_update/pallas_call | solution.py:355
  159.6 1.0 convolution_add_fusion
  160.6 0.7 pad_maximum_fusion.4
  (116 shorter events, 9.2 us)
Async XLA Ops:
  0.6 49.4 %copy-start = (bf16[768,256]{1,0:T(8,128)(2,1)S(1)}, bf16[768,256]{1,0:T(8,128)(2,1)}, u32[]{:S(2)}) copy-start(bf16[768,256]{1,0:T(8,128)(2,1)} %param.15) | copy-start | bytes 1179652
  0.6 4.3 %copy-start.6 = (s32[1,512]{1,0:T(1,128)S(1)}, s32[1,512]{1,0:T(1,128)}, u32[]{:S(2)}) copy-start(s32[1,512]{1,0:T(1,128)} %param.19) | copy-start | bytes 6148
  0.7 4.3 %copy-start.7 = (s32[1024]{0:T(1024)S(1)}, s32[1024]{0:T(1024)}, u32[]{:S(2)}) copy-start(s32[1024]{0:T(1024)} %param.18) | copy-start | bytes 12292
  1.4 1.0 copy-start.1
  2.5 2.5 %copy-start.2 = (bf16[1024,256]{1,0:T(8,128)(2,1)S(1)}, bf16[1024,256]{1,0:T(8,128)(2,1)}, u32[]{:S(2)}) copy-start(bf16[1024,256]{1,0:T(8,128)(2,1)} %grad_ref.3) | copy-start | bytes 1572868
  5.0 4.3 %collective-permute-start = (f32[1536,256]{1,0:T(8,128)}, f32[1536,256]{1,0:T(8,128)S(1)}, u32[]{:S(2)}, u32[]{:S(2)}) collective-permute-start(f32[1536,256]{1,0:T(8,128)} %segment_sums.2), channel_id=1, source_target_pairs={{0,4},{4,0},{1,5},{5,1},{2,6},{6,2},{3,7},{7,3},{8,12},{12,8},{9,1... | collective-permute-start | bytes 4718600 | tf_op jit(solution)/shard_map/ppermute | solution.py:39
  9.2 2.6 %copy-start.5 = (f32[768]{0:T(1024)S(1)}, f32[768]{0:T(1024)}, u32[]{:S(2)}) copy-start(f32[768]{0:T(1024)} %param.12) | copy-start | bytes 9220
  11.8 36.7 %all-to-all-start = ((f32[64,24,256]{2,1,0:T(8,128)}), f32[64,24,256]{2,1,0:T(8,128)}, u32[]{:S(2)}, u32[]{:S(2)}) async-start(f32[64,24,256]{2,1,0:T(8,128)} %bitcast.4), calls=%async_computation | async-start | bytes 3145728 | tf_op jit(solution)/shard_map/all_to_all | solution.py:401
  61.8 11.6 %collective-permute-start.1 = (f32[64,40,256]{2,1,0:T(8,128)S(1)}, f32[64,40,256]{2,1,0:T(8,128)S(1)}, u32[]{:S(2)}, u32[]{:S(2)}) collective-permute-start(f32[64,40,256]{2,1,0:T(8,128)S(1)} %get-tuple-element.53), channel_id=1, source_target_pairs={{0,4},{4,0},{1,5},{5,1},{2,6},{6,2},{3,7},{7,3},{8,12},{12,8},{9,1... | collective-permute-start | bytes 7864328 | tf_op jit(solution)/shard_map/ppermute | solution.py:39
  67.2 5.8 %collective-permute-start.5 = (f32[64,32,256]{2,1,0:T(8,128)S(1)}, f32[64,32,256]{2,1,0:T(8,128)S(1)}, u32[]{:S(2)}, u32[]{:S(2)}) collective-permute-start(f32[64,32,256]{2,1,0:T(8,128)S(1)} %get-tuple-element.58), channel_id=1, source_target_pairs={{0,4},{4,0},{1,5},{5,1},{2,6},{6,2},{3,7},{7,3},{8,12},{12,8},{9,1... | collective-permute-start | bytes 6291464 | tf_op jit(solution)/shard_map/ppermute | solution.py:39
  72.9 4.2 %collective-permute-start.3 = (f32[64,32,256]{2,1,0:T(8,128)S(1)}, f32[64,32,256]{2,1,0:T(8,128)S(1)}, u32[]{:S(2)}, u32[]{:S(2)}) collective-permute-start(f32[64,32,256]{2,1,0:T(8,128)S(1)} %get-tuple-element.56), channel_id=1, source_target_pairs={{0,4},{4,0},{1,5},{5,1},{2,6},{6,2},{3,7},{7,3},{8,12},{12,8},{9,1... | collective-permute-start | bytes 6291464 | tf_op jit(solution)/shard_map/ppermute | solution.py:39
  73.8 18.7 %collective-permute-start.2 = (f32[4,4,2,40,256]{4,3,2,1,0:T(8,128)S(1)}, f32[4,4,2,40,256]{4,3,2,1,0:T(8,128)S(1)}, u32[]{:S(2)}, u32[]{:S(2)}) collective-permute-start(f32[4,4,2,40,256]{4,3,2,1,0:T(8,128)S(1)} %slice.184), channel_id=1, source_target_pairs={{0,1},{1,0},{2,3},{3,2},{4,7},{5,6},{6,5},{7,4},{8,9},{9,8},{10,11... | collective-permute-start | bytes 3932168 | tf_op jit(solution)/shard_map/ppermute | solution.py:78
  74.8 3.8 %slice-start = ((s8[4718592]{0:T(1024)(128)(4,1)}), s8[4194304]{0:T(1024)(128)(4,1)S(1)}, s32[]{:S(2)}) async-start(s8[4718592]{0:T(1024)(128)(4,1)} %bitcast.43), calls=%async_computation.2 | async-start | bytes 8388608
  74.9 15.5 %collective-permute-start.6 = (f32[2,4,4,32,256]{4,3,2,1,0:T(8,128)S(1)}, f32[2,4,4,32,256]{4,3,2,1,0:T(8,128)S(1)}, u32[]{:S(2)}, u32[]{:S(2)}) collective-permute-start(f32[2,4,4,32,256]{4,3,2,1,0:T(8,128)S(1)} %bitcast.52), channel_id=1, source_target_pairs={{0,32},{1,33},{2,34},{3,35},{4,100},{5,101},{6,102},{7,103},{8,40}... | collective-permute-start | bytes 3145736 | tf_op jit(solution)/shard_map/ppermute | solution.py:78
  77.1 1.5 slice-start.1
  77.1 1.8 %copy-start.3 = (bf16[24,64,768]{2,1,0:T(8,128)(2,1)S(1)}, bf16[24,64,768]{2,1,0:T(8,128)(2,1)}, u32[]{:S(2)}) copy-start(bf16[24,64,768]{2,1,0:T(8,128)(2,1)} %param.11) | copy-start | bytes 7077892
  77.6 14.9 %collective-permute-start.4 = (f32[4,2,4,32,256]{4,3,2,1,0:T(8,128)S(1)}, f32[4,2,4,32,256]{4,3,2,1,0:T(8,128)S(1)}, u32[]{:S(2)}, u32[]{:S(2)}) collective-permute-start(f32[4,2,4,32,256]{4,3,2,1,0:T(8,128)S(1)} %slice.185), channel_id=1, source_target_pairs={{0,8},{1,9},{2,10},{3,11},{4,28},{5,29},{6,30},{7,31},{8,0},{9,1},... | collective-permute-start | bytes 3145736 | tf_op jit(solution)/shard_map/ppermute | solution.py:78
  93.0 6.6 %copy-start.4 = (f32[2,4,4,32,256]{4,3,2,1,0:T(8,128)}, f32[2,4,4,32,256]{4,3,2,1,0:T(8,128)S(1)}, u32[]{:S(2)}) copy-start(f32[2,4,4,32,256]{4,3,2,1,0:T(8,128)S(1)} %add.165) | copy-start | bytes 3145732
  93.1 19.1 %collective-permute-start.7 = (f32[4,4,1,40,256]{4,3,2,1,0:T(8,128)S(1)}, f32[4,4,1,40,256]{4,3,2,1,0:T(8,128)}, u32[]{:S(2)}, u32[]{:S(2)}) collective-permute-start(f32[4,4,1,40,256]{4,3,2,1,0:T(8,128)S(1)} %slice.147), channel_id=1, source_target_pairs={{0,3},{1,2},{2,1},{3,0},{4,5},{5,4},{6,7},{7,6},{8,11},{9,10},{10,... | collective-permute-start | bytes 1966088 | tf_op jit(solution)/shard_map/ppermute | solution.py:78
  96.1 12.3 %collective-permute-start.8 = (f32[4,1,4,32,256]{4,3,2,1,0:T(8,128)}, f32[4,1,4,32,256]{4,3,2,1,0:T(8,128)}, u32[]{:S(2)}, u32[]{:S(2)}) collective-permute-start(f32[4,1,4,32,256]{4,3,2,1,0:T(8,128)} %slice.148), channel_id=1, source_target_pairs={{0,24},{1,25},{2,26},{3,27},{4,12},{5,13},{6,14},{7,15},{8,16},{9,... | collective-permute-start | bytes 1572872 | tf_op jit(solution)/shard_map/ppermute | solution.py:78
  99.6 12.6 %collective-permute-start.9 = (f32[1,4,4,32,256]{4,3,2,1,0:T(8,128)}, f32[1,4,4,32,256]{4,3,2,1,0:T(8,128)}, u32[]{:S(2)}, u32[]{:S(2)}) collective-permute-start(f32[1,4,4,32,256]{4,3,2,1,0:T(8,128)} %slice.149), channel_id=1, source_target_pairs={{0,96},{1,97},{2,98},{3,99},{4,36},{5,37},{6,38},{7,39},{8,104},{9... | collective-permute-start | bytes 1572872 | tf_op jit(solution)/shard_map/ppermute | solution.py:78
  102.6 5.7 %collective-permute-start.10 = (f32[8,768]{1,0:T(8,128)S(1)}, f32[8,768]{1,0:T(8,128)S(1)}, u32[]{:S(2)}, u32[]{:S(2)}) collective-permute-start(f32[8,768]{1,0:T(8,128)S(1)} %get-tuple-element.69), channel_id=1, source_target_pairs={{0,4},{4,0},{1,5},{5,1},{2,6},{6,2},{3,7},{7,3},{8,12},{12,8},{9,1... | collective-permute-start | bytes 73736 | tf_op jit(solution)/shard_map/ppermute | solution.py:39
  102.6 26.7 %all-to-all-start.1 = ((f32[128,4,384]{2,1,0:T(4,128)}), f32[128,4,384]{2,1,0:T(4,128)}, u32[]{:S(2)}, u32[]{:S(2)}) async-start(f32[128,4,384]{2,1,0:T(4,128)} %reshape.251), calls=%async_computation.1 | async-start | bytes 1572864 | tf_op jit(solution)/shard_map/all_to_all | solution.py:452
  113.5 6.7 %collective-permute-start.15 = (f32[1,4,2,32,256]{4,3,2,1,0:T(8,128)S(1)}, f32[1,4,2,32,256]{4,3,2,1,0:T(8,128)S(1)}, u32[]{:S(2)}, u32[]{:S(2)}) collective-permute-start(f32[1,4,2,32,256]{4,3,2,1,0:T(8,128)S(1)} %slice.198), channel_id=1, source_target_pairs={{0,1},{1,0},{2,3},{3,2},{4,7},{5,6},{6,5},{7,4},{8,9},{9,8},{10,11... | collective-permute-start | bytes 786440 | tf_op jit(solution)/shard_map/ppermute | solution.py:78
  114.9 8.5 %collective-permute-start.11 = (f32[4,2,1,48,256]{4,3,2,1,0:T(8,128)S(1)}, f32[4,2,1,48,256]{4,3,2,1,0:T(8,128)S(1)}, u32[]{:S(2)}, u32[]{:S(2)}) collective-permute-start(f32[4,2,1,48,256]{4,3,2,1,0:T(8,128)S(1)} %pad_maximum_fusion.3), channel_id=1, source_target_pairs={{0,8},{1,9},{2,10},{3,11},{4,28},{5,29},{6,30},{7,31},{8,0},{9,1},... | collective-permute-start | bytes 1179656 | tf_op jit(solution)/shard_map/ppermute | solution.py:78
  116.1 9.6 %collective-permute-start.13 = (f32[2,1,4,32,256]{4,3,2,1,0:T(8,128)S(1)}, f32[2,1,4,32,256]{4,3,2,1,0:T(8,128)S(1)}, u32[]{:S(2)}, u32[]{:S(2)}) collective-permute-start(f32[2,1,4,32,256]{4,3,2,1,0:T(8,128)S(1)} %slice.195), channel_id=1, source_target_pairs={{0,32},{1,33},{2,34},{3,35},{4,100},{5,101},{6,102},{7,103},{8,40}... | collective-permute-start | bytes 786440 | tf_op jit(solution)/shard_map/ppermute | solution.py:78
  120.3 9.1 %collective-permute-start.16 = (f32[1,4,1,32,256]{4,3,2,1,0:T(8,128)S(1)}, f32[1,4,1,32,256]{4,3,2,1,0:T(8,128)S(1)}, u32[]{:S(2)}, u32[]{:S(2)}) collective-permute-start(f32[1,4,1,32,256]{4,3,2,1,0:T(8,128)S(1)} %slice.199), channel_id=1, source_target_pairs={{0,3},{1,2},{2,1},{3,0},{4,5},{5,4},{6,7},{7,6},{8,11},{9,10},{10,... | collective-permute-start | bytes 393224 | tf_op jit(solution)/shard_map/ppermute | solution.py:78
  123.5 8.8 %collective-permute-start.12 = (f32[4,1,1,48,256]{4,3,2,1,0:T(8,128)S(1)}, f32[4,1,1,48,256]{4,3,2,1,0:T(8,128)S(1)}, u32[]{:S(2)}, u32[]{:S(2)}) collective-permute-start(f32[4,1,1,48,256]{4,3,2,1,0:T(8,128)S(1)} %slice.193), channel_id=1, source_target_pairs={{0,24},{1,25},{2,26},{3,27},{4,12},{5,13},{6,14},{7,15},{8,16},{9,... | collective-permute-start | bytes 589832 | tf_op jit(solution)/shard_map/ppermute | solution.py:78
  125.8 6.5 %collective-permute-start.14 = (f32[1,1,4,32,256]{4,3,2,1,0:T(8,128)S(1)}, f32[1,1,4,32,256]{4,3,2,1,0:T(8,128)S(1)}, u32[]{:S(2)}, u32[]{:S(2)}) collective-permute-start(f32[1,1,4,32,256]{4,3,2,1,0:T(8,128)S(1)} %slice.196), channel_id=1, source_target_pairs={{0,96},{1,97},{2,98},{3,99},{4,36},{5,37},{6,38},{7,39},{8,104},{9... | collective-permute-start | bytes 393224 | tf_op jit(solution)/shard_map/ppermute | solution.py:78
  132.3 8.0 %collective-permute-start.17 = (f32[2,1,1,48,256]{4,3,2,1,0:T(8,128)S(1)}, f32[2,1,1,48,256]{4,3,2,1,0:T(8,128)S(1)}, u32[]{:S(2)}, u32[]{:S(2)}) collective-permute-start(f32[2,1,1,48,256]{4,3,2,1,0:T(8,128)S(1)} %slice.201), channel_id=1, source_target_pairs={{0,32},{1,33},{2,34},{3,35},{4,100},{5,101},{6,102},{7,103},{8,40}... | collective-permute-start | bytes 294920 | tf_op jit(solution)/shard_map/ppermute | solution.py:78
  132.7 4.3 %collective-permute-start.19 = (f32[1,1,2,32,256]{4,3,2,1,0:T(8,128)S(1)}, f32[1,1,2,32,256]{4,3,2,1,0:T(8,128)S(1)}, u32[]{:S(2)}, u32[]{:S(2)}) collective-permute-start(f32[1,1,2,32,256]{4,3,2,1,0:T(8,128)S(1)} %slice.206), channel_id=1, source_target_pairs={{0,1},{1,0},{2,3},{3,2},{4,7},{5,6},{6,5},{7,4},{8,9},{9,8},{10,11... | collective-permute-start | bytes 196616 | tf_op jit(solution)/shard_map/ppermute | solution.py:78
  133.4 4.9 %collective-permute-start.21 = (f32[1,2,1,32,256]{4,3,2,1,0:T(8,128)S(1)}, f32[1,2,1,32,256]{4,3,2,1,0:T(8,128)S(1)}, u32[]{:S(2)}, u32[]{:S(2)}) collective-permute-start(f32[1,2,1,32,256]{4,3,2,1,0:T(8,128)S(1)} %slice.211), channel_id=1, source_target_pairs={{0,8},{1,9},{2,10},{3,11},{4,28},{5,29},{6,30},{7,31},{8,0},{9,1},... | collective-permute-start | bytes 196616 | tf_op jit(solution)/shard_map/ppermute | solution.py:78
  137.1 6.8 %collective-permute-start.20 = (f32[1,1,1,32,256]{4,3,2,1,0:T(8,128)S(1)}, f32[1,1,1,32,256]{4,3,2,1,0:T(8,128)S(1)}, u32[]{:S(2)}, u32[]{:S(2)}) collective-permute-start(f32[1,1,1,32,256]{4,3,2,1,0:T(8,128)S(1)} %slice.208), channel_id=1, source_target_pairs={{0,3},{1,2},{2,1},{3,0},{4,5},{5,4},{6,7},{7,6},{8,11},{9,10},{10,... | collective-permute-start | bytes 98312 | tf_op jit(solution)/shard_map/ppermute | solution.py:78
  138.4 5.5 %collective-permute-start.22 = (f32[1,1,1,32,256]{4,3,2,1,0:T(8,128)S(1)}, f32[1,1,1,32,256]{4,3,2,1,0:T(8,128)S(1)}, u32[]{:S(2)}, u32[]{:S(2)}) collective-permute-start(f32[1,1,1,32,256]{4,3,2,1,0:T(8,128)S(1)} %slice.213), channel_id=1, source_target_pairs={{0,24},{1,25},{2,26},{3,27},{4,12},{5,13},{6,14},{7,15},{8,16},{9,... | collective-permute-start | bytes 98312 | tf_op jit(solution)/shard_map/ppermute | solution.py:78
  140.4 5.5 %collective-permute-start.18 = (f32[1,1,1,48,256]{4,3,2,1,0:T(8,128)S(1)}, f32[1,1,1,48,256]{4,3,2,1,0:T(8,128)S(1)}, u32[]{:S(2)}, u32[]{:S(2)}) collective-permute-start(f32[1,1,1,48,256]{4,3,2,1,0:T(8,128)S(1)} %slice.203), channel_id=1, source_target_pairs={{0,96},{1,97},{2,98},{3,99},{4,36},{5,37},{6,38},{7,39},{8,104},{9... | collective-permute-start | bytes 147464 | tf_op jit(solution)/shard_map/ppermute | solution.py:78
  146.0 11.9 %collective-permute-start.23 = (f32[112,256]{1,0:T(8,128)S(1)}, f32[112,256]{1,0:T(8,128)S(1)}, u32[]{:S(2)}, u32[]{:S(2)}) collective-permute-start(f32[112,256]{1,0:T(8,128)S(1)} %get-tuple-element.96), channel_id=1, source_target_pairs={{0,1},{1,0},{2,3},{3,2},{4,5},{5,4},{6,7},{7,6},{8,9},{9,8},{10,11... | collective-permute-start | bytes 344072 | tf_op jit(solution)/shard_map/ppermute | solution.py:44
  146.6 11.3 %collective-permute-start.24 = (f32[112,256]{1,0:T(8,128)S(1)}, f32[112,256]{1,0:T(8,128)S(1)}, u32[]{:S(2)}, u32[]{:S(2)}) collective-permute-start(f32[112,256]{1,0:T(8,128)S(1)} %get-tuple-element.96), channel_id=1, source_target_pairs={{0,2},{1,3},{2,0},{3,1},{4,6},{5,7},{6,4},{7,5},{8,10},{9,11},{10,... | collective-permute-start | bytes 344072 | tf_op jit(solution)/shard_map/ppermute | solution.py:44
  149.3 8.7 %collective-permute-start.25 = (f32[112,256]{1,0:T(8,128)S(1)}, f32[112,256]{1,0:T(8,128)S(1)}, u32[]{:S(2)}, u32[]{:S(2)}) collective-permute-start(f32[112,256]{1,0:T(8,128)S(1)} %get-tuple-element.96), channel_id=1, source_target_pairs={{0,3},{1,2},{2,1},{3,0},{4,7},{5,6},{6,5},{7,4},{8,11},{9,10},{10,... | collective-permute-start | bytes 344072 | tf_op jit(solution)/shard_map/ppermute | solution.py:44

commit v9 on v8

--- a/solution.py
+++ b/solution.py
@@ -118,7 +118,7 @@
         compiler_params=pltpu.CompilerParams(vmem_limit_bytes=24 << 20),
         cost_estimate=cost(2 * samples * width_e * count, 4 * width_e * count),
         name="segment_sums",
-    )(key.reshape(1, samples), sample_grad, *more)
+    )(key.reshape(1, samples), pltpu.with_memory_space_constraint(sample_grad, pltpu.HBM), *more)
 
 
 def forward_kernel(units, titles_ref, gain_ref, w_ref, normed_ref, slope_ref, act_ref, mean_ref):
@@ -350,7 +350,7 @@
 
 def row_update(arrived, table, accum):
     rows, width_e = table.shape
-    step = 512
+    step = 256
     tile = pl.BlockSpec((step, width_e), lambda i: (i, 0))
     return pl.pallas_call(
         rows_kernel,
@@ -457,10 +457,9 @@
     parts[0] = jnp.concatenate([parts[0], gain_term], axis=3)
     parts, _ = halve(parts, "yzx", False)
     parts, (row_all,) = halve(parts, "yzx", True, (row_all,))
-    new_table, new_accum = row_update(
-        row_all.reshape(slot_count, width_e + 128), table, accum
-    )
-    parts, _ = halve(parts, "zxy", False)
+    row_all = row_all.reshape(slot_count, width_e + 128)
+    parts, (row_all,) = halve(parts, "zxy", False, (row_all,))
+    new_table, new_accum = row_update(row_all, table, accum)
     parts, _ = halve(parts, "zxy", True)
 
     flat = [part.reshape(-1, width_e) for part in parts]

time: 162 us -> 165 us (1.019)
  Pallas kernels: 60.8 us -> 65 us
  local copies, waits for them, and re-layouts: 9.74 us -> 6.34 us
  waiting for transfers between devices: 19.3 us -> 21 us
    pallas_call x1, Pallas kernels: 5.76 us -> 7.92 us  [row_update(): pl.pallas_call(rows_kernel, grid=(rows // step,), in_specs=[pl.BlockSpec(...]
    pallas_call x2, Pallas kernels: 4.98 us -> 7.06 us  [segment_sums(): pl.pallas_call(item_kernel, grid=(count // step,), in_specs=[pl.BlockSpec...]
  transfers between devices with their start and end apart: 28 -> 28, of which waited for: 9 -> 12; matrix products, arithmetic and copies ran while one was open for 10% -> 9% of each run, Pallas kernels for 30% -> 31%
where the time goes in v9:
time: 165 us; the launch traced here: 164 us
  Pallas kernels  65 us (39%)
  starting transfers between devices  51.9 us (31%)
  waiting for transfers between devices  21 us (13%)
  matrix products  9.57 us (6%)
  other arithmetic  8.86 us (5%)
  local copies, waits for them, and re-layouts  6.34 us (4%)
    ppermute x18, starting transfers between devices, halve(): lax.ppermute(lax.slice_in_dim(part, middle, None, axis=dim), DEVICES, par...  28.8 us
    pallas_call x1, Pallas kernels, forward(): pl.pallas_call(functools.partial(forward_kernel, units), grid=(hidden //...  20.5 us
    ppermute x18, waiting for transfers between devices, halve(): lax.ppermute(lax.slice_in_dim(part, middle, None, axis=dim), DEVICES, par...  19.1 us
    pallas_call x3, Pallas kernels, up_products(): pl.pallas_call(kernel, grid_spec=pltpu.PrefetchScalarGridSpec(num_scalar_...  18 us
    all_to_all x1, starting transfers between devices, per_device(): item_all = lax.all_to_all(mine, CHIPS, 0, 0, tiled=True)  11.7 us
    pallas_call x1, Pallas kernels, title_grads(): pl.pallas_call(titles_kernel, grid=(rows // step,), in_specs=[pl.BlockSpe...  11.5 us
    pallas_call x1, Pallas kernels, row_update(): pl.pallas_call(rows_kernel, grid=(rows // step,), in_specs=[pl.BlockSpec(...  7.92 us
    pallas_call x2, Pallas kernels, segment_sums(): pl.pallas_call(item_kernel, grid=(count // step,), in_specs=[pl.BlockSpec...  7.06 us
  transfers between devices with their start and end apart: 28, of which 12 were waited for; matrix products, arithmetic and copies ran while one was open for 9% of the time, Pallas kernels for 31%

profile of v9, /device:TPU:0, one launch (start us, length us, event | category | flops | bytes accessed | tf_op | source)
XLA Modules:
  0.0 163.9 jit_solution(5379464633217968800)
XLA Ops:
  0.7 0.8 broadcast_select_fusion
  1.5 3.5 %segment_sums.2 = f32[1536,256]{1,0:T(8,128)} custom-call(s32[1,1024]{1,0:T(1,128)S(1)} %bitcast.42, bf16[1024,256]{1,0:T(8,128)(2,1)} %grad_ref.3), custom_call_target="tpu_custom_call" | custom-call | flops 805306368 | bytes 1572864 | tf_op jit(solution)/shard_map/segment_sums/pallas_call | solution.py:108
  6.1 1.1 reshape.251
  7.3 1.3 collective-permute-done.refs_0_
  8.6 3.5 %segment_sums.3 = f32[1536,256]{1,0:T(8,128)} custom-call(s32[1,1024]{1,0:T(1,128)S(1)} %bitcast.41, bf16[1024,256]{1,0:T(8,128)(2,1)} %grad_ref.3, f32[1536,256]{1,0:T(8,128)S(1)} %collective-permute-done.refs_0_), custom_call_target="tpu_custom_call" | custom-call | flops 805306368 | bytes 1572864 | tf_op jit(solution)/shard_map/segment_sums/pallas_call | solution.py:108
  12.2 11.7 %all-to-all-start = ((f32[64,24,256]{2,1,0:T(8,128)}), f32[64,24,256]{2,1,0:T(8,128)}, u32[]{:S(2)}, u32[]{:S(2)}) async-start(f32[64,24,256]{2,1,0:T(8,128)} %bitcast.4), calls=%async_computation | async-start | bytes 3145728 | tf_op jit(solution)/shard_map/all_to_all | solution.py:401
  23.9 20.5 %forward.1 = (bf16[1536,768]{1,0:T(8,128)(2,1)S(1)}, bf16[1536,3072]{1,0:T(8,128)(2,1)}, f32[24,3072]{1,0:T(8,128)S(1)}, f32[24,768]{1,0:T(8,128)S(1)}) custom-call(bf16[1536,768]{1,0:T(8,128)(2,1)} %bitcast.45, f32[1,768]{1,0:T(1,128)S(1)} %reshape.250.gain_ref, bf16[768,3072]{1,0:T(8,128)(2,1)} %w_ref.3), custom_call_target="tpu_custom_call" | custom-call | flops 28991029248 | bytes 18874368 | tf_op jit(solution)/shard_map/forward/pallas_call | solution.py:156
  44.5 3.8 %fusion.3.pool_ref = bf16[24,1024]{1,0:T(8,128)(2,1)S(1)} fusion(s32[1024]{0:T(1024)S(1)} %fusion.31, f32[24,768]{1,0:T(8,128)S(1)} %get-tuple-element.51, bf16[24,3072]{1,0:T(8,128)(2,1)S(1)} %convert_element_type.35.mean_ref, bf16[3072,768]{1,0:T(8,128)(2,1)} %param.14), kind=kOutput, calls=%fused_computation.8 | convolution fusion | flops 151842816 | bytes 4993024 | tf_op jit(solution)/shard_map/dot_general | solution.py:424
  48.5 1.5 reduce_sum.29.grad_ref
  50.3 3.7 %convolution_multiply_fusion.act_ref = f32[24,3072]{1,0:T(8,128)S(1)} fusion(bf16[3072,768]{1,0:T(8,128)(2,1)} %param.14, f32[24,768]{1,0:T(8,128)S(1)} %fusion.46.pool_ref), kind=kOutput, calls=%fused_computation | convolution fusion | flops 113338368 | bytes 5087232 | tf_op jit(solution)/shard_map/dot_general | solution.py:29
  54.0 7.8 %first_products.1 = (bf16[1536,3072]{1,0:T(8,128)(2,1)S(1)}, f32[64,40,256]{2,1,0:T(8,128)S(1)}, f32[64,40,256]{2,1,0:T(8,128)S(1)}) custom-call(s32[1]{0:T(128)} %bitcast.core_ref, s32[3,4]{1,0:T(4,128)S(1)} %pad_add_fusion.keep_at, s32[3,4]{1,0:T(4,128)S(1)} %pad_add_fusion.1.send_at, bf16[1536,3072]{1,0:T(8,128)(2,1)} %get-tuple-element.49.slope_ref, ...), custom_call_target="tpu_custom_call" | custom-call | flops 2415919104 | bytes 18874368 | tf_op jit(solution)/shard_map/first_products/pallas_call | solution.py:267
  62.0 5.1 %other_products.3 = (f32[64,32,256]{2,1,0:T(8,128)S(1)}, f32[64,32,256]{2,1,0:T(8,128)S(1)}) custom-call(s32[1]{0:T(128)} %bitcast.core_ref, s32[3,4]{1,0:T(4,128)S(1)} %pad_add_fusion.keep_at, s32[3,4]{1,0:T(4,128)S(1)} %pad_add_fusion.1.send_at, bf16[1536,3072]{1,0:T(8,128)(2,1)S(1)} %get-tuple-element.58.pre_ref, ...), custom_call_target="tpu_custom_call" | custom-call | flops 2415919104 | bytes 18874368 | tf_op jit(solution)/shard_map/other_products/pallas_call | solution.py:267
  67.7 5.1 %other_products.2 = (f32[64,32,256]{2,1,0:T(8,128)S(1)}, f32[64,32,256]{2,1,0:T(8,128)S(1)}) custom-call(s32[1]{0:T(128)} %bitcast.core_ref, s32[3,4]{1,0:T(4,128)S(1)} %pad_add_fusion.keep_at, s32[3,4]{1,0:T(4,128)S(1)} %pad_add_fusion.1.send_at, bf16[1536,3072]{1,0:T(8,128)(2,1)S(1)} %get-tuple-element.58.pre_ref, ...), custom_call_target="tpu_custom_call" | custom-call | flops 2415919104 | bytes 18874368 | tf_op jit(solution)/shard_map/other_products/pallas_call | solution.py:267
  73.8 1.3 collective-permute-start.2
  75.2 1.6 collective-permute-start.6
  77.6 1.3 collective-permute-start.4
  79.0 11.5 %title_grads.1 = (bf16[1536,768]{1,0:T(8,128)(2,1)}, f32[8,768]{1,0:T(8,128)S(1)}) custom-call(bf16[1536,3072]{1,0:T(8,128)(2,1)S(1)} %get-tuple-element.58.pre_ref, bf16[768,3072]{1,0:T(8,128)(2,1)S(1)} %bitcast.44, bf16[1536,768]{1,0:T(8,128)(2,1)S(1)} %bitcast.46, f32[1,768]{1,0:T(1,128)S(1)} %reshape.250.gain_ref, f32[24,768]{1,0:T(8,128)S(1)} %fusion.46.pool_ref), custom_call_target="tpu_custom_call" | custom-call | flops 7247757312 | bytes 9437184 | tf_op jit(solution)/shard_map/title_grads/pallas_call | solution.py:312
  90.5 2.0 %collective-permute-done.4 = f32[4,2,4,32,256]{4,3,2,1,0:T(8,128)S(1)} collective-permute-done((f32[4,2,4,32,256]{4,3,2,1,0:T(8,128)S(1)}, f32[4,2,4,32,256]{4,3,2,1,0:T(8,128)S(1)}, u32[]{:S(2)}, u32[]{:S(2)}) %collective-permute-start.4) | collective-permute-done | bytes 1048608 | tf_op jit(solution)/shard_map/ppermute | solution.py:78
  93.1 2.5 %collective-permute-start.7 = (f32[4,4,1,40,256]{4,3,2,1,0:T(8,128)S(1)}, f32[4,4,1,40,256]{4,3,2,1,0:T(8,128)}, u32[]{:S(2)}, u32[]{:S(2)}) collective-permute-start(f32[4,4,1,40,256]{4,3,2,1,0:T(8,128)S(1)} %slice.147), channel_id=1, source_target_pairs={{0,3},{1,2},{2,1},{3,0},{4,5},{5,4},{6,7},{7,6},{8,11},{9,10},{10,... | collective-permute-start | bytes 1966088 | tf_op jit(solution)/shard_map/ppermute | solution.py:78
  95.6 0.9 slice.148
  96.4 2.7 %collective-permute-start.8 = (f32[4,1,4,32,256]{4,3,2,1,0:T(8,128)}, f32[4,1,4,32,256]{4,3,2,1,0:T(8,128)}, u32[]{:S(2)}, u32[]{:S(2)}) collective-permute-start(f32[4,1,4,32,256]{4,3,2,1,0:T(8,128)} %slice.148), channel_id=1, source_target_pairs={{0,24},{1,25},{2,26},{3,27},{4,12},{5,13},{6,14},{7,15},{8,16},{9,... | collective-permute-start | bytes 1572872 | tf_op jit(solution)/shard_map/ppermute | solution.py:78
  99.1 0.8 slice.149
  100.0 3.0 %collective-permute-start.9 = (f32[1,4,4,32,256]{4,3,2,1,0:T(8,128)}, f32[1,4,4,32,256]{4,3,2,1,0:T(8,128)}, u32[]{:S(2)}, u32[]{:S(2)}) collective-permute-start(f32[1,4,4,32,256]{4,3,2,1,0:T(8,128)} %slice.149), channel_id=1, source_target_pairs={{0,96},{1,97},{2,98},{3,99},{4,36},{5,37},{6,38},{7,39},{8,104},{9... | collective-permute-start | bytes 1572872 | tf_op jit(solution)/shard_map/ppermute | solution.py:78
  102.9 5.7 %all-to-all-start.1 = ((f32[128,4,384]{2,1,0:T(4,128)}), f32[128,4,384]{2,1,0:T(4,128)}, u32[]{:S(2)}, u32[]{:S(2)}) async-start(f32[128,4,384]{2,1,0:T(4,128)} %reshape.251), calls=%async_computation.1 | async-start | bytes 1572864 | tf_op jit(solution)/shard_map/all_to_all | solution.py:452
  108.7 3.8 %collective-permute-done.9 = f32[1,4,4,32,256]{4,3,2,1,0:T(8,128)} collective-permute-done((f32[1,4,4,32,256]{4,3,2,1,0:T(8,128)}, f32[1,4,4,32,256]{4,3,2,1,0:T(8,128)}, u32[]{:S(2)}, u32[]{:S(2)}) %collective-permute-start.9) | collective-permute-done | bytes 524320 | tf_op jit(solution)/shard_map/ppermute | solution.py:78
  112.5 1.3 slice_add_fusion.3
  113.9 1.2 slice_add_fusion.2
  115.3 1.1 slice_add_fusion.4
  116.7 3.8 %collective-permute-done.15 = f32[1,4,2,32,256]{4,3,2,1,0:T(8,128)S(1)} collective-permute-done((f32[1,4,2,32,256]{4,3,2,1,0:T(8,128)S(1)}, f32[1,4,2,32,256]{4,3,2,1,0:T(8,128)S(1)}, u32[]{:S(2)}, u32[]{:S(2)}) %collective-permute-start.15) | collective-permute-done | bytes 262176 | tf_op jit(solution)/shard_map/ppermute | solution.py:78
  120.6 2.4 %collective-permute-start.16 = (f32[1,4,1,32,256]{4,3,2,1,0:T(8,128)S(1)}, f32[1,4,1,32,256]{4,3,2,1,0:T(8,128)S(1)}, u32[]{:S(2)}, u32[]{:S(2)}) collective-permute-start(f32[1,4,1,32,256]{4,3,2,1,0:T(8,128)S(1)} %slice.199), channel_id=1, source_target_pairs={{0,3},{1,2},{2,1},{3,0},{4,5},{5,4},{6,7},{7,6},{8,11},{9,10},{10,... | collective-permute-start | bytes 393224 | tf_op jit(solution)/shard_map/ppermute | solution.py:78
  123.0 0.7 collective-permute-done.11
  123.8 2.2 %collective-permute-start.12 = (f32[4,1,1,48,256]{4,3,2,1,0:T(8,128)S(1)}, f32[4,1,1,48,256]{4,3,2,1,0:T(8,128)S(1)}, u32[]{:S(2)}, u32[]{:S(2)}) collective-permute-start(f32[4,1,1,48,256]{4,3,2,1,0:T(8,128)S(1)} %slice.193), channel_id=1, source_target_pairs={{0,24},{1,25},{2,26},{3,27},{4,12},{5,13},{6,14},{7,15},{8,16},{9,... | collective-permute-start | bytes 589832 | tf_op jit(solution)/shard_map/ppermute | solution.py:78
  126.1 3.6 %collective-permute-start.14 = (f32[1,1,4,32,256]{4,3,2,1,0:T(8,128)S(1)}, f32[1,1,4,32,256]{4,3,2,1,0:T(8,128)S(1)}, u32[]{:S(2)}, u32[]{:S(2)}) collective-permute-start(f32[1,1,4,32,256]{4,3,2,1,0:T(8,128)S(1)} %slice.196), channel_id=1, source_target_pairs={{0,96},{1,97},{2,98},{3,99},{4,36},{5,37},{6,38},{7,39},{8,104},{9... | collective-permute-start | bytes 393224 | tf_op jit(solution)/shard_map/ppermute | solution.py:78
  129.7 2.9 %collective-permute-done.14 = f32[1,1,4,32,256]{4,3,2,1,0:T(8,128)S(1)} collective-permute-done((f32[1,1,4,32,256]{4,3,2,1,0:T(8,128)S(1)}, f32[1,1,4,32,256]{4,3,2,1,0:T(8,128)S(1)}, u32[]{:S(2)}, u32[]{:S(2)}) %collective-permute-start.14) | collective-permute-done | bytes 131104 | tf_op jit(solution)/shard_map/ppermute | solution.py:78
  133.4 1.5 collective-permute-start.18
  134.8 1.4 reshape.255.arrived_ref
  136.2 0.8 collective-permute-done.19
  137.0 0.7 collective-permute-done.18
  137.7 3.3 %collective-permute-start.20 = (f32[1,1,1,48,256]{4,3,2,1,0:T(8,128)S(1)}, f32[1,1,1,48,256]{4,3,2,1,0:T(8,128)S(1)}, u32[]{:S(2)}, u32[]{:S(2)}) collective-permute-start(f32[1,1,1,48,256]{4,3,2,1,0:T(8,128)S(1)} %slice.207), channel_id=1, source_target_pairs={{0,96},{1,97},{2,98},{3,99},{4,36},{5,37},{6,38},{7,39},{8,104},{9... | collective-permute-start | bytes 147464 | tf_op jit(solution)/shard_map/ppermute | solution.py:78
  141.0 1.5 collective-permute-start.21
  142.5 0.9 collective-permute-start.22
  143.5 2.8 %collective-permute-done.21 = f32[1,1,1,32,256]{4,3,2,1,0:T(8,128)S(1)} collective-permute-done((f32[1,1,1,32,256]{4,3,2,1,0:T(8,128)S(1)}, f32[1,1,1,32,256]{4,3,2,1,0:T(8,128)S(1)}, u32[]{:S(2)}, u32[]{:S(2)}) %collective-permute-start.21) | collective-permute-done | bytes 32800 | tf_op jit(solution)/shard_map/ppermute | solution.py:78
  146.2 1.5 collective-permute-done.22
  148.4 2.8 %collective-permute-start.24 = (f32[112,256]{1,0:T(8,128)S(1)}, f32[112,256]{1,0:T(8,128)S(1)}, u32[]{:S(2)}, u32[]{:S(2)}) collective-permute-start(f32[112,256]{1,0:T(8,128)S(1)} %get-tuple-element.104), channel_id=1, source_target_pairs={{0,2},{1,3},{2,0},{3,1},{4,6},{5,7},{6,4},{7,5},{8,10},{9,11},{10,... | collective-permute-start | bytes 344072 | tf_op jit(solution)/shard_map/ppermute | solution.py:44
  151.2 1.4 collective-permute-start.25
  152.6 7.9 %row_update.1 = (f32[2048,256]{1,0:T(8,128)}, f32[2048,256]{1,0:T(8,128)}) custom-call(f32[512,384]{1,0:T(8,128)S(1)} %reshape.255.arrived_ref, f32[2048,256]{1,0:T(8,128)} %table_ref.1, f32[2048,256]{1,0:T(8,128)} %accum_ref.1), custom_call_target="tpu_custom_call" | custom-call | flops 1073741824 | bytes 8388608 | tf_op jit(solution)/shard_map/row_update/pallas_call | solution.py:355
  162.2 1.0 convolution_add_fusion
  163.2 0.7 pad_maximum_fusion.4
  (114 shorter events, 8.6 us)
Async XLA Ops:
  0.6 49.4 %copy-start = (bf16[768,256]{1,0:T(8,128)(2,1)S(1)}, bf16[768,256]{1,0:T(8,128)(2,1)}, u32[]{:S(2)}) copy-start(bf16[768,256]{1,0:T(8,128)(2,1)} %param.15) | copy-start | bytes 1179652
  0.6 4.4 %copy-start.3 = (bf16[1024,256]{1,0:T(8,128)(2,1)S(1)}, bf16[1024,256]{1,0:T(8,128)(2,1)}, u32[]{:S(2)}) copy-start(bf16[1024,256]{1,0:T(8,128)(2,1)} %grad_ref.3) | copy-start | bytes 1572868
  0.7 4.4 %copy-start.5 = (s32[1,512]{1,0:T(1,128)S(1)}, s32[1,512]{1,0:T(1,128)}, u32[]{:S(2)}) copy-start(s32[1,512]{1,0:T(1,128)} %param.19) | copy-start | bytes 6148
  0.7 4.4 %copy-start.6 = (s32[1024]{0:T(1024)S(1)}, s32[1024]{0:T(1024)}, u32[]{:S(2)}) copy-start(s32[1024]{0:T(1024)} %param.18) | copy-start | bytes 12292
  5.0 3.6 %collective-permute-start = (f32[1536,256]{1,0:T(8,128)}, f32[1536,256]{1,0:T(8,128)S(1)}, u32[]{:S(2)}, u32[]{:S(2)}) collective-permute-start(f32[1536,256]{1,0:T(8,128)} %segment_sums.2), channel_id=1, source_target_pairs={{0,4},{4,0},{1,5},{5,1},{2,6},{6,2},{3,7},{7,3},{8,12},{12,8},{9,1... | collective-permute-start | bytes 4718600 | tf_op jit(solution)/shard_map/ppermute | solution.py:39
  7.2 5.0 %copy-start.4 = (f32[768]{0:T(1024)S(1)}, f32[768]{0:T(1024)}, u32[]{:S(2)}) copy-start(f32[768]{0:T(1024)} %param.12) | copy-start | bytes 9220
  12.2 36.3 %all-to-all-start = ((f32[64,24,256]{2,1,0:T(8,128)}), f32[64,24,256]{2,1,0:T(8,128)}, u32[]{:S(2)}, u32[]{:S(2)}) async-start(f32[64,24,256]{2,1,0:T(8,128)} %bitcast.4), calls=%async_computation | async-start | bytes 3145728 | tf_op jit(solution)/shard_map/all_to_all | solution.py:401
  61.7 11.6 %collective-permute-start.1 = (f32[64,40,256]{2,1,0:T(8,128)S(1)}, f32[64,40,256]{2,1,0:T(8,128)S(1)}, u32[]{:S(2)}, u32[]{:S(2)}) collective-permute-start(f32[64,40,256]{2,1,0:T(8,128)S(1)} %get-tuple-element.57), channel_id=1, source_target_pairs={{0,4},{4,0},{1,5},{5,1},{2,6},{6,2},{3,7},{7,3},{8,12},{12,8},{9,1... | collective-permute-start | bytes 7864328 | tf_op jit(solution)/shard_map/ppermute | solution.py:39
  67.1 5.8 %collective-permute-start.5 = (f32[64,32,256]{2,1,0:T(8,128)S(1)}, f32[64,32,256]{2,1,0:T(8,128)S(1)}, u32[]{:S(2)}, u32[]{:S(2)}) collective-permute-start(f32[64,32,256]{2,1,0:T(8,128)S(1)} %get-tuple-element.62), channel_id=1, source_target_pairs={{0,4},{4,0},{1,5},{5,1},{2,6},{6,2},{3,7},{7,3},{8,12},{12,8},{9,1... | collective-permute-start | bytes 6291464 | tf_op jit(solution)/shard_map/ppermute | solution.py:39
  72.8 4.2 %collective-permute-start.3 = (f32[64,32,256]{2,1,0:T(8,128)S(1)}, f32[64,32,256]{2,1,0:T(8,128)S(1)}, u32[]{:S(2)}, u32[]{:S(2)}) collective-permute-start(f32[64,32,256]{2,1,0:T(8,128)S(1)} %get-tuple-element.60), channel_id=1, source_target_pairs={{0,4},{4,0},{1,5},{5,1},{2,6},{6,2},{3,7},{7,3},{8,12},{12,8},{9,1... | collective-permute-start | bytes 6291464 | tf_op jit(solution)/shard_map/ppermute | solution.py:39
  73.8 18.7 %collective-permute-start.2 = (f32[4,4,2,40,256]{4,3,2,1,0:T(8,128)S(1)}, f32[4,4,2,40,256]{4,3,2,1,0:T(8,128)S(1)}, u32[]{:S(2)}, u32[]{:S(2)}) collective-permute-start(f32[4,4,2,40,256]{4,3,2,1,0:T(8,128)S(1)} %slice.184), channel_id=1, source_target_pairs={{0,1},{1,0},{2,3},{3,2},{4,7},{5,6},{6,5},{7,4},{8,9},{9,8},{10,11... | collective-permute-start | bytes 3932168 | tf_op jit(solution)/shard_map/ppermute | solution.py:78
  75.1 3.8 %slice-start = ((s8[4718592]{0:T(1024)(128)(4,1)}), s8[4194304]{0:T(1024)(128)(4,1)S(1)}, s32[]{:S(2)}) async-start(s8[4718592]{0:T(1024)(128)(4,1)} %bitcast.43), calls=%async_computation.2 | async-start | bytes 8388608
  75.2 15.2 %collective-permute-start.6 = (f32[2,4,4,32,256]{4,3,2,1,0:T(8,128)S(1)}, f32[2,4,4,32,256]{4,3,2,1,0:T(8,128)S(1)}, u32[]{:S(2)}, u32[]{:S(2)}) collective-permute-start(f32[2,4,4,32,256]{4,3,2,1,0:T(8,128)S(1)} %bitcast.52), channel_id=1, source_target_pairs={{0,32},{1,33},{2,34},{3,35},{4,100},{5,101},{6,102},{7,103},{8,40}... | collective-permute-start | bytes 3145736 | tf_op jit(solution)/shard_map/ppermute | solution.py:78
  77.1 1.8 %slice-start.1 = ((s8[4718592]{0:T(1024)(128)(4,1)}), s8[524288]{0:T(1024)(128)(4,1)S(1)}, s32[]{:S(2)}) async-start(s8[4718592]{0:T(1024)(128)(4,1)} %bitcast.43), calls=%async_computation.3 | async-start | bytes 1048576
  77.1 1.9 %copy-start.1 = (bf16[24,64,768]{2,1,0:T(8,128)(2,1)S(1)}, bf16[24,64,768]{2,1,0:T(8,128)(2,1)}, u32[]{:S(2)}) copy-start(bf16[24,64,768]{2,1,0:T(8,128)(2,1)} %param.11) | copy-start | bytes 7077892
  77.6 14.9 %collective-permute-start.4 = (f32[4,2,4,32,256]{4,3,2,1,0:T(8,128)S(1)}, f32[4,2,4,32,256]{4,3,2,1,0:T(8,128)S(1)}, u32[]{:S(2)}, u32[]{:S(2)}) collective-permute-start(f32[4,2,4,32,256]{4,3,2,1,0:T(8,128)S(1)} %slice.185), channel_id=1, source_target_pairs={{0,8},{1,9},{2,10},{3,11},{4,28},{5,29},{6,30},{7,31},{8,0},{9,1},... | collective-permute-start | bytes 3145736 | tf_op jit(solution)/shard_map/ppermute | solution.py:78
  93.0 7.0 %copy-start.2 = (f32[2,4,4,32,256]{4,3,2,1,0:T(8,128)}, f32[2,4,4,32,256]{4,3,2,1,0:T(8,128)S(1)}, u32[]{:S(2)}) copy-start(f32[2,4,4,32,256]{4,3,2,1,0:T(8,128)S(1)} %add.165) | copy-start | bytes 3145732
  93.1 19.5 %collective-permute-start.7 = (f32[4,4,1,40,256]{4,3,2,1,0:T(8,128)S(1)}, f32[4,4,1,40,256]{4,3,2,1,0:T(8,128)}, u32[]{:S(2)}, u32[]{:S(2)}) collective-permute-start(f32[4,4,1,40,256]{4,3,2,1,0:T(8,128)S(1)} %slice.147), channel_id=1, source_target_pairs={{0,3},{1,2},{2,1},{3,0},{4,5},{5,4},{6,7},{7,6},{8,11},{9,10},{10,... | collective-permute-start | bytes 1966088 | tf_op jit(solution)/shard_map/ppermute | solution.py:78
  96.4 12.2 %collective-permute-start.8 = (f32[4,1,4,32,256]{4,3,2,1,0:T(8,128)}, f32[4,1,4,32,256]{4,3,2,1,0:T(8,128)}, u32[]{:S(2)}, u32[]{:S(2)}) collective-permute-start(f32[4,1,4,32,256]{4,3,2,1,0:T(8,128)} %slice.148), channel_id=1, source_target_pairs={{0,24},{1,25},{2,26},{3,27},{4,12},{5,13},{6,14},{7,15},{8,16},{9,... | collective-permute-start | bytes 1572872 | tf_op jit(solution)/shard_map/ppermute | solution.py:78
  100.0 12.6 %collective-permute-start.9 = (f32[1,4,4,32,256]{4,3,2,1,0:T(8,128)}, f32[1,4,4,32,256]{4,3,2,1,0:T(8,128)}, u32[]{:S(2)}, u32[]{:S(2)}) collective-permute-start(f32[1,4,4,32,256]{4,3,2,1,0:T(8,128)} %slice.149), channel_id=1, source_target_pairs={{0,96},{1,97},{2,98},{3,99},{4,36},{5,37},{6,38},{7,39},{8,104},{9... | collective-permute-start | bytes 1572872 | tf_op jit(solution)/shard_map/ppermute | solution.py:78
  102.9 5.7 %collective-permute-start.10 = (f32[8,768]{1,0:T(8,128)S(1)}, f32[8,768]{1,0:T(8,128)S(1)}, u32[]{:S(2)}, u32[]{:S(2)}) collective-permute-start(f32[8,768]{1,0:T(8,128)S(1)} %get-tuple-element.73), channel_id=1, source_target_pairs={{0,4},{4,0},{1,5},{5,1},{2,6},{6,2},{3,7},{7,3},{8,12},{12,8},{9,1... | collective-permute-start | bytes 73736 | tf_op jit(solution)/shard_map/ppermute | solution.py:39
  102.9 26.7 %all-to-all-start.1 = ((f32[128,4,384]{2,1,0:T(4,128)}), f32[128,4,384]{2,1,0:T(4,128)}, u32[]{:S(2)}, u32[]{:S(2)}) async-start(f32[128,4,384]{2,1,0:T(4,128)} %reshape.251), calls=%async_computation.1 | async-start | bytes 1572864 | tf_op jit(solution)/shard_map/all_to_all | solution.py:452
  113.8 6.7 %collective-permute-start.15 = (f32[1,4,2,32,256]{4,3,2,1,0:T(8,128)S(1)}, f32[1,4,2,32,256]{4,3,2,1,0:T(8,128)S(1)}, u32[]{:S(2)}, u32[]{:S(2)}) collective-permute-start(f32[1,4,2,32,256]{4,3,2,1,0:T(8,128)S(1)} %slice.198), channel_id=1, source_target_pairs={{0,1},{1,0},{2,3},{3,2},{4,7},{5,6},{6,5},{7,4},{8,9},{9,8},{10,11... | collective-permute-start | bytes 786440 | tf_op jit(solution)/shard_map/ppermute | solution.py:78
  115.2 8.5 %collective-permute-start.11 = (f32[4,2,1,48,256]{4,3,2,1,0:T(8,128)S(1)}, f32[4,2,1,48,256]{4,3,2,1,0:T(8,128)S(1)}, u32[]{:S(2)}, u32[]{:S(2)}) collective-permute-start(f32[4,2,1,48,256]{4,3,2,1,0:T(8,128)S(1)} %pad_maximum_fusion.3), channel_id=1, source_target_pairs={{0,8},{1,9},{2,10},{3,11},{4,28},{5,29},{6,30},{7,31},{8,0},{9,1},... | collective-permute-start | bytes 1179656 | tf_op jit(solution)/shard_map/ppermute | solution.py:78
  116.5 9.6 %collective-permute-start.13 = (f32[2,1,4,32,256]{4,3,2,1,0:T(8,128)S(1)}, f32[2,1,4,32,256]{4,3,2,1,0:T(8,128)S(1)}, u32[]{:S(2)}, u32[]{:S(2)}) collective-permute-start(f32[2,1,4,32,256]{4,3,2,1,0:T(8,128)S(1)} %slice.195), channel_id=1, source_target_pairs={{0,32},{1,33},{2,34},{3,35},{4,100},{5,101},{6,102},{7,103},{8,40}... | collective-permute-start | bytes 786440 | tf_op jit(solution)/shard_map/ppermute | solution.py:78
  120.6 9.1 %collective-permute-start.16 = (f32[1,4,1,32,256]{4,3,2,1,0:T(8,128)S(1)}, f32[1,4,1,32,256]{4,3,2,1,0:T(8,128)S(1)}, u32[]{:S(2)}, u32[]{:S(2)}) collective-permute-start(f32[1,4,1,32,256]{4,3,2,1,0:T(8,128)S(1)} %slice.199), channel_id=1, source_target_pairs={{0,3},{1,2},{2,1},{3,0},{4,5},{5,4},{6,7},{7,6},{8,11},{9,10},{10,... | collective-permute-start | bytes 393224 | tf_op jit(solution)/shard_map/ppermute | solution.py:78
  123.8 8.8 %collective-permute-start.12 = (f32[4,1,1,48,256]{4,3,2,1,0:T(8,128)S(1)}, f32[4,1,1,48,256]{4,3,2,1,0:T(8,128)S(1)}, u32[]{:S(2)}, u32[]{:S(2)}) collective-permute-start(f32[4,1,1,48,256]{4,3,2,1,0:T(8,128)S(1)} %slice.193), channel_id=1, source_target_pairs={{0,24},{1,25},{2,26},{3,27},{4,12},{5,13},{6,14},{7,15},{8,16},{9,... | collective-permute-start | bytes 589832 | tf_op jit(solution)/shard_map/ppermute | solution.py:78
  126.1 6.5 %collective-permute-start.14 = (f32[1,1,4,32,256]{4,3,2,1,0:T(8,128)S(1)}, f32[1,1,4,32,256]{4,3,2,1,0:T(8,128)S(1)}, u32[]{:S(2)}, u32[]{:S(2)}) collective-permute-start(f32[1,1,4,32,256]{4,3,2,1,0:T(8,128)S(1)} %slice.196), channel_id=1, source_target_pairs={{0,96},{1,97},{2,98},{3,99},{4,36},{5,37},{6,38},{7,39},{8,104},{9... | collective-permute-start | bytes 393224 | tf_op jit(solution)/shard_map/ppermute | solution.py:78
  132.7 4.3 %collective-permute-start.19 = (f32[1,2,1,32,256]{4,3,2,1,0:T(8,128)S(1)}, f32[1,2,1,32,256]{4,3,2,1,0:T(8,128)S(1)}, u32[]{:S(2)}, u32[]{:S(2)}) collective-permute-start(f32[1,2,1,32,256]{4,3,2,1,0:T(8,128)S(1)} %slice.205), channel_id=1, source_target_pairs={{0,8},{1,9},{2,10},{3,11},{4,28},{5,29},{6,30},{7,31},{8,0},{9,1},... | collective-permute-start | bytes 196616 | tf_op jit(solution)/shard_map/ppermute | solution.py:78
  133.0 4.7 %collective-permute-start.17 = (f32[2,1,1,48,256]{4,3,2,1,0:T(8,128)S(1)}, f32[2,1,1,48,256]{4,3,2,1,0:T(8,128)S(1)}, u32[]{:S(2)}, u32[]{:S(2)}) collective-permute-start(f32[2,1,1,48,256]{4,3,2,1,0:T(8,128)S(1)} %slice.201), channel_id=1, source_target_pairs={{0,32},{1,33},{2,34},{3,35},{4,100},{5,101},{6,102},{7,103},{8,40}... | collective-permute-start | bytes 294920 | tf_op jit(solution)/shard_map/ppermute | solution.py:78
  133.4 4.3 %collective-permute-start.18 = (f32[1,1,2,32,256]{4,3,2,1,0:T(8,128)S(1)}, f32[1,1,2,32,256]{4,3,2,1,0:T(8,128)S(1)}, u32[]{:S(2)}, u32[]{:S(2)}) collective-permute-start(f32[1,1,2,32,256]{4,3,2,1,0:T(8,128)S(1)} %slice.203), channel_id=1, source_target_pairs={{0,1},{1,0},{2,3},{3,2},{4,7},{5,6},{6,5},{7,4},{8,9},{9,8},{10,11... | collective-permute-start | bytes 196616 | tf_op jit(solution)/shard_map/ppermute | solution.py:78
  137.7 10.0 %collective-permute-start.20 = (f32[1,1,1,48,256]{4,3,2,1,0:T(8,128)S(1)}, f32[1,1,1,48,256]{4,3,2,1,0:T(8,128)S(1)}, u32[]{:S(2)}, u32[]{:S(2)}) collective-permute-start(f32[1,1,1,48,256]{4,3,2,1,0:T(8,128)S(1)} %slice.207), channel_id=1, source_target_pairs={{0,96},{1,97},{2,98},{3,99},{4,36},{5,37},{6,38},{7,39},{8,104},{9... | collective-permute-start | bytes 147464 | tf_op jit(solution)/shard_map/ppermute | solution.py:78
  141.0 5.2 %collective-permute-start.21 = (f32[1,1,1,32,256]{4,3,2,1,0:T(8,128)S(1)}, f32[1,1,1,32,256]{4,3,2,1,0:T(8,128)S(1)}, u32[]{:S(2)}, u32[]{:S(2)}) collective-permute-start(f32[1,1,1,32,256]{4,3,2,1,0:T(8,128)S(1)} %slice.210), channel_id=1, source_target_pairs={{0,3},{1,2},{2,1},{3,0},{4,5},{5,4},{6,7},{7,6},{8,11},{9,10},{10,... | collective-permute-start | bytes 98312 | tf_op jit(solution)/shard_map/ppermute | solution.py:78
  142.5 5.2 %collective-permute-start.22 = (f32[1,1,1,32,256]{4,3,2,1,0:T(8,128)S(1)}, f32[1,1,1,32,256]{4,3,2,1,0:T(8,128)S(1)}, u32[]{:S(2)}, u32[]{:S(2)}) collective-permute-start(f32[1,1,1,32,256]{4,3,2,1,0:T(8,128)S(1)} %slice.213), channel_id=1, source_target_pairs={{0,24},{1,25},{2,26},{3,27},{4,12},{5,13},{6,14},{7,15},{8,16},{9,... | collective-permute-start | bytes 98312 | tf_op jit(solution)/shard_map/ppermute | solution.py:78
  147.8 12.7 %collective-permute-start.23 = (f32[112,256]{1,0:T(8,128)S(1)}, f32[112,256]{1,0:T(8,128)S(1)}, u32[]{:S(2)}, u32[]{:S(2)}) collective-permute-start(f32[112,256]{1,0:T(8,128)S(1)} %get-tuple-element.104), channel_id=1, source_target_pairs={{0,1},{1,0},{2,3},{3,2},{4,5},{5,4},{6,7},{7,6},{8,9},{9,8},{10,11... | collective-permute-start | bytes 344072 | tf_op jit(solution)/shard_map/ppermute | solution.py:44
  148.4 12.1 %collective-permute-start.24 = (f32[112,256]{1,0:T(8,128)S(1)}, f32[112,256]{1,0:T(8,128)S(1)}, u32[]{:S(2)}, u32[]{:S(2)}) collective-permute-start(f32[112,256]{1,0:T(8,128)S(1)} %get-tuple-element.104), channel_id=1, source_target_pairs={{0,2},{1,3},{2,0},{3,1},{4,6},{5,7},{6,4},{7,5},{8,10},{9,11},{10,... | collective-permute-start | bytes 344072 | tf_op jit(solution)/shard_map/ppermute | solution.py:44
  151.2 9.3 %collective-permute-start.25 = (f32[112,256]{1,0:T(8,128)S(1)}, f32[112,256]{1,0:T(8,128)S(1)}, u32[]{:S(2)}, u32[]{:S(2)}) collective-permute-start(f32[112,256]{1,0:T(8,128)S(1)} %get-tuple-element.104), channel_id=1, source_target_pairs={{0,3},{1,2},{2,1},{3,0},{4,7},{5,6},{6,5},{7,4},{8,11},{9,10},{10,... | collective-permute-start | bytes 344072 | tf_op jit(solution)/shard_map/ppermute | solution.py:44

commit v10 on v8

--- a/solution.py
+++ b/solution.py
@@ -208,14 +208,15 @@
 
 
 def first_kernel(
-    units, core_ref, keep_at, send_at, slope_ref, act_ref, mean_ref, pool_ref, grad_ref,
-    normed_ref, pre_ref, *out_refs
+    units, core_ref, keep_at, send_at, slope_ref, mean_ref, pool_ref, grad_ref,
+    pool_grad_ref, down_ref, normed_ref, pre_ref, *out_refs
 ):
     rows, block = slope_ref.shape
     length, step = rows // units, rows // units * 8
+    d_act = contract_last(pool_grad_ref[...], down_ref[...]) * (1.0 / length)
     for r in range(units // 8):
         slope = slope_ref[r * step : (r + 1) * step, :].astype(jnp.float32)
-        d_pre = slope.reshape(8, length, block) * act_ref[r * 8 : (r + 1) * 8, :][:, None, :]
+        d_pre = slope.reshape(8, length, block) * d_act[r * 8 : (r + 1) * 8, :][:, None, :]
         pre_ref[r * step : (r + 1) * step, :] = d_pre.reshape(step, block).astype(jnp.bfloat16)
     up = contract_first(pre_ref[...], normed_ref[...])
     down = contract_first(mean_ref[...], grad_ref[...])
@@ -243,7 +244,7 @@
     slots = 2 * sides * sides
     part = hidden // sides // slots
     tall = [part + 8 + 8 * (index == 0) for index in indices for _ in range(2)]
-    first = len(left) == 2
+    first = len(left) == 3
 
     def columns(array):
         return pl.BlockSpec((array.shape[0], array.shape[1] // sides), lambda i, c, k, s: (0, i))
@@ -258,7 +259,13 @@
 
     out_specs = [sums(h, 1 + n % 2) for n, h in enumerate(tall)]
     out_shape = [jax.ShapeDtypeStruct((sides * slots // 2, h, width_e), jnp.float32) for h in tall]
+    extra = []
     if first:
+        width = left[1].shape[1]
+        extra = [
+            pl.BlockSpec((units, width), lambda i, c, k, s: (0, 0)),
+            pl.BlockSpec((hidden // sides, width), lambda i, c, k, s: (i, 0)),
+        ]
         kernel = functools.partial(first_kernel, units)
         out_specs.insert(0, columns(left[0]))
         out_shape.insert(0, pltpu.VMEM((rows, hidden), jnp.bfloat16))
@@ -269,9 +276,9 @@
         grid_spec=pltpu.PrefetchScalarGridSpec(
             num_scalar_prefetch=3,
             grid=(sides,),
-            in_specs=[columns(array) for array in left]
-            + [columns(mean_act_b), columns(pooled_b)]
+            in_specs=[columns(left[0]), columns(mean_act_b), columns(pooled_b)]
             + [pl.BlockSpec(grad_b.shape, lambda i, c, k, s: (0, 0))]
+            + extra
             + [lanes(index) for index in indices],
             out_specs=out_specs,
         ),
@@ -279,7 +286,7 @@
         compiler_params=pltpu.CompilerParams(vmem_limit_bytes=VMEM),
         cost_estimate=cost(2 * rows * width_e * len(indices) * hidden, 4 * rows * hidden),
         name="first_products" if first else "other_products",
-    )(*tables, *left, mean_act_b, pooled_b, grad_b, *[normed_b] * len(indices))
+    )(*tables, left[0], mean_act_b, pooled_b, grad_b, *left[1:], *[normed_b] * len(indices))
 
 
 def titles_kernel(pre_ref, w_ref, titles_ref, gain_ref, pool_ref, out_ref, gain_out):
@@ -350,7 +357,7 @@
 
 def row_update(arrived, table, accum):
     rows, width_e = table.shape
-    step = 512
+    step = 1024
     tile = pl.BlockSpec((step, width_e), lambda i: (i, 0))
     return pl.pallas_call(
         rows_kernel,
@@ -358,7 +365,7 @@
         in_specs=[pl.BlockSpec(arrived.shape, lambda i: (0, 0)), tile, tile],
         out_specs=[tile, tile],
         out_shape=[jax.ShapeDtypeStruct((rows, width_e), jnp.float32)] * 2,
-        compiler_params=pltpu.CompilerParams(vmem_limit_bytes=16 << 20),
+        compiler_params=pltpu.CompilerParams(vmem_limit_bytes=24 << 20),
         cost_estimate=cost(4 * rows * width_e * arrived.shape[0], 16 * rows * width_e),
         name="row_update",
     )(
@@ -429,7 +436,7 @@
     item_grad = jnp.sum(item_all, axis=0)
     grad_b = item_grad.astype(jnp.bfloat16)
     d_pooled = contract_last(grad_b, w_proj)
-    d_act = contract_last(d_pooled.astype(jnp.bfloat16), w_down) / length
+    d_pooled_b = d_pooled.astype(jnp.bfloat16)
 
     here = [(lax.axis_index(name), lax.axis_size(name)) for name in CHIPS]
     keep_at = jnp.stack([slot_of(core, at, size) for at, size in here])
@@ -437,7 +444,7 @@
     tables = (core.reshape(1), keep_at, send_at)
     items = (normed_b, mean_act_b, pooled_b, grad_b)
     slope = pltpu.with_memory_space_constraint(slope, pltpu.HBM)
-    d_pre, *sums = up_products(tables, (0,), (slope, d_act), *items)
+    d_pre, *sums = up_products(tables, (0,), (slope, d_pooled_b, w_down), *items)
     d_pre = pltpu.with_memory_space_constraint(d_pre, pltpu.VMEM)
     for index in (1, 2):
         sums += up_products(tables, (index,), (d_pre,), *items)

time: 162 us -> 162 us (level)
  matrix products: 9.58 us -> 5.89 us
  local copies, waits for them, and re-layouts: 9.74 us -> 12.1 us
    dot_general x4 -> x3, matrix products: 5.16 us -> 1.48 us  [contract_last(): lax.dot_general(left, right, (((1,), (1,)), ((), ())), preferred_element_...]
    unnamed x20 -> x22, local copies, waits for them, and re-layouts: 1.45 us -> 3.77 us
    pallas_call x3, Pallas kernels: 18.1 us -> 20.2 us  [up_products(): pl.pallas_call(kernel, grid_spec=pltpu.PrefetchScalarGridSpec(num_scalar_...]
  transfers between devices with their start and end apart: 28 -> 28, of which waited for: 9 -> 9; matrix products, arithmetic and copies ran while one was open for 10% -> 10% of each run, Pallas kernels for 30% -> 29%
where the time goes in v10:
time: 162 us; the launch traced here: 161 us
  Pallas kernels  61.9 us (38%)
  starting transfers between devices  52.5 us (32%)
  waiting for transfers between devices  18.9 us (12%)
  local copies, waits for them, and re-layouts  12.1 us (7%)
  other arithmetic  8.83 us (5%)
  matrix products  5.89 us (4%)
    ppermute x18, starting transfers between devices, halve(): lax.ppermute(lax.slice_in_dim(part, middle, None, axis=dim), DEVICES, par...  29.4 us
    pallas_call x1, Pallas kernels, forward(): pl.pallas_call(functools.partial(forward_kernel, units), grid=(hidden //...  20.5 us
    pallas_call x3, Pallas kernels, up_products(): pl.pallas_call(kernel, grid_spec=pltpu.PrefetchScalarGridSpec(num_scalar_...  20.2 us
    ppermute x18, waiting for transfers between devices, halve(): lax.ppermute(lax.slice_in_dim(part, middle, None, axis=dim), DEVICES, par...  17.7 us
    all_to_all x1, starting transfers between devices, per_device(): item_all = lax.all_to_all(mine, CHIPS, 0, 0, tiled=True)  11.7 us
    pallas_call x1, Pallas kernels, title_grads(): pl.pallas_call(titles_kernel, grid=(rows // step,), in_specs=[pl.BlockSpe...  11.6 us
    all_to_all x1, starting transfers between devices, per_device(): row_all = lax.all_to_all(row_part, DEVICES, 0, 0, tiled=True)  5.67 us
    pallas_call x2, Pallas kernels, segment_sums(): pl.pallas_call(item_kernel, grid=(count // step,), in_specs=[pl.BlockSpec...  4.98 us
  transfers between devices with their start and end apart: 28, of which 9 were waited for; matrix products, arithmetic and copies ran while one was open for 10% of the time, Pallas kernels for 29%

profile of v10, /device:TPU:0, one launch (start us, length us, event | category | flops | bytes accessed | tf_op | source)
XLA Modules:
  0.0 161.5 jit_solution(171170575716973306)
XLA Ops:
  0.7 0.8 broadcast_select_fusion
  1.4 1.0 copy-done.2
  2.5 2.5 %segment_sums.2 = f32[1536,256]{1,0:T(8,128)} custom-call(s32[1,1024]{1,0:T(1,128)S(1)} %bitcast.41, bf16[1024,256]{1,0:T(8,128)(2,1)S(1)} %copy-done.2), custom_call_target="tpu_custom_call" | custom-call | flops 805306368 | bytes 1572864 | tf_op jit(solution)/shard_map/segment_sums/pallas_call | solution.py:108
  5.8 1.1 copy.19
  6.9 2.2 %reshape.251 = f32[128,4,384]{2,1,0:T(4,128)} reshape(f32[512,384]{1,0:T(8,128)} %copy.19) | data formatting | bytes 1572864 | tf_op jit(solution)/shard_map/reshape | solution.py:423
  9.3 2.5 %segment_sums.3 = f32[1536,256]{1,0:T(8,128)} custom-call(s32[1,1024]{1,0:T(1,128)S(1)} %bitcast.40, bf16[1024,256]{1,0:T(8,128)(2,1)S(1)} %copy-done.3, f32[1536,256]{1,0:T(8,128)S(1)} %collective-permute-done.refs_0_), custom_call_target="tpu_custom_call" | custom-call | flops 805306368 | bytes 1572864 | tf_op jit(solution)/shard_map/segment_sums/pallas_call | solution.py:108
  11.8 11.7 %all-to-all-start = ((f32[64,24,256]{2,1,0:T(8,128)}), f32[64,24,256]{2,1,0:T(8,128)}, u32[]{:S(2)}, u32[]{:S(2)}) async-start(f32[64,24,256]{2,1,0:T(8,128)} %bitcast.4), calls=%async_computation | async-start | bytes 3145728 | tf_op jit(solution)/shard_map/all_to_all | solution.py:408
  23.5 20.5 %forward.1 = (bf16[1536,768]{1,0:T(8,128)(2,1)S(1)}, bf16[1536,3072]{1,0:T(8,128)(2,1)}, f32[24,3072]{1,0:T(8,128)S(1)}, f32[24,768]{1,0:T(8,128)S(1)}) custom-call(bf16[1536,768]{1,0:T(8,128)(2,1)} %bitcast.44, f32[1,768]{1,0:T(1,128)S(1)} %reshape.250.gain_ref, bf16[768,3072]{1,0:T(8,128)(2,1)} %w_ref.3), custom_call_target="tpu_custom_call" | custom-call | flops 28991029248 | bytes 18874368 | tf_op jit(solution)/shard_map/forward/pallas_call | solution.py:156
  44.1 3.8 %fusion.3.pool_ref = bf16[24,1024]{1,0:T(8,128)(2,1)S(1)} fusion(s32[1024]{0:T(1024)S(1)} %fusion.30, f32[24,768]{1,0:T(8,128)S(1)} %get-tuple-element.48, bf16[24,3072]{1,0:T(8,128)(2,1)S(1)} %convert_element_type.35.mean_ref, bf16[3072,768]{1,0:T(8,128)(2,1)} %down_ref.1), kind=kOutput, calls=%fused_computation.7 | convolution fusion | flops 151842816 | bytes 4993024 | tf_op jit(solution)/shard_map/dot_general | solution.py:431
  48.5 1.5 reduce_sum.29.grad_ref
  50.3 2.4 %copy-done.1 = bf16[3072,768]{1,0:T(8,128)(2,1)S(1)} copy-done((bf16[3072,768]{1,0:T(8,128)(2,1)S(1)}, bf16[3072,768]{1,0:T(8,128)(2,1)}, u32[]{:S(2)}) %copy-start.1) | copy-done | bytes 4718616
  52.6 10.0 %first_products.1 = (bf16[1536,3072]{1,0:T(8,128)(2,1)S(1)}, f32[64,40,256]{2,1,0:T(8,128)S(1)}, f32[64,40,256]{2,1,0:T(8,128)S(1)}) custom-call(s32[1]{0:T(128)} %bitcast.core_ref, s32[3,4]{1,0:T(4,128)S(1)} %pad_add_fusion.keep_at, s32[3,4]{1,0:T(4,128)S(1)} %pad_add_fusion.1.send_at, bf16[1536,3072]{1,0:T(8,128)(2,1)} %get-tuple-element.45.slope_ref, ...), custom_call_target="tpu_custom_call" | custom-call | flops 2415919104 | bytes 18874368 | tf_op jit(solution)/shard_map/first_products/pallas_call | solution.py:274
  62.7 5.1 %other_products.3 = (f32[64,32,256]{2,1,0:T(8,128)S(1)}, f32[64,32,256]{2,1,0:T(8,128)S(1)}) custom-call(s32[1]{0:T(128)} %bitcast.core_ref, s32[3,4]{1,0:T(4,128)S(1)} %pad_add_fusion.keep_at, s32[3,4]{1,0:T(4,128)S(1)} %pad_add_fusion.1.send_at, bf16[1536,3072]{1,0:T(8,128)(2,1)S(1)} %get-tuple-element.54.pre_ref, ...), custom_call_target="tpu_custom_call" | custom-call | flops 2415919104 | bytes 18874368 | tf_op jit(solution)/shard_map/other_products/pallas_call | solution.py:274
  67.8 0.8 collective-permute-start.5
  68.5 5.1 %other_products.2 = (f32[64,32,256]{2,1,0:T(8,128)S(1)}, f32[64,32,256]{2,1,0:T(8,128)S(1)}) custom-call(s32[1]{0:T(128)} %bitcast.core_ref, s32[3,4]{1,0:T(4,128)S(1)} %pad_add_fusion.keep_at, s32[3,4]{1,0:T(4,128)S(1)} %pad_add_fusion.1.send_at, bf16[1536,3072]{1,0:T(8,128)(2,1)S(1)} %get-tuple-element.54.pre_ref, ...), custom_call_target="tpu_custom_call" | custom-call | flops 2415919104 | bytes 18874368 | tf_op jit(solution)/shard_map/other_products/pallas_call | solution.py:274
  74.6 0.9 collective-permute-start.2
  75.8 1.5 collective-permute-start.6
  78.4 1.0 collective-permute-start.4
  79.7 11.6 %title_grads.1 = (bf16[1536,768]{1,0:T(8,128)(2,1)}, f32[8,768]{1,0:T(8,128)S(1)}) custom-call(bf16[1536,3072]{1,0:T(8,128)(2,1)S(1)} %get-tuple-element.54.pre_ref, bf16[768,3072]{1,0:T(8,128)(2,1)S(1)} %bitcast.43, bf16[1536,768]{1,0:T(8,128)(2,1)S(1)} %bitcast.45, f32[1,768]{1,0:T(1,128)S(1)} %reshape.250.gain_ref, f32[24,768]{1,0:T(8,128)S(1)} %get-tuple-element.98.pool_ref), custom_call_target="tpu_custom_call" | custom-call | flops 7247757312 | bytes 9437184 | tf_op jit(solution)/shard_map/title_grads/pallas_call | solution.py:319
  91.4 1.9 %collective-permute-done.4 = f32[4,2,4,32,256]{4,3,2,1,0:T(8,128)S(1)} collective-permute-done((f32[4,2,4,32,256]{4,3,2,1,0:T(8,128)S(1)}, f32[4,2,4,32,256]{4,3,2,1,0:T(8,128)S(1)}, u32[]{:S(2)}, u32[]{:S(2)}) %collective-permute-start.4) | collective-permute-done | bytes 1048608 | tf_op jit(solution)/shard_map/ppermute | solution.py:78
  93.9 2.1 %collective-permute-start.7 = (f32[4,4,1,40,256]{4,3,2,1,0:T(8,128)S(1)}, f32[4,4,1,40,256]{4,3,2,1,0:T(8,128)}, u32[]{:S(2)}, u32[]{:S(2)}) collective-permute-start(f32[4,4,1,40,256]{4,3,2,1,0:T(8,128)S(1)} %slice.147), channel_id=1, source_target_pairs={{0,3},{1,2},{2,1},{3,0},{4,5},{5,4},{6,7},{7,6},{8,11},{9,10},{10,... | collective-permute-start | bytes 1966088 | tf_op jit(solution)/shard_map/ppermute | solution.py:78
  96.0 0.8 slice.148
  96.9 2.7 %collective-permute-start.8 = (f32[4,1,4,32,256]{4,3,2,1,0:T(8,128)}, f32[4,1,4,32,256]{4,3,2,1,0:T(8,128)}, u32[]{:S(2)}, u32[]{:S(2)}) collective-permute-start(f32[4,1,4,32,256]{4,3,2,1,0:T(8,128)} %slice.148), channel_id=1, source_target_pairs={{0,24},{1,25},{2,26},{3,27},{4,12},{5,13},{6,14},{7,15},{8,16},{9,... | collective-permute-start | bytes 1572872 | tf_op jit(solution)/shard_map/ppermute | solution.py:78
  99.6 0.8 slice.149
  100.4 3.0 %collective-permute-start.9 = (f32[1,4,4,32,256]{4,3,2,1,0:T(8,128)}, f32[1,4,4,32,256]{4,3,2,1,0:T(8,128)}, u32[]{:S(2)}, u32[]{:S(2)}) collective-permute-start(f32[1,4,4,32,256]{4,3,2,1,0:T(8,128)} %slice.149), channel_id=1, source_target_pairs={{0,96},{1,97},{2,98},{3,99},{4,36},{5,37},{6,38},{7,39},{8,104},{9... | collective-permute-start | bytes 1572872 | tf_op jit(solution)/shard_map/ppermute | solution.py:78
  103.4 5.7 %all-to-all-start.1 = ((f32[128,4,384]{2,1,0:T(4,128)}), f32[128,4,384]{2,1,0:T(4,128)}, u32[]{:S(2)}, u32[]{:S(2)}) async-start(f32[128,4,384]{2,1,0:T(4,128)} %reshape.251), calls=%async_computation.1 | async-start | bytes 1572864 | tf_op jit(solution)/shard_map/all_to_all | solution.py:459
  109.1 3.8 %collective-permute-done.9 = f32[1,4,4,32,256]{4,3,2,1,0:T(8,128)} collective-permute-done((f32[1,4,4,32,256]{4,3,2,1,0:T(8,128)}, f32[1,4,4,32,256]{4,3,2,1,0:T(8,128)}, u32[]{:S(2)}, u32[]{:S(2)}) %collective-permute-start.9) | collective-permute-done | bytes 524320 | tf_op jit(solution)/shard_map/ppermute | solution.py:78
  113.0 1.3 slice_add_fusion.3
  114.4 1.2 slice_add_fusion.2
  115.8 1.1 slice_add_fusion.4
  117.2 3.8 %collective-permute-done.15 = f32[1,4,2,32,256]{4,3,2,1,0:T(8,128)S(1)} collective-permute-done((f32[1,4,2,32,256]{4,3,2,1,0:T(8,128)S(1)}, f32[1,4,2,32,256]{4,3,2,1,0:T(8,128)S(1)}, u32[]{:S(2)}, u32[]{:S(2)}) %collective-permute-start.15) | collective-permute-done | bytes 262176 | tf_op jit(solution)/shard_map/ppermute | solution.py:78
  121.1 2.2 %collective-permute-start.16 = (f32[1,4,1,32,256]{4,3,2,1,0:T(8,128)S(1)}, f32[1,4,1,32,256]{4,3,2,1,0:T(8,128)S(1)}, u32[]{:S(2)}, u32[]{:S(2)}) collective-permute-start(f32[1,4,1,32,256]{4,3,2,1,0:T(8,128)S(1)} %slice.199), channel_id=1, source_target_pairs={{0,3},{1,2},{2,1},{3,0},{4,5},{5,4},{6,7},{7,6},{8,11},{9,10},{10,... | collective-permute-start | bytes 393224 | tf_op jit(solution)/shard_map/ppermute | solution.py:78
  123.2 0.9 collective-permute-done.11
  124.2 2.0 %collective-permute-start.12 = (f32[4,1,1,48,256]{4,3,2,1,0:T(8,128)S(1)}, f32[4,1,1,48,256]{4,3,2,1,0:T(8,128)S(1)}, u32[]{:S(2)}, u32[]{:S(2)}) collective-permute-start(f32[4,1,1,48,256]{4,3,2,1,0:T(8,128)S(1)} %slice.193), channel_id=1, source_target_pairs={{0,24},{1,25},{2,26},{3,27},{4,12},{5,13},{6,14},{7,15},{8,16},{9,... | collective-permute-start | bytes 589832 | tf_op jit(solution)/shard_map/ppermute | solution.py:78
  126.3 3.6 %collective-permute-start.14 = (f32[1,1,4,32,256]{4,3,2,1,0:T(8,128)S(1)}, f32[1,1,4,32,256]{4,3,2,1,0:T(8,128)S(1)}, u32[]{:S(2)}, u32[]{:S(2)}) collective-permute-start(f32[1,1,4,32,256]{4,3,2,1,0:T(8,128)S(1)} %slice.196), channel_id=1, source_target_pairs={{0,96},{1,97},{2,98},{3,99},{4,36},{5,37},{6,38},{7,39},{8,104},{9... | collective-permute-start | bytes 393224 | tf_op jit(solution)/shard_map/ppermute | solution.py:78
  129.9 2.9 %collective-permute-done.14 = f32[1,1,4,32,256]{4,3,2,1,0:T(8,128)S(1)} collective-permute-done((f32[1,1,4,32,256]{4,3,2,1,0:T(8,128)S(1)}, f32[1,1,4,32,256]{4,3,2,1,0:T(8,128)S(1)}, u32[]{:S(2)}, u32[]{:S(2)}) %collective-permute-start.14) | collective-permute-done | bytes 131104 | tf_op jit(solution)/shard_map/ppermute | solution.py:78
  134.0 1.5 collective-permute-start.21
  135.5 2.1 %collective-permute-done.19 = f32[1,1,2,32,256]{4,3,2,1,0:T(8,128)S(1)} collective-permute-done((f32[1,1,2,32,256]{4,3,2,1,0:T(8,128)S(1)}, f32[1,1,2,32,256]{4,3,2,1,0:T(8,128)S(1)}, u32[]{:S(2)}, u32[]{:S(2)}) %collective-permute-start.19) | collective-permute-done | bytes 65568 | tf_op jit(solution)/shard_map/ppermute | solution.py:78
  137.6 1.3 collective-permute-start.20
  139.0 2.5 %collective-permute-start.22 = (f32[1,1,1,32,256]{4,3,2,1,0:T(8,128)S(1)}, f32[1,1,1,32,256]{4,3,2,1,0:T(8,128)S(1)}, u32[]{:S(2)}, u32[]{:S(2)}) collective-permute-start(f32[1,1,1,32,256]{4,3,2,1,0:T(8,128)S(1)} %slice.213), channel_id=1, source_target_pairs={{0,24},{1,25},{2,26},{3,27},{4,12},{5,13},{6,14},{7,15},{8,16},{9,... | collective-permute-start | bytes 98312 | tf_op jit(solution)/shard_map/ppermute | solution.py:78
  141.5 3.6 %collective-permute-start.18 = (f32[1,1,1,48,256]{4,3,2,1,0:T(8,128)S(1)}, f32[1,1,1,48,256]{4,3,2,1,0:T(8,128)S(1)}, u32[]{:S(2)}, u32[]{:S(2)}) collective-permute-start(f32[1,1,1,48,256]{4,3,2,1,0:T(8,128)S(1)} %slice.203), channel_id=1, source_target_pairs={{0,96},{1,97},{2,98},{3,99},{4,36},{5,37},{6,38},{7,39},{8,104},{9... | collective-permute-start | bytes 147464 | tf_op jit(solution)/shard_map/ppermute | solution.py:78
  145.2 2.0 %collective-permute-done.18 = f32[1,1,1,48,256]{4,3,2,1,0:T(8,128)S(1)} collective-permute-done((f32[1,1,1,48,256]{4,3,2,1,0:T(8,128)S(1)}, f32[1,1,1,48,256]{4,3,2,1,0:T(8,128)S(1)}, u32[]{:S(2)}, u32[]{:S(2)}) %collective-permute-start.18) | collective-permute-done | bytes 49184 | tf_op jit(solution)/shard_map/ppermute | solution.py:78
  147.4 2.5 %collective-permute-start.24 = (f32[112,256]{1,0:T(8,128)S(1)}, f32[112,256]{1,0:T(8,128)S(1)}, u32[]{:S(2)}, u32[]{:S(2)}) collective-permute-start(f32[112,256]{1,0:T(8,128)S(1)} %get-tuple-element.96), channel_id=1, source_target_pairs={{0,2},{1,3},{2,0},{3,1},{4,6},{5,7},{6,4},{7,5},{8,10},{9,11},{10,... | collective-permute-start | bytes 344072 | tf_op jit(solution)/shard_map/ppermute | solution.py:44
  149.9 2.2 %collective-permute-start.25 = (f32[112,256]{1,0:T(8,128)S(1)}, f32[112,256]{1,0:T(8,128)S(1)}, u32[]{:S(2)}, u32[]{:S(2)}) collective-permute-start(f32[112,256]{1,0:T(8,128)S(1)} %get-tuple-element.96), channel_id=1, source_target_pairs={{0,3},{1,2},{2,1},{3,0},{4,7},{5,6},{6,5},{7,4},{8,11},{9,10},{10,... | collective-permute-start | bytes 344072 | tf_op jit(solution)/shard_map/ppermute | solution.py:44
  152.0 1.4 reshape.262.arrived_ref
  153.4 4.6 %row_update.1 = (f32[2048,256]{1,0:T(8,128)}, f32[2048,256]{1,0:T(8,128)}) custom-call(f32[512,384]{1,0:T(8,128)S(1)} %reshape.262.arrived_ref, f32[2048,256]{1,0:T(8,128)} %table_ref.1, f32[2048,256]{1,0:T(8,128)} %accum_ref.1), custom_call_target="tpu_custom_call" | custom-call | flops 1073741824 | bytes 8388608 | tf_op jit(solution)/shard_map/row_update/pallas_call | solution.py:362
  159.7 1.0 convolution_add_fusion
  160.7 0.7 pad_maximum_fusion.4
  (117 shorter events, 8.6 us)
Async XLA Ops:
  0.6 49.4 %copy-start = (bf16[768,256]{1,0:T(8,128)(2,1)S(1)}, bf16[768,256]{1,0:T(8,128)(2,1)}, u32[]{:S(2)}) copy-start(bf16[768,256]{1,0:T(8,128)(2,1)} %param.15) | copy-start | bytes 1179652
  0.6 4.3 %copy-start.7 = (s32[1,512]{1,0:T(1,128)S(1)}, s32[1,512]{1,0:T(1,128)}, u32[]{:S(2)}) copy-start(s32[1,512]{1,0:T(1,128)} %param.19) | copy-start | bytes 6148
  0.7 4.3 %copy-start.8 = (s32[1024]{0:T(1024)S(1)}, s32[1024]{0:T(1024)}, u32[]{:S(2)}) copy-start(s32[1024]{0:T(1024)} %param.18) | copy-start | bytes 12292
  1.4 1.0 copy-start.2
  2.5 2.5 %copy-start.3 = (bf16[1024,256]{1,0:T(8,128)(2,1)S(1)}, bf16[1024,256]{1,0:T(8,128)(2,1)}, u32[]{:S(2)}) copy-start(bf16[1024,256]{1,0:T(8,128)(2,1)} %grad_ref.3) | copy-start | bytes 1572868
  5.0 4.3 %collective-permute-start = (f32[1536,256]{1,0:T(8,128)}, f32[1536,256]{1,0:T(8,128)S(1)}, u32[]{:S(2)}, u32[]{:S(2)}) collective-permute-start(f32[1536,256]{1,0:T(8,128)} %segment_sums.2), channel_id=1, source_target_pairs={{0,4},{4,0},{1,5},{5,1},{2,6},{6,2},{3,7},{7,3},{8,12},{12,8},{9,1... | collective-permute-start | bytes 4718600 | tf_op jit(solution)/shard_map/ppermute | solution.py:39
  9.2 2.6 %copy-start.6 = (f32[768]{0:T(1024)S(1)}, f32[768]{0:T(1024)}, u32[]{:S(2)}) copy-start(f32[768]{0:T(1024)} %param.12) | copy-start | bytes 9220
  11.8 36.7 %all-to-all-start = ((f32[64,24,256]{2,1,0:T(8,128)}), f32[64,24,256]{2,1,0:T(8,128)}, u32[]{:S(2)}, u32[]{:S(2)}) async-start(f32[64,24,256]{2,1,0:T(8,128)} %bitcast.4), calls=%async_computation | async-start | bytes 3145728 | tf_op jit(solution)/shard_map/all_to_all | solution.py:408
  50.3 2.4 %copy-start.1 = (bf16[3072,768]{1,0:T(8,128)(2,1)S(1)}, bf16[3072,768]{1,0:T(8,128)(2,1)}, u32[]{:S(2)}) copy-start(bf16[3072,768]{1,0:T(8,128)(2,1)} %down_ref.1) | copy-start | bytes 14155780
  62.6 11.6 %collective-permute-start.1 = (f32[64,40,256]{2,1,0:T(8,128)S(1)}, f32[64,40,256]{2,1,0:T(8,128)S(1)}, u32[]{:S(2)}, u32[]{:S(2)}) collective-permute-start(f32[64,40,256]{2,1,0:T(8,128)S(1)} %get-tuple-element.53), channel_id=1, source_target_pairs={{0,4},{4,0},{1,5},{5,1},{2,6},{6,2},{3,7},{7,3},{8,12},{12,8},{9,1... | collective-permute-start | bytes 7864328 | tf_op jit(solution)/shard_map/ppermute | solution.py:39
  67.8 6.0 %collective-permute-start.5 = (f32[64,32,256]{2,1,0:T(8,128)S(1)}, f32[64,32,256]{2,1,0:T(8,128)S(1)}, u32[]{:S(2)}, u32[]{:S(2)}) collective-permute-start(f32[64,32,256]{2,1,0:T(8,128)S(1)} %get-tuple-element.58), channel_id=1, source_target_pairs={{0,4},{4,0},{1,5},{5,1},{2,6},{6,2},{3,7},{7,3},{8,12},{12,8},{9,1... | collective-permute-start | bytes 6291464 | tf_op jit(solution)/shard_map/ppermute | solution.py:39
  73.7 4.2 %collective-permute-start.3 = (f32[64,32,256]{2,1,0:T(8,128)S(1)}, f32[64,32,256]{2,1,0:T(8,128)S(1)}, u32[]{:S(2)}, u32[]{:S(2)}) collective-permute-start(f32[64,32,256]{2,1,0:T(8,128)S(1)} %get-tuple-element.56), channel_id=1, source_target_pairs={{0,4},{4,0},{1,5},{5,1},{2,6},{6,2},{3,7},{7,3},{8,12},{12,8},{9,1... | collective-permute-start | bytes 6291464 | tf_op jit(solution)/shard_map/ppermute | solution.py:39
  74.6 18.7 %collective-permute-start.2 = (f32[4,4,2,40,256]{4,3,2,1,0:T(8,128)S(1)}, f32[4,4,2,40,256]{4,3,2,1,0:T(8,128)S(1)}, u32[]{:S(2)}, u32[]{:S(2)}) collective-permute-start(f32[4,4,2,40,256]{4,3,2,1,0:T(8,128)S(1)} %slice.184), channel_id=1, source_target_pairs={{0,1},{1,0},{2,3},{3,2},{4,7},{5,6},{6,5},{7,4},{8,9},{9,8},{10,11... | collective-permute-start | bytes 3932168 | tf_op jit(solution)/shard_map/ppermute | solution.py:78
  75.6 3.8 %slice-start = ((s8[4718592]{0:T(1024)(128)(4,1)}), s8[4194304]{0:T(1024)(128)(4,1)S(1)}, s32[]{:S(2)}) async-start(s8[4718592]{0:T(1024)(128)(4,1)} %bitcast.42), calls=%async_computation.2 | async-start | bytes 8388608
  75.8 15.6 %collective-permute-start.6 = (f32[2,4,4,32,256]{4,3,2,1,0:T(8,128)S(1)}, f32[2,4,4,32,256]{4,3,2,1,0:T(8,128)S(1)}, u32[]{:S(2)}, u32[]{:S(2)}) collective-permute-start(f32[2,4,4,32,256]{4,3,2,1,0:T(8,128)S(1)} %bitcast.51), channel_id=1, source_target_pairs={{0,32},{1,33},{2,34},{3,35},{4,100},{5,101},{6,102},{7,103},{8,40}... | collective-permute-start | bytes 3145736 | tf_op jit(solution)/shard_map/ppermute | solution.py:78
  77.9 1.5 slice-start.1
  77.9 1.8 %copy-start.4 = (bf16[24,64,768]{2,1,0:T(8,128)(2,1)S(1)}, bf16[24,64,768]{2,1,0:T(8,128)(2,1)}, u32[]{:S(2)}) copy-start(bf16[24,64,768]{2,1,0:T(8,128)(2,1)} %param.11) | copy-start | bytes 7077892
  78.4 14.9 %collective-permute-start.4 = (f32[4,2,4,32,256]{4,3,2,1,0:T(8,128)S(1)}, f32[4,2,4,32,256]{4,3,2,1,0:T(8,128)S(1)}, u32[]{:S(2)}, u32[]{:S(2)}) collective-permute-start(f32[4,2,4,32,256]{4,3,2,1,0:T(8,128)S(1)} %slice.185), channel_id=1, source_target_pairs={{0,8},{1,9},{2,10},{3,11},{4,28},{5,29},{6,30},{7,31},{8,0},{9,1},... | collective-permute-start | bytes 3145736 | tf_op jit(solution)/shard_map/ppermute | solution.py:78
  93.8 6.6 %copy-start.5 = (f32[2,4,4,32,256]{4,3,2,1,0:T(8,128)}, f32[2,4,4,32,256]{4,3,2,1,0:T(8,128)S(1)}, u32[]{:S(2)}) copy-start(f32[2,4,4,32,256]{4,3,2,1,0:T(8,128)S(1)} %add.165) | copy-start | bytes 3145732
  93.9 19.1 %collective-permute-start.7 = (f32[4,4,1,40,256]{4,3,2,1,0:T(8,128)S(1)}, f32[4,4,1,40,256]{4,3,2,1,0:T(8,128)}, u32[]{:S(2)}, u32[]{:S(2)}) collective-permute-start(f32[4,4,1,40,256]{4,3,2,1,0:T(8,128)S(1)} %slice.147), channel_id=1, source_target_pairs={{0,3},{1,2},{2,1},{3,0},{4,5},{5,4},{6,7},{7,6},{8,11},{9,10},{10,... | collective-permute-start | bytes 1966088 | tf_op jit(solution)/shard_map/ppermute | solution.py:78
  96.9 12.2 %collective-permute-start.8 = (f32[4,1,4,32,256]{4,3,2,1,0:T(8,128)}, f32[4,1,4,32,256]{4,3,2,1,0:T(8,128)}, u32[]{:S(2)}, u32[]{:S(2)}) collective-permute-start(f32[4,1,4,32,256]{4,3,2,1,0:T(8,128)} %slice.148), channel_id=1, source_target_pairs={{0,24},{1,25},{2,26},{3,27},{4,12},{5,13},{6,14},{7,15},{8,16},{9,... | collective-permute-start | bytes 1572872 | tf_op jit(solution)/shard_map/ppermute | solution.py:78
  100.4 12.6 %collective-permute-start.9 = (f32[1,4,4,32,256]{4,3,2,1,0:T(8,128)}, f32[1,4,4,32,256]{4,3,2,1,0:T(8,128)}, u32[]{:S(2)}, u32[]{:S(2)}) collective-permute-start(f32[1,4,4,32,256]{4,3,2,1,0:T(8,128)} %slice.149), channel_id=1, source_target_pairs={{0,96},{1,97},{2,98},{3,99},{4,36},{5,37},{6,38},{7,39},{8,104},{9... | collective-permute-start | bytes 1572872 | tf_op jit(solution)/shard_map/ppermute | solution.py:78
  103.4 5.7 %collective-permute-start.10 = (f32[8,768]{1,0:T(8,128)S(1)}, f32[8,768]{1,0:T(8,128)S(1)}, u32[]{:S(2)}, u32[]{:S(2)}) collective-permute-start(f32[8,768]{1,0:T(8,128)S(1)} %get-tuple-element.69), channel_id=1, source_target_pairs={{0,4},{4,0},{1,5},{5,1},{2,6},{6,2},{3,7},{7,3},{8,12},{12,8},{9,1... | collective-permute-start | bytes 73736 | tf_op jit(solution)/shard_map/ppermute | solution.py:39
  103.4 26.5 %all-to-all-start.1 = ((f32[128,4,384]{2,1,0:T(4,128)}), f32[128,4,384]{2,1,0:T(4,128)}, u32[]{:S(2)}, u32[]{:S(2)}) async-start(f32[128,4,384]{2,1,0:T(4,128)} %reshape.251), calls=%async_computation.1 | async-start | bytes 1572864 | tf_op jit(solution)/shard_map/all_to_all | solution.py:459
  114.3 6.7 %collective-permute-start.15 = (f32[1,4,2,32,256]{4,3,2,1,0:T(8,128)S(1)}, f32[1,4,2,32,256]{4,3,2,1,0:T(8,128)S(1)}, u32[]{:S(2)}, u32[]{:S(2)}) collective-permute-start(f32[1,4,2,32,256]{4,3,2,1,0:T(8,128)S(1)} %slice.198), channel_id=1, source_target_pairs={{0,1},{1,0},{2,3},{3,2},{4,7},{5,6},{6,5},{7,4},{8,9},{9,8},{10,11... | collective-permute-start | bytes 786440 | tf_op jit(solution)/shard_map/ppermute | solution.py:78
  115.7 8.5 %collective-permute-start.11 = (f32[4,2,1,48,256]{4,3,2,1,0:T(8,128)S(1)}, f32[4,2,1,48,256]{4,3,2,1,0:T(8,128)S(1)}, u32[]{:S(2)}, u32[]{:S(2)}) collective-permute-start(f32[4,2,1,48,256]{4,3,2,1,0:T(8,128)S(1)} %pad_maximum_fusion.3), channel_id=1, source_target_pairs={{0,8},{1,9},{2,10},{3,11},{4,28},{5,29},{6,30},{7,31},{8,0},{9,1},... | collective-permute-start | bytes 1179656 | tf_op jit(solution)/shard_map/ppermute | solution.py:78
  116.9 9.4 %collective-permute-start.13 = (f32[2,1,4,32,256]{4,3,2,1,0:T(8,128)S(1)}, f32[2,1,4,32,256]{4,3,2,1,0:T(8,128)S(1)}, u32[]{:S(2)}, u32[]{:S(2)}) collective-permute-start(f32[2,1,4,32,256]{4,3,2,1,0:T(8,128)S(1)} %slice.195), channel_id=1, source_target_pairs={{0,32},{1,33},{2,34},{3,35},{4,100},{5,101},{6,102},{7,103},{8,40}... | collective-permute-start | bytes 786440 | tf_op jit(solution)/shard_map/ppermute | solution.py:78
  121.1 8.8 %collective-permute-start.16 = (f32[1,4,1,32,256]{4,3,2,1,0:T(8,128)S(1)}, f32[1,4,1,32,256]{4,3,2,1,0:T(8,128)S(1)}, u32[]{:S(2)}, u32[]{:S(2)}) collective-permute-start(f32[1,4,1,32,256]{4,3,2,1,0:T(8,128)S(1)} %slice.199), channel_id=1, source_target_pairs={{0,3},{1,2},{2,1},{3,0},{4,5},{5,4},{6,7},{7,6},{8,11},{9,10},{10,... | collective-permute-start | bytes 393224 | tf_op jit(solution)/shard_map/ppermute | solution.py:78
  124.2 8.6 %collective-permute-start.12 = (f32[4,1,1,48,256]{4,3,2,1,0:T(8,128)S(1)}, f32[4,1,1,48,256]{4,3,2,1,0:T(8,128)S(1)}, u32[]{:S(2)}, u32[]{:S(2)}) collective-permute-start(f32[4,1,1,48,256]{4,3,2,1,0:T(8,128)S(1)} %slice.193), channel_id=1, source_target_pairs={{0,24},{1,25},{2,26},{3,27},{4,12},{5,13},{6,14},{7,15},{8,16},{9,... | collective-permute-start | bytes 589832 | tf_op jit(solution)/shard_map/ppermute | solution.py:78
  126.3 6.5 %collective-permute-start.14 = (f32[1,1,4,32,256]{4,3,2,1,0:T(8,128)S(1)}, f32[1,1,4,32,256]{4,3,2,1,0:T(8,128)S(1)}, u32[]{:S(2)}, u32[]{:S(2)}) collective-permute-start(f32[1,1,4,32,256]{4,3,2,1,0:T(8,128)S(1)} %slice.196), channel_id=1, source_target_pairs={{0,96},{1,97},{2,98},{3,99},{4,36},{5,37},{6,38},{7,39},{8,104},{9... | collective-permute-start | bytes 393224 | tf_op jit(solution)/shard_map/ppermute | solution.py:78
  132.9 8.6 %collective-permute-start.17 = (f32[2,1,1,48,256]{4,3,2,1,0:T(8,128)S(1)}, f32[2,1,1,48,256]{4,3,2,1,0:T(8,128)S(1)}, u32[]{:S(2)}, u32[]{:S(2)}) collective-permute-start(f32[2,1,1,48,256]{4,3,2,1,0:T(8,128)S(1)} %slice.201), channel_id=1, source_target_pairs={{0,32},{1,33},{2,34},{3,35},{4,100},{5,101},{6,102},{7,103},{8,40}... | collective-permute-start | bytes 294920 | tf_op jit(solution)/shard_map/ppermute | solution.py:78
  133.3 4.3 %collective-permute-start.19 = (f32[1,1,2,32,256]{4,3,2,1,0:T(8,128)S(1)}, f32[1,1,2,32,256]{4,3,2,1,0:T(8,128)S(1)}, u32[]{:S(2)}, u32[]{:S(2)}) collective-permute-start(f32[1,1,2,32,256]{4,3,2,1,0:T(8,128)S(1)} %slice.206), channel_id=1, source_target_pairs={{0,1},{1,0},{2,3},{3,2},{4,7},{5,6},{6,5},{7,4},{8,9},{9,8},{10,11... | collective-permute-start | bytes 196616 | tf_op jit(solution)/shard_map/ppermute | solution.py:78
  134.0 5.0 %collective-permute-start.21 = (f32[1,2,1,32,256]{4,3,2,1,0:T(8,128)S(1)}, f32[1,2,1,32,256]{4,3,2,1,0:T(8,128)S(1)}, u32[]{:S(2)}, u32[]{:S(2)}) collective-permute-start(f32[1,2,1,32,256]{4,3,2,1,0:T(8,128)S(1)} %slice.211), channel_id=1, source_target_pairs={{0,8},{1,9},{2,10},{3,11},{4,28},{5,29},{6,30},{7,31},{8,0},{9,1},... | collective-permute-start | bytes 196616 | tf_op jit(solution)/shard_map/ppermute | solution.py:78
  137.6 7.5 %collective-permute-start.20 = (f32[1,1,1,32,256]{4,3,2,1,0:T(8,128)S(1)}, f32[1,1,1,32,256]{4,3,2,1,0:T(8,128)S(1)}, u32[]{:S(2)}, u32[]{:S(2)}) collective-permute-start(f32[1,1,1,32,256]{4,3,2,1,0:T(8,128)S(1)} %slice.208), channel_id=1, source_target_pairs={{0,3},{1,2},{2,1},{3,0},{4,5},{5,4},{6,7},{7,6},{8,11},{9,10},{10,... | collective-permute-start | bytes 98312 | tf_op jit(solution)/shard_map/ppermute | solution.py:78
  139.0 6.2 %collective-permute-start.22 = (f32[1,1,1,32,256]{4,3,2,1,0:T(8,128)S(1)}, f32[1,1,1,32,256]{4,3,2,1,0:T(8,128)S(1)}, u32[]{:S(2)}, u32[]{:S(2)}) collective-permute-start(f32[1,1,1,32,256]{4,3,2,1,0:T(8,128)S(1)} %slice.213), channel_id=1, source_target_pairs={{0,24},{1,25},{2,26},{3,27},{4,12},{5,13},{6,14},{7,15},{8,16},{9,... | collective-permute-start | bytes 98312 | tf_op jit(solution)/shard_map/ppermute | solution.py:78
  141.5 5.7 %collective-permute-start.18 = (f32[1,1,1,48,256]{4,3,2,1,0:T(8,128)S(1)}, f32[1,1,1,48,256]{4,3,2,1,0:T(8,128)S(1)}, u32[]{:S(2)}, u32[]{:S(2)}) collective-permute-start(f32[1,1,1,48,256]{4,3,2,1,0:T(8,128)S(1)} %slice.203), channel_id=1, source_target_pairs={{0,96},{1,97},{2,98},{3,99},{4,36},{5,37},{6,38},{7,39},{8,104},{9... | collective-permute-start | bytes 147464 | tf_op jit(solution)/shard_map/ppermute | solution.py:78
  147.2 10.8 %collective-permute-start.23 = (f32[112,256]{1,0:T(8,128)S(1)}, f32[112,256]{1,0:T(8,128)S(1)}, u32[]{:S(2)}, u32[]{:S(2)}) collective-permute-start(f32[112,256]{1,0:T(8,128)S(1)} %get-tuple-element.96), channel_id=1, source_target_pairs={{0,1},{1,0},{2,3},{3,2},{4,5},{5,4},{6,7},{7,6},{8,9},{9,8},{10,11... | collective-permute-start | bytes 344072 | tf_op jit(solution)/shard_map/ppermute | solution.py:44
  147.4 10.6 %collective-permute-start.24 = (f32[112,256]{1,0:T(8,128)S(1)}, f32[112,256]{1,0:T(8,128)S(1)}, u32[]{:S(2)}, u32[]{:S(2)}) collective-permute-start(f32[112,256]{1,0:T(8,128)S(1)} %get-tuple-element.96), channel_id=1, source_target_pairs={{0,2},{1,3},{2,0},{3,1},{4,6},{5,7},{6,4},{7,5},{8,10},{9,11},{10,... | collective-permute-start | bytes 344072 | tf_op jit(solution)/shard_map/ppermute | solution.py:44
  149.9 8.2 %collective-permute-start.25 = (f32[112,256]{1,0:T(8,128)S(1)}, f32[112,256]{1,0:T(8,128)S(1)}, u32[]{:S(2)}, u32[]{:S(2)}) collective-permute-start(f32[112,256]{1,0:T(8,128)S(1)} %get-tuple-element.96), channel_id=1, source_target_pairs={{0,3},{1,2},{2,1},{3,0},{4,7},{5,6},{6,5},{7,4},{8,11},{9,10},{10,... | collective-permute-start | bytes 344072 | tf_op jit(solution)/shard_map/ppermute | solution.py:44

commit v11 on v8

--- a/solution.py
+++ b/solution.py
@@ -350,7 +350,7 @@
 
 def row_update(arrived, table, accum):
     rows, width_e = table.shape
-    step = 512
+    step = 1024
     tile = pl.BlockSpec((step, width_e), lambda i: (i, 0))
     return pl.pallas_call(
         rows_kernel,
@@ -358,7 +358,7 @@
         in_specs=[pl.BlockSpec(arrived.shape, lambda i: (0, 0)), tile, tile],
         out_specs=[tile, tile],
         out_shape=[jax.ShapeDtypeStruct((rows, width_e), jnp.float32)] * 2,
-        compiler_params=pltpu.CompilerParams(vmem_limit_bytes=16 << 20),
+        compiler_params=pltpu.CompilerParams(vmem_limit_bytes=24 << 20),
         cost_estimate=cost(4 * rows * width_e * arrived.shape[0], 16 * rows * width_e),
         name="row_update",
     )(

time: 162 us -> 161 us (level)
  transfers between devices with their start and end apart: 28 -> 28, of which waited for: 9 -> 9; matrix products, arithmetic and copies ran while one was open for 10% -> 10% of each run, Pallas kernels for 30% -> 29%
where the time goes in v11:
time: 161 us; the launch traced here: 160 us
  Pallas kernels  59.7 us (37%)
  starting transfers between devices  51.8 us (32%)
  waiting for transfers between devices  19.3 us (12%)
  local copies, waits for them, and re-layouts  9.74 us (6%)
  matrix products  9.58 us (6%)
  other arithmetic  8.83 us (5%)
    ppermute x18, starting transfers between devices, halve(): lax.ppermute(lax.slice_in_dim(part, middle, None, axis=dim), DEVICES, par...  28.7 us
    pallas_call x1, Pallas kernels, forward(): pl.pallas_call(functools.partial(forward_kernel, units), grid=(hidden //...  20.5 us
    pallas_call x3, Pallas kernels, up_products(): pl.pallas_call(kernel, grid_spec=pltpu.PrefetchScalarGridSpec(num_scalar_...  18.1 us
    ppermute x18, waiting for transfers between devices, halve(): lax.ppermute(lax.slice_in_dim(part, middle, None, axis=dim), DEVICES, par...  18 us
    all_to_all x1, starting transfers between devices, per_device(): item_all = lax.all_to_all(mine, CHIPS, 0, 0, tiled=True)  11.7 us
    pallas_call x1, Pallas kernels, title_grads(): pl.pallas_call(titles_kernel, grid=(rows // step,), in_specs=[pl.BlockSpe...  11.5 us
    all_to_all x1, starting transfers between devices, per_device(): row_all = lax.all_to_all(row_part, DEVICES, 0, 0, tiled=True)  5.69 us
    dot_general x4, matrix products, contract_last(): lax.dot_general(left, right, (((1,), (1,)), ((), ())), preferred_element_...  5.16 us
  transfers between devices with their start and end apart: 28, of which 9 were waited for; matrix products, arithmetic and copies ran while one was open for 10% of the time, Pallas kernels for 29%

profile of v11, /device:TPU:0, one launch (start us, length us, event | category | flops | bytes accessed | tf_op | source)
XLA Modules:
  0.0 160.2 jit_solution(11762326307757502874)
XLA Ops:
  0.7 0.8 broadcast_select_fusion
  1.4 1.0 copy-done.1
  2.5 2.5 %segment_sums.2 = f32[1536,256]{1,0:T(8,128)} custom-call(s32[1,1024]{1,0:T(1,128)S(1)} %bitcast.42, bf16[1024,256]{1,0:T(8,128)(2,1)S(1)} %copy-done.1), custom_call_target="tpu_custom_call" | custom-call | flops 805306368 | bytes 1572864 | tf_op jit(solution)/shard_map/segment_sums/pallas_call | solution.py:108
  5.0 0.7 fusion.1
  5.8 1.1 copy.19
  6.9 2.3 %reshape.251 = f32[128,4,384]{2,1,0:T(4,128)} reshape(f32[512,384]{1,0:T(8,128)} %copy.19) | data formatting | bytes 1572864 | tf_op jit(solution)/shard_map/reshape | solution.py:416
  9.3 2.5 %segment_sums.3 = f32[1536,256]{1,0:T(8,128)} custom-call(s32[1,1024]{1,0:T(1,128)S(1)} %bitcast.41, bf16[1024,256]{1,0:T(8,128)(2,1)S(1)} %copy-done.2, f32[1536,256]{1,0:T(8,128)S(1)} %collective-permute-done.refs_0_), custom_call_target="tpu_custom_call" | custom-call | flops 805306368 | bytes 1572864 | tf_op jit(solution)/shard_map/segment_sums/pallas_call | solution.py:108
  11.8 11.7 %all-to-all-start = ((f32[64,24,256]{2,1,0:T(8,128)}), f32[64,24,256]{2,1,0:T(8,128)}, u32[]{:S(2)}, u32[]{:S(2)}) async-start(f32[64,24,256]{2,1,0:T(8,128)} %bitcast.4), calls=%async_computation | async-start | bytes 3145728 | tf_op jit(solution)/shard_map/all_to_all | solution.py:401
  23.5 20.5 %forward.1 = (bf16[1536,768]{1,0:T(8,128)(2,1)S(1)}, bf16[1536,3072]{1,0:T(8,128)(2,1)}, f32[24,3072]{1,0:T(8,128)S(1)}, f32[24,768]{1,0:T(8,128)S(1)}) custom-call(bf16[1536,768]{1,0:T(8,128)(2,1)} %bitcast.45, f32[1,768]{1,0:T(1,128)S(1)} %reshape.250.gain_ref, bf16[768,3072]{1,0:T(8,128)(2,1)} %w_ref.3), custom_call_target="tpu_custom_call" | custom-call | flops 28991029248 | bytes 18874368 | tf_op jit(solution)/shard_map/forward/pallas_call | solution.py:156
  44.1 3.8 %fusion.3.pool_ref = bf16[24,1024]{1,0:T(8,128)(2,1)S(1)} fusion(s32[1024]{0:T(1024)S(1)} %fusion.31, f32[24,768]{1,0:T(8,128)S(1)} %get-tuple-element.47, bf16[24,3072]{1,0:T(8,128)(2,1)S(1)} %convert_element_type.35.mean_ref, bf16[3072,768]{1,0:T(8,128)(2,1)} %param.14), kind=kOutput, calls=%fused_computation.8 | convolution fusion | flops 151842816 | bytes 4993024 | tf_op jit(solution)/shard_map/dot_general | solution.py:424
  48.5 1.5 reduce_sum.29.grad_ref
  50.3 3.7 %convolution_multiply_fusion.act_ref = f32[24,3072]{1,0:T(8,128)S(1)} fusion(bf16[3072,768]{1,0:T(8,128)(2,1)} %param.14, f32[24,768]{1,0:T(8,128)S(1)} %fusion.46.pool_ref), kind=kOutput, calls=%fused_computation | convolution fusion | flops 113338368 | bytes 5087232 | tf_op jit(solution)/shard_map/dot_general | solution.py:29
  53.9 7.8 %first_products.1 = (bf16[1536,3072]{1,0:T(8,128)(2,1)S(1)}, f32[64,40,256]{2,1,0:T(8,128)S(1)}, f32[64,40,256]{2,1,0:T(8,128)S(1)}) custom-call(s32[1]{0:T(128)} %bitcast.core_ref, s32[3,4]{1,0:T(4,128)S(1)} %pad_add_fusion.keep_at, s32[3,4]{1,0:T(4,128)S(1)} %pad_add_fusion.1.send_at, bf16[1536,3072]{1,0:T(8,128)(2,1)} %get-tuple-element.45.slope_ref, ...), custom_call_target="tpu_custom_call" | custom-call | flops 2415919104 | bytes 18874368 | tf_op jit(solution)/shard_map/first_products/pallas_call | solution.py:267
  62.1 5.1 %other_products.3 = (f32[64,32,256]{2,1,0:T(8,128)S(1)}, f32[64,32,256]{2,1,0:T(8,128)S(1)}) custom-call(s32[1]{0:T(128)} %bitcast.core_ref, s32[3,4]{1,0:T(4,128)S(1)} %pad_add_fusion.keep_at, s32[3,4]{1,0:T(4,128)S(1)} %pad_add_fusion.1.send_at, bf16[1536,3072]{1,0:T(8,128)(2,1)S(1)} %get-tuple-element.54.pre_ref, ...), custom_call_target="tpu_custom_call" | custom-call | flops 2415919104 | bytes 18874368 | tf_op jit(solution)/shard_map/other_products/pallas_call | solution.py:267
  67.7 5.1 %other_products.2 = (f32[64,32,256]{2,1,0:T(8,128)S(1)}, f32[64,32,256]{2,1,0:T(8,128)S(1)}) custom-call(s32[1]{0:T(128)} %bitcast.core_ref, s32[3,4]{1,0:T(4,128)S(1)} %pad_add_fusion.keep_at, s32[3,4]{1,0:T(4,128)S(1)} %pad_add_fusion.1.send_at, bf16[1536,3072]{1,0:T(8,128)(2,1)S(1)} %get-tuple-element.54.pre_ref, ...), custom_call_target="tpu_custom_call" | custom-call | flops 2415919104 | bytes 18874368 | tf_op jit(solution)/shard_map/other_products/pallas_call | solution.py:267
  73.8 1.0 collective-permute-start.2
  74.9 1.5 collective-permute-start.6
  77.6 0.9 collective-permute-start.4
  78.9 11.5 %title_grads.1 = (bf16[1536,768]{1,0:T(8,128)(2,1)}, f32[8,768]{1,0:T(8,128)S(1)}) custom-call(bf16[1536,3072]{1,0:T(8,128)(2,1)S(1)} %get-tuple-element.54.pre_ref, bf16[768,3072]{1,0:T(8,128)(2,1)S(1)} %bitcast.44, bf16[1536,768]{1,0:T(8,128)(2,1)S(1)} %bitcast.46, f32[1,768]{1,0:T(1,128)S(1)} %reshape.250.gain_ref, f32[24,768]{1,0:T(8,128)S(1)} %fusion.46.pool_ref), custom_call_target="tpu_custom_call" | custom-call | flops 7247757312 | bytes 9437184 | tf_op jit(solution)/shard_map/title_grads/pallas_call | solution.py:312
  90.5 2.0 %collective-permute-done.4 = f32[4,2,4,32,256]{4,3,2,1,0:T(8,128)S(1)} collective-permute-done((f32[4,2,4,32,256]{4,3,2,1,0:T(8,128)S(1)}, f32[4,2,4,32,256]{4,3,2,1,0:T(8,128)S(1)}, u32[]{:S(2)}, u32[]{:S(2)}) %collective-permute-start.4) | collective-permute-done | bytes 1048608 | tf_op jit(solution)/shard_map/ppermute | solution.py:78
  93.1 2.2 %collective-permute-start.7 = (f32[4,4,1,40,256]{4,3,2,1,0:T(8,128)S(1)}, f32[4,4,1,40,256]{4,3,2,1,0:T(8,128)}, u32[]{:S(2)}, u32[]{:S(2)}) collective-permute-start(f32[4,4,1,40,256]{4,3,2,1,0:T(8,128)S(1)} %slice.147), channel_id=1, source_target_pairs={{0,3},{1,2},{2,1},{3,0},{4,5},{5,4},{6,7},{7,6},{8,11},{9,10},{10,... | collective-permute-start | bytes 1966088 | tf_op jit(solution)/shard_map/ppermute | solution.py:78
  95.3 0.8 slice.148
  96.1 2.7 %collective-permute-start.8 = (f32[4,1,4,32,256]{4,3,2,1,0:T(8,128)}, f32[4,1,4,32,256]{4,3,2,1,0:T(8,128)}, u32[]{:S(2)}, u32[]{:S(2)}) collective-permute-start(f32[4,1,4,32,256]{4,3,2,1,0:T(8,128)} %slice.148), channel_id=1, source_target_pairs={{0,24},{1,25},{2,26},{3,27},{4,12},{5,13},{6,14},{7,15},{8,16},{9,... | collective-permute-start | bytes 1572872 | tf_op jit(solution)/shard_map/ppermute | solution.py:78
  98.8 0.8 slice.149
  99.6 3.0 %collective-permute-start.9 = (f32[1,4,4,32,256]{4,3,2,1,0:T(8,128)}, f32[1,4,4,32,256]{4,3,2,1,0:T(8,128)}, u32[]{:S(2)}, u32[]{:S(2)}) collective-permute-start(f32[1,4,4,32,256]{4,3,2,1,0:T(8,128)} %slice.149), channel_id=1, source_target_pairs={{0,96},{1,97},{2,98},{3,99},{4,36},{5,37},{6,38},{7,39},{8,104},{9... | collective-permute-start | bytes 1572872 | tf_op jit(solution)/shard_map/ppermute | solution.py:78
  102.6 5.7 %all-to-all-start.1 = ((f32[128,4,384]{2,1,0:T(4,128)}), f32[128,4,384]{2,1,0:T(4,128)}, u32[]{:S(2)}, u32[]{:S(2)}) async-start(f32[128,4,384]{2,1,0:T(4,128)} %reshape.251), calls=%async_computation.1 | async-start | bytes 1572864 | tf_op jit(solution)/shard_map/all_to_all | solution.py:452
  108.4 3.8 %collective-permute-done.9 = f32[1,4,4,32,256]{4,3,2,1,0:T(8,128)} collective-permute-done((f32[1,4,4,32,256]{4,3,2,1,0:T(8,128)}, f32[1,4,4,32,256]{4,3,2,1,0:T(8,128)}, u32[]{:S(2)}, u32[]{:S(2)}) %collective-permute-start.9) | collective-permute-done | bytes 524320 | tf_op jit(solution)/shard_map/ppermute | solution.py:78
  112.2 1.3 slice_add_fusion.3
  113.6 1.2 slice_add_fusion.2
  115.0 1.1 slice_add_fusion.4
  116.4 3.8 %collective-permute-done.15 = f32[1,4,2,32,256]{4,3,2,1,0:T(8,128)S(1)} collective-permute-done((f32[1,4,2,32,256]{4,3,2,1,0:T(8,128)S(1)}, f32[1,4,2,32,256]{4,3,2,1,0:T(8,128)S(1)}, u32[]{:S(2)}, u32[]{:S(2)}) %collective-permute-start.15) | collective-permute-done | bytes 262176 | tf_op jit(solution)/shard_map/ppermute | solution.py:78
  120.3 2.4 %collective-permute-start.16 = (f32[1,4,1,32,256]{4,3,2,1,0:T(8,128)S(1)}, f32[1,4,1,32,256]{4,3,2,1,0:T(8,128)S(1)}, u32[]{:S(2)}, u32[]{:S(2)}) collective-permute-start(f32[1,4,1,32,256]{4,3,2,1,0:T(8,128)S(1)} %slice.199), channel_id=1, source_target_pairs={{0,3},{1,2},{2,1},{3,0},{4,5},{5,4},{6,7},{7,6},{8,11},{9,10},{10,... | collective-permute-start | bytes 393224 | tf_op jit(solution)/shard_map/ppermute | solution.py:78
  122.7 0.7 collective-permute-done.11
  123.5 2.3 %collective-permute-start.12 = (f32[4,1,1,48,256]{4,3,2,1,0:T(8,128)S(1)}, f32[4,1,1,48,256]{4,3,2,1,0:T(8,128)S(1)}, u32[]{:S(2)}, u32[]{:S(2)}) collective-permute-start(f32[4,1,1,48,256]{4,3,2,1,0:T(8,128)S(1)} %slice.193), channel_id=1, source_target_pairs={{0,24},{1,25},{2,26},{3,27},{4,12},{5,13},{6,14},{7,15},{8,16},{9,... | collective-permute-start | bytes 589832 | tf_op jit(solution)/shard_map/ppermute | solution.py:78
  125.8 3.6 %collective-permute-start.14 = (f32[1,1,4,32,256]{4,3,2,1,0:T(8,128)S(1)}, f32[1,1,4,32,256]{4,3,2,1,0:T(8,128)S(1)}, u32[]{:S(2)}, u32[]{:S(2)}) collective-permute-start(f32[1,1,4,32,256]{4,3,2,1,0:T(8,128)S(1)} %slice.196), channel_id=1, source_target_pairs={{0,96},{1,97},{2,98},{3,99},{4,36},{5,37},{6,38},{7,39},{8,104},{9... | collective-permute-start | bytes 393224 | tf_op jit(solution)/shard_map/ppermute | solution.py:78
  129.3 2.9 %collective-permute-done.14 = f32[1,1,4,32,256]{4,3,2,1,0:T(8,128)S(1)} collective-permute-done((f32[1,1,4,32,256]{4,3,2,1,0:T(8,128)S(1)}, f32[1,1,4,32,256]{4,3,2,1,0:T(8,128)S(1)}, u32[]{:S(2)}, u32[]{:S(2)}) %collective-permute-start.14) | collective-permute-done | bytes 131104 | tf_op jit(solution)/shard_map/ppermute | solution.py:78
  133.4 1.1 collective-permute-start.21
  134.5 2.6 %collective-permute-done.19 = f32[1,1,2,32,256]{4,3,2,1,0:T(8,128)S(1)} collective-permute-done((f32[1,1,2,32,256]{4,3,2,1,0:T(8,128)S(1)}, f32[1,1,2,32,256]{4,3,2,1,0:T(8,128)S(1)}, u32[]{:S(2)}, u32[]{:S(2)}) %collective-permute-start.19) | collective-permute-done | bytes 65568 | tf_op jit(solution)/shard_map/ppermute | solution.py:78
  137.1 1.2 collective-permute-start.20
  138.4 2.0 %collective-permute-start.22 = (f32[1,1,1,32,256]{4,3,2,1,0:T(8,128)S(1)}, f32[1,1,1,32,256]{4,3,2,1,0:T(8,128)S(1)}, u32[]{:S(2)}, u32[]{:S(2)}) collective-permute-start(f32[1,1,1,32,256]{4,3,2,1,0:T(8,128)S(1)} %slice.213), channel_id=1, source_target_pairs={{0,24},{1,25},{2,26},{3,27},{4,12},{5,13},{6,14},{7,15},{8,16},{9,... | collective-permute-start | bytes 98312 | tf_op jit(solution)/shard_map/ppermute | solution.py:78
  140.4 3.5 %collective-permute-start.18 = (f32[1,1,1,48,256]{4,3,2,1,0:T(8,128)S(1)}, f32[1,1,1,48,256]{4,3,2,1,0:T(8,128)S(1)}, u32[]{:S(2)}, u32[]{:S(2)}) collective-permute-start(f32[1,1,1,48,256]{4,3,2,1,0:T(8,128)S(1)} %slice.203), channel_id=1, source_target_pairs={{0,96},{1,97},{2,98},{3,99},{4,36},{5,37},{6,38},{7,39},{8,104},{9... | collective-permute-start | bytes 147464 | tf_op jit(solution)/shard_map/ppermute | solution.py:78
  143.9 2.0 %collective-permute-done.18 = f32[1,1,1,48,256]{4,3,2,1,0:T(8,128)S(1)} collective-permute-done((f32[1,1,1,48,256]{4,3,2,1,0:T(8,128)S(1)}, f32[1,1,1,48,256]{4,3,2,1,0:T(8,128)S(1)}, u32[]{:S(2)}, u32[]{:S(2)}) %collective-permute-start.18) | collective-permute-done | bytes 49184 | tf_op jit(solution)/shard_map/ppermute | solution.py:78
  146.6 2.7 %collective-permute-start.24 = (f32[112,256]{1,0:T(8,128)S(1)}, f32[112,256]{1,0:T(8,128)S(1)}, u32[]{:S(2)}, u32[]{:S(2)}) collective-permute-start(f32[112,256]{1,0:T(8,128)S(1)} %get-tuple-element.96), channel_id=1, source_target_pairs={{0,2},{1,3},{2,0},{3,1},{4,6},{5,7},{6,4},{7,5},{8,10},{9,11},{10,... | collective-permute-start | bytes 344072 | tf_op jit(solution)/shard_map/ppermute | solution.py:44
  149.3 1.5 collective-permute-start.25
  150.8 1.4 reshape.262.arrived_ref
  152.2 4.6 %row_update.1 = (f32[2048,256]{1,0:T(8,128)}, f32[2048,256]{1,0:T(8,128)}) custom-call(f32[512,384]{1,0:T(8,128)S(1)} %reshape.262.arrived_ref, f32[2048,256]{1,0:T(8,128)} %table_ref.1, f32[2048,256]{1,0:T(8,128)} %accum_ref.1), custom_call_target="tpu_custom_call" | custom-call | flops 1073741824 | bytes 8388608 | tf_op jit(solution)/shard_map/row_update/pallas_call | solution.py:355
  158.5 1.0 convolution_add_fusion
  159.5 0.7 pad_maximum_fusion.4
  (116 shorter events, 9.2 us)
Async XLA Ops:
  0.6 49.4 %copy-start = (bf16[768,256]{1,0:T(8,128)(2,1)S(1)}, bf16[768,256]{1,0:T(8,128)(2,1)}, u32[]{:S(2)}) copy-start(bf16[768,256]{1,0:T(8,128)(2,1)} %param.15) | copy-start | bytes 1179652
  0.6 4.3 %copy-start.6 = (s32[1,512]{1,0:T(1,128)S(1)}, s32[1,512]{1,0:T(1,128)}, u32[]{:S(2)}) copy-start(s32[1,512]{1,0:T(1,128)} %param.19) | copy-start | bytes 6148
  0.7 4.3 %copy-start.7 = (s32[1024]{0:T(1024)S(1)}, s32[1024]{0:T(1024)}, u32[]{:S(2)}) copy-start(s32[1024]{0:T(1024)} %param.18) | copy-start | bytes 12292
  1.4 1.0 copy-start.1
  2.5 2.5 %copy-start.2 = (bf16[1024,256]{1,0:T(8,128)(2,1)S(1)}, bf16[1024,256]{1,0:T(8,128)(2,1)}, u32[]{:S(2)}) copy-start(bf16[1024,256]{1,0:T(8,128)(2,1)} %grad_ref.3) | copy-start | bytes 1572868
  5.0 4.3 %collective-permute-start = (f32[1536,256]{1,0:T(8,128)}, f32[1536,256]{1,0:T(8,128)S(1)}, u32[]{:S(2)}, u32[]{:S(2)}) collective-permute-start(f32[1536,256]{1,0:T(8,128)} %segment_sums.2), channel_id=1, source_target_pairs={{0,4},{4,0},{1,5},{5,1},{2,6},{6,2},{3,7},{7,3},{8,12},{12,8},{9,1... | collective-permute-start | bytes 4718600 | tf_op jit(solution)/shard_map/ppermute | solution.py:39
  9.2 2.6 %copy-start.5 = (f32[768]{0:T(1024)S(1)}, f32[768]{0:T(1024)}, u32[]{:S(2)}) copy-start(f32[768]{0:T(1024)} %param.12) | copy-start | bytes 9220
  11.8 36.7 %all-to-all-start = ((f32[64,24,256]{2,1,0:T(8,128)}), f32[64,24,256]{2,1,0:T(8,128)}, u32[]{:S(2)}, u32[]{:S(2)}) async-start(f32[64,24,256]{2,1,0:T(8,128)} %bitcast.4), calls=%async_computation | async-start | bytes 3145728 | tf_op jit(solution)/shard_map/all_to_all | solution.py:401
  61.8 11.6 %collective-permute-start.1 = (f32[64,40,256]{2,1,0:T(8,128)S(1)}, f32[64,40,256]{2,1,0:T(8,128)S(1)}, u32[]{:S(2)}, u32[]{:S(2)}) collective-permute-start(f32[64,40,256]{2,1,0:T(8,128)S(1)} %get-tuple-element.53), channel_id=1, source_target_pairs={{0,4},{4,0},{1,5},{5,1},{2,6},{6,2},{3,7},{7,3},{8,12},{12,8},{9,1... | collective-permute-start | bytes 7864328 | tf_op jit(solution)/shard_map/ppermute | solution.py:39
  67.2 5.8 %collective-permute-start.5 = (f32[64,32,256]{2,1,0:T(8,128)S(1)}, f32[64,32,256]{2,1,0:T(8,128)S(1)}, u32[]{:S(2)}, u32[]{:S(2)}) collective-permute-start(f32[64,32,256]{2,1,0:T(8,128)S(1)} %get-tuple-element.58), channel_id=1, source_target_pairs={{0,4},{4,0},{1,5},{5,1},{2,6},{6,2},{3,7},{7,3},{8,12},{12,8},{9,1... | collective-permute-start | bytes 6291464 | tf_op jit(solution)/shard_map/ppermute | solution.py:39
  72.9 4.2 %collective-permute-start.3 = (f32[64,32,256]{2,1,0:T(8,128)S(1)}, f32[64,32,256]{2,1,0:T(8,128)S(1)}, u32[]{:S(2)}, u32[]{:S(2)}) collective-permute-start(f32[64,32,256]{2,1,0:T(8,128)S(1)} %get-tuple-element.56), channel_id=1, source_target_pairs={{0,4},{4,0},{1,5},{5,1},{2,6},{6,2},{3,7},{7,3},{8,12},{12,8},{9,1... | collective-permute-start | bytes 6291464 | tf_op jit(solution)/shard_map/ppermute | solution.py:39
  73.8 18.7 %collective-permute-start.2 = (f32[4,4,2,40,256]{4,3,2,1,0:T(8,128)S(1)}, f32[4,4,2,40,256]{4,3,2,1,0:T(8,128)S(1)}, u32[]{:S(2)}, u32[]{:S(2)}) collective-permute-start(f32[4,4,2,40,256]{4,3,2,1,0:T(8,128)S(1)} %slice.184), channel_id=1, source_target_pairs={{0,1},{1,0},{2,3},{3,2},{4,7},{5,6},{6,5},{7,4},{8,9},{9,8},{10,11... | collective-permute-start | bytes 3932168 | tf_op jit(solution)/shard_map/ppermute | solution.py:78
  74.8 3.8 %slice-start = ((s8[4718592]{0:T(1024)(128)(4,1)}), s8[4194304]{0:T(1024)(128)(4,1)S(1)}, s32[]{:S(2)}) async-start(s8[4718592]{0:T(1024)(128)(4,1)} %bitcast.43), calls=%async_computation.2 | async-start | bytes 8388608
  74.9 15.5 %collective-permute-start.6 = (f32[2,4,4,32,256]{4,3,2,1,0:T(8,128)S(1)}, f32[2,4,4,32,256]{4,3,2,1,0:T(8,128)S(1)}, u32[]{:S(2)}, u32[]{:S(2)}) collective-permute-start(f32[2,4,4,32,256]{4,3,2,1,0:T(8,128)S(1)} %bitcast.52), channel_id=1, source_target_pairs={{0,32},{1,33},{2,34},{3,35},{4,100},{5,101},{6,102},{7,103},{8,40}... | collective-permute-start | bytes 3145736 | tf_op jit(solution)/shard_map/ppermute | solution.py:78
  77.1 1.5 slice-start.1
  77.1 1.8 %copy-start.3 = (bf16[24,64,768]{2,1,0:T(8,128)(2,1)S(1)}, bf16[24,64,768]{2,1,0:T(8,128)(2,1)}, u32[]{:S(2)}) copy-start(bf16[24,64,768]{2,1,0:T(8,128)(2,1)} %param.11) | copy-start | bytes 7077892
  77.6 14.9 %collective-permute-start.4 = (f32[4,2,4,32,256]{4,3,2,1,0:T(8,128)S(1)}, f32[4,2,4,32,256]{4,3,2,1,0:T(8,128)S(1)}, u32[]{:S(2)}, u32[]{:S(2)}) collective-permute-start(f32[4,2,4,32,256]{4,3,2,1,0:T(8,128)S(1)} %slice.185), channel_id=1, source_target_pairs={{0,8},{1,9},{2,10},{3,11},{4,28},{5,29},{6,30},{7,31},{8,0},{9,1},... | collective-permute-start | bytes 3145736 | tf_op jit(solution)/shard_map/ppermute | solution.py:78
  93.0 6.6 %copy-start.4 = (f32[2,4,4,32,256]{4,3,2,1,0:T(8,128)}, f32[2,4,4,32,256]{4,3,2,1,0:T(8,128)S(1)}, u32[]{:S(2)}) copy-start(f32[2,4,4,32,256]{4,3,2,1,0:T(8,128)S(1)} %add.165) | copy-start | bytes 3145732
  93.1 19.1 %collective-permute-start.7 = (f32[4,4,1,40,256]{4,3,2,1,0:T(8,128)S(1)}, f32[4,4,1,40,256]{4,3,2,1,0:T(8,128)}, u32[]{:S(2)}, u32[]{:S(2)}) collective-permute-start(f32[4,4,1,40,256]{4,3,2,1,0:T(8,128)S(1)} %slice.147), channel_id=1, source_target_pairs={{0,3},{1,2},{2,1},{3,0},{4,5},{5,4},{6,7},{7,6},{8,11},{9,10},{10,... | collective-permute-start | bytes 1966088 | tf_op jit(solution)/shard_map/ppermute | solution.py:78
  96.1 12.3 %collective-permute-start.8 = (f32[4,1,4,32,256]{4,3,2,1,0:T(8,128)}, f32[4,1,4,32,256]{4,3,2,1,0:T(8,128)}, u32[]{:S(2)}, u32[]{:S(2)}) collective-permute-start(f32[4,1,4,32,256]{4,3,2,1,0:T(8,128)} %slice.148), channel_id=1, source_target_pairs={{0,24},{1,25},{2,26},{3,27},{4,12},{5,13},{6,14},{7,15},{8,16},{9,... | collective-permute-start | bytes 1572872 | tf_op jit(solution)/shard_map/ppermute | solution.py:78
  99.6 12.6 %collective-permute-start.9 = (f32[1,4,4,32,256]{4,3,2,1,0:T(8,128)}, f32[1,4,4,32,256]{4,3,2,1,0:T(8,128)}, u32[]{:S(2)}, u32[]{:S(2)}) collective-permute-start(f32[1,4,4,32,256]{4,3,2,1,0:T(8,128)} %slice.149), channel_id=1, source_target_pairs={{0,96},{1,97},{2,98},{3,99},{4,36},{5,37},{6,38},{7,39},{8,104},{9... | collective-permute-start | bytes 1572872 | tf_op jit(solution)/shard_map/ppermute | solution.py:78
  102.6 5.7 %collective-permute-start.10 = (f32[8,768]{1,0:T(8,128)S(1)}, f32[8,768]{1,0:T(8,128)S(1)}, u32[]{:S(2)}, u32[]{:S(2)}) collective-permute-start(f32[8,768]{1,0:T(8,128)S(1)} %get-tuple-element.69), channel_id=1, source_target_pairs={{0,4},{4,0},{1,5},{5,1},{2,6},{6,2},{3,7},{7,3},{8,12},{12,8},{9,1... | collective-permute-start | bytes 73736 | tf_op jit(solution)/shard_map/ppermute | solution.py:39
  102.6 26.7 %all-to-all-start.1 = ((f32[128,4,384]{2,1,0:T(4,128)}), f32[128,4,384]{2,1,0:T(4,128)}, u32[]{:S(2)}, u32[]{:S(2)}) async-start(f32[128,4,384]{2,1,0:T(4,128)} %reshape.251), calls=%async_computation.1 | async-start | bytes 1572864 | tf_op jit(solution)/shard_map/all_to_all | solution.py:452
  113.5 6.7 %collective-permute-start.15 = (f32[1,4,2,32,256]{4,3,2,1,0:T(8,128)S(1)}, f32[1,4,2,32,256]{4,3,2,1,0:T(8,128)S(1)}, u32[]{:S(2)}, u32[]{:S(2)}) collective-permute-start(f32[1,4,2,32,256]{4,3,2,1,0:T(8,128)S(1)} %slice.198), channel_id=1, source_target_pairs={{0,1},{1,0},{2,3},{3,2},{4,7},{5,6},{6,5},{7,4},{8,9},{9,8},{10,11... | collective-permute-start | bytes 786440 | tf_op jit(solution)/shard_map/ppermute | solution.py:78
  114.9 8.5 %collective-permute-start.11 = (f32[4,2,1,48,256]{4,3,2,1,0:T(8,128)S(1)}, f32[4,2,1,48,256]{4,3,2,1,0:T(8,128)S(1)}, u32[]{:S(2)}, u32[]{:S(2)}) collective-permute-start(f32[4,2,1,48,256]{4,3,2,1,0:T(8,128)S(1)} %pad_maximum_fusion.3), channel_id=1, source_target_pairs={{0,8},{1,9},{2,10},{3,11},{4,28},{5,29},{6,30},{7,31},{8,0},{9,1},... | collective-permute-start | bytes 1179656 | tf_op jit(solution)/shard_map/ppermute | solution.py:78
  116.1 9.6 %collective-permute-start.13 = (f32[2,1,4,32,256]{4,3,2,1,0:T(8,128)S(1)}, f32[2,1,4,32,256]{4,3,2,1,0:T(8,128)S(1)}, u32[]{:S(2)}, u32[]{:S(2)}) collective-permute-start(f32[2,1,4,32,256]{4,3,2,1,0:T(8,128)S(1)} %slice.195), channel_id=1, source_target_pairs={{0,32},{1,33},{2,34},{3,35},{4,100},{5,101},{6,102},{7,103},{8,40}... | collective-permute-start | bytes 786440 | tf_op jit(solution)/shard_map/ppermute | solution.py:78
  120.3 9.1 %collective-permute-start.16 = (f32[1,4,1,32,256]{4,3,2,1,0:T(8,128)S(1)}, f32[1,4,1,32,256]{4,3,2,1,0:T(8,128)S(1)}, u32[]{:S(2)}, u32[]{:S(2)}) collective-permute-start(f32[1,4,1,32,256]{4,3,2,1,0:T(8,128)S(1)} %slice.199), channel_id=1, source_target_pairs={{0,3},{1,2},{2,1},{3,0},{4,5},{5,4},{6,7},{7,6},{8,11},{9,10},{10,... | collective-permute-start | bytes 393224 | tf_op jit(solution)/shard_map/ppermute | solution.py:78
  123.5 8.8 %collective-permute-start.12 = (f32[4,1,1,48,256]{4,3,2,1,0:T(8,128)S(1)}, f32[4,1,1,48,256]{4,3,2,1,0:T(8,128)S(1)}, u32[]{:S(2)}, u32[]{:S(2)}) collective-permute-start(f32[4,1,1,48,256]{4,3,2,1,0:T(8,128)S(1)} %slice.193), channel_id=1, source_target_pairs={{0,24},{1,25},{2,26},{3,27},{4,12},{5,13},{6,14},{7,15},{8,16},{9,... | collective-permute-start | bytes 589832 | tf_op jit(solution)/shard_map/ppermute | solution.py:78
  125.8 6.5 %collective-permute-start.14 = (f32[1,1,4,32,256]{4,3,2,1,0:T(8,128)S(1)}, f32[1,1,4,32,256]{4,3,2,1,0:T(8,128)S(1)}, u32[]{:S(2)}, u32[]{:S(2)}) collective-permute-start(f32[1,1,4,32,256]{4,3,2,1,0:T(8,128)S(1)} %slice.196), channel_id=1, source_target_pairs={{0,96},{1,97},{2,98},{3,99},{4,36},{5,37},{6,38},{7,39},{8,104},{9... | collective-permute-start | bytes 393224 | tf_op jit(solution)/shard_map/ppermute | solution.py:78
  132.3 8.0 %collective-permute-start.17 = (f32[2,1,1,48,256]{4,3,2,1,0:T(8,128)S(1)}, f32[2,1,1,48,256]{4,3,2,1,0:T(8,128)S(1)}, u32[]{:S(2)}, u32[]{:S(2)}) collective-permute-start(f32[2,1,1,48,256]{4,3,2,1,0:T(8,128)S(1)} %slice.201), channel_id=1, source_target_pairs={{0,32},{1,33},{2,34},{3,35},{4,100},{5,101},{6,102},{7,103},{8,40}... | collective-permute-start | bytes 294920 | tf_op jit(solution)/shard_map/ppermute | solution.py:78
  132.7 4.3 %collective-permute-start.19 = (f32[1,1,2,32,256]{4,3,2,1,0:T(8,128)S(1)}, f32[1,1,2,32,256]{4,3,2,1,0:T(8,128)S(1)}, u32[]{:S(2)}, u32[]{:S(2)}) collective-permute-start(f32[1,1,2,32,256]{4,3,2,1,0:T(8,128)S(1)} %slice.206), channel_id=1, source_target_pairs={{0,1},{1,0},{2,3},{3,2},{4,7},{5,6},{6,5},{7,4},{8,9},{9,8},{10,11... | collective-permute-start | bytes 196616 | tf_op jit(solution)/shard_map/ppermute | solution.py:78
  133.4 4.9 %collective-permute-start.21 = (f32[1,2,1,32,256]{4,3,2,1,0:T(8,128)S(1)}, f32[1,2,1,32,256]{4,3,2,1,0:T(8,128)S(1)}, u32[]{:S(2)}, u32[]{:S(2)}) collective-permute-start(f32[1,2,1,32,256]{4,3,2,1,0:T(8,128)S(1)} %slice.211), channel_id=1, source_target_pairs={{0,8},{1,9},{2,10},{3,11},{4,28},{5,29},{6,30},{7,31},{8,0},{9,1},... | collective-permute-start | bytes 196616 | tf_op jit(solution)/shard_map/ppermute | solution.py:78
  137.1 6.8 %collective-permute-start.20 = (f32[1,1,1,32,256]{4,3,2,1,0:T(8,128)S(1)}, f32[1,1,1,32,256]{4,3,2,1,0:T(8,128)S(1)}, u32[]{:S(2)}, u32[]{:S(2)}) collective-permute-start(f32[1,1,1,32,256]{4,3,2,1,0:T(8,128)S(1)} %slice.208), channel_id=1, source_target_pairs={{0,3},{1,2},{2,1},{3,0},{4,5},{5,4},{6,7},{7,6},{8,11},{9,10},{10,... | collective-permute-start | bytes 98312 | tf_op jit(solution)/shard_map/ppermute | solution.py:78
  138.4 5.5 %collective-permute-start.22 = (f32[1,1,1,32,256]{4,3,2,1,0:T(8,128)S(1)}, f32[1,1,1,32,256]{4,3,2,1,0:T(8,128)S(1)}, u32[]{:S(2)}, u32[]{:S(2)}) collective-permute-start(f32[1,1,1,32,256]{4,3,2,1,0:T(8,128)S(1)} %slice.213), channel_id=1, source_target_pairs={{0,24},{1,25},{2,26},{3,27},{4,12},{5,13},{6,14},{7,15},{8,16},{9,... | collective-permute-start | bytes 98312 | tf_op jit(solution)/shard_map/ppermute | solution.py:78
  140.4 5.5 %collective-permute-start.18 = (f32[1,1,1,48,256]{4,3,2,1,0:T(8,128)S(1)}, f32[1,1,1,48,256]{4,3,2,1,0:T(8,128)S(1)}, u32[]{:S(2)}, u32[]{:S(2)}) collective-permute-start(f32[1,1,1,48,256]{4,3,2,1,0:T(8,128)S(1)} %slice.203), channel_id=1, source_target_pairs={{0,96},{1,97},{2,98},{3,99},{4,36},{5,37},{6,38},{7,39},{8,104},{9... | collective-permute-start | bytes 147464 | tf_op jit(solution)/shard_map/ppermute | solution.py:78
  146.0 10.8 %collective-permute-start.23 = (f32[112,256]{1,0:T(8,128)S(1)}, f32[112,256]{1,0:T(8,128)S(1)}, u32[]{:S(2)}, u32[]{:S(2)}) collective-permute-start(f32[112,256]{1,0:T(8,128)S(1)} %get-tuple-element.96), channel_id=1, source_target_pairs={{0,1},{1,0},{2,3},{3,2},{4,5},{5,4},{6,7},{7,6},{8,9},{9,8},{10,11... | collective-permute-start | bytes 344072 | tf_op jit(solution)/shard_map/ppermute | solution.py:44
  146.6 10.1 %collective-permute-start.24 = (f32[112,256]{1,0:T(8,128)S(1)}, f32[112,256]{1,0:T(8,128)S(1)}, u32[]{:S(2)}, u32[]{:S(2)}) collective-permute-start(f32[112,256]{1,0:T(8,128)S(1)} %get-tuple-element.96), channel_id=1, source_target_pairs={{0,2},{1,3},{2,0},{3,1},{4,6},{5,7},{6,4},{7,5},{8,10},{9,11},{10,... | collective-permute-start | bytes 344072 | tf_op jit(solution)/shard_map/ppermute | solution.py:44
  149.3 7.5 %collective-permute-start.25 = (f32[112,256]{1,0:T(8,128)S(1)}, f32[112,256]{1,0:T(8,128)S(1)}, u32[]{:S(2)}, u32[]{:S(2)}) collective-permute-start(f32[112,256]{1,0:T(8,128)S(1)} %get-tuple-element.96), channel_id=1, source_target_pairs={{0,3},{1,2},{2,1},{3,0},{4,7},{5,6},{6,5},{7,4},{8,11},{9,10},{10,... | collective-permute-start | bytes 344072 | tf_op jit(solution)/shard_map/ppermute | solution.py:44
